TPU v7x, 32 devices: a whole 2x2x4 slice. The times are simulated.
32 devices in a mesh: scene: 2 (over y), row: 16 (over z, x, core).
Axes of the slice: x: 2, y: 2, z: 4, core: 2. Of those that a mesh axis runs over, the one named last changes fastest.
Arguments:
- adjoint_seed: float32 [64, 8192], P(None, ('scene', 'row')), parts along dimension 1, may hold values from -1 to 1
- radiosity: bfloat16 [64, 8192], P(None, ('scene', 'row')), parts along dimension 1, may hold values from -6 to 6
- emission: bfloat16 [64, 8192], P(None, ('scene', 'row')), parts along dimension 1, may hold values from -6 to 6
- reflectance: float32 [8192], P(('scene', 'row')), parts along dimension 0, may hold values from 0.2 to 0.9
- area: float32 [8192], P(('scene', 'row')), parts along dimension 0, may hold values from 0.5 to 4
- position: float32 [3, 8192], P(None, ('scene', 'row')), parts along dimension 1, may hold values from -4 to 4
- visibility: int32 [64, 32], P(('scene', 'row')), parts along dimension 0, may hold values from -2147483648 to 2147483647, as said below
Outputs:
- adjoint_field: float32 [64, 8192], P(None, ('scene', 'row')), parts along dimension 1
- reflect_grad: float32 [8192], P(('scene', 'row')), parts along dimension 0
There are 2 independent parts, one for each index of `scene`. A program takes and returns all parts, laid end to end along the dimension named above; each array names one. Nothing has to cross between parts.
Inputs may be any that keep to these rules, and one draw needn't show every extreme that they name: visibility is symmetric: visibility[I, J] equals visibility[J, I]; its words use all 32 bits.
All inputs are finite; a program needn't handle non-finite values.
Results may differ from a plain program's by a relative error of at most 0.0026.
Values may be sent and summed in bfloat16 or wider, within the bound.
No kernel may reach another device: no remote copies, remote signals or barrier semaphores. Data moves between devices by JAX's collectives and lax.ppermute only.
A program may use at most 64 MiB of HBM per device.

v0:
```python
import functools
import math

import jax
import jax.numpy as jnp
from jax import lax
from jax.experimental import pallas as pl
from jax.experimental.pallas import tpu as pltpu
from jax.sharding import PartitionSpec as P

TILE = 128
SWEEPS = 2
GROUP = 16
LINE = 4
EXTRA = 16
TERMS = 32
VMEM_BYTES = 48 * 1024 * 1024
GRID_BYTES = 8 * 1024 * 1024


def three_terms(value):
    high = value.astype(jnp.bfloat16).astype(jnp.float32)
    rest = value - high
    middle = rest.astype(jnp.bfloat16).astype(jnp.float32)
    return high, middle, rest - middle


def times_transpose(values, kernel):
    return lax.dot_general(
        values, kernel, (((1,), (1,)), ((), ())), preferred_element_type=jnp.float32
    )


def times(values, kernel):
    return jnp.dot(values, kernel, preferred_element_type=jnp.float32)


def finish(
    scale, total, seed_ref, area_ref, reflectance_ref, radiosity_ref, emission_ref, adjoint_ref, grad_ref
):
    adjoint = seed_ref[...] + (area_ref[...] * scale) * total
    adjoint_ref[...] = adjoint
    change = radiosity_ref[...].astype(jnp.float32) - emission_ref[...].astype(jnp.float32)
    grad_ref[...] = jnp.sum(adjoint * change, axis=0, keepdims=True) / reflectance_ref[...]


def prepare(
    scale,
    pos_ref,
    seed_ref,
    reflectance_ref,
    area_ref,
    words_ref,
    packed_ref,
    boost_ref,
    rows,
):
    rhs_count = seed_ref.shape[0]
    rows[...] = jnp.zeros_like(rows)
    for term, value in enumerate(three_terms(pos_ref[...])):
        rows[3 * term : 3 * term + 3, :] = value
    weight = area_ref[...] * scale
    for term, value in enumerate(three_terms(weight * reflectance_ref[...])):
        rows[9 + term : 10 + term, :] = value
    count = words_ref.shape[1]
    for place in range(4):
        part = (jnp.right_shift(words_ref[...], 8 * place) & 255).astype(jnp.float32)
        for local in range(words_ref.shape[0]):
            start = local * TILE
            rows[12 + place : 13 + place, start : start + count] = part[local : local + 1]
    packed_ref[:rhs_count] = (reflectance_ref[...] * seed_ref[...]).astype(jnp.bfloat16)
    packed_ref[rhs_count:] = rows[...].astype(jnp.bfloat16)
    boost_ref[...] = seed_ref[...] * (1.0 / weight)


def distance_terms(position, terms, as_rows):
    high, middle, low = three_terms(position)
    norm = jnp.sum(position * position, axis=0, keepdims=True)
    terms[...] = jnp.zeros_like(terms)
    if as_rows:
        for at, value in enumerate((high, high, high, middle, middle, low)):
            terms[3 * at : 3 * at + 3, :] = -2.0 * value
        ones, norms, norm = 21, 18, norm + 1.0
    else:
        for at, value in enumerate((high, middle, low, high, middle, high)):
            terms[3 * at : 3 * at + 3, :] = value
        ones, norms = 18, 21
    terms[ones : ones + 3, :] = jnp.ones_like(high)
    for at, value in enumerate(three_terms(norm)):
        terms[norms + at : norms + at + 1, :] = value


def shift_up(direct, group, lane):
    return 31 - jnp.where(direct, 8 * (group // 2) + lane // 16, 8 * (lane // 32) + group)


def form_blocks(line, column, at, distance, words, kernel_ref):
    t, s = at // LINE, at % LINE
    lane = lax.broadcasted_iota(jnp.int32, (8, TILE), 1)
    row_chunk = line * LINE + jnp.bitwise_xor(column, t)
    direct = row_chunk < jnp.bitwise_xor(line, s) * LINE + column
    for row_block in range(2):
        for col_block in range(2):
            word = words[s, col_block * TILE + 2 * row_chunk + row_block]
            lanes = slice(col_block * TILE, (col_block + 1) * TILE)
            for group in range(TILE // GROUP):
                first = row_block * TILE + group * GROUP
                seen = jnp.left_shift(word, shift_up(direct, group, lane)) < 0
                value = 1.0 / distance[first : first + GROUP, lanes]
                halves = [jnp.where(seen, value[:8], 0.0), jnp.where(seen, value[8:], 0.0)]
                kernel_ref[at, first : first + GROUP, lanes] = jnp.concatenate(halves).astype(
                    jnp.bfloat16
                )


def form_own(me, distance, words, kernel_ref):
    lane = lax.broadcasted_iota(jnp.int32, (TILE, TILE), 1)
    row = lax.broadcasted_iota(jnp.int32, (TILE, TILE), 0)
    for row_block in range(2):
        for col_block in range(2):
            i, j = row + row_block * TILE, lane + col_block * TILE
            low, high = jnp.minimum(i, j) % TILE, jnp.maximum(i, j) % TILE
            word = words[0, col_block * TILE + 2 * me + row_block]
            seen = jnp.left_shift(word, 31 - (8 * (low // 32) + high // 16)) < 0
            rows = slice(row_block * TILE, (row_block + 1) * TILE)
            lanes = slice(col_block * TILE, (col_block + 1) * TILE)
            value = jnp.where(seen, 1.0 / distance[rows, lanes], 0.0)
            kernel_ref[0, rows, lanes] = value.astype(jnp.bfloat16)


def grid_first(
    me_ref,
    z0_ref,
    z1_ref,
    z2_ref,
    z3_ref,
    c1_ref,
    c2_ref,
    c3_ref,
    boost_ref,
    kernel_ref,
    partial_ref,
    sent_ref,
    words_vmem,
    words,
    terms,
    row_terms,
    col_terms,
    distance,
    sem,
):
    rhs_count = boost_ref.shape[0]
    me = me_ref[0]
    line, column = me // LINE, me % LINE
    lines = (z0_ref, z1_ref, z2_ref, z3_ref)
    positions = []
    for s in range(LINE):
        extra = lines[s][rhs_count:, :].astype(jnp.float32)
        value = extra[12:16].astype(jnp.int32)
        word = value[0:1]
        for place in range(1, 4):
            word = jnp.bitwise_or(word, jnp.left_shift(value[place : place + 1], 8 * place))
        words_vmem[s : s + 1, :] = word
        positions.append(extra[0:3] + extra[3:6] + extra[6:9])
    copy = pltpu.make_async_copy(words_vmem, words, sem)
    copy.start()
    for s in range(LINE):
        distance_terms(positions[s], terms, False)
        col_terms[s] = terms[...].astype(jnp.bfloat16)
    for t, ref in enumerate((None, c1_ref, c2_ref, c3_ref)):
        distance_terms(positions[0] if ref is None else ref[...], terms, True)
        row_terms[t] = jnp.transpose(terms[...]).astype(jnp.bfloat16)
    copy.wait()

    def form(at, carry):
        distance[...] = times(row_terms[at // LINE], col_terms[at % LINE])
        form_blocks(line, column, at, distance, words, kernel_ref)
        return carry

    lax.fori_loop(1, LINE * LINE, form, 0)
    distance[...] = times(row_terms[0], col_terms[0])
    form_own(me, distance, words, kernel_ref)

    for t in range(LINE):
        held = boost_ref[...] if t == 0 else None
        for s in range(LINE):
            term = times_transpose(lines[s][:rhs_count, :], kernel_ref[LINE * t + s])
            held = term if held is None else held + term
        partial_ref[t] = held
        sent_ref[t * rhs_count : (t + 1) * rhs_count] = held.astype(jnp.bfloat16)
    sent_ref[LINE * rhs_count :] = z0_ref[rhs_count:]


def grid_middle(partial_ref, core_ref, own_ref, both_ref, sent_ref, rows):
    rhs_count = partial_ref.shape[1]
    for t in range(LINE):
        start = (t ^ 1) * rhs_count
        both = partial_ref[t] + core_ref[start : start + rhs_count].astype(jnp.float32)
        both_ref[t] = both
        sent_ref[t * rhs_count : (t + 1) * rhs_count] = both.astype(jnp.bfloat16)
    rows[...] = jnp.zeros_like(rows)
    for at, ref in enumerate((own_ref, core_ref)):
        rows[3 * at : 3 * at + 3, :] = ref[-EXTRA:, :].astype(jnp.float32)[9:12]
    sent_ref[LINE * rhs_count :] = rows[...].astype(jnp.bfloat16)


def grid_second(me_ref, kernel_ref, both_ref, own_ref, x_ref, sum_ref, sent_ref):
    line = me_ref[0] // LINE
    rhs_count = sum_ref.shape[0]
    scaled = []
    for t in range(LINE):
        terms = (own_ref, x_ref)[t // 2][LINE * rhs_count :, :].astype(jnp.float32)
        at = 3 * (t % 2)
        factor = terms[at : at + 1] + terms[at + 1 : at + 2] + terms[at + 2 : at + 3]
        start = (t ^ 2) * rhs_count
        total = both_ref[t] + x_ref[start : start + rhs_count].astype(jnp.float32)
        scaled.append((factor * total).astype(jnp.bfloat16))
    for s in range(LINE):
        held = times(scaled[0], kernel_ref[s])
        for t in range(1, LINE):
            held = held + times(scaled[t], kernel_ref[LINE * t + s])
        if s == 0:
            sum_ref[...] = held
        sent_ref[jnp.bitwise_xor(line, s)] = held.astype(jnp.bfloat16)


def grid_last(scale, me_ref, sum_ref, lines_ref, *rest):
    line = me_ref[0] // LINE
    total = sum_ref[...]
    for s in range(1, LINE):
        total = total + lines_ref[jnp.bitwise_xor(line, s)].astype(jnp.float32)
    finish(scale, total, *rest)


def on_grid(adjoint_seed, radiosity, emission, reflectance, area, position, visibility):
    rhs_count, own_width = adjoint_seed.shape
    devices = LINE * LINE
    my_index = lax.axis_index("row").astype(jnp.int32).reshape(1)
    scale = 1.0 / math.sqrt(own_width * devices)
    area = area.reshape(1, own_width)
    reflectance = reflectance.reshape(1, own_width)
    smem = pl.BlockSpec(memory_space=pltpu.SMEM)
    vmem = pl.BlockSpec(memory_space=pltpu.VMEM)
    params = pltpu.CompilerParams(vmem_limit_bytes=GRID_BYTES)
    shaped = jax.ShapeDtypeStruct
    field = (rhs_count, own_width)

    def send(value, step):
        return lax.ppermute(value, "row", [(at, at ^ step) for at in range(devices)])

    columns = [send(position, step) for step in range(1, LINE)]
    packed, boost = pl.pallas_call(
        functools.partial(prepare, scale),
        in_specs=[vmem] * 5,
        out_specs=[vmem] * 2,
        out_shape=[
            shaped((rhs_count + EXTRA, own_width), jnp.bfloat16),
            shaped(field, jnp.float32),
        ],
        scratch_shapes=[pltpu.VMEM((EXTRA, own_width), jnp.float32)],
        compiler_params=params,
        name="prepare",
    )(position, adjoint_seed, reflectance, area, visibility)
    lines = [packed] + [send(packed, LINE * step) for step in range(1, LINE)]
    sent = shaped((LINE * rhs_count + EXTRA, own_width), jnp.bfloat16)
    kernel, partial, terms = pl.pallas_call(
        grid_first,
        in_specs=[smem] + [vmem] * 8,
        out_specs=[vmem] * 3,
        out_shape=[
            shaped((devices, own_width, own_width), jnp.bfloat16),
            shaped((LINE,) + field, jnp.float32),
            sent,
        ],
        scratch_shapes=[
            pltpu.VMEM((LINE, own_width), jnp.int32),
            pltpu.SMEM((LINE, own_width), jnp.int32),
            pltpu.VMEM((TERMS, own_width), jnp.float32),
            pltpu.VMEM((LINE, own_width, TERMS), jnp.bfloat16),
            pltpu.VMEM((LINE, TERMS, own_width), jnp.bfloat16),
            pltpu.VMEM((own_width, own_width), jnp.float32),
            pltpu.SemaphoreType.DMA,
        ],
        compiler_params=params,
        name="grid_first",
    )(my_index, *lines, *columns, boost)
    both, terms = pl.pallas_call(
        grid_middle,
        in_specs=[vmem] * 3,
        out_specs=[vmem] * 2,
        out_shape=[shaped((LINE,) + field, jnp.float32), sent],
        scratch_shapes=[pltpu.VMEM((EXTRA, own_width), jnp.float32)],
        compiler_params=params,
        name="grid_middle",
    )(partial, send(terms, 1), packed)
    own_sum, sums = pl.pallas_call(
        grid_second,
        in_specs=[smem] + [vmem] * 4,
        out_specs=[vmem] * 2,
        out_shape=[shaped(field, jnp.float32), shaped((LINE,) + field, jnp.bfloat16)],
        compiler_params=params,
        name="grid_second",
    )(my_index, kernel, both, terms, send(terms, 2))
    groups = [[LINE * at + column for at in range(LINE)] for column in range(LINE)]
    sums = lax.all_to_all(sums, "row", 0, 0, axis_index_groups=groups)
    adjoint, grad = pl.pallas_call(
        functools.partial(grid_last, scale),
        in_specs=[smem] + [vmem] * 7,
        out_specs=[vmem, vmem],
        out_shape=[shaped(field, jnp.float32), shaped((1, own_width), jnp.float32)],
        compiler_params=params,
        name="grid_last",
    )(my_index, own_sum, sums, adjoint_seed, area, reflectance, radiosity, emission)
    return adjoint, grad.reshape(own_width)


def spread_rows(pos_ref, spread):
    for coord in range(3):
        for block in range(spread.shape[1]):
            line = pos_ref[coord : coord + 1, block * TILE : (block + 1) * TILE]
            spread[coord, block] = jnp.transpose(jnp.broadcast_to(line, (TILE, TILE)))


def inverse_square(spread, pos_ref, at, own_block, rows, other_block):
    lanes = pl.ds(other_block * TILE, TILE)
    total = 1.0
    for coord in range(3):
        delta = spread[coord, own_block, rows, :] - pos_ref[at, coord : coord + 1, lanes]
        total = total + delta * delta
    return 1.0 / total


def form_part(me, at, part, words_ref, pos_ref, spread, kernel_ref):
    blocks = spread.shape[1]
    lane = lax.broadcasted_iota(jnp.int32, (GROUP, TILE), 1)
    for own_block in range(blocks):
        row_block = me * blocks + own_block
        for other_block in range(blocks):
            col_block = part * blocks + other_block
            word = words_ref[own_block, col_block]
            direct = row_block < col_block
            for group in range(TILE // GROUP):
                rows = slice(group * GROUP, (group + 1) * GROUP)
                bit = jnp.where(direct, 8 * (group // 2) + lane // 16, 8 * (lane // 32) + group)
                seen = (jnp.right_shift(word, bit) & 1) != 0
                value = inverse_square(spread, pos_ref, at, own_block, rows, other_block)
                value = jnp.where(seen, value, 0.0).astype(jnp.bfloat16)
                kernel_ref[
                    at,
                    own_block * TILE + group * GROUP : own_block * TILE + (group + 1) * GROUP,
                    other_block * TILE : (other_block + 1) * TILE,
                ] = value


def form_diagonal(me, at, words_ref, pos_ref, spread, kernel_ref):
    blocks = spread.shape[1]
    lane = lax.broadcasted_iota(jnp.int32, (TILE, TILE), 1)
    row = lax.broadcasted_iota(jnp.int32, (TILE, TILE), 0)
    low, high = jnp.minimum(row, lane), jnp.maximum(row, lane)
    bit = 8 * (low // 32) + high // 16
    for block in range(blocks):
        word = words_ref[block, me * blocks + block]
        seen = (jnp.right_shift(word, bit) & 1) != 0
        value = inverse_square(spread, pos_ref, at, block, slice(0, TILE), block)
        value = jnp.where(seen, value, 0.0).astype(jnp.bfloat16)
        kernel_ref[
            at, block * TILE : (block + 1) * TILE, block * TILE : (block + 1) * TILE
        ] = value


def gather_sum(every_ref, kernel_ref):
    total = times_transpose(every_ref[0], kernel_ref[0])
    for at in range(1, every_ref.shape[0]):
        total += times_transpose(every_ref[at], kernel_ref[at])
    return total


def first_sweep(
    scale,
    me_ref,
    words_ref,
    own_pos_ref,
    pos_ref,
    every_ref,
    seed_ref,
    area_ref,
    reflectance_ref,
    kernel_ref,
    scaled_ref,
    spread,
    total,
):
    step = pl.program_id(0)
    chunk = pos_ref.shape[0]
    me = me_ref[0]

    @pl.when(step == 0)
    def _():
        spread_rows(own_pos_ref, spread)
        total[...] = jnp.zeros_like(total)

    def form(at, carry):
        form_part(me, at, step * chunk + at, words_ref, pos_ref, spread, kernel_ref)
        return carry

    lax.fori_loop(0, chunk, form, 0)

    @pl.when((me >= step * chunk) & (me < (step + 1) * chunk))
    def _():
        form_diagonal(me, me - step * chunk, words_ref, pos_ref, spread, kernel_ref)

    total[...] += gather_sum(every_ref, kernel_ref)

    @pl.when(step == pl.num_programs(0) - 1)
    def _():
        adjoint = seed_ref[...] + (area_ref[...] * scale) * total[...]
        scaled_ref[...] = (reflectance_ref[...] * adjoint).astype(jnp.bfloat16)


def last_sweep(
    scale,
    kernel_ref,
    every_ref,
    seed_ref,
    area_ref,
    reflectance_ref,
    radiosity_ref,
    emission_ref,
    adjoint_ref,
    grad_ref,
    total,
):
    step = pl.program_id(0)

    @pl.when(step == 0)
    def _():
        total[...] = jnp.zeros_like(total)

    total[...] += gather_sum(every_ref, kernel_ref)

    @pl.when(step == pl.num_programs(0) - 1)
    def _():
        finish(
            scale,
            total[...],
            seed_ref,
            area_ref,
            reflectance_ref,
            radiosity_ref,
            emission_ref,
            adjoint_ref,
            grad_ref,
        )


def whole(shape):
    return pl.BlockSpec(shape, lambda step: (0,) * len(shape))


def parts(chunk, shape):
    return pl.BlockSpec((chunk,) + shape, lambda step: (step,) + (0,) * len(shape))


def on_rows(adjoint_seed, radiosity, emission, reflectance, area, position, visibility):
    rhs_count, own_width = adjoint_seed.shape
    devices = lax.axis_size("row")
    my_index = lax.axis_index("row").astype(jnp.int32).reshape(1)
    local_blocks = own_width // TILE
    scale = 1.0 / math.sqrt(own_width * devices)
    chunk = math.gcd(devices, 16)
    area = area.reshape(1, own_width)
    reflectance = reflectance.reshape(1, own_width)
    smem = pl.BlockSpec(memory_space=pltpu.SMEM)
    params = pltpu.CompilerParams(
        dimension_semantics=("arbitrary",), vmem_limit_bytes=VMEM_BYTES
    )

    all_pos = lax.all_gather(position, "row")
    every = lax.all_gather((reflectance * adjoint_seed).astype(jnp.bfloat16), "row")
    kernel, scaled = pl.pallas_call(
        functools.partial(first_sweep, scale),
        grid=(devices // chunk,),
        in_specs=[
            smem,
            smem,
            whole((3, own_width)),
            parts(chunk, (3, own_width)),
            parts(chunk, (rhs_count, own_width)),
            whole((rhs_count, own_width)),
            whole((1, own_width)),
            whole((1, own_width)),
        ],
        out_specs=[parts(chunk, (own_width, own_width)), whole((rhs_count, own_width))],
        out_shape=[
            jax.ShapeDtypeStruct((devices, own_width, own_width), jnp.bfloat16),
            jax.ShapeDtypeStruct((rhs_count, own_width), jnp.bfloat16),
        ],
        scratch_shapes=[
            pltpu.VMEM((3, local_blocks, TILE, TILE), jnp.float32),
            pltpu.VMEM((rhs_count, own_width), jnp.float32),
        ],
        compiler_params=params,
        name="first_sweep",
    )(my_index, visibility, position, all_pos, every, adjoint_seed, area, reflectance)

    every = lax.all_gather(scaled, "row")
    adjoint, grad = pl.pallas_call(
        functools.partial(last_sweep, scale),
        grid=(devices // chunk,),
        in_specs=[
            parts(chunk, (own_width, own_width)),
            parts(chunk, (rhs_count, own_width)),
            whole((rhs_count, own_width)),
            whole((1, own_width)),
            whole((1, own_width)),
            whole((rhs_count, own_width)),
            whole((rhs_count, own_width)),
        ],
        out_specs=[whole((rhs_count, own_width)), whole((1, own_width))],
        out_shape=[
            jax.ShapeDtypeStruct((rhs_count, own_width), jnp.float32),
            jax.ShapeDtypeStruct((1, own_width), jnp.float32),
        ],
        scratch_shapes=[pltpu.VMEM((rhs_count, own_width), jnp.float32)],
        compiler_params=params,
        name="last_sweep",
    )(kernel, every, adjoint_seed, area, reflectance, radiosity, emission)
    return adjoint, grad.reshape(own_width)


def on_device(adjoint_seed, *rest):
    on_grid_shape = lax.axis_size("row") == LINE * LINE and adjoint_seed.shape[1] == 2 * TILE
    return (on_grid if on_grid_shape else on_rows)(adjoint_seed, *rest)


def solution(mesh):
    placed = (
        P(None, ("scene", "row")),
        P(None, ("scene", "row")),
        P(None, ("scene", "row")),
        P(("scene", "row")),
        P(("scene", "row")),
        P(None, ("scene", "row")),
        P(("scene", "row"), None),
    )
    return jax.shard_map(
        on_device,
        mesh=mesh,
        in_specs=placed,
        out_specs=(P(None, ("scene", "row")), P(("scene", "row"))),
        check_vma=False,
    )
```

profile of v0, /device:TPU:0, one launch (start us, length us, event | category | flops | bytes accessed | tf_op | source)
XLA Modules:
  0.0 39.2 jit_solution(13059424812733487655)
XLA Ops:
  0.6 0.0 copy-start.7
  0.6 0.0 copy-start.5
  0.7 0.0 copy-start
  0.7 0.8 %copy-done = f32[64,256]{1,0:T(8,128)S(1)} copy-done((f32[64,256]{1,0:T(8,128)S(1)}, f32[64,256]{1,0:T(8,128)}, u32[]{:S(2)}) %copy-start) | copy-done | bytes 65560
  1.5 0.0 copy-start.4
  1.5 0.7 %copy-done.4 = f32[256]{0:T(256)S(1)} copy-done((f32[256]{0:T(256)S(1)}, f32[256]{0:T(256)}, u32[]{:S(2)}) %copy-start.4) | copy-done | bytes 1048
  2.2 0.0 copy-start.6
  2.2 0.7 %copy-done.6 = f32[256]{0:T(256)S(1)} copy-done((f32[256]{0:T(256)S(1)}, f32[256]{0:T(256)}, u32[]{:S(2)}) %copy-start.6) | copy-done | bytes 1048
  2.9 0.0 copy-start.8
  2.9 0.7 %copy-done.8 = s32[2,32]{1,0:T(2,128)S(1)} copy-done((s32[2,32]{1,0:T(2,128)S(1)}, s32[2,32]{1,0:T(2,128)}, u32[]{:S(2)}) %copy-start.8) | copy-done | bytes 280
  3.5 0.0 copy-start.1
  3.5 0.0 copy-start.2
  3.5 0.0 copy-start.3
  3.5 0.7 %prepare.1 = (bf16[80,256]{1,0:T(8,128)(2,1)S(1)}, f32[64,256]{1,0:T(8,128)S(1)}) custom-call(f32[3,256]{1,0:T(4,128)} %pos_ref.1, f32[64,256]{1,0:T(8,128)S(1)} %copy-done, f32[1,256]{1,0:T(1,128)S(1)} %bitcast.4, f32[1,256]{1,0:T(1,128)S(1)} %bitcast.6, s32[2,32]{1,0:T(2,128)S(1)} %copy-done.8), custom_call_target="tpu_custom_call" | custom-call | tf_op jit(solution)/shard_map/prepare/pallas_call | solution.py:252
  4.3 5.1 %collective-permute-start.2 = (bf16[80,256]{1,0:T(8,128)(2,1)S(1)}, bf16[80,256]{1,0:T(8,128)(2,1)S(1)}, u32[]{:S(2)}, u32[]{:S(2)}) collective-permute-start(bf16[80,256]{1,0:T(8,128)(2,1)S(1)} %get-tuple-element.13.z0_ref.own_ref), channel_id=1, source_target_pairs={{0,12},{1,13},{2,14},{3,15},{4,8},{5,9},{6,10},{7,11},{8,4},{9,5},... | collective-permute-start | bytes 122888 | tf_op jit(solution)/shard_map/ppermute | solution.py:249
  9.4 0.0 collective-permute-start.1
  9.4 0.6 %collective-permute-start = (bf16[80,256]{1,0:T(8,128)(2,1)S(1)}, bf16[80,256]{1,0:T(8,128)(2,1)S(1)}, u32[]{:S(2)}, u32[]{:S(2)}) collective-permute-start(bf16[80,256]{1,0:T(8,128)(2,1)S(1)} %get-tuple-element.13.z0_ref.own_ref), channel_id=1, source_target_pairs={{0,4},{1,5},{2,6},{3,7},{4,0},{5,1},{6,2},{7,3},{8,12},{9,13},{10,... | collective-permute-start | bytes 122888 | tf_op jit(solution)/shard_map/ppermute | solution.py:249
  10.0 0.0 collective-permute-start.3
  10.1 1.7 %collective-permute-start.5 = (f32[3,256]{1,0:T(4,128)}, f32[3,256]{1,0:T(4,128)S(1)}, u32[]{:S(2)}, u32[]{:S(2)}) collective-permute-start(f32[3,256]{1,0:T(4,128)} %pos_ref.1), channel_id=1, source_target_pairs={{0,3},{1,2},{2,1},{3,0},{4,7},{5,6},{6,5},{7,4},{8,11},{9,10},{10,... | collective-permute-start | bytes 9224 | tf_op jit(solution)/shard_map/ppermute | solution.py:249
  11.8 0.0 collective-permute-done.3.c1_ref
  11.8 1.3 %collective-permute-start.4 = (f32[3,256]{1,0:T(4,128)}, f32[3,256]{1,0:T(4,128)S(1)}, u32[]{:S(2)}, u32[]{:S(2)}) collective-permute-start(f32[3,256]{1,0:T(4,128)} %pos_ref.1), channel_id=1, source_target_pairs={{0,2},{1,3},{2,0},{3,1},{4,6},{5,7},{6,4},{7,5},{8,10},{9,11},{10,... | collective-permute-start | bytes 9224 | tf_op jit(solution)/shard_map/ppermute | solution.py:249
  13.1 0.3 collective-permute-done.5.c3_ref
  13.3 2.3 %collective-permute-done.4.c2_ref = f32[3,256]{1,0:T(4,128)S(1)} collective-permute-done((f32[3,256]{1,0:T(4,128)}, f32[3,256]{1,0:T(4,128)S(1)}, u32[]{:S(2)}, u32[]{:S(2)}) %collective-permute-start.4) | collective-permute-done | bytes 3104 | tf_op jit(solution)/shard_map/ppermute | solution.py:249
  15.6 0.0 collective-permute-done.2.z3_ref
  15.6 0.0 collective-permute-done.1.z2_ref
  15.6 0.0 collective-permute-done.z1_ref
  15.6 4.5 %grid_first.1 = (bf16[16,256,256]{2,1,0:T(8,128)(2,1)S(1)}, f32[4,64,256]{2,1,0:T(8,128)S(1)}, bf16[272,256]{1,0:T(8,128)(2,1)S(1)}) custom-call(s32[1]{0:T(128)} %bitcast.me_ref, bf16[80,256]{1,0:T(8,128)(2,1)S(1)} %get-tuple-element.13.z0_ref.own_ref, bf16[80,256]{1,0:T(8,128)(2,1)S(1)} %collective-permute-done.z1_ref, ...), custom_call_target="tpu_custom_call" | custom-call | tf_op jit(solution)/shard_map/grid_first/pallas_call | solution.py:266
  20.2 0.1 collective-permute-start.6
  20.2 1.3 %collective-permute-done.6.core_ref = bf16[272,256]{1,0:T(8,128)(2,1)S(1)} collective-permute-done((bf16[272,256]{1,0:T(8,128)(2,1)S(1)}, bf16[272,256]{1,0:T(8,128)(2,1)S(1)}, u32[]{:S(2)}, u32[]{:S(2)}) %collective-permute-start.6) | collective-permute-done | bytes 139296 | tf_op jit(solution)/shard_map/ppermute | solution.py:249
  21.6 1.3 %collective-permute-start.7 = (bf16[272,256]{1,0:T(8,128)(2,1)S(1)}, bf16[272,256]{1,0:T(8,128)(2,1)S(1)}, u32[]{:S(2)}, u32[]{:S(2)}) collective-permute-start(bf16[272,256]{1,0:T(8,128)(2,1)S(1)} %get-tuple-element.19.own_ref), channel_id=1, source_target_pairs={{0,2},{1,3},{2,0},{3,1},{4,6},{5,7},{6,4},{7,5},{8,10},{9,11},{10,... | collective-permute-start | bytes 417800 | tf_op jit(solution)/shard_map/ppermute | solution.py:249
  22.9 4.5 %collective-permute-done.7.x_ref = bf16[272,256]{1,0:T(8,128)(2,1)S(1)} collective-permute-done((bf16[272,256]{1,0:T(8,128)(2,1)S(1)}, bf16[272,256]{1,0:T(8,128)(2,1)S(1)}, u32[]{:S(2)}, u32[]{:S(2)}) %collective-permute-start.7) | collective-permute-done | bytes 139296 | tf_op jit(solution)/shard_map/ppermute | solution.py:249
  27.4 0.5 %grid_second.1 = (f32[64,256]{1,0:T(8,128)S(1)}, bf16[4,64,256]{2,1,0:T(8,128)(2,1)S(1)}) custom-call(s32[1]{0:T(128)} %bitcast.me_ref, bf16[16,256,256]{2,1,0:T(8,128)(2,1)S(1)} %get-tuple-element.15.kernel_ref, f32[4,64,256]{2,1,0:T(8,128)S(1)} %get-tuple-element.18.both_ref, bf16[272,256]{1,0:T(8,128)(2,1)S(1)} %get-tuple-element.19.own_ref, ...), custom_call_target="tpu_custom_call" | custom-call | tf_op jit(solution)/shard_map/grid_second/pallas_call | solution.py:296
  27.9 10.6 %all_to_all.5.lines_ref = bf16[4,64,256]{2,1,0:T(8,128)(2,1)S(1)} all-to-all(bf16[4,64,256]{2,1,0:T(8,128)(2,1)S(1)} %get-tuple-element.21), channel_id=1, replica_groups={{0,4,8,12},{1,5,9,13},{2,6,10,14},{3,7,11,15},{16,20,24,28},{17,21,25,2..., dimensions={0} | all-to-all | bytes 262144 | tf_op jit(solution)/shard_map/all_to_all | solution.py:305
  38.5 0.0 copy-done.7
  38.5 0.0 copy-done.5
  38.5 0.0 copy-done.1
  38.5 0.0 copy-done.2
  38.5 0.0 copy-done.3
  38.5 0.7 %grid_last.1 = (f32[64,256]{1,0:T(8,128)}, f32[1,256]{1,0:T(1,128)}) custom-call(s32[1]{0:T(128)} %bitcast.me_ref, f32[64,256]{1,0:T(8,128)S(1)} %get-tuple-element.20.sum_ref, bf16[4,64,256]{2,1,0:T(8,128)(2,1)S(1)} %all_to_all.5.lines_ref, f32[64,256]{1,0:T(8,128)S(1)} %copy-done.1, f32[1,256]{1,0:T(1,128)S(1)} %bitcast.7, f32[1,256]{1,0:T(1,128)S(1)} %bitcast.5, ...), custom_call_target="tpu_custom_call" | custom-call | tf_op jit(solution)/shard_map/grid_last/pallas_call | solution.py:306
  (1 shorter events, 0.0 us)
Async XLA Ops:
  0.6 37.9 %copy-start.7 = (f32[256]{0:T(256)S(1)}, f32[256]{0:T(256)}, u32[]{:S(2)}) copy-start(f32[256]{0:T(256)} %param.11) | copy-start | bytes 3076
  0.6 37.9 %copy-start.5 = (f32[256]{0:T(256)S(1)}, f32[256]{0:T(256)}, u32[]{:S(2)}) copy-start(f32[256]{0:T(256)} %param.10) | copy-start | bytes 3076
  0.7 0.9 %copy-start = (f32[64,256]{1,0:T(8,128)S(1)}, f32[64,256]{1,0:T(8,128)}, u32[]{:S(2)}) copy-start(f32[64,256]{1,0:T(8,128)} %rest_0_.1) | copy-start | bytes 196612
  1.5 0.7 %copy-start.4 = (f32[256]{0:T(256)S(1)}, f32[256]{0:T(256)}, u32[]{:S(2)}) copy-start(f32[256]{0:T(256)} %param.10) | copy-start | bytes 3076
  2.2 0.7 %copy-start.6 = (f32[256]{0:T(256)S(1)}, f32[256]{0:T(256)}, u32[]{:S(2)}) copy-start(f32[256]{0:T(256)} %param.11) | copy-start | bytes 3076
  2.9 0.7 %copy-start.8 = (s32[2,32]{1,0:T(2,128)S(1)}, s32[2,32]{1,0:T(2,128)}, u32[]{:S(2)}) copy-start(s32[2,32]{1,0:T(2,128)} %words_ref.1) | copy-start | bytes 772
  3.5 35.0 %copy-start.1 = (f32[64,256]{1,0:T(8,128)S(1)}, f32[64,256]{1,0:T(8,128)}, u32[]{:S(2)}) copy-start(f32[64,256]{1,0:T(8,128)} %rest_0_.1) | copy-start | bytes 196612
  3.5 35.0 %copy-start.2 = (bf16[64,256]{1,0:T(8,128)(2,1)S(1)}, bf16[64,256]{1,0:T(8,128)(2,1)}, u32[]{:S(2)}) copy-start(bf16[64,256]{1,0:T(8,128)(2,1)} %rest_3_.1) | copy-start | bytes 98308
  3.5 35.0 %copy-start.3 = (bf16[64,256]{1,0:T(8,128)(2,1)S(1)}, bf16[64,256]{1,0:T(8,128)(2,1)}, u32[]{:S(2)}) copy-start(bf16[64,256]{1,0:T(8,128)(2,1)} %rest_4_.1) | copy-start | bytes 98308
  4.3 11.3 %collective-permute-start.2 = (bf16[80,256]{1,0:T(8,128)(2,1)S(1)}, bf16[80,256]{1,0:T(8,128)(2,1)S(1)}, u32[]{:S(2)}, u32[]{:S(2)}) collective-permute-start(bf16[80,256]{1,0:T(8,128)(2,1)S(1)} %get-tuple-element.13.z0_ref.own_ref), channel_id=1, source_target_pairs={{0,12},{1,13},{2,14},{3,15},{4,8},{5,9},{6,10},{7,11},{8,4},{9,5},... | collective-permute-start | bytes 122888 | tf_op jit(solution)/shard_map/ppermute | solution.py:249
  9.4 6.2 %collective-permute-start.1 = (bf16[80,256]{1,0:T(8,128)(2,1)S(1)}, bf16[80,256]{1,0:T(8,128)(2,1)S(1)}, u32[]{:S(2)}, u32[]{:S(2)}) collective-permute-start(bf16[80,256]{1,0:T(8,128)(2,1)S(1)} %get-tuple-element.13.z0_ref.own_ref), channel_id=1, source_target_pairs={{0,8},{1,9},{2,10},{3,11},{4,12},{5,13},{6,14},{7,15},{8,0},{9,1},... | collective-permute-start | bytes 122888 | tf_op jit(solution)/shard_map/ppermute | solution.py:249
  9.4 6.2 %collective-permute-start = (bf16[80,256]{1,0:T(8,128)(2,1)S(1)}, bf16[80,256]{1,0:T(8,128)(2,1)S(1)}, u32[]{:S(2)}, u32[]{:S(2)}) collective-permute-start(bf16[80,256]{1,0:T(8,128)(2,1)S(1)} %get-tuple-element.13.z0_ref.own_ref), channel_id=1, source_target_pairs={{0,4},{1,5},{2,6},{3,7},{4,0},{5,1},{6,2},{7,3},{8,12},{9,13},{10,... | collective-permute-start | bytes 122888 | tf_op jit(solution)/shard_map/ppermute | solution.py:249
  10.0 1.8 %collective-permute-start.3 = (f32[3,256]{1,0:T(4,128)}, f32[3,256]{1,0:T(4,128)S(1)}, u32[]{:S(2)}, u32[]{:S(2)}) collective-permute-start(f32[3,256]{1,0:T(4,128)} %pos_ref.1), channel_id=1, source_target_pairs={{0,1},{1,0},{2,3},{3,2},{4,5},{5,4},{6,7},{7,6},{8,9},{9,8},{10,11... | collective-permute-start | bytes 9224 | tf_op jit(solution)/shard_map/ppermute | solution.py:249
  10.1 3.3 %collective-permute-start.5 = (f32[3,256]{1,0:T(4,128)}, f32[3,256]{1,0:T(4,128)S(1)}, u32[]{:S(2)}, u32[]{:S(2)}) collective-permute-start(f32[3,256]{1,0:T(4,128)} %pos_ref.1), channel_id=1, source_target_pairs={{0,3},{1,2},{2,1},{3,0},{4,7},{5,6},{6,5},{7,4},{8,11},{9,10},{10,... | collective-permute-start | bytes 9224 | tf_op jit(solution)/shard_map/ppermute | solution.py:249
  11.8 3.8 %collective-permute-start.4 = (f32[3,256]{1,0:T(4,128)}, f32[3,256]{1,0:T(4,128)S(1)}, u32[]{:S(2)}, u32[]{:S(2)}) collective-permute-start(f32[3,256]{1,0:T(4,128)} %pos_ref.1), channel_id=1, source_target_pairs={{0,2},{1,3},{2,0},{3,1},{4,6},{5,7},{6,4},{7,5},{8,10},{9,11},{10,... | collective-permute-start | bytes 9224 | tf_op jit(solution)/shard_map/ppermute | solution.py:249
  20.2 1.4 %collective-permute-start.6 = (bf16[272,256]{1,0:T(8,128)(2,1)S(1)}, bf16[272,256]{1,0:T(8,128)(2,1)S(1)}, u32[]{:S(2)}, u32[]{:S(2)}) collective-permute-start(bf16[272,256]{1,0:T(8,128)(2,1)S(1)} %get-tuple-element.17), channel_id=1, source_target_pairs={{0,1},{1,0},{2,3},{3,2},{4,5},{5,4},{6,7},{7,6},{8,9},{9,8},{10,11... | collective-permute-start | bytes 417800 | tf_op jit(solution)/shard_map/ppermute | solution.py:249
  21.6 5.8 %collective-permute-start.7 = (bf16[272,256]{1,0:T(8,128)(2,1)S(1)}, bf16[272,256]{1,0:T(8,128)(2,1)S(1)}, u32[]{:S(2)}, u32[]{:S(2)}) collective-permute-start(bf16[272,256]{1,0:T(8,128)(2,1)S(1)} %get-tuple-element.19.own_ref), channel_id=1, source_target_pairs={{0,2},{1,3},{2,0},{3,1},{4,6},{5,7},{6,4},{7,5},{8,10},{9,11},{10,... | collective-permute-start | bytes 417800 | tf_op jit(solution)/shard_map/ppermute | solution.py:249
where the time goes:
time: 39.5 us; the launch traced here: 39.2 us
  blocking collectives  10.6 us (27%)
  starting transfers between devices  10.2 us (26%)
  waiting for transfers between devices  8.38 us (21%)
  Pallas kernels  6.45 us (16%)
  local copies, waits for them, and re-layouts  2.9 us (7%)
  between operations  0.72 us (2%)
    all_to_all x1, blocking collectives, on_grid(): sums = lax.all_to_all(sums, 'row', 0, 0, axis_index_groups=groups)  10.6 us
    ppermute x8, starting transfers between devices, send(): lax.ppermute(value, 'row', [(at, at ^ step) for at in range(devices)])  10.2 us
    ppermute x8, waiting for transfers between devices, send(): lax.ppermute(value, 'row', [(at, at ^ step) for at in range(devices)])  8.38 us
    pallas_call x1, Pallas kernels, on_grid(): pl.pallas_call(grid_first, in_specs=[smem] + [vmem] * 8, out_specs=[vmem]...  4.51 us
    unnamed x18, local copies, waits for them, and re-layouts  2.9 us
  transfers between devices with their start and end apart: 8, of which 4 were waited for; matrix products, arithmetic and copies ran while one was open for 0% of the time, Pallas kernels for 0%

commit v1 on v0

--- a/solution.py
+++ b/solution.py
@@ -44,19 +44,19 @@
     grad_ref[...] = jnp.sum(adjoint * change, axis=0, keepdims=True) / reflectance_ref[...]
 
 
-def prepare(
-    scale,
-    pos_ref,
-    seed_ref,
-    reflectance_ref,
-    area_ref,
-    words_ref,
-    packed_ref,
-    boost_ref,
-    rows,
-):
+def prepare(scale, *refs):
+    arguments, (packed_ref, boost_ref, rows, *held, sems) = refs[:5], refs[5:]
+    copies = [
+        pltpu.make_async_copy(argument, ref, sems.at[at])
+        for at, (argument, ref) in enumerate(zip(arguments, held))
+    ]
+    for copy in copies:
+        copy.start()
+    rows[...] = jnp.zeros_like(rows)
+    for copy in copies:
+        copy.wait()
+    pos_ref, words_ref, area_ref, reflectance_ref, seed_ref = held
     rhs_count = seed_ref.shape[0]
-    rows[...] = jnp.zeros_like(rows)
     for term, value in enumerate(three_terms(pos_ref[...])):
         rows[3 * term : 3 * term + 3, :] = value
     weight = area_ref[...] * scale
@@ -94,101 +94,145 @@
     return 31 - jnp.where(direct, 8 * (group // 2) + lane // 16, 8 * (lane // 32) + group)
 
 
-def form_blocks(line, column, at, distance, words, kernel_ref):
-    t, s = at // LINE, at % LINE
+def kernel_values(distance, word, shift):
+    value = pl.reciprocal(distance, approx=True)
+    seen = jnp.left_shift(word, shift) < 0
+    halves = [jnp.where(seen, value[:8], 0.0), jnp.where(seen, value[8:], 0.0)]
+    return jnp.concatenate(halves).astype(jnp.bfloat16)
+
+
+def form_block(t, s, line, column, distance, words, out_ref):
     lane = lax.broadcasted_iota(jnp.int32, (8, TILE), 1)
     row_chunk = line * LINE + jnp.bitwise_xor(column, t)
     direct = row_chunk < jnp.bitwise_xor(line, s) * LINE + column
+    for group in range(TILE // GROUP):
+        shift = shift_up(direct, group, lane)
+        for row_block in range(2):
+            first = row_block * TILE + group * GROUP
+            for col_block in range(2):
+                word = words[s, col_block * TILE + 2 * row_chunk + row_block]
+                lanes = slice(col_block * TILE, (col_block + 1) * TILE)
+                out_ref[first : first + GROUP, lanes] = kernel_values(
+                    distance[first : first + GROUP, lanes], word, shift
+                )
+
+
+def form_own(me, distance, words, out_ref):
+    lane = lax.broadcasted_iota(jnp.int32, (8, TILE), 1)
+    row = lax.broadcasted_iota(jnp.int32, (8, TILE), 0)
     for row_block in range(2):
         for col_block in range(2):
-            word = words[s, col_block * TILE + 2 * row_chunk + row_block]
+            word = words[0, col_block * TILE + 2 * me + row_block]
             lanes = slice(col_block * TILE, (col_block + 1) * TILE)
             for group in range(TILE // GROUP):
                 first = row_block * TILE + group * GROUP
-                seen = jnp.left_shift(word, shift_up(direct, group, lane)) < 0
-                value = 1.0 / distance[first : first + GROUP, lanes]
-                halves = [jnp.where(seen, value[:8], 0.0), jnp.where(seen, value[8:], 0.0)]
-                kernel_ref[at, first : first + GROUP, lanes] = jnp.concatenate(halves).astype(
+                halves = []
+                for half in range(first, first + GROUP, 8):
+                    i, j = row + half, lane + col_block * TILE
+                    low, high = jnp.minimum(i, j) % TILE, jnp.maximum(i, j) % TILE
+                    seen = jnp.left_shift(word, 31 - (8 * (low // 32) + high // 16)) < 0
+                    value = pl.reciprocal(distance[half : half + 8, lanes], approx=True)
+                    halves.append(jnp.where(seen, value, 0.0))
+                out_ref[first : first + GROUP, lanes] = jnp.concatenate(halves).astype(
                     jnp.bfloat16
                 )
 
 
-def form_own(me, distance, words, kernel_ref):
-    lane = lax.broadcasted_iota(jnp.int32, (TILE, TILE), 1)
-    row = lax.broadcasted_iota(jnp.int32, (TILE, TILE), 0)
-    for row_block in range(2):
-        for col_block in range(2):
-            i, j = row + row_block * TILE, lane + col_block * TILE
-            low, high = jnp.minimum(i, j) % TILE, jnp.maximum(i, j) % TILE
-            word = words[0, col_block * TILE + 2 * me + row_block]
-            seen = jnp.left_shift(word, 31 - (8 * (low // 32) + high // 16)) < 0
-            rows = slice(row_block * TILE, (row_block + 1) * TILE)
-            lanes = slice(col_block * TILE, (col_block + 1) * TILE)
-            value = jnp.where(seen, 1.0 / distance[rows, lanes], 0.0)
-            kernel_ref[0, rows, lanes] = value.astype(jnp.bfloat16)
-
-
-def grid_first(
+def read_extra(ref, rhs_count):
+    extra = ref[rhs_count:, :].astype(jnp.float32)
+    value = extra[12:16].astype(jnp.int32)
+    word = value[0:1]
+    for place in range(1, 4):
+        word = jnp.bitwise_or(word, jnp.left_shift(value[place : place + 1], 8 * place))
+    return extra[0:3] + extra[3:6] + extra[6:9], word
+
+
+def grid_near(
     me_ref,
-    z0_ref,
+    own_ref,
+    core_ref,
+    pair_ref,
+    boost_ref,
+    kernel_ref,
+    partial_ref,
+    row_terms,
+    words_vmem,
+    words,
+    terms,
+    distance,
+    sem,
+):
+    rhs_count = boost_ref.shape[0]
+    me = me_ref[0]
+    line, column = me // LINE, me % LINE
+    position, words_vmem[0:1, :] = read_extra(own_ref, rhs_count)
+    copy = pltpu.make_async_copy(words_vmem, words, sem)
+    copy.start()
+    distance_terms(position, terms, False)
+    col_terms = terms[...].astype(jnp.bfloat16)
+    for t, value in enumerate((position, core_ref[...], pair_ref[0], pair_ref[1])):
+        distance_terms(value, terms, True)
+        row_terms[t] = jnp.transpose(terms[...]).astype(jnp.bfloat16)
+    copy.wait()
+    own = own_ref[:rhs_count, :]
+    for t in range(LINE):
+        distance[...] = times(row_terms[t], col_terms)
+        if t == 0:
+            form_own(me, distance, words, kernel_ref.at[t])
+        else:
+            form_block(t, 0, line, column, distance, words, kernel_ref.at[t])
+        held = times_transpose(own, kernel_ref[t])
+        partial_ref[t] = held + boost_ref[...] if t == 0 else held
+
+
+def grid_far(
+    me_ref,
     z1_ref,
     z2_ref,
     z3_ref,
-    c1_ref,
-    c2_ref,
-    c3_ref,
-    boost_ref,
+    own_ref,
+    near_ref,
+    row_terms,
     kernel_ref,
     partial_ref,
     sent_ref,
     words_vmem,
     words,
     terms,
-    row_terms,
     col_terms,
     distance,
     sem,
 ):
-    rhs_count = boost_ref.shape[0]
+    rhs_count = near_ref.shape[1]
     me = me_ref[0]
     line, column = me // LINE, me % LINE
-    lines = (z0_ref, z1_ref, z2_ref, z3_ref)
+    lines = (z1_ref, z2_ref, z3_ref)
     positions = []
-    for s in range(LINE):
-        extra = lines[s][rhs_count:, :].astype(jnp.float32)
-        value = extra[12:16].astype(jnp.int32)
-        word = value[0:1]
-        for place in range(1, 4):
-            word = jnp.bitwise_or(word, jnp.left_shift(value[place : place + 1], 8 * place))
-        words_vmem[s : s + 1, :] = word
-        positions.append(extra[0:3] + extra[3:6] + extra[6:9])
+    for s, ref in enumerate(lines, 1):
+        position, words_vmem[s : s + 1, :] = read_extra(ref, rhs_count)
+        positions.append(position)
     copy = pltpu.make_async_copy(words_vmem, words, sem)
     copy.start()
-    for s in range(LINE):
-        distance_terms(positions[s], terms, False)
+    for s, position in enumerate(positions):
+        distance_terms(position, terms, False)
         col_terms[s] = terms[...].astype(jnp.bfloat16)
-    for t, ref in enumerate((None, c1_ref, c2_ref, c3_ref)):
-        distance_terms(positions[0] if ref is None else ref[...], terms, True)
-        row_terms[t] = jnp.transpose(terms[...]).astype(jnp.bfloat16)
     copy.wait()
 
-    def form(at, carry):
-        distance[...] = times(row_terms[at // LINE], col_terms[at % LINE])
-        form_blocks(line, column, at, distance, words, kernel_ref)
+    def form(t, carry):
+        held = near_ref[t]
+        for s in range(1, LINE):
+            at = (LINE - 1) * t + s - 1
+            slot = distance.at[s - 1]
+            slot[...] = times(row_terms[t], col_terms[s - 1])
+            form_block(t, s, line, column, slot, words, kernel_ref.at[at])
+            held += times_transpose(lines[s - 1][:rhs_count, :], kernel_ref[at])
+        partial_ref[t] = held
+        start = pl.multiple_of(t * rhs_count, rhs_count)
+        sent_ref[pl.ds(start, rhs_count), :] = held.astype(jnp.bfloat16)
         return carry
 
-    lax.fori_loop(1, LINE * LINE, form, 0)
-    distance[...] = times(row_terms[0], col_terms[0])
-    form_own(me, distance, words, kernel_ref)
-
-    for t in range(LINE):
-        held = boost_ref[...] if t == 0 else None
-        for s in range(LINE):
-            term = times_transpose(lines[s][:rhs_count, :], kernel_ref[LINE * t + s])
-            held = term if held is None else held + term
-        partial_ref[t] = held
-        sent_ref[t * rhs_count : (t + 1) * rhs_count] = held.astype(jnp.bfloat16)
-    sent_ref[LINE * rhs_count :] = z0_ref[rhs_count:]
+    lax.fori_loop(0, LINE, form, 0)
+    sent_ref[LINE * rhs_count :] = own_ref[rhs_count:]
 
 
 def grid_middle(partial_ref, core_ref, own_ref, both_ref, sent_ref, rows):
@@ -204,9 +248,10 @@
     sent_ref[LINE * rhs_count :] = rows[...].astype(jnp.bfloat16)
 
 
-def grid_second(me_ref, kernel_ref, both_ref, own_ref, x_ref, sum_ref, sent_ref):
-    line = me_ref[0] // LINE
-    rhs_count = sum_ref.shape[0]
+def grid_second(
+    near_ref, far_ref, both_ref, own_ref, x_ref, q0_ref, q1_ref, q2_ref, q3_ref
+):
+    rhs_count = q0_ref.shape[0]
     scaled = []
     for t in range(LINE):
         terms = (own_ref, x_ref)[t // 2][LINE * rhs_count :, :].astype(jnp.float32)
@@ -215,20 +260,19 @@
         start = (t ^ 2) * rhs_count
         total = both_ref[t] + x_ref[start : start + rhs_count].astype(jnp.float32)
         scaled.append((factor * total).astype(jnp.bfloat16))
-    for s in range(LINE):
-        held = times(scaled[0], kernel_ref[s])
-        for t in range(1, LINE):
-            held = held + times(scaled[t], kernel_ref[LINE * t + s])
-        if s == 0:
-            sum_ref[...] = held
-        sent_ref[jnp.bitwise_xor(line, s)] = held.astype(jnp.bfloat16)
-
-
-def grid_last(scale, me_ref, sum_ref, lines_ref, *rest):
-    line = me_ref[0] // LINE
-    total = sum_ref[...]
-    for s in range(1, LINE):
-        total = total + lines_ref[jnp.bitwise_xor(line, s)].astype(jnp.float32)
+    for s, out_ref in enumerate((q0_ref, q1_ref, q2_ref, q3_ref)):
+        held = None
+        for t in range(LINE):
+            kernel = near_ref[t] if s == 0 else far_ref[(LINE - 1) * t + s - 1]
+            term = times(scaled[t], kernel)
+            held = term if held is None else held + term
+        out_ref[...] = held.astype(out_ref.dtype)
+
+
+def grid_last(scale, q0_ref, q1_ref, q2_ref, q3_ref, *rest):
+    total = q0_ref[...]
+    for ref in (q1_ref, q2_ref, q3_ref):
+        total = total + ref[...].astype(jnp.float32)
     finish(scale, total, *rest)
 
 
@@ -248,42 +292,62 @@
     def send(value, step):
         return lax.ppermute(value, "row", [(at, at ^ step) for at in range(devices)])
 
-    columns = [send(position, step) for step in range(1, LINE)]
+    core = send(position, 1)
+    arguments = (position, visibility, area, reflectance, adjoint_seed)
     packed, boost = pl.pallas_call(
         functools.partial(prepare, scale),
-        in_specs=[vmem] * 5,
+        in_specs=[pl.BlockSpec(memory_space=pltpu.HBM)] * 5,
         out_specs=[vmem] * 2,
         out_shape=[
             shaped((rhs_count + EXTRA, own_width), jnp.bfloat16),
             shaped(field, jnp.float32),
         ],
-        scratch_shapes=[pltpu.VMEM((EXTRA, own_width), jnp.float32)],
+        scratch_shapes=[pltpu.VMEM((EXTRA, own_width), jnp.float32)]
+        + [pltpu.VMEM(value.shape, value.dtype) for value in arguments]
+        + [pltpu.SemaphoreType.DMA((5,))],
         compiler_params=params,
         name="prepare",
-    )(position, adjoint_seed, reflectance, area, visibility)
-    lines = [packed] + [send(packed, LINE * step) for step in range(1, LINE)]
-    sent = shaped((LINE * rhs_count + EXTRA, own_width), jnp.bfloat16)
-    kernel, partial, terms = pl.pallas_call(
-        grid_first,
-        in_specs=[smem] + [vmem] * 8,
+    )(*[pltpu.with_memory_space_constraint(value, pltpu.HBM) for value in arguments])
+    pair = send(jnp.stack([position, core]), 2)
+    lines = [send(packed, LINE * step) for step in range(1, LINE)]
+    words_scratch = [
+        pltpu.VMEM((LINE, own_width), jnp.int32),
+        pltpu.SMEM((LINE, own_width), jnp.int32),
+        pltpu.VMEM((TERMS, own_width), jnp.float32),
+    ]
+    near, partial, row_terms = pl.pallas_call(
+        grid_near,
+        in_specs=[smem] + [vmem] * 4,
         out_specs=[vmem] * 3,
         out_shape=[
-            shaped((devices, own_width, own_width), jnp.bfloat16),
+            shaped((LINE, own_width, own_width), jnp.bfloat16),
+            shaped((LINE,) + field, jnp.float32),
+            shaped((LINE, own_width, TERMS), jnp.bfloat16),
+        ],
+        scratch_shapes=words_scratch
+        + [pltpu.VMEM((own_width, own_width), jnp.float32), pltpu.SemaphoreType.DMA],
+        compiler_params=params,
+        name="grid_near",
+    )(my_index, packed, core, pair, boost)
+    sent = shaped((LINE * rhs_count + EXTRA, own_width), jnp.bfloat16)
+    far, partial, terms = pl.pallas_call(
+        grid_far,
+        in_specs=[smem] + [vmem] * 6,
+        out_specs=[vmem] * 3,
+        out_shape=[
+            shaped((devices - LINE, own_width, own_width), jnp.bfloat16),
             shaped((LINE,) + field, jnp.float32),
             sent,
         ],
-        scratch_shapes=[
-            pltpu.VMEM((LINE, own_width), jnp.int32),
-            pltpu.SMEM((LINE, own_width), jnp.int32),
-            pltpu.VMEM((TERMS, own_width), jnp.float32),
-            pltpu.VMEM((LINE, own_width, TERMS), jnp.bfloat16),
-            pltpu.VMEM((LINE, TERMS, own_width), jnp.bfloat16),
-            pltpu.VMEM((own_width, own_width), jnp.float32),
+        scratch_shapes=words_scratch
+        + [
+            pltpu.VMEM((LINE - 1, TERMS, own_width), jnp.bfloat16),
+            pltpu.VMEM((LINE - 1, own_width, own_width), jnp.float32),
             pltpu.SemaphoreType.DMA,
         ],
         compiler_params=params,
-        name="grid_first",
-    )(my_index, *lines, *columns, boost)
+        name="grid_far",
+    )(my_index, *lines, packed, partial, row_terms)
     both, terms = pl.pallas_call(
         grid_middle,
         in_specs=[vmem] * 3,
@@ -293,24 +357,23 @@
         compiler_params=params,
         name="grid_middle",
     )(partial, send(terms, 1), packed)
-    own_sum, sums = pl.pallas_call(
+    sums = pl.pallas_call(
         grid_second,
-        in_specs=[smem] + [vmem] * 4,
-        out_specs=[vmem] * 2,
-        out_shape=[shaped(field, jnp.float32), shaped((LINE,) + field, jnp.bfloat16)],
+        in_specs=[vmem] * 5,
+        out_specs=[vmem] * LINE,
+        out_shape=[shaped(field, jnp.float32)] + [shaped(field, jnp.bfloat16)] * (LINE - 1),
         compiler_params=params,
         name="grid_second",
-    )(my_index, kernel, both, terms, send(terms, 2))
-    groups = [[LINE * at + column for at in range(LINE)] for column in range(LINE)]
-    sums = lax.all_to_all(sums, "row", 0, 0, axis_index_groups=groups)
+    )(near, far, both, terms, send(terms, 2))
+    sums = [sums[0]] + [send(sums[step], LINE * step) for step in range(1, LINE)]
     adjoint, grad = pl.pallas_call(
         functools.partial(grid_last, scale),
-        in_specs=[smem] + [vmem] * 7,
+        in_specs=[vmem] * 9,
         out_specs=[vmem, vmem],
         out_shape=[shaped(field, jnp.float32), shaped((1, own_width), jnp.float32)],
         compiler_params=params,
         name="grid_last",
-    )(my_index, own_sum, sums, adjoint_seed, area, reflectance, radiosity, emission)
+    )(*sums, adjoint_seed, area, reflectance, radiosity, emission)
     return adjoint, grad.reshape(own_width)
 
 

time: 39.5 us -> 34.9 us (0.88)
  blocking collectives: 10.6 us -> 0 us
  waiting for transfers between devices: 8.38 us -> 13.1 us
  starting transfers between devices: 10.2 us -> 13.7 us
  local copies, waits for them, and re-layouts: 2.9 us -> 0.03 us
  other arithmetic: 0 us -> 0.69 us
    all_to_all x1 -> x0, blocking collectives: 10.6 us -> none  [on_grid(): sums = lax.all_to_all(sums, 'row', 0, 0, axis_index_groups=groups)]
    ppermute x8 -> x10, waiting for transfers between devices: 8.38 us -> 13.1 us  [send(): lax.ppermute(value, 'row', [(at, at ^ step) for at in range(devices)])]
    ppermute x8 -> x10, starting transfers between devices: 10.2 us -> 13.7 us  [send(): lax.ppermute(value, 'row', [(at, at ^ step) for at in range(devices)])]
    unnamed x18 -> x10, local copies, waits for them, and re-layouts: 2.9 us -> 0.03 us
    another operation x0 -> x1, other arithmetic: none -> 0.69 us  [on_grid(): pair = send(jnp.stack([position, core]), 2)]
    pallas_call x4 -> x5, Pallas kernels: 6.41 us -> 6.36 us  [the longest x1 2.79 us: on_grid(): pl.pallas_call(grid_far, in_specs=[smem] + [vmem] * 6, out_specs=[vmem] *...]
  transfers between devices with their start and end apart: 8 -> 10, of which waited for: 4 -> 5; matrix products, arithmetic and copies ran while one was open for 0% -> 2% of each run, Pallas kernels for 0% -> 7%
where the time goes in v1:
time: 34.9 us; the launch traced here: 34.7 us
  starting transfers between devices  13.7 us (39%)
  waiting for transfers between devices  13.1 us (38%)
  Pallas kernels  6.4 us (18%)
  between operations  0.76 us (2%)
  other arithmetic  0.69 us (2%)
    ppermute x10, starting transfers between devices, send(): lax.ppermute(value, 'row', [(at, at ^ step) for at in range(devices)])  13.7 us
    ppermute x10, waiting for transfers between devices, send(): lax.ppermute(value, 'row', [(at, at ^ step) for at in range(devices)])  13.1 us
    pallas_call x1, Pallas kernels, on_grid(): pl.pallas_call(grid_far, in_specs=[smem] + [vmem] * 6, out_specs=[vmem] *...  2.79 us
    pallas_call x1, Pallas kernels, on_grid(): pl.pallas_call(grid_near, in_specs=[smem] + [vmem] * 4, out_specs=[vmem]...  1.45 us
    pallas_call x1, Pallas kernels, on_grid(): pl.pallas_call(functools.partial(prepare, scale), in_specs=[pl.BlockSpec(...  0.97 us
  transfers between devices with their start and end apart: 10, of which 5 were waited for; matrix products, arithmetic and copies ran while one was open for 2% of the time, Pallas kernels for 7%

profile of v1, /device:TPU:0, one launch (start us, length us, event | category | flops | bytes accessed | tf_op | source)
XLA Modules:
  0.0 34.7 jit_solution(1338896906765901394)
XLA Ops:
  0.6 0.5 %collective-permute-start = (f32[3,256]{1,0:T(4,128)}, f32[3,256]{1,0:T(4,128)S(1)}, u32[]{:S(2)}, u32[]{:S(2)}) collective-permute-start(f32[3,256]{1,0:T(4,128)} %refs_0_.1), channel_id=1, source_target_pairs={{0,1},{1,0},{2,3},{3,2},{4,5},{5,4},{6,7},{7,6},{8,9},{9,8},{10,11... | collective-permute-start | bytes 9224 | tf_op jit(solution)/shard_map/ppermute | solution.py:293
  1.1 1.0 %prepare.1 = (bf16[80,256]{1,0:T(8,128)(2,1)S(1)}, f32[64,256]{1,0:T(8,128)S(1)}) custom-call(f32[3,256]{1,0:T(4,128)} %refs_0_.1, s32[2,32]{1,0:T(2,128)} %refs_1_.1, f32[1,256]{1,0:T(1,128)} %bitcast.7, f32[1,256]{1,0:T(1,128)} %bitcast.9, f32[64,256]{1,0:T(8,128)} %rest_0_.1), custom_call_target="tpu_custom_call" | custom-call | tf_op jit(solution)/shard_map/prepare/pallas_call | solution.py:297
  2.1 4.7 %collective-permute-start.4 = (bf16[80,256]{1,0:T(8,128)(2,1)S(1)}, bf16[80,256]{1,0:T(8,128)(2,1)S(1)}, u32[]{:S(2)}, u32[]{:S(2)}) collective-permute-start(bf16[80,256]{1,0:T(8,128)(2,1)S(1)} %get-tuple-element.18.own_ref), channel_id=1, source_target_pairs={{0,12},{1,13},{2,14},{3,15},{4,8},{5,9},{6,10},{7,11},{8,4},{9,5},... | collective-permute-start | bytes 122888 | tf_op jit(solution)/shard_map/ppermute | solution.py:293
  6.8 0.0 collective-permute-start.3
  6.8 0.6 %collective-permute-start.2 = (bf16[80,256]{1,0:T(8,128)(2,1)S(1)}, bf16[80,256]{1,0:T(8,128)(2,1)S(1)}, u32[]{:S(2)}, u32[]{:S(2)}) collective-permute-start(bf16[80,256]{1,0:T(8,128)(2,1)S(1)} %get-tuple-element.18.own_ref), channel_id=1, source_target_pairs={{0,4},{1,5},{2,6},{3,7},{4,0},{5,1},{6,2},{7,3},{8,12},{9,13},{10,... | collective-permute-start | bytes 122888 | tf_op jit(solution)/shard_map/ppermute | solution.py:293
  7.5 0.0 collective-permute-done.core_ref
  7.5 0.7 %pad_maximum_fusion = f32[2,3,256]{2,1,0:T(4,128)S(1)} fusion(f32[1,3,256]{2,1,0:T(4,128)S(1)} %bitcast.6, f32[1,3,256]{2,1,0:T(4,128)} %bitcast.11), kind=kLoop, calls=%fused_computation | loop fusion | flops 1536 | bytes 12288 | tf_op jit(solution)/shard_map/stack | solution.py:311
  8.1 1.6 %collective-permute-start.1 = (f32[2,3,256]{2,1,0:T(4,128)S(1)}, f32[2,3,256]{2,1,0:T(4,128)S(1)}, u32[]{:S(2)}, u32[]{:S(2)}) collective-permute-start(f32[2,3,256]{2,1,0:T(4,128)S(1)} %pad_maximum_fusion), channel_id=1, source_target_pairs={{0,2},{1,3},{2,0},{3,1},{4,6},{5,7},{6,4},{7,5},{8,10},{9,11},{10,... | collective-permute-start | bytes 18440 | tf_op jit(solution)/shard_map/ppermute | solution.py:293
  9.8 2.0 %collective-permute-done.1.pair_ref = f32[2,3,256]{2,1,0:T(4,128)S(1)} collective-permute-done((f32[2,3,256]{2,1,0:T(4,128)S(1)}, f32[2,3,256]{2,1,0:T(4,128)S(1)}, u32[]{:S(2)}, u32[]{:S(2)}) %collective-permute-start.1) | collective-permute-done | bytes 6176 | tf_op jit(solution)/shard_map/ppermute | solution.py:293
  11.8 1.5 %grid_near.1 = (bf16[4,256,256]{2,1,0:T(8,128)(2,1)S(1)}, f32[4,64,256]{2,1,0:T(8,128)S(1)}, bf16[4,256,32]{2,1,0:T(8,128)(2,1)S(1)}) custom-call(s32[1]{0:T(128)} %bitcast.me_ref, bf16[80,256]{1,0:T(8,128)(2,1)S(1)} %get-tuple-element.18.own_ref, f32[3,256]{1,0:T(4,128)S(1)} %collective-permute-done.core_ref, ...), custom_call_target="tpu_custom_call" | custom-call | tf_op jit(solution)/shard_map/grid_near/pallas_call | solution.py:318
  13.3 0.0 collective-permute-done.4.z3_ref
  13.3 0.0 collective-permute-done.3.z2_ref
  13.3 0.0 collective-permute-done.2.z1_ref
  13.3 2.8 %grid_far.1 = (bf16[12,256,256]{2,1,0:T(8,128)(2,1)S(1)}, f32[4,64,256]{2,1,0:T(8,128)S(1)}, bf16[272,256]{1,0:T(8,128)(2,1)S(1)}) custom-call(s32[1]{0:T(128)} %bitcast.me_ref, bf16[80,256]{1,0:T(8,128)(2,1)S(1)} %collective-permute-done.2.z1_ref, bf16[80,256]{1,0:T(8,128)(2,1)S(1)} %collective-permute-done.3.z2_ref, ...), custom_call_target="tpu_custom_call" | custom-call | tf_op jit(solution)/shard_map/grid_far/pallas_call | solution.py:333
  16.1 0.0 copy-start
  16.1 0.0 copy-start.1
  16.1 0.0 copy-start.2
  16.1 0.0 copy-start.3
  16.1 0.0 copy-start.4
  16.1 0.1 collective-permute-start.5
  16.2 1.3 %collective-permute-done.5.core_ref = bf16[272,256]{1,0:T(8,128)(2,1)S(1)} collective-permute-done((bf16[272,256]{1,0:T(8,128)(2,1)S(1)}, bf16[272,256]{1,0:T(8,128)(2,1)S(1)}, u32[]{:S(2)}, u32[]{:S(2)}) %collective-permute-start.5) | collective-permute-done | bytes 139296 | tf_op jit(solution)/shard_map/ppermute | solution.py:293
  17.6 1.7 %collective-permute-start.6 = (bf16[272,256]{1,0:T(8,128)(2,1)S(1)}, bf16[272,256]{1,0:T(8,128)(2,1)S(1)}, u32[]{:S(2)}, u32[]{:S(2)}) collective-permute-start(bf16[272,256]{1,0:T(8,128)(2,1)S(1)} %get-tuple-element.27.own_ref), channel_id=1, source_target_pairs={{0,2},{1,3},{2,0},{3,1},{4,6},{5,7},{6,4},{7,5},{8,10},{9,11},{10,... | collective-permute-start | bytes 417800 | tf_op jit(solution)/shard_map/ppermute | solution.py:293
  19.3 4.1 %collective-permute-done.6.x_ref = bf16[272,256]{1,0:T(8,128)(2,1)S(1)} collective-permute-done((bf16[272,256]{1,0:T(8,128)(2,1)S(1)}, bf16[272,256]{1,0:T(8,128)(2,1)S(1)}, u32[]{:S(2)}, u32[]{:S(2)}) %collective-permute-start.6) | collective-permute-done | bytes 139296 | tf_op jit(solution)/shard_map/ppermute | solution.py:293
  23.4 0.5 %grid_second.1 = (f32[64,256]{1,0:T(8,128)S(1)}, bf16[64,256]{1,0:T(8,128)(2,1)S(1)}, bf16[64,256]{1,0:T(8,128)(2,1)S(1)}, bf16[64,256]{1,0:T(8,128)(2,1)S(1)}) custom-call(bf16[4,256,256]{2,1,0:T(8,128)(2,1)S(1)} %get-tuple-element.20.near_ref, bf16[12,256,256]{2,1,0:T(8,128)(2,1)S(1)} %get-tuple-element.23.far_ref, ...), custom_call_target="tpu_custom_call" | custom-call | tf_op jit(solution)/shard_map/grid_second/pallas_call | solution.py:360
  23.9 1.4 %collective-permute-start.7 = (bf16[64,256]{1,0:T(8,128)(2,1)S(1)}, bf16[64,256]{1,0:T(8,128)(2,1)S(1)}, u32[]{:S(2)}, u32[]{:S(2)}) collective-permute-start(bf16[64,256]{1,0:T(8,128)(2,1)S(1)} %get-tuple-element.29), channel_id=1, source_target_pairs={{0,4},{1,5},{2,6},{3,7},{4,0},{5,1},{6,2},{7,3},{8,12},{9,13},{10,... | collective-permute-start | bytes 98312 | tf_op jit(solution)/shard_map/ppermute | solution.py:293
  25.3 2.9 %collective-permute-start.8 = (bf16[64,256]{1,0:T(8,128)(2,1)S(1)}, bf16[64,256]{1,0:T(8,128)(2,1)S(1)}, u32[]{:S(2)}, u32[]{:S(2)}) collective-permute-start(bf16[64,256]{1,0:T(8,128)(2,1)S(1)} %get-tuple-element.30), channel_id=1, source_target_pairs={{0,8},{1,9},{2,10},{3,11},{4,12},{5,13},{6,14},{7,15},{8,0},{9,1},... | collective-permute-start | bytes 98312 | tf_op jit(solution)/shard_map/ppermute | solution.py:293
  28.3 0.1 collective-permute-start.9
  28.3 0.0 collective-permute-done.7.q1_ref
  28.4 2.2 %collective-permute-done.8.q2_ref = bf16[64,256]{1,0:T(8,128)(2,1)S(1)} collective-permute-done((bf16[64,256]{1,0:T(8,128)(2,1)S(1)}, bf16[64,256]{1,0:T(8,128)(2,1)S(1)}, u32[]{:S(2)}, u32[]{:S(2)}) %collective-permute-start.8) | collective-permute-done | bytes 32800 | tf_op jit(solution)/shard_map/ppermute | solution.py:293
  30.5 3.5 %collective-permute-done.9.q3_ref = bf16[64,256]{1,0:T(8,128)(2,1)S(1)} collective-permute-done((bf16[64,256]{1,0:T(8,128)(2,1)S(1)}, bf16[64,256]{1,0:T(8,128)(2,1)S(1)}, u32[]{:S(2)}, u32[]{:S(2)}) %collective-permute-start.9) | collective-permute-done | bytes 32800 | tf_op jit(solution)/shard_map/ppermute | solution.py:293
  34.0 0.0 copy-done
  34.0 0.0 copy-done.1
  34.0 0.0 copy-done.2
  34.0 0.0 copy-done.3
  34.0 0.0 copy-done.4
  34.0 0.7 %grid_last.1 = (f32[64,256]{1,0:T(8,128)}, f32[1,256]{1,0:T(1,128)}) custom-call(f32[64,256]{1,0:T(8,128)S(1)} %get-tuple-element.28.q0_ref, bf16[64,256]{1,0:T(8,128)(2,1)S(1)} %collective-permute-done.7.q1_ref, bf16[64,256]{1,0:T(8,128)(2,1)S(1)} %collective-permute-done.8.q2_ref, bf16[64,256]{1,0:T(8,128)(2,1)S(1)} %collective-permute-done.9.q3_ref, ...), custom_call_target="tpu_custom_call" | custom-call | tf_op jit(solution)/shard_map/grid_last/pallas_call | solution.py:369
  (1 shorter events, 0.0 us)
Async XLA Ops:
  0.6 6.8 %collective-permute-start = (f32[3,256]{1,0:T(4,128)}, f32[3,256]{1,0:T(4,128)S(1)}, u32[]{:S(2)}, u32[]{:S(2)}) collective-permute-start(f32[3,256]{1,0:T(4,128)} %refs_0_.1), channel_id=1, source_target_pairs={{0,1},{1,0},{2,3},{3,2},{4,5},{5,4},{6,7},{7,6},{8,9},{9,8},{10,11... | collective-permute-start | bytes 9224 | tf_op jit(solution)/shard_map/ppermute | solution.py:293
  2.1 11.1 %collective-permute-start.4 = (bf16[80,256]{1,0:T(8,128)(2,1)S(1)}, bf16[80,256]{1,0:T(8,128)(2,1)S(1)}, u32[]{:S(2)}, u32[]{:S(2)}) collective-permute-start(bf16[80,256]{1,0:T(8,128)(2,1)S(1)} %get-tuple-element.18.own_ref), channel_id=1, source_target_pairs={{0,12},{1,13},{2,14},{3,15},{4,8},{5,9},{6,10},{7,11},{8,4},{9,5},... | collective-permute-start | bytes 122888 | tf_op jit(solution)/shard_map/ppermute | solution.py:293
  6.8 6.5 %collective-permute-start.3 = (bf16[80,256]{1,0:T(8,128)(2,1)S(1)}, bf16[80,256]{1,0:T(8,128)(2,1)S(1)}, u32[]{:S(2)}, u32[]{:S(2)}) collective-permute-start(bf16[80,256]{1,0:T(8,128)(2,1)S(1)} %get-tuple-element.18.own_ref), channel_id=1, source_target_pairs={{0,8},{1,9},{2,10},{3,11},{4,12},{5,13},{6,14},{7,15},{8,0},{9,1},... | collective-permute-start | bytes 122888 | tf_op jit(solution)/shard_map/ppermute | solution.py:293
  6.8 6.5 %collective-permute-start.2 = (bf16[80,256]{1,0:T(8,128)(2,1)S(1)}, bf16[80,256]{1,0:T(8,128)(2,1)S(1)}, u32[]{:S(2)}, u32[]{:S(2)}) collective-permute-start(bf16[80,256]{1,0:T(8,128)(2,1)S(1)} %get-tuple-element.18.own_ref), channel_id=1, source_target_pairs={{0,4},{1,5},{2,6},{3,7},{4,0},{5,1},{6,2},{7,3},{8,12},{9,13},{10,... | collective-permute-start | bytes 122888 | tf_op jit(solution)/shard_map/ppermute | solution.py:293
  8.1 3.7 %collective-permute-start.1 = (f32[2,3,256]{2,1,0:T(4,128)S(1)}, f32[2,3,256]{2,1,0:T(4,128)S(1)}, u32[]{:S(2)}, u32[]{:S(2)}) collective-permute-start(f32[2,3,256]{2,1,0:T(4,128)S(1)} %pad_maximum_fusion), channel_id=1, source_target_pairs={{0,2},{1,3},{2,0},{3,1},{4,6},{5,7},{6,4},{7,5},{8,10},{9,11},{10,... | collective-permute-start | bytes 18440 | tf_op jit(solution)/shard_map/ppermute | solution.py:293
  16.1 17.9 %copy-start = (f32[64,256]{1,0:T(8,128)S(1)}, f32[64,256]{1,0:T(8,128)}, u32[]{:S(2)}) copy-start(f32[64,256]{1,0:T(8,128)} %rest_0_.1) | copy-start | bytes 196612
  16.1 17.9 %copy-start.1 = (bf16[64,256]{1,0:T(8,128)(2,1)S(1)}, bf16[64,256]{1,0:T(8,128)(2,1)}, u32[]{:S(2)}) copy-start(bf16[64,256]{1,0:T(8,128)(2,1)} %rest_3_.1) | copy-start | bytes 98308
  16.1 17.9 %copy-start.2 = (bf16[64,256]{1,0:T(8,128)(2,1)S(1)}, bf16[64,256]{1,0:T(8,128)(2,1)}, u32[]{:S(2)}) copy-start(bf16[64,256]{1,0:T(8,128)(2,1)} %rest_4_.1) | copy-start | bytes 98308
  16.1 17.9 %copy-start.3 = (f32[256]{0:T(256)S(1)}, f32[256]{0:T(256)}, u32[]{:S(2)}) copy-start(f32[256]{0:T(256)} %param.11) | copy-start | bytes 3076
  16.1 17.9 %copy-start.4 = (f32[256]{0:T(256)S(1)}, f32[256]{0:T(256)}, u32[]{:S(2)}) copy-start(f32[256]{0:T(256)} %param.10) | copy-start | bytes 3076
  16.1 1.4 %collective-permute-start.5 = (bf16[272,256]{1,0:T(8,128)(2,1)S(1)}, bf16[272,256]{1,0:T(8,128)(2,1)S(1)}, u32[]{:S(2)}, u32[]{:S(2)}) collective-permute-start(bf16[272,256]{1,0:T(8,128)(2,1)S(1)} %get-tuple-element.25), channel_id=1, source_target_pairs={{0,1},{1,0},{2,3},{3,2},{4,5},{5,4},{6,7},{7,6},{8,9},{9,8},{10,11... | collective-permute-start | bytes 417800 | tf_op jit(solution)/shard_map/ppermute | solution.py:293
  17.6 5.8 %collective-permute-start.6 = (bf16[272,256]{1,0:T(8,128)(2,1)S(1)}, bf16[272,256]{1,0:T(8,128)(2,1)S(1)}, u32[]{:S(2)}, u32[]{:S(2)}) collective-permute-start(bf16[272,256]{1,0:T(8,128)(2,1)S(1)} %get-tuple-element.27.own_ref), channel_id=1, source_target_pairs={{0,2},{1,3},{2,0},{3,1},{4,6},{5,7},{6,4},{7,5},{8,10},{9,11},{10,... | collective-permute-start | bytes 417800 | tf_op jit(solution)/shard_map/ppermute | solution.py:293
  23.9 4.5 %collective-permute-start.7 = (bf16[64,256]{1,0:T(8,128)(2,1)S(1)}, bf16[64,256]{1,0:T(8,128)(2,1)S(1)}, u32[]{:S(2)}, u32[]{:S(2)}) collective-permute-start(bf16[64,256]{1,0:T(8,128)(2,1)S(1)} %get-tuple-element.29), channel_id=1, source_target_pairs={{0,4},{1,5},{2,6},{3,7},{4,0},{5,1},{6,2},{7,3},{8,12},{9,13},{10,... | collective-permute-start | bytes 98312 | tf_op jit(solution)/shard_map/ppermute | solution.py:293
  25.3 5.2 %collective-permute-start.8 = (bf16[64,256]{1,0:T(8,128)(2,1)S(1)}, bf16[64,256]{1,0:T(8,128)(2,1)S(1)}, u32[]{:S(2)}, u32[]{:S(2)}) collective-permute-start(bf16[64,256]{1,0:T(8,128)(2,1)S(1)} %get-tuple-element.30), channel_id=1, source_target_pairs={{0,8},{1,9},{2,10},{3,11},{4,12},{5,13},{6,14},{7,15},{8,0},{9,1},... | collective-permute-start | bytes 98312 | tf_op jit(solution)/shard_map/ppermute | solution.py:293
  28.3 5.7 %collective-permute-start.9 = (bf16[64,256]{1,0:T(8,128)(2,1)S(1)}, bf16[64,256]{1,0:T(8,128)(2,1)S(1)}, u32[]{:S(2)}, u32[]{:S(2)}) collective-permute-start(bf16[64,256]{1,0:T(8,128)(2,1)S(1)} %get-tuple-element.31), channel_id=1, source_target_pairs={{0,12},{1,13},{2,14},{3,15},{4,8},{5,9},{6,10},{7,11},{8,4},{9,5},... | collective-permute-start | bytes 98312 | tf_op jit(solution)/shard_map/ppermute | solution.py:293

commit v2 on v1

--- a/solution.py
+++ b/solution.py
@@ -45,7 +45,7 @@
 
 
 def prepare(scale, *refs):
-    arguments, (packed_ref, boost_ref, rows, *held, sems) = refs[:5], refs[5:]
+    arguments, (packed_ref, boost_ref, spot_ref, rows, *held, sems) = refs[:5], refs[5:]
     copies = [
         pltpu.make_async_copy(argument, ref, sems.at[at])
         for at, (argument, ref) in enumerate(zip(arguments, held))
@@ -71,6 +71,7 @@
     packed_ref[:rhs_count] = (reflectance_ref[...] * seed_ref[...]).astype(jnp.bfloat16)
     packed_ref[rhs_count:] = rows[...].astype(jnp.bfloat16)
     boost_ref[...] = seed_ref[...] * (1.0 / weight)
+    spot_ref[...] = pos_ref[...]
 
 
 def distance_terms(position, terms, as_rows):
@@ -94,26 +95,24 @@
     return 31 - jnp.where(direct, 8 * (group // 2) + lane // 16, 8 * (lane // 32) + group)
 
 
-def kernel_values(distance, word, shift):
-    value = pl.reciprocal(distance, approx=True)
-    seen = jnp.left_shift(word, shift) < 0
-    halves = [jnp.where(seen, value[:8], 0.0), jnp.where(seen, value[8:], 0.0)]
-    return jnp.concatenate(halves).astype(jnp.bfloat16)
-
-
 def form_block(t, s, line, column, distance, words, out_ref):
     lane = lax.broadcasted_iota(jnp.int32, (8, TILE), 1)
     row_chunk = line * LINE + jnp.bitwise_xor(column, t)
     direct = row_chunk < jnp.bitwise_xor(line, s) * LINE + column
-    for group in range(TILE // GROUP):
-        shift = shift_up(direct, group, lane)
-        for row_block in range(2):
-            first = row_block * TILE + group * GROUP
-            for col_block in range(2):
-                word = words[s, col_block * TILE + 2 * row_chunk + row_block]
-                lanes = slice(col_block * TILE, (col_block + 1) * TILE)
-                out_ref[first : first + GROUP, lanes] = kernel_values(
-                    distance[first : first + GROUP, lanes], word, shift
+    shifts = [shift_up(direct, group, lane) for group in range(TILE // GROUP)]
+    for row_block in range(2):
+        for col_block in range(2):
+            word = jnp.full(lane.shape, words[s, col_block * TILE + 2 * row_chunk + row_block])
+            lanes = slice(col_block * TILE, (col_block + 1) * TILE)
+            for group, shift in enumerate(shifts):
+                first = row_block * TILE + group * GROUP
+                seen = jnp.left_shift(word, shift) < 0
+                halves = []
+                for half in range(first, first + GROUP, 8):
+                    value = pl.reciprocal(distance[half : half + 8, lanes], approx=True)
+                    halves.append(jnp.where(seen, value, 0.0))
+                out_ref[first : first + GROUP, lanes] = jnp.concatenate(halves).astype(
+                    jnp.bfloat16
                 )
 
 
@@ -175,64 +174,74 @@
         row_terms[t] = jnp.transpose(terms[...]).astype(jnp.bfloat16)
     copy.wait()
     own = own_ref[:rhs_count, :]
-    for t in range(LINE):
-        distance[...] = times(row_terms[t], col_terms)
-        if t == 0:
-            form_own(me, distance, words, kernel_ref.at[t])
-        else:
-            form_block(t, 0, line, column, distance, words, kernel_ref.at[t])
+
+    def measure(t):
+        distance[t % 2] = times(row_terms[t], col_terms)
+
+    def add(t):
         held = times_transpose(own, kernel_ref[t])
         partial_ref[t] = held + boost_ref[...] if t == 0 else held
 
-
-def grid_far(
-    me_ref,
-    z1_ref,
-    z2_ref,
-    z3_ref,
-    own_ref,
-    near_ref,
-    row_terms,
-    kernel_ref,
-    partial_ref,
-    sent_ref,
-    words_vmem,
-    words,
-    terms,
-    col_terms,
-    distance,
-    sem,
-):
-    rhs_count = near_ref.shape[1]
+    measure(0)
+    for t in range(LINE):
+        if t + 1 < LINE:
+            measure(t + 1)
+        if t == 0:
+            form_own(me, distance.at[0], words, kernel_ref.at[0])
+        else:
+            form_block(t, 0, line, column, distance.at[t % 2], words, kernel_ref.at[t])
+            add(t - 1)
+    add(LINE - 1)
+
+
+def grid_lines(steps, last, me_ref, *refs):
+    count = len(steps)
+    lines, (own_ref, before_ref, row_terms, kernel_ref, partial_ref, *refs) = (
+        refs[:count],
+        refs[count:],
+    )
+    sent_ref, refs = (refs[0], refs[1:]) if last else (None, refs)
+    words_vmem, words, terms, col_terms, distance, sem = refs
+    rhs_count = before_ref.shape[1]
     me = me_ref[0]
     line, column = me // LINE, me % LINE
-    lines = (z1_ref, z2_ref, z3_ref)
     positions = []
-    for s, ref in enumerate(lines, 1):
+    for s, ref in zip(steps, lines):
         position, words_vmem[s : s + 1, :] = read_extra(ref, rhs_count)
         positions.append(position)
     copy = pltpu.make_async_copy(words_vmem, words, sem)
     copy.start()
-    for s, position in enumerate(positions):
+    for at, position in enumerate(positions):
         distance_terms(position, terms, False)
-        col_terms[s] = terms[...].astype(jnp.bfloat16)
+        col_terms[at] = terms[...].astype(jnp.bfloat16)
     copy.wait()
-
-    def form(t, carry):
-        held = near_ref[t]
-        for s in range(1, LINE):
-            at = (LINE - 1) * t + s - 1
-            slot = distance.at[s - 1]
-            slot[...] = times(row_terms[t], col_terms[s - 1])
-            form_block(t, s, line, column, slot, words, kernel_ref.at[at])
-            held += times_transpose(lines[s - 1][:rhs_count, :], kernel_ref[at])
-        partial_ref[t] = held
-        start = pl.multiple_of(t * rhs_count, rhs_count)
-        sent_ref[pl.ds(start, rhs_count), :] = held.astype(jnp.bfloat16)
-        return carry
-
-    lax.fori_loop(0, LINE, form, 0)
-    sent_ref[LINE * rhs_count :] = own_ref[rhs_count:]
+    blocks = [(t, at) for t in range(LINE) for at in range(count)]
+    held = {}
+
+    def measure(place):
+        t, at = blocks[place]
+        distance[place % 2] = times(row_terms[t], col_terms[at])
+
+    def add(place):
+        t, at = blocks[place]
+        held[t] = held.get(t, before_ref[t]) + times_transpose(
+            lines[at][:rhs_count, :], kernel_ref[place]
+        )
+        if at == count - 1:
+            partial_ref[t] = held[t]
+            if last:
+                sent_ref[t * rhs_count : (t + 1) * rhs_count] = held[t].astype(jnp.bfloat16)
+
+    measure(0)
+    for place, (t, at) in enumerate(blocks):
+        if place + 1 < len(blocks):
+            measure(place + 1)
+        form_block(t, steps[at], line, column, distance.at[place % 2], words, kernel_ref.at[place])
+        if place:
+            add(place - 1)
+    add(len(blocks) - 1)
+    if last:
+        sent_ref[LINE * rhs_count :] = own_ref[rhs_count:]
 
 
 def grid_middle(partial_ref, core_ref, own_ref, both_ref, sent_ref, rows):
@@ -248,28 +257,31 @@
     sent_ref[LINE * rhs_count :] = rows[...].astype(jnp.bfloat16)
 
 
-def grid_second(
-    near_ref, far_ref, both_ref, own_ref, x_ref, q0_ref, q1_ref, q2_ref, q3_ref
-):
-    rhs_count = q0_ref.shape[0]
-    scaled = []
+def grid_second(far_ref, both_ref, own_ref, x_ref, scaled_ref, q2_ref, q3_ref):
+    rhs_count = q2_ref.shape[0]
     for t in range(LINE):
         terms = (own_ref, x_ref)[t // 2][LINE * rhs_count :, :].astype(jnp.float32)
         at = 3 * (t % 2)
         factor = terms[at : at + 1] + terms[at + 1 : at + 2] + terms[at + 2 : at + 3]
         start = (t ^ 2) * rhs_count
         total = both_ref[t] + x_ref[start : start + rhs_count].astype(jnp.float32)
-        scaled.append((factor * total).astype(jnp.bfloat16))
-    for s, out_ref in enumerate((q0_ref, q1_ref, q2_ref, q3_ref)):
-        held = None
-        for t in range(LINE):
-            kernel = near_ref[t] if s == 0 else far_ref[(LINE - 1) * t + s - 1]
-            term = times(scaled[t], kernel)
-            held = term if held is None else held + term
+        scaled_ref[t] = (factor * total).astype(jnp.bfloat16)
+    for at, out_ref in enumerate((q2_ref, q3_ref)):
+        held = times(scaled_ref[0], far_ref[at])
+        for t in range(1, LINE):
+            held = held + times(scaled_ref[t], far_ref[2 * t + at])
+        out_ref[...] = held.astype(jnp.bfloat16)
+
+
+def grid_third(near_ref, next_ref, scaled_ref, q0_ref, q1_ref):
+    for kernel_ref, out_ref in ((next_ref, q1_ref), (near_ref, q0_ref)):
+        held = times(scaled_ref[0], kernel_ref[0])
+        for t in range(1, LINE):
+            held = held + times(scaled_ref[t], kernel_ref[t])
         out_ref[...] = held.astype(out_ref.dtype)
 
 
-def grid_last(scale, q0_ref, q1_ref, q2_ref, q3_ref, *rest):
+def grid_last(scale, q3_ref, q2_ref, q1_ref, q0_ref, *rest):
     total = q0_ref[...]
     for ref in (q1_ref, q2_ref, q3_ref):
         total = total + ref[...].astype(jnp.float32)
@@ -292,15 +304,15 @@
     def send(value, step):
         return lax.ppermute(value, "row", [(at, at ^ step) for at in range(devices)])
 
-    core = send(position, 1)
     arguments = (position, visibility, area, reflectance, adjoint_seed)
-    packed, boost = pl.pallas_call(
+    packed, boost, spot = pl.pallas_call(
         functools.partial(prepare, scale),
         in_specs=[pl.BlockSpec(memory_space=pltpu.HBM)] * 5,
-        out_specs=[vmem] * 2,
+        out_specs=[vmem] * 3,
         out_shape=[
             shaped((rhs_count + EXTRA, own_width), jnp.bfloat16),
             shaped(field, jnp.float32),
+            shaped(position.shape, jnp.float32),
         ],
         scratch_shapes=[pltpu.VMEM((EXTRA, own_width), jnp.float32)]
         + [pltpu.VMEM(value.shape, value.dtype) for value in arguments]
@@ -308,13 +320,17 @@
         compiler_params=params,
         name="prepare",
     )(*[pltpu.with_memory_space_constraint(value, pltpu.HBM) for value in arguments])
-    pair = send(jnp.stack([position, core]), 2)
-    lines = [send(packed, LINE * step) for step in range(1, LINE)]
+    line3, line2 = send(packed, 3 * LINE), send(packed, 2 * LINE)
+    core = send(position, 1)
+    later, core = lax.optimization_barrier((packed, core))
+    line1 = send(later, LINE)
+    pair = send(jnp.stack([spot, core]), 2)
     words_scratch = [
         pltpu.VMEM((LINE, own_width), jnp.int32),
         pltpu.SMEM((LINE, own_width), jnp.int32),
         pltpu.VMEM((TERMS, own_width), jnp.float32),
     ]
+    distance = pltpu.VMEM((2, own_width, own_width), jnp.float32)
     near, partial, row_terms = pl.pallas_call(
         grid_near,
         in_specs=[smem] + [vmem] * 4,
@@ -324,30 +340,35 @@
             shaped((LINE,) + field, jnp.float32),
             shaped((LINE, own_width, TERMS), jnp.bfloat16),
         ],
-        scratch_shapes=words_scratch
-        + [pltpu.VMEM((own_width, own_width), jnp.float32), pltpu.SemaphoreType.DMA],
+        scratch_shapes=words_scratch + [distance, pltpu.SemaphoreType.DMA],
         compiler_params=params,
         name="grid_near",
     )(my_index, packed, core, pair, boost)
     sent = shaped((LINE * rhs_count + EXTRA, own_width), jnp.bfloat16)
-    far, partial, terms = pl.pallas_call(
-        grid_far,
-        in_specs=[smem] + [vmem] * 6,
-        out_specs=[vmem] * 3,
-        out_shape=[
-            shaped((devices - LINE, own_width, own_width), jnp.bfloat16),
-            shaped((LINE,) + field, jnp.float32),
-            sent,
-        ],
-        scratch_shapes=words_scratch
-        + [
-            pltpu.VMEM((LINE - 1, TERMS, own_width), jnp.bfloat16),
-            pltpu.VMEM((LINE - 1, own_width, own_width), jnp.float32),
-            pltpu.SemaphoreType.DMA,
-        ],
-        compiler_params=params,
-        name="grid_far",
-    )(my_index, *lines, packed, partial, row_terms)
+
+    def form_lines(steps, last, name, *operands):
+        count = len(steps)
+        return pl.pallas_call(
+            functools.partial(grid_lines, steps, last),
+            in_specs=[smem] + [vmem] * (count + 3),
+            out_specs=[vmem] * (3 if last else 2),
+            out_shape=[
+                shaped((LINE * count, own_width, own_width), jnp.bfloat16),
+                shaped((LINE,) + field, jnp.float32),
+            ]
+            + [sent] * last,
+            scratch_shapes=words_scratch
+            + [
+                pltpu.VMEM((count, TERMS, own_width), jnp.bfloat16),
+                distance,
+                pltpu.SemaphoreType.DMA,
+            ],
+            compiler_params=params,
+            name=name,
+        )(my_index, *operands, row_terms)
+
+    next_, partial = form_lines((1,), False, "grid_next", line1, packed, partial)
+    far, partial, terms = form_lines((2, 3), True, "grid_far", line2, line3, packed, partial)
     both, terms = pl.pallas_call(
         grid_middle,
         in_specs=[vmem] * 3,
@@ -357,15 +378,29 @@
         compiler_params=params,
         name="grid_middle",
     )(partial, send(terms, 1), packed)
-    sums = pl.pallas_call(
+    scaled, sum2, sum3 = pl.pallas_call(
         grid_second,
-        in_specs=[vmem] * 5,
-        out_specs=[vmem] * LINE,
-        out_shape=[shaped(field, jnp.float32)] + [shaped(field, jnp.bfloat16)] * (LINE - 1),
+        in_specs=[vmem] * 4,
+        out_specs=[vmem] * 3,
+        out_shape=[shaped((LINE,) + field, jnp.bfloat16)] + [shaped(field, jnp.bfloat16)] * 2,
         compiler_params=params,
         name="grid_second",
-    )(near, far, both, terms, send(terms, 2))
-    sums = [sums[0]] + [send(sums[step], LINE * step) for step in range(1, LINE)]
+    )(far, both, terms, send(terms, 2))
+    sum3, sum2 = send(sum3, 3 * LINE), send(sum2, 2 * LINE)
+    sum0, sum1 = pl.pallas_call(
+        grid_third,
+        in_specs=[vmem] * 3,
+        out_specs=[vmem] * 2,
+        out_shape=[shaped(field, jnp.float32), shaped(field, jnp.bfloat16)],
+        compiler_params=params,
+        cost_estimate=pl.CostEstimate(
+            flops=4 * LINE * rhs_count * own_width**2,
+            bytes_accessed=4 * LINE * own_width**2 + 12 * rhs_count * own_width,
+            transcendentals=0,
+        ),
+        name="grid_third",
+    )(near, next_, scaled)
+    sum1 = send(sum1, LINE)
     adjoint, grad = pl.pallas_call(
         functools.partial(grid_last, scale),
         in_specs=[vmem] * 9,
@@ -373,7 +408,7 @@
         out_shape=[shaped(field, jnp.float32), shaped((1, own_width), jnp.float32)],
         compiler_params=params,
         name="grid_last",
-    )(*sums, adjoint_seed, area, reflectance, radiosity, emission)
+    )(sum3, sum2, sum1, sum0, adjoint_seed, area, reflectance, radiosity, emission)
     return adjoint, grad.reshape(own_width)
 
 

time: 34.9 us -> 32.5 us (0.931)
  waiting for transfers between devices: 13.1 us -> 11.2 us
  other arithmetic: 0.69 us -> 0.01 us
    ppermute x10, waiting for transfers between devices: 13.1 us -> 11.2 us  [send(): lax.ppermute(value, 'row', [(at, at ^ step) for at in range(devices)])]
    another operation x1, other arithmetic: 0.69 us -> 0.01 us  [on_grid(): pair = send(jnp.stack([spot, core]), 2)]
    pallas_call x2 -> x4, Pallas kernels: 3.27 us -> 3.3 us  [the longest x2 2.69 us: form_lines(): pl.pallas_call(functools.partial(grid_lines, steps, last), in_specs=[smem...]
  transfers between devices with their start and end apart: 10 -> 10, of which waited for: 5 -> 5; matrix products, arithmetic and copies ran while one was open for 2% -> 0% of each run, Pallas kernels for 7% -> 12%
where the time goes in v2:
time: 32.5 us; the launch traced here: 32.3 us
  starting transfers between devices  13.8 us (42%)
  waiting for transfers between devices  11.2 us (34%)
  Pallas kernels  6.49 us (20%)
  between operations  0.77 us (2%)
    ppermute x10, starting transfers between devices, send(): lax.ppermute(value, 'row', [(at, at ^ step) for at in range(devices)])  13.8 us
    ppermute x10, waiting for transfers between devices, send(): lax.ppermute(value, 'row', [(at, at ^ step) for at in range(devices)])  11.2 us
    pallas_call x2, Pallas kernels, form_lines(): pl.pallas_call(functools.partial(grid_lines, steps, last), in_specs=[smem...  2.69 us
    pallas_call x1, Pallas kernels, on_grid(): pl.pallas_call(grid_near, in_specs=[smem] + [vmem] * 4, out_specs=[vmem]...  1.51 us
    pallas_call x1, Pallas kernels, on_grid(): pl.pallas_call(functools.partial(prepare, scale), in_specs=[pl.BlockSpec(...  0.97 us
    pallas_call x1, Pallas kernels, on_grid(): pl.pallas_call(functools.partial(grid_last, scale), in_specs=[vmem] * 9,...  0.67 us
  transfers between devices with their start and end apart: 10, of which 5 were waited for; matrix products, arithmetic and copies ran while one was open for 0% of the time, Pallas kernels for 12%

profile of v2, /device:TPU:0, one launch (start us, length us, event | category | flops | bytes accessed | tf_op | source)
XLA Modules:
  0.0 32.3 jit_solution(3784797188458606631)
XLA Ops:
  0.6 0.5 %collective-permute-start.2 = (f32[3,256]{1,0:T(4,128)}, f32[3,256]{1,0:T(4,128)S(1)}, u32[]{:S(2)}, u32[]{:S(2)}) collective-permute-start(f32[3,256]{1,0:T(4,128)} %refs_0_.1), channel_id=1, source_target_pairs={{0,1},{1,0},{2,3},{3,2},{4,5},{5,4},{6,7},{7,6},{8,9},{9,8},{10,11... | collective-permute-start | bytes 9224 | tf_op jit(solution)/shard_map/ppermute | solution.py:305
  1.1 1.0 %prepare.1 = (bf16[80,256]{1,0:T(8,128)(2,1)S(1)}, f32[64,256]{1,0:T(8,128)S(1)}, f32[3,256]{1,0:T(4,128)S(1)}) custom-call(f32[3,256]{1,0:T(4,128)} %refs_0_.1, s32[2,32]{1,0:T(2,128)} %refs_1_.1, f32[1,256]{1,0:T(1,128)} %bitcast.7, f32[1,256]{1,0:T(1,128)} %bitcast.9, f32[64,256]{1,0:T(8,128)} %rest_0_.1), custom_call_target="tpu_custom_call" | custom-call | tf_op jit(solution)/shard_map/prepare/pallas_call | solution.py:308
  2.1 4.7 %collective-permute-start.1 = (bf16[80,256]{1,0:T(8,128)(2,1)S(1)}, bf16[80,256]{1,0:T(8,128)(2,1)S(1)}, u32[]{:S(2)}, u32[]{:S(2)}) collective-permute-start(bf16[80,256]{1,0:T(8,128)(2,1)S(1)} %get-tuple-element.25.own_ref.refs_1_.refs_2_), channel_id=1, source_target_pairs={{0,12},{1,13},{2,14},{3,15},{4,8},{5,9},{6,10},{7,11},{8,4},{9,5},... | collective-permute-start | bytes 122888 | tf_op jit(solution)/shard_map/ppermute | solution.py:305
  6.8 0.0 collective-permute-start
  6.8 0.0 collective-permute-done.2.core_ref
  6.8 0.6 %collective-permute-start.3 = (bf16[80,256]{1,0:T(8,128)(2,1)S(1)}, bf16[80,256]{1,0:T(8,128)(2,1)S(1)}, u32[]{:S(2)}, u32[]{:S(2)}) collective-permute-start(bf16[80,256]{1,0:T(8,128)(2,1)S(1)} %get-tuple-element.25.own_ref.refs_1_.refs_2_), channel_id=1, source_target_pairs={{0,4},{1,5},{2,6},{3,7},{4,0},{5,1},{6,2},{7,3},{8,12},{9,13},{10,... | collective-permute-start | bytes 122888 | tf_op jit(solution)/shard_map/ppermute | solution.py:305
  7.5 1.6 %collective-permute-start.4 = (f32[2,3,256]{2,1,0:T(4,128)S(1)}, f32[2,3,256]{2,1,0:T(4,128)S(1)}, u32[]{:S(2)}, u32[]{:S(2)}) collective-permute-start(f32[2,3,256]{2,1,0:T(4,128)S(1)} %pad_maximum_fusion), channel_id=1, source_target_pairs={{0,2},{1,3},{2,0},{3,1},{4,6},{5,7},{6,4},{7,5},{8,10},{9,11},{10,... | collective-permute-start | bytes 18440 | tf_op jit(solution)/shard_map/ppermute | solution.py:305
  9.1 2.0 %collective-permute-done.4.pair_ref = f32[2,3,256]{2,1,0:T(4,128)S(1)} collective-permute-done((f32[2,3,256]{2,1,0:T(4,128)S(1)}, f32[2,3,256]{2,1,0:T(4,128)S(1)}, u32[]{:S(2)}, u32[]{:S(2)}) %collective-permute-start.4) | collective-permute-done | bytes 6176 | tf_op jit(solution)/shard_map/ppermute | solution.py:305
  11.1 1.5 %grid_near.1 = (bf16[4,256,256]{2,1,0:T(8,128)(2,1)S(1)}, f32[4,64,256]{2,1,0:T(8,128)S(1)}, bf16[4,256,32]{2,1,0:T(8,128)(2,1)S(1)}) custom-call(s32[1]{0:T(128)} %bitcast.me_ref, bf16[80,256]{1,0:T(8,128)(2,1)S(1)} %get-tuple-element.25.own_ref.refs_1_.refs_2_, f32[3,256]{1,0:T(4,128)S(1)} %collective-permute-done.2.core_ref, ...), custom_call_target="tpu_custom_call" | custom-call | tf_op jit(solution)/shard_map/grid_near/pallas_call | solution.py:334
  12.6 0.0 collective-permute-done.3.refs_0_
  12.6 1.3 %grid_next.1 = (bf16[4,256,256]{2,1,0:T(8,128)(2,1)S(1)}, f32[4,64,256]{2,1,0:T(8,128)S(1)}) custom-call(s32[1]{0:T(128)} %bitcast.me_ref, bf16[80,256]{1,0:T(8,128)(2,1)S(1)} %collective-permute-done.3.refs_0_, bf16[80,256]{1,0:T(8,128)(2,1)S(1)} %get-tuple-element.25.own_ref.refs_1_.refs_2_, f32[4,64,256]{2,1,0:T(8,128)S(1)} %get-tuple-element.29.refs_2_, ...), custom_call_target="tpu_custom_call" | custom-call | tf_op jit(solution)/shard_map/grid_next/pallas_call | solution.py:351
  13.9 0.0 collective-permute-done.1.refs_1_
  13.9 0.0 collective-permute-done.refs_0_
  13.9 1.4 %grid_far.1 = (bf16[8,256,256]{2,1,0:T(8,128)(2,1)S(1)}, f32[4,64,256]{2,1,0:T(8,128)S(1)}, bf16[272,256]{1,0:T(8,128)(2,1)S(1)}) custom-call(s32[1]{0:T(128)} %bitcast.me_ref, bf16[80,256]{1,0:T(8,128)(2,1)S(1)} %collective-permute-done.refs_0_, bf16[80,256]{1,0:T(8,128)(2,1)S(1)} %collective-permute-done.1.refs_1_, ...), custom_call_target="tpu_custom_call" | custom-call | tf_op jit(solution)/shard_map/grid_far/pallas_call | solution.py:351
  15.4 0.1 collective-permute-start.5
  15.4 1.3 %collective-permute-done.5.core_ref = bf16[272,256]{1,0:T(8,128)(2,1)S(1)} collective-permute-done((bf16[272,256]{1,0:T(8,128)(2,1)S(1)}, bf16[272,256]{1,0:T(8,128)(2,1)S(1)}, u32[]{:S(2)}, u32[]{:S(2)}) %collective-permute-start.5) | collective-permute-done | bytes 139296 | tf_op jit(solution)/shard_map/ppermute | solution.py:305
  16.8 1.7 %collective-permute-start.6 = (bf16[272,256]{1,0:T(8,128)(2,1)S(1)}, bf16[272,256]{1,0:T(8,128)(2,1)S(1)}, u32[]{:S(2)}, u32[]{:S(2)}) collective-permute-start(bf16[272,256]{1,0:T(8,128)(2,1)S(1)} %get-tuple-element.36.own_ref), channel_id=1, source_target_pairs={{0,2},{1,3},{2,0},{3,1},{4,6},{5,7},{6,4},{7,5},{8,10},{9,11},{10,... | collective-permute-start | bytes 417800 | tf_op jit(solution)/shard_map/ppermute | solution.py:305
  18.5 4.1 %collective-permute-done.6.x_ref = bf16[272,256]{1,0:T(8,128)(2,1)S(1)} collective-permute-done((bf16[272,256]{1,0:T(8,128)(2,1)S(1)}, bf16[272,256]{1,0:T(8,128)(2,1)S(1)}, u32[]{:S(2)}, u32[]{:S(2)}) %collective-permute-start.6) | collective-permute-done | bytes 139296 | tf_op jit(solution)/shard_map/ppermute | solution.py:305
  22.6 0.3 grid_second.1
  22.9 3.8 %collective-permute-start.7 = (bf16[64,256]{1,0:T(8,128)(2,1)S(1)}, bf16[64,256]{1,0:T(8,128)(2,1)S(1)}, u32[]{:S(2)}, u32[]{:S(2)}) collective-permute-start(bf16[64,256]{1,0:T(8,128)(2,1)S(1)} %get-tuple-element.37), channel_id=1, source_target_pairs={{0,12},{1,13},{2,14},{3,15},{4,8},{5,9},{6,10},{7,11},{8,4},{9,5},... | collective-permute-start | bytes 98312 | tf_op jit(solution)/shard_map/ppermute | solution.py:305
  26.7 0.0 collective-permute-start.8
  26.8 0.0 copy-start
  26.8 0.0 copy-start.1
  26.8 0.0 copy-start.2
  26.8 0.3 grid_third.1
  27.1 0.0 copy-start.4
  27.1 0.0 copy-start.3
  27.1 0.7 %collective-permute-start.9 = (bf16[64,256]{1,0:T(8,128)(2,1)S(1)}, bf16[64,256]{1,0:T(8,128)(2,1)S(1)}, u32[]{:S(2)}, u32[]{:S(2)}) collective-permute-start(bf16[64,256]{1,0:T(8,128)(2,1)S(1)} %get-tuple-element.42), channel_id=1, source_target_pairs={{0,4},{1,5},{2,6},{3,7},{4,0},{5,1},{6,2},{7,3},{8,12},{9,13},{10,... | collective-permute-start | bytes 98312 | tf_op jit(solution)/shard_map/ppermute | solution.py:305
  27.8 0.9 %collective-permute-done.7.q3_ref = bf16[64,256]{1,0:T(8,128)(2,1)S(1)} collective-permute-done((bf16[64,256]{1,0:T(8,128)(2,1)S(1)}, bf16[64,256]{1,0:T(8,128)(2,1)S(1)}, u32[]{:S(2)}, u32[]{:S(2)}) %collective-permute-start.7) | collective-permute-done | bytes 32800 | tf_op jit(solution)/shard_map/ppermute | solution.py:305
  28.7 2.8 %collective-permute-done.8.q2_ref = bf16[64,256]{1,0:T(8,128)(2,1)S(1)} collective-permute-done((bf16[64,256]{1,0:T(8,128)(2,1)S(1)}, bf16[64,256]{1,0:T(8,128)(2,1)S(1)}, u32[]{:S(2)}, u32[]{:S(2)}) %collective-permute-start.8) | collective-permute-done | bytes 32800 | tf_op jit(solution)/shard_map/ppermute | solution.py:305
  31.6 0.0 collective-permute-done.9.q1_ref
  31.6 0.0 copy-done
  31.6 0.0 copy-done.1
  31.6 0.0 copy-done.2
  31.6 0.0 copy-done.4
  31.6 0.0 copy-done.3
  31.6 0.7 %grid_last.1 = (f32[64,256]{1,0:T(8,128)}, f32[1,256]{1,0:T(1,128)}) custom-call(bf16[64,256]{1,0:T(8,128)(2,1)S(1)} %collective-permute-done.7.q3_ref, bf16[64,256]{1,0:T(8,128)(2,1)S(1)} %collective-permute-done.8.q2_ref, bf16[64,256]{1,0:T(8,128)(2,1)S(1)} %collective-permute-done.9.q1_ref, f32[64,256]{1,0:T(8,128)S(1)} %get-tuple-element.43.q0_ref, ...), custom_call_target="tpu_custom_call" | custom-call | tf_op jit(solution)/shard_map/grid_last/pallas_call | solution.py:404
  (2 shorter events, 0.0 us)
Async XLA Ops:
  0.6 6.2 %collective-permute-start.2 = (f32[3,256]{1,0:T(4,128)}, f32[3,256]{1,0:T(4,128)S(1)}, u32[]{:S(2)}, u32[]{:S(2)}) collective-permute-start(f32[3,256]{1,0:T(4,128)} %refs_0_.1), channel_id=1, source_target_pairs={{0,1},{1,0},{2,3},{3,2},{4,5},{5,4},{6,7},{7,6},{8,9},{9,8},{10,11... | collective-permute-start | bytes 9224 | tf_op jit(solution)/shard_map/ppermute | solution.py:305
  2.1 11.8 %collective-permute-start.1 = (bf16[80,256]{1,0:T(8,128)(2,1)S(1)}, bf16[80,256]{1,0:T(8,128)(2,1)S(1)}, u32[]{:S(2)}, u32[]{:S(2)}) collective-permute-start(bf16[80,256]{1,0:T(8,128)(2,1)S(1)} %get-tuple-element.25.own_ref.refs_1_.refs_2_), channel_id=1, source_target_pairs={{0,12},{1,13},{2,14},{3,15},{4,8},{5,9},{6,10},{7,11},{8,4},{9,5},... | collective-permute-start | bytes 122888 | tf_op jit(solution)/shard_map/ppermute | solution.py:305
  6.8 7.1 %collective-permute-start = (bf16[80,256]{1,0:T(8,128)(2,1)S(1)}, bf16[80,256]{1,0:T(8,128)(2,1)S(1)}, u32[]{:S(2)}, u32[]{:S(2)}) collective-permute-start(bf16[80,256]{1,0:T(8,128)(2,1)S(1)} %get-tuple-element.25.own_ref.refs_1_.refs_2_), channel_id=1, source_target_pairs={{0,8},{1,9},{2,10},{3,11},{4,12},{5,13},{6,14},{7,15},{8,0},{9,1},... | collective-permute-start | bytes 122888 | tf_op jit(solution)/shard_map/ppermute | solution.py:305
  6.8 5.8 %collective-permute-start.3 = (bf16[80,256]{1,0:T(8,128)(2,1)S(1)}, bf16[80,256]{1,0:T(8,128)(2,1)S(1)}, u32[]{:S(2)}, u32[]{:S(2)}) collective-permute-start(bf16[80,256]{1,0:T(8,128)(2,1)S(1)} %get-tuple-element.25.own_ref.refs_1_.refs_2_), channel_id=1, source_target_pairs={{0,4},{1,5},{2,6},{3,7},{4,0},{5,1},{6,2},{7,3},{8,12},{9,13},{10,... | collective-permute-start | bytes 122888 | tf_op jit(solution)/shard_map/ppermute | solution.py:305
  7.5 3.7 %collective-permute-start.4 = (f32[2,3,256]{2,1,0:T(4,128)S(1)}, f32[2,3,256]{2,1,0:T(4,128)S(1)}, u32[]{:S(2)}, u32[]{:S(2)}) collective-permute-start(f32[2,3,256]{2,1,0:T(4,128)S(1)} %pad_maximum_fusion), channel_id=1, source_target_pairs={{0,2},{1,3},{2,0},{3,1},{4,6},{5,7},{6,4},{7,5},{8,10},{9,11},{10,... | collective-permute-start | bytes 18440 | tf_op jit(solution)/shard_map/ppermute | solution.py:305
  15.4 1.4 %collective-permute-start.5 = (bf16[272,256]{1,0:T(8,128)(2,1)S(1)}, bf16[272,256]{1,0:T(8,128)(2,1)S(1)}, u32[]{:S(2)}, u32[]{:S(2)}) collective-permute-start(bf16[272,256]{1,0:T(8,128)(2,1)S(1)} %get-tuple-element.34), channel_id=1, source_target_pairs={{0,1},{1,0},{2,3},{3,2},{4,5},{5,4},{6,7},{7,6},{8,9},{9,8},{10,11... | collective-permute-start | bytes 417800 | tf_op jit(solution)/shard_map/ppermute | solution.py:305
  16.8 5.8 %collective-permute-start.6 = (bf16[272,256]{1,0:T(8,128)(2,1)S(1)}, bf16[272,256]{1,0:T(8,128)(2,1)S(1)}, u32[]{:S(2)}, u32[]{:S(2)}) collective-permute-start(bf16[272,256]{1,0:T(8,128)(2,1)S(1)} %get-tuple-element.36.own_ref), channel_id=1, source_target_pairs={{0,2},{1,3},{2,0},{3,1},{4,6},{5,7},{6,4},{7,5},{8,10},{9,11},{10,... | collective-permute-start | bytes 417800 | tf_op jit(solution)/shard_map/ppermute | solution.py:305
  22.9 5.8 %collective-permute-start.7 = (bf16[64,256]{1,0:T(8,128)(2,1)S(1)}, bf16[64,256]{1,0:T(8,128)(2,1)S(1)}, u32[]{:S(2)}, u32[]{:S(2)}) collective-permute-start(bf16[64,256]{1,0:T(8,128)(2,1)S(1)} %get-tuple-element.37), channel_id=1, source_target_pairs={{0,12},{1,13},{2,14},{3,15},{4,8},{5,9},{6,10},{7,11},{8,4},{9,5},... | collective-permute-start | bytes 98312 | tf_op jit(solution)/shard_map/ppermute | solution.py:305
  26.7 4.8 %collective-permute-start.8 = (bf16[64,256]{1,0:T(8,128)(2,1)S(1)}, bf16[64,256]{1,0:T(8,128)(2,1)S(1)}, u32[]{:S(2)}, u32[]{:S(2)}) collective-permute-start(bf16[64,256]{1,0:T(8,128)(2,1)S(1)} %get-tuple-element.38), channel_id=1, source_target_pairs={{0,8},{1,9},{2,10},{3,11},{4,12},{5,13},{6,14},{7,15},{8,0},{9,1},... | collective-permute-start | bytes 98312 | tf_op jit(solution)/shard_map/ppermute | solution.py:305
  26.8 4.8 %copy-start = (f32[64,256]{1,0:T(8,128)S(1)}, f32[64,256]{1,0:T(8,128)}, u32[]{:S(2)}) copy-start(f32[64,256]{1,0:T(8,128)} %rest_0_.1) | copy-start | bytes 196612
  26.8 4.8 %copy-start.1 = (bf16[64,256]{1,0:T(8,128)(2,1)S(1)}, bf16[64,256]{1,0:T(8,128)(2,1)}, u32[]{:S(2)}) copy-start(bf16[64,256]{1,0:T(8,128)(2,1)} %rest_3_.1) | copy-start | bytes 98308
  26.8 4.8 %copy-start.2 = (bf16[64,256]{1,0:T(8,128)(2,1)S(1)}, bf16[64,256]{1,0:T(8,128)(2,1)}, u32[]{:S(2)}) copy-start(bf16[64,256]{1,0:T(8,128)(2,1)} %rest_4_.1) | copy-start | bytes 98308
  27.1 4.5 %copy-start.4 = (f32[256]{0:T(256)S(1)}, f32[256]{0:T(256)}, u32[]{:S(2)}) copy-start(f32[256]{0:T(256)} %param.10) | copy-start | bytes 3076
  27.1 4.5 %copy-start.3 = (f32[256]{0:T(256)S(1)}, f32[256]{0:T(256)}, u32[]{:S(2)}) copy-start(f32[256]{0:T(256)} %param.11) | copy-start | bytes 3076
  27.1 4.5 %collective-permute-start.9 = (bf16[64,256]{1,0:T(8,128)(2,1)S(1)}, bf16[64,256]{1,0:T(8,128)(2,1)S(1)}, u32[]{:S(2)}, u32[]{:S(2)}) collective-permute-start(bf16[64,256]{1,0:T(8,128)(2,1)S(1)} %get-tuple-element.42), channel_id=1, source_target_pairs={{0,4},{1,5},{2,6},{3,7},{4,0},{5,1},{6,2},{7,3},{8,12},{9,13},{10,... | collective-permute-start | bytes 98312 | tf_op jit(solution)/shard_map/ppermute | solution.py:305

commit v3 on v2

--- a/solution.py
+++ b/solution.py
@@ -16,6 +16,10 @@
 TERMS = 32
 VMEM_BYTES = 48 * 1024 * 1024
 GRID_BYTES = 8 * 1024 * 1024
+
+
+NEAR = [(0, 0), (1, 0)]
+REST = [(t, s) for t in range(LINE) for s in range(LINE) if (t, s) not in NEAR]
 
 
 def three_terms(value):
@@ -95,18 +99,30 @@
     return 31 - jnp.where(direct, 8 * (group // 2) + lane // 16, 8 * (lane // 32) + group)
 
 
-def form_block(t, s, line, column, distance, words, out_ref):
+def block_words(word, t, line, column):
+    start = 2 * (line * LINE + jnp.bitwise_xor(column, t))
+    splats = []
+    for col_block in range(2):
+        lanes = jnp.broadcast_to(word[:, col_block * TILE : (col_block + 1) * TILE], (8, TILE))
+        lanes = pltpu.roll(lanes, TILE - start, 1)
+        splats.append(
+            [jnp.broadcast_to(lanes[:, at : at + 1], (8, TILE)) for at in range(2)]
+        )
+    return splats
+
+
+def form_block(t, s, line, column, distance, word, out_ref):
     lane = lax.broadcasted_iota(jnp.int32, (8, TILE), 1)
     row_chunk = line * LINE + jnp.bitwise_xor(column, t)
     direct = row_chunk < jnp.bitwise_xor(line, s) * LINE + column
     shifts = [shift_up(direct, group, lane) for group in range(TILE // GROUP)]
+    splats = block_words(word, t, line, column)
     for row_block in range(2):
         for col_block in range(2):
-            word = jnp.full(lane.shape, words[s, col_block * TILE + 2 * row_chunk + row_block])
             lanes = slice(col_block * TILE, (col_block + 1) * TILE)
             for group, shift in enumerate(shifts):
                 first = row_block * TILE + group * GROUP
-                seen = jnp.left_shift(word, shift) < 0
+                seen = jnp.left_shift(splats[col_block][row_block], shift) < 0
                 halves = []
                 for half in range(first, first + GROUP, 8):
                     value = pl.reciprocal(distance[half : half + 8, lanes], approx=True)
@@ -116,12 +132,12 @@
                 )
 
 
-def form_own(me, distance, words, out_ref):
+def form_own(line, column, distance, word, out_ref):
     lane = lax.broadcasted_iota(jnp.int32, (8, TILE), 1)
     row = lax.broadcasted_iota(jnp.int32, (8, TILE), 0)
+    splats = block_words(word, 0, line, column)
     for row_block in range(2):
         for col_block in range(2):
-            word = words[0, col_block * TILE + 2 * me + row_block]
             lanes = slice(col_block * TILE, (col_block + 1) * TILE)
             for group in range(TILE // GROUP):
                 first = row_block * TILE + group * GROUP
@@ -129,7 +145,8 @@
                 for half in range(first, first + GROUP, 8):
                     i, j = row + half, lane + col_block * TILE
                     low, high = jnp.minimum(i, j) % TILE, jnp.maximum(i, j) % TILE
-                    seen = jnp.left_shift(word, 31 - (8 * (low // 32) + high // 16)) < 0
+                    shift = 31 - (8 * (low // 32) + high // 16)
+                    seen = jnp.left_shift(splats[col_block][row_block], shift) < 0
                     value = pl.reciprocal(distance[half : half + 8, lanes], approx=True)
                     halves.append(jnp.where(seen, value, 0.0))
                 out_ref[first : first + GROUP, lanes] = jnp.concatenate(halves).astype(
@@ -146,102 +163,123 @@
     return extra[0:3] + extra[3:6] + extra[6:9], word
 
 
+def form_all(blocks, line, column, row_terms, col_terms, words, fields, start, refs, finish_row):
+    kernel_ref, distance = refs
+    held = {}
+
+    def measure(place):
+        t, s = blocks[place]
+        distance[place % 2] = times(row_terms(t), col_terms(s))
+
+    def add(place):
+        t, s = blocks[place]
+        term = times_transpose(fields[s], kernel_ref[place])
+        held[t] = (held[t] if t in held else start(t)) + term
+        if place + 1 == len(blocks) or blocks[place + 1][0] != t:
+            finish_row(t, held[t])
+
+    measure(0)
+    for place, (t, s) in enumerate(blocks):
+        if place + 1 < len(blocks):
+            measure(place + 1)
+        slot, out_ref = distance.at[place % 2], kernel_ref.at[place]
+        if t == 0 and s == 0:
+            form_own(line, column, slot, words[s], out_ref)
+        else:
+            form_block(t, s, line, column, slot, words[s], out_ref)
+        if place:
+            add(place - 1)
+    add(len(blocks) - 1)
+
+
 def grid_near(
     me_ref,
     own_ref,
     core_ref,
-    pair_ref,
     boost_ref,
     kernel_ref,
     partial_ref,
     row_terms,
-    words_vmem,
-    words,
+    col_terms,
     terms,
     distance,
-    sem,
 ):
     rhs_count = boost_ref.shape[0]
-    me = me_ref[0]
-    line, column = me // LINE, me % LINE
-    position, words_vmem[0:1, :] = read_extra(own_ref, rhs_count)
-    copy = pltpu.make_async_copy(words_vmem, words, sem)
-    copy.start()
-    distance_terms(position, terms, False)
-    col_terms = terms[...].astype(jnp.bfloat16)
-    for t, value in enumerate((position, core_ref[...], pair_ref[0], pair_ref[1])):
-        distance_terms(value, terms, True)
-        row_terms[t] = jnp.transpose(terms[...]).astype(jnp.bfloat16)
-    copy.wait()
-    own = own_ref[:rhs_count, :]
-
-    def measure(t):
-        distance[t % 2] = times(row_terms[t], col_terms)
-
-    def add(t):
-        held = times_transpose(own, kernel_ref[t])
-        partial_ref[t] = held + boost_ref[...] if t == 0 else held
-
-    measure(0)
-    for t in range(LINE):
-        if t + 1 < LINE:
-            measure(t + 1)
-        if t == 0:
-            form_own(me, distance.at[0], words, kernel_ref.at[0])
-        else:
-            form_block(t, 0, line, column, distance.at[t % 2], words, kernel_ref.at[t])
-            add(t - 1)
-    add(LINE - 1)
-
-
-def grid_lines(steps, last, me_ref, *refs):
-    count = len(steps)
-    lines, (own_ref, before_ref, row_terms, kernel_ref, partial_ref, *refs) = (
-        refs[:count],
-        refs[count:],
+    line, column = me_ref[0] // LINE, me_ref[0] % LINE
+    position, word = read_extra(own_ref, rhs_count)
+    distance_terms(position, terms.at[0], False)
+    col_terms[...] = terms[0].astype(jnp.bfloat16)
+    for t, value in enumerate((position, core_ref[...])):
+        distance_terms(value, terms.at[1 + t], True)
+        row_terms[t] = jnp.transpose(terms[1 + t]).astype(jnp.bfloat16)
+
+    def finish_row(t, value):
+        partial_ref[t] = value
+
+    form_all(
+        NEAR,
+        line,
+        column,
+        lambda t: row_terms[t],
+        lambda s: col_terms[...],
+        [word],
+        [own_ref[:rhs_count, :]],
+        lambda t: boost_ref[...] if t == 0 else 0.0,
+        (kernel_ref, distance),
+        finish_row,
     )
-    sent_ref, refs = (refs[0], refs[1:]) if last else (None, refs)
-    words_vmem, words, terms, col_terms, distance, sem = refs
+
+
+def grid_rest(
+    me_ref,
+    own_ref,
+    z1_ref,
+    z2_ref,
+    z3_ref,
+    pair_ref,
+    before_ref,
+    row_ref,
+    col_ref,
+    kernel_ref,
+    partial_ref,
+    sent_ref,
+    terms,
+    row_terms,
+    col_terms,
+    distance,
+):
     rhs_count = before_ref.shape[1]
-    me = me_ref[0]
-    line, column = me // LINE, me % LINE
-    positions = []
-    for s, ref in zip(steps, lines):
-        position, words_vmem[s : s + 1, :] = read_extra(ref, rhs_count)
-        positions.append(position)
-    copy = pltpu.make_async_copy(words_vmem, words, sem)
-    copy.start()
-    for at, position in enumerate(positions):
-        distance_terms(position, terms, False)
-        col_terms[at] = terms[...].astype(jnp.bfloat16)
-    copy.wait()
-    blocks = [(t, at) for t in range(LINE) for at in range(count)]
-    held = {}
-
-    def measure(place):
-        t, at = blocks[place]
-        distance[place % 2] = times(row_terms[t], col_terms[at])
-
-    def add(place):
-        t, at = blocks[place]
-        held[t] = held.get(t, before_ref[t]) + times_transpose(
-            lines[at][:rhs_count, :], kernel_ref[place]
-        )
-        if at == count - 1:
-            partial_ref[t] = held[t]
-            if last:
-                sent_ref[t * rhs_count : (t + 1) * rhs_count] = held[t].astype(jnp.bfloat16)
-
-    measure(0)
-    for place, (t, at) in enumerate(blocks):
-        if place + 1 < len(blocks):
-            measure(place + 1)
-        form_block(t, steps[at], line, column, distance.at[place % 2], words, kernel_ref.at[place])
-        if place:
-            add(place - 1)
-    add(len(blocks) - 1)
-    if last:
-        sent_ref[LINE * rhs_count :] = own_ref[rhs_count:]
+    line, column = me_ref[0] // LINE, me_ref[0] % LINE
+    lines = (own_ref, z1_ref, z2_ref, z3_ref)
+    words = []
+    for s, ref in enumerate(lines):
+        position, word = read_extra(ref, rhs_count)
+        words.append(word)
+        if s:
+            distance_terms(position, terms.at[s], False)
+            col_terms[s] = terms[s].astype(jnp.bfloat16)
+    for t in range(2):
+        slot = terms.at[LINE * t]
+        distance_terms(pair_ref[t], slot, True)
+        row_terms[t] = jnp.transpose(slot[...]).astype(jnp.bfloat16)
+
+    def finish_row(t, value):
+        partial_ref[t] = value
+        sent_ref[t * rhs_count : (t + 1) * rhs_count] = value.astype(jnp.bfloat16)
+
+    form_all(
+        REST,
+        line,
+        column,
+        lambda t: row_ref[t] if t < 2 else row_terms[t - 2],
+        lambda s: col_terms[s] if s else col_ref[...],
+        words,
+        [ref[:rhs_count, :] for ref in lines],
+        lambda t: before_ref[t] if t < 2 else 0.0,
+        (kernel_ref, distance),
+        finish_row,
+    )
+    sent_ref[LINE * rhs_count :] = own_ref[rhs_count:]
 
 
 def grid_middle(partial_ref, core_ref, own_ref, both_ref, sent_ref, rows):
@@ -257,7 +295,17 @@
     sent_ref[LINE * rhs_count :] = rows[...].astype(jnp.bfloat16)
 
 
-def grid_second(far_ref, both_ref, own_ref, x_ref, scaled_ref, q2_ref, q3_ref):
+def product(scaled_ref, near_ref, rest_ref, s):
+    held = None
+    for t in range(LINE):
+        near = (t, s) in NEAR
+        kernel = near_ref[NEAR.index((t, s))] if near else rest_ref[REST.index((t, s))]
+        term = times(scaled_ref[t], kernel)
+        held = term if held is None else held + term
+    return held
+
+
+def grid_second(rest_ref, both_ref, own_ref, x_ref, scaled_ref, q2_ref, q3_ref):
     rhs_count = q2_ref.shape[0]
     for t in range(LINE):
         terms = (own_ref, x_ref)[t // 2][LINE * rhs_count :, :].astype(jnp.float32)
@@ -266,19 +314,13 @@
         start = (t ^ 2) * rhs_count
         total = both_ref[t] + x_ref[start : start + rhs_count].astype(jnp.float32)
         scaled_ref[t] = (factor * total).astype(jnp.bfloat16)
-    for at, out_ref in enumerate((q2_ref, q3_ref)):
-        held = times(scaled_ref[0], far_ref[at])
-        for t in range(1, LINE):
-            held = held + times(scaled_ref[t], far_ref[2 * t + at])
-        out_ref[...] = held.astype(jnp.bfloat16)
-
-
-def grid_third(near_ref, next_ref, scaled_ref, q0_ref, q1_ref):
-    for kernel_ref, out_ref in ((next_ref, q1_ref), (near_ref, q0_ref)):
-        held = times(scaled_ref[0], kernel_ref[0])
-        for t in range(1, LINE):
-            held = held + times(scaled_ref[t], kernel_ref[t])
-        out_ref[...] = held.astype(out_ref.dtype)
+    q3_ref[...] = product(scaled_ref, None, rest_ref, 3).astype(jnp.bfloat16)
+    q2_ref[...] = product(scaled_ref, None, rest_ref, 2).astype(jnp.bfloat16)
+
+
+def grid_third(near_ref, rest_ref, scaled_ref, q0_ref, q1_ref):
+    q1_ref[...] = product(scaled_ref, None, rest_ref, 1).astype(jnp.bfloat16)
+    q0_ref[...] = product(scaled_ref, near_ref, rest_ref, 0)
 
 
 def grid_last(scale, q3_ref, q2_ref, q1_ref, q0_ref, *rest):
@@ -320,55 +362,44 @@
         compiler_params=params,
         name="prepare",
     )(*[pltpu.with_memory_space_constraint(value, pltpu.HBM) for value in arguments])
-    line3, line2 = send(packed, 3 * LINE), send(packed, 2 * LINE)
+    lines = [send(packed, LINE * step) for step in range(1, LINE)]
     core = send(position, 1)
-    later, core = lax.optimization_barrier((packed, core))
-    line1 = send(later, LINE)
     pair = send(jnp.stack([spot, core]), 2)
-    words_scratch = [
-        pltpu.VMEM((LINE, own_width), jnp.int32),
-        pltpu.SMEM((LINE, own_width), jnp.int32),
-        pltpu.VMEM((TERMS, own_width), jnp.float32),
-    ]
+    terms = (TERMS, own_width)
     distance = pltpu.VMEM((2, own_width, own_width), jnp.float32)
-    near, partial, row_terms = pl.pallas_call(
+    near, partial, row_terms, col_terms = pl.pallas_call(
         grid_near,
-        in_specs=[smem] + [vmem] * 4,
+        in_specs=[smem] + [vmem] * 3,
+        out_specs=[vmem] * 4,
+        out_shape=[
+            shaped((len(NEAR), own_width, own_width), jnp.bfloat16),
+            shaped((2,) + field, jnp.float32),
+            shaped((2, own_width, TERMS), jnp.bfloat16),
+            shaped(terms, jnp.bfloat16),
+        ],
+        scratch_shapes=[pltpu.VMEM((3,) + terms, jnp.float32), distance],
+        compiler_params=params,
+        name="grid_near",
+    )(my_index, packed, core, boost)
+    sent = shaped((LINE * rhs_count + EXTRA, own_width), jnp.bfloat16)
+    rest, partial, terms = pl.pallas_call(
+        grid_rest,
+        in_specs=[smem] + [vmem] * 8,
         out_specs=[vmem] * 3,
         out_shape=[
-            shaped((LINE, own_width, own_width), jnp.bfloat16),
+            shaped((len(REST), own_width, own_width), jnp.bfloat16),
             shaped((LINE,) + field, jnp.float32),
-            shaped((LINE, own_width, TERMS), jnp.bfloat16),
-        ],
-        scratch_shapes=words_scratch + [distance, pltpu.SemaphoreType.DMA],
-        compiler_params=params,
-        name="grid_near",
-    )(my_index, packed, core, pair, boost)
-    sent = shaped((LINE * rhs_count + EXTRA, own_width), jnp.bfloat16)
-
-    def form_lines(steps, last, name, *operands):
-        count = len(steps)
-        return pl.pallas_call(
-            functools.partial(grid_lines, steps, last),
-            in_specs=[smem] + [vmem] * (count + 3),
-            out_specs=[vmem] * (3 if last else 2),
-            out_shape=[
-                shaped((LINE * count, own_width, own_width), jnp.bfloat16),
-                shaped((LINE,) + field, jnp.float32),
-            ]
-            + [sent] * last,
-            scratch_shapes=words_scratch
-            + [
-                pltpu.VMEM((count, TERMS, own_width), jnp.bfloat16),
-                distance,
-                pltpu.SemaphoreType.DMA,
-            ],
-            compiler_params=params,
-            name=name,
-        )(my_index, *operands, row_terms)
-
-    next_, partial = form_lines((1,), False, "grid_next", line1, packed, partial)
-    far, partial, terms = form_lines((2, 3), True, "grid_far", line2, line3, packed, partial)
+            sent,
+        ],
+        scratch_shapes=[
+            pltpu.VMEM((LINE + 1,) + terms, jnp.float32),
+            pltpu.VMEM((2, own_width, TERMS), jnp.bfloat16),
+            pltpu.VMEM((LINE,) + terms, jnp.bfloat16),
+            distance,
+        ],
+        compiler_params=params,
+        name="grid_rest",
+    )(my_index, packed, *lines, pair, partial, row_terms, col_terms)
     both, terms = pl.pallas_call(
         grid_middle,
         in_specs=[vmem] * 3,
@@ -385,7 +416,7 @@
         out_shape=[shaped((LINE,) + field, jnp.bfloat16)] + [shaped(field, jnp.bfloat16)] * 2,
         compiler_params=params,
         name="grid_second",
-    )(far, both, terms, send(terms, 2))
+    )(rest, both, terms, send(terms, 2))
     sum3, sum2 = send(sum3, 3 * LINE), send(sum2, 2 * LINE)
     sum0, sum1 = pl.pallas_call(
         grid_third,
@@ -399,7 +430,7 @@
             transcendentals=0,
         ),
         name="grid_third",
-    )(near, next_, scaled)
+    )(near, rest, scaled)
     sum1 = send(sum1, LINE)
     adjoint, grad = pl.pallas_call(
         functools.partial(grid_last, scale),

time: 32.5 us -> 29.8 us (0.917)
  Pallas kernels: 6.49 us -> 4.48 us
  waiting for transfers between devices: 11.2 us -> 10.7 us
    pallas_call x3 -> x2, Pallas kernels: 4.2 us -> 2.18 us  [the longest x1 1.48 us: on_grid(): pl.pallas_call(grid_rest, in_specs=[smem] + [vmem] * 8, out_specs=[vmem]...]
    ppermute x10, waiting for transfers between devices: 11.2 us -> 10.7 us  [send(): lax.ppermute(value, 'row', [(at, at ^ step) for at in range(devices)])]
  transfers between devices with their start and end apart: 10 -> 10, of which waited for: 5 -> 6; matrix products, arithmetic and copies ran while one was open for 0% -> 0% of each run, Pallas kernels for 12% -> 7%
where the time goes in v3:
time: 29.8 us; the launch traced here: 29.6 us
  starting transfers between devices  13.7 us (46%)
  waiting for transfers between devices  10.7 us (36%)
  Pallas kernels  4.48 us (15%)
  between operations  0.73 us (2%)
    ppermute x10, starting transfers between devices, send(): lax.ppermute(value, 'row', [(at, at ^ step) for at in range(devices)])  13.7 us
    ppermute x10, waiting for transfers between devices, send(): lax.ppermute(value, 'row', [(at, at ^ step) for at in range(devices)])  10.7 us
    pallas_call x1, Pallas kernels, on_grid(): pl.pallas_call(grid_rest, in_specs=[smem] + [vmem] * 8, out_specs=[vmem]...  1.48 us
    pallas_call x1, Pallas kernels, on_grid(): pl.pallas_call(functools.partial(prepare, scale), in_specs=[pl.BlockSpec(...  0.97 us
    pallas_call x1, Pallas kernels, on_grid(): pl.pallas_call(grid_near, in_specs=[smem] + [vmem] * 3, out_specs=[vmem]...  0.7 us
    pallas_call x1, Pallas kernels, on_grid(): pl.pallas_call(functools.partial(grid_last, scale), in_specs=[vmem] * 9,...  0.67 us
  transfers between devices with their start and end apart: 10, of which 6 were waited for; matrix products, arithmetic and copies ran while one was open for 0% of the time, Pallas kernels for 7%

profile of v3, /device:TPU:0, one launch (start us, length us, event | category | flops | bytes accessed | tf_op | source)
XLA Modules:
  0.0 29.6 jit_solution(15225270848059410556)
XLA Ops:
  0.6 0.5 %collective-permute-start.3 = (f32[3,256]{1,0:T(4,128)}, f32[3,256]{1,0:T(4,128)S(1)}, u32[]{:S(2)}, u32[]{:S(2)}) collective-permute-start(f32[3,256]{1,0:T(4,128)} %refs_0_.1), channel_id=1, source_target_pairs={{0,1},{1,0},{2,3},{3,2},{4,5},{5,4},{6,7},{7,6},{8,9},{9,8},{10,11... | collective-permute-start | bytes 9224 | tf_op jit(solution)/shard_map/ppermute | solution.py:347
  1.1 1.0 %prepare.1 = (bf16[80,256]{1,0:T(8,128)(2,1)S(1)}, f32[64,256]{1,0:T(8,128)S(1)}, f32[3,256]{1,0:T(4,128)S(1)}) custom-call(f32[3,256]{1,0:T(4,128)} %refs_0_.1, s32[2,32]{1,0:T(2,128)} %refs_1_.1, f32[1,256]{1,0:T(1,128)} %bitcast.7, f32[1,256]{1,0:T(1,128)} %bitcast.9, f32[64,256]{1,0:T(8,128)} %rest_0_.1), custom_call_target="tpu_custom_call" | custom-call | tf_op jit(solution)/shard_map/prepare/pallas_call | solution.py:350
  2.1 4.7 %collective-permute-start.2 = (bf16[80,256]{1,0:T(8,128)(2,1)S(1)}, bf16[80,256]{1,0:T(8,128)(2,1)S(1)}, u32[]{:S(2)}, u32[]{:S(2)}) collective-permute-start(bf16[80,256]{1,0:T(8,128)(2,1)S(1)} %get-tuple-element.21.own_ref), channel_id=1, source_target_pairs={{0,12},{1,13},{2,14},{3,15},{4,8},{5,9},{6,10},{7,11},{8,4},{9,5},... | collective-permute-start | bytes 122888 | tf_op jit(solution)/shard_map/ppermute | solution.py:347
  6.8 0.0 collective-permute-start.1
  6.8 0.6 %collective-permute-start = (bf16[80,256]{1,0:T(8,128)(2,1)S(1)}, bf16[80,256]{1,0:T(8,128)(2,1)S(1)}, u32[]{:S(2)}, u32[]{:S(2)}) collective-permute-start(bf16[80,256]{1,0:T(8,128)(2,1)S(1)} %get-tuple-element.21.own_ref), channel_id=1, source_target_pairs={{0,4},{1,5},{2,6},{3,7},{4,0},{5,1},{6,2},{7,3},{8,12},{9,13},{10,... | collective-permute-start | bytes 122888 | tf_op jit(solution)/shard_map/ppermute | solution.py:347
  7.5 0.0 collective-permute-done.3.core_ref
  7.5 1.7 %collective-permute-start.4 = (f32[2,3,256]{2,1,0:T(4,128)S(1)}, f32[2,3,256]{2,1,0:T(4,128)S(1)}, u32[]{:S(2)}, u32[]{:S(2)}) collective-permute-start(f32[2,3,256]{2,1,0:T(4,128)S(1)} %pad_maximum_fusion), channel_id=1, source_target_pairs={{0,2},{1,3},{2,0},{3,1},{4,6},{5,7},{6,4},{7,5},{8,10},{9,11},{10,... | collective-permute-start | bytes 18440 | tf_op jit(solution)/shard_map/ppermute | solution.py:347
  9.2 0.7 %grid_near.1 = (bf16[2,256,256]{2,1,0:T(8,128)(2,1)S(1)}, f32[2,64,256]{2,1,0:T(8,128)S(1)}, bf16[2,256,32]{2,1,0:T(8,128)(2,1)S(1)}, bf16[32,256]{1,0:T(8,128)(2,1)S(1)}) custom-call(s32[1]{0:T(128)} %bitcast.me_ref, bf16[80,256]{1,0:T(8,128)(2,1)S(1)} %get-tuple-element.21.own_ref, f32[3,256]{1,0:T(4,128)S(1)} %collective-permute-done.3.core_ref, ...), custom_call_target="tpu_custom_call" | custom-call | tf_op jit(solution)/shard_map/grid_near/pallas_call | solution.py:370
  9.9 1.3 %collective-permute-done.4.pair_ref = f32[2,3,256]{2,1,0:T(4,128)S(1)} collective-permute-done((f32[2,3,256]{2,1,0:T(4,128)S(1)}, f32[2,3,256]{2,1,0:T(4,128)S(1)}, u32[]{:S(2)}, u32[]{:S(2)}) %collective-permute-start.4) | collective-permute-done | bytes 6176 | tf_op jit(solution)/shard_map/ppermute | solution.py:347
  11.2 0.0 collective-permute-done.2.z3_ref
  11.2 0.5 %collective-permute-done.1.z2_ref = bf16[80,256]{1,0:T(8,128)(2,1)S(1)} collective-permute-done((bf16[80,256]{1,0:T(8,128)(2,1)S(1)}, bf16[80,256]{1,0:T(8,128)(2,1)S(1)}, u32[]{:S(2)}, u32[]{:S(2)}) %collective-permute-start.1) | collective-permute-done | bytes 40992 | tf_op jit(solution)/shard_map/ppermute | solution.py:347
  11.7 0.0 collective-permute-done.z1_ref
  11.7 1.5 %grid_rest.1 = (bf16[14,256,256]{2,1,0:T(8,128)(2,1)S(1)}, f32[4,64,256]{2,1,0:T(8,128)S(1)}, bf16[272,256]{1,0:T(8,128)(2,1)S(1)}) custom-call(s32[1]{0:T(128)} %bitcast.me_ref, bf16[80,256]{1,0:T(8,128)(2,1)S(1)} %get-tuple-element.21.own_ref, bf16[80,256]{1,0:T(8,128)(2,1)S(1)} %collective-permute-done.z1_ref, ...), custom_call_target="tpu_custom_call" | custom-call | tf_op jit(solution)/shard_map/grid_rest/pallas_call | solution.py:385
  13.2 0.1 collective-permute-start.5
  13.3 1.3 %collective-permute-done.5.core_ref = bf16[272,256]{1,0:T(8,128)(2,1)S(1)} collective-permute-done((bf16[272,256]{1,0:T(8,128)(2,1)S(1)}, bf16[272,256]{1,0:T(8,128)(2,1)S(1)}, u32[]{:S(2)}, u32[]{:S(2)}) %collective-permute-start.5) | collective-permute-done | bytes 139296 | tf_op jit(solution)/shard_map/ppermute | solution.py:347
  14.7 1.6 %collective-permute-start.6 = (bf16[272,256]{1,0:T(8,128)(2,1)S(1)}, bf16[272,256]{1,0:T(8,128)(2,1)S(1)}, u32[]{:S(2)}, u32[]{:S(2)}) collective-permute-start(bf16[272,256]{1,0:T(8,128)(2,1)S(1)} %get-tuple-element.31.own_ref), channel_id=1, source_target_pairs={{0,2},{1,3},{2,0},{3,1},{4,6},{5,7},{6,4},{7,5},{8,10},{9,11},{10,... | collective-permute-start | bytes 417800 | tf_op jit(solution)/shard_map/ppermute | solution.py:347
  16.2 4.2 %collective-permute-done.6.x_ref = bf16[272,256]{1,0:T(8,128)(2,1)S(1)} collective-permute-done((bf16[272,256]{1,0:T(8,128)(2,1)S(1)}, bf16[272,256]{1,0:T(8,128)(2,1)S(1)}, u32[]{:S(2)}, u32[]{:S(2)}) %collective-permute-start.6) | collective-permute-done | bytes 139296 | tf_op jit(solution)/shard_map/ppermute | solution.py:347
  20.5 0.0 copy-start
  20.5 0.0 copy-start.1
  20.5 0.0 copy-start.2
  20.5 0.0 copy-start.3
  20.5 0.0 copy-start.4
  20.5 0.3 %grid_second.1 = (bf16[4,64,256]{2,1,0:T(8,128)(2,1)S(1)}, bf16[64,256]{1,0:T(8,128)(2,1)S(1)}, bf16[64,256]{1,0:T(8,128)(2,1)S(1)}) custom-call(bf16[14,256,256]{2,1,0:T(8,128)(2,1)S(1)} %get-tuple-element.27.rest_ref, f32[4,64,256]{2,1,0:T(8,128)S(1)} %get-tuple-element.30.both_ref, bf16[272,256]{1,0:T(8,128)(2,1)S(1)} %get-tuple-element.31.own_ref, ...), custom_call_target="tpu_custom_call" | custom-call | tf_op jit(solution)/shard_map/grid_second/pallas_call | solution.py:412
  20.8 3.3 %collective-permute-start.7 = (bf16[64,256]{1,0:T(8,128)(2,1)S(1)}, bf16[64,256]{1,0:T(8,128)(2,1)S(1)}, u32[]{:S(2)}, u32[]{:S(2)}) collective-permute-start(bf16[64,256]{1,0:T(8,128)(2,1)S(1)} %get-tuple-element.32), channel_id=1, source_target_pairs={{0,12},{1,13},{2,14},{3,15},{4,8},{5,9},{6,10},{7,11},{8,4},{9,5},... | collective-permute-start | bytes 98312 | tf_op jit(solution)/shard_map/ppermute | solution.py:347
  24.1 0.0 collective-permute-start.8
  24.1 0.3 %grid_third.1 = (f32[64,256]{1,0:T(8,128)S(1)}, bf16[64,256]{1,0:T(8,128)(2,1)S(1)}) custom-call(bf16[2,256,256]{2,1,0:T(8,128)(2,1)S(1)} %get-tuple-element.34.near_ref, bf16[14,256,256]{2,1,0:T(8,128)(2,1)S(1)} %get-tuple-element.27.rest_ref, bf16[4,64,256]{2,1,0:T(8,128)(2,1)S(1)} %get-tuple-element.35.scaled_ref), custom_call_target="tpu_custom_call" | custom-call | flops 67108864 | bytes 1245184 | tf_op jit(solution)/shard_map/grid_third/pallas_call | solution.py:421
  24.4 1.2 %collective-permute-start.9 = (bf16[64,256]{1,0:T(8,128)(2,1)S(1)}, bf16[64,256]{1,0:T(8,128)(2,1)S(1)}, u32[]{:S(2)}, u32[]{:S(2)}) collective-permute-start(bf16[64,256]{1,0:T(8,128)(2,1)S(1)} %get-tuple-element.36), channel_id=1, source_target_pairs={{0,4},{1,5},{2,6},{3,7},{4,0},{5,1},{6,2},{7,3},{8,12},{9,13},{10,... | collective-permute-start | bytes 98312 | tf_op jit(solution)/shard_map/ppermute | solution.py:347
  25.6 1.0 %collective-permute-done.7.q3_ref = bf16[64,256]{1,0:T(8,128)(2,1)S(1)} collective-permute-done((bf16[64,256]{1,0:T(8,128)(2,1)S(1)}, bf16[64,256]{1,0:T(8,128)(2,1)S(1)}, u32[]{:S(2)}, u32[]{:S(2)}) %collective-permute-start.7) | collective-permute-done | bytes 32800 | tf_op jit(solution)/shard_map/ppermute | solution.py:347
  26.7 2.2 %collective-permute-done.8.q2_ref = bf16[64,256]{1,0:T(8,128)(2,1)S(1)} collective-permute-done((bf16[64,256]{1,0:T(8,128)(2,1)S(1)}, bf16[64,256]{1,0:T(8,128)(2,1)S(1)}, u32[]{:S(2)}, u32[]{:S(2)}) %collective-permute-start.8) | collective-permute-done | bytes 32800 | tf_op jit(solution)/shard_map/ppermute | solution.py:347
  28.9 0.0 collective-permute-done.9.q1_ref
  28.9 0.0 copy-done
  28.9 0.0 copy-done.1
  28.9 0.0 copy-done.2
  28.9 0.0 copy-done.3
  28.9 0.0 copy-done.4
  28.9 0.7 %grid_last.1 = (f32[64,256]{1,0:T(8,128)}, f32[1,256]{1,0:T(1,128)}) custom-call(bf16[64,256]{1,0:T(8,128)(2,1)S(1)} %collective-permute-done.7.q3_ref, bf16[64,256]{1,0:T(8,128)(2,1)S(1)} %collective-permute-done.8.q2_ref, bf16[64,256]{1,0:T(8,128)(2,1)S(1)} %collective-permute-done.9.q1_ref, f32[64,256]{1,0:T(8,128)S(1)} %get-tuple-element.37.q0_ref, ...), custom_call_target="tpu_custom_call" | custom-call | tf_op jit(solution)/shard_map/grid_last/pallas_call | solution.py:435
  (2 shorter events, 0.0 us)
Async XLA Ops:
  0.6 6.8 %collective-permute-start.3 = (f32[3,256]{1,0:T(4,128)}, f32[3,256]{1,0:T(4,128)S(1)}, u32[]{:S(2)}, u32[]{:S(2)}) collective-permute-start(f32[3,256]{1,0:T(4,128)} %refs_0_.1), channel_id=1, source_target_pairs={{0,1},{1,0},{2,3},{3,2},{4,5},{5,4},{6,7},{7,6},{8,9},{9,8},{10,11... | collective-permute-start | bytes 9224 | tf_op jit(solution)/shard_map/ppermute | solution.py:347
  2.1 9.0 %collective-permute-start.2 = (bf16[80,256]{1,0:T(8,128)(2,1)S(1)}, bf16[80,256]{1,0:T(8,128)(2,1)S(1)}, u32[]{:S(2)}, u32[]{:S(2)}) collective-permute-start(bf16[80,256]{1,0:T(8,128)(2,1)S(1)} %get-tuple-element.21.own_ref), channel_id=1, source_target_pairs={{0,12},{1,13},{2,14},{3,15},{4,8},{5,9},{6,10},{7,11},{8,4},{9,5},... | collective-permute-start | bytes 122888 | tf_op jit(solution)/shard_map/ppermute | solution.py:347
  6.8 4.9 %collective-permute-start.1 = (bf16[80,256]{1,0:T(8,128)(2,1)S(1)}, bf16[80,256]{1,0:T(8,128)(2,1)S(1)}, u32[]{:S(2)}, u32[]{:S(2)}) collective-permute-start(bf16[80,256]{1,0:T(8,128)(2,1)S(1)} %get-tuple-element.21.own_ref), channel_id=1, source_target_pairs={{0,8},{1,9},{2,10},{3,11},{4,12},{5,13},{6,14},{7,15},{8,0},{9,1},... | collective-permute-start | bytes 122888 | tf_op jit(solution)/shard_map/ppermute | solution.py:347
  6.8 4.9 %collective-permute-start = (bf16[80,256]{1,0:T(8,128)(2,1)S(1)}, bf16[80,256]{1,0:T(8,128)(2,1)S(1)}, u32[]{:S(2)}, u32[]{:S(2)}) collective-permute-start(bf16[80,256]{1,0:T(8,128)(2,1)S(1)} %get-tuple-element.21.own_ref), channel_id=1, source_target_pairs={{0,4},{1,5},{2,6},{3,7},{4,0},{5,1},{6,2},{7,3},{8,12},{9,13},{10,... | collective-permute-start | bytes 122888 | tf_op jit(solution)/shard_map/ppermute | solution.py:347
  7.5 3.7 %collective-permute-start.4 = (f32[2,3,256]{2,1,0:T(4,128)S(1)}, f32[2,3,256]{2,1,0:T(4,128)S(1)}, u32[]{:S(2)}, u32[]{:S(2)}) collective-permute-start(f32[2,3,256]{2,1,0:T(4,128)S(1)} %pad_maximum_fusion), channel_id=1, source_target_pairs={{0,2},{1,3},{2,0},{3,1},{4,6},{5,7},{6,4},{7,5},{8,10},{9,11},{10,... | collective-permute-start | bytes 18440 | tf_op jit(solution)/shard_map/ppermute | solution.py:347
  13.2 1.4 %collective-permute-start.5 = (bf16[272,256]{1,0:T(8,128)(2,1)S(1)}, bf16[272,256]{1,0:T(8,128)(2,1)S(1)}, u32[]{:S(2)}, u32[]{:S(2)}) collective-permute-start(bf16[272,256]{1,0:T(8,128)(2,1)S(1)} %get-tuple-element.29), channel_id=1, source_target_pairs={{0,1},{1,0},{2,3},{3,2},{4,5},{5,4},{6,7},{7,6},{8,9},{9,8},{10,11... | collective-permute-start | bytes 417800 | tf_op jit(solution)/shard_map/ppermute | solution.py:347
  14.7 5.8 %collective-permute-start.6 = (bf16[272,256]{1,0:T(8,128)(2,1)S(1)}, bf16[272,256]{1,0:T(8,128)(2,1)S(1)}, u32[]{:S(2)}, u32[]{:S(2)}) collective-permute-start(bf16[272,256]{1,0:T(8,128)(2,1)S(1)} %get-tuple-element.31.own_ref), channel_id=1, source_target_pairs={{0,2},{1,3},{2,0},{3,1},{4,6},{5,7},{6,4},{7,5},{8,10},{9,11},{10,... | collective-permute-start | bytes 417800 | tf_op jit(solution)/shard_map/ppermute | solution.py:347
  20.5 8.4 %copy-start = (f32[64,256]{1,0:T(8,128)S(1)}, f32[64,256]{1,0:T(8,128)}, u32[]{:S(2)}) copy-start(f32[64,256]{1,0:T(8,128)} %rest_0_.1) | copy-start | bytes 196612
  20.5 8.4 %copy-start.1 = (bf16[64,256]{1,0:T(8,128)(2,1)S(1)}, bf16[64,256]{1,0:T(8,128)(2,1)}, u32[]{:S(2)}) copy-start(bf16[64,256]{1,0:T(8,128)(2,1)} %rest_3_.1) | copy-start | bytes 98308
  20.5 8.4 %copy-start.2 = (bf16[64,256]{1,0:T(8,128)(2,1)S(1)}, bf16[64,256]{1,0:T(8,128)(2,1)}, u32[]{:S(2)}) copy-start(bf16[64,256]{1,0:T(8,128)(2,1)} %rest_4_.1) | copy-start | bytes 98308
  20.5 8.5 %copy-start.3 = (f32[256]{0:T(256)S(1)}, f32[256]{0:T(256)}, u32[]{:S(2)}) copy-start(f32[256]{0:T(256)} %param.11) | copy-start | bytes 3076
  20.5 8.5 %copy-start.4 = (f32[256]{0:T(256)S(1)}, f32[256]{0:T(256)}, u32[]{:S(2)}) copy-start(f32[256]{0:T(256)} %param.10) | copy-start | bytes 3076
  20.8 5.9 %collective-permute-start.7 = (bf16[64,256]{1,0:T(8,128)(2,1)S(1)}, bf16[64,256]{1,0:T(8,128)(2,1)S(1)}, u32[]{:S(2)}, u32[]{:S(2)}) collective-permute-start(bf16[64,256]{1,0:T(8,128)(2,1)S(1)} %get-tuple-element.32), channel_id=1, source_target_pairs={{0,12},{1,13},{2,14},{3,15},{4,8},{5,9},{6,10},{7,11},{8,4},{9,5},... | collective-permute-start | bytes 98312 | tf_op jit(solution)/shard_map/ppermute | solution.py:347
  24.1 4.8 %collective-permute-start.8 = (bf16[64,256]{1,0:T(8,128)(2,1)S(1)}, bf16[64,256]{1,0:T(8,128)(2,1)S(1)}, u32[]{:S(2)}, u32[]{:S(2)}) collective-permute-start(bf16[64,256]{1,0:T(8,128)(2,1)S(1)} %get-tuple-element.33), channel_id=1, source_target_pairs={{0,8},{1,9},{2,10},{3,11},{4,12},{5,13},{6,14},{7,15},{8,0},{9,1},... | collective-permute-start | bytes 98312 | tf_op jit(solution)/shard_map/ppermute | solution.py:347
  24.4 4.5 %collective-permute-start.9 = (bf16[64,256]{1,0:T(8,128)(2,1)S(1)}, bf16[64,256]{1,0:T(8,128)(2,1)S(1)}, u32[]{:S(2)}, u32[]{:S(2)}) collective-permute-start(bf16[64,256]{1,0:T(8,128)(2,1)S(1)} %get-tuple-element.36), channel_id=1, source_target_pairs={{0,4},{1,5},{2,6},{3,7},{4,0},{5,1},{6,2},{7,3},{8,12},{9,13},{10,... | collective-permute-start | bytes 98312 | tf_op jit(solution)/shard_map/ppermute | solution.py:347

commit v4 on v3

--- a/solution.py
+++ b/solution.py
@@ -49,7 +49,7 @@
 
 
 def prepare(scale, *refs):
-    arguments, (packed_ref, boost_ref, spot_ref, rows, *held, sems) = refs[:5], refs[5:]
+    arguments, (packed_ref, spot_ref, rows, *held, sems) = refs[:5], refs[5:]
     copies = [
         pltpu.make_async_copy(argument, ref, sems.at[at])
         for at, (argument, ref) in enumerate(zip(arguments, held))
@@ -74,7 +74,6 @@
             rows[12 + place : 13 + place, start : start + count] = part[local : local + 1]
     packed_ref[:rhs_count] = (reflectance_ref[...] * seed_ref[...]).astype(jnp.bfloat16)
     packed_ref[rhs_count:] = rows[...].astype(jnp.bfloat16)
-    boost_ref[...] = seed_ref[...] * (1.0 / weight)
     spot_ref[...] = pos_ref[...]
 
 
@@ -193,18 +192,29 @@
 
 
 def grid_near(
+    scale,
     me_ref,
     own_ref,
     core_ref,
-    boost_ref,
+    seed_hbm,
+    area_hbm,
     kernel_ref,
     partial_ref,
     row_terms,
     col_terms,
     terms,
     distance,
+    seed_ref,
+    area_ref,
+    sems,
 ):
-    rhs_count = boost_ref.shape[0]
+    copies = [
+        pltpu.make_async_copy(seed_hbm, seed_ref, sems.at[0]),
+        pltpu.make_async_copy(area_hbm, area_ref, sems.at[1]),
+    ]
+    for copy in copies:
+        copy.start()
+    rhs_count = seed_ref.shape[0]
     line, column = me_ref[0] // LINE, me_ref[0] % LINE
     position, word = read_extra(own_ref, rhs_count)
     distance_terms(position, terms.at[0], False)
@@ -224,10 +234,13 @@
         lambda s: col_terms[...],
         [word],
         [own_ref[:rhs_count, :]],
-        lambda t: boost_ref[...] if t == 0 else 0.0,
+        lambda t: 0.0,
         (kernel_ref, distance),
         finish_row,
     )
+    for copy in copies:
+        copy.wait()
+    partial_ref[0] = partial_ref[0] + seed_ref[...] * (1.0 / (area_ref[...] * scale))
 
 
 def grid_rest(
@@ -282,52 +295,62 @@
     sent_ref[LINE * rhs_count :] = own_ref[rhs_count:]
 
 
-def grid_middle(partial_ref, core_ref, own_ref, both_ref, sent_ref, rows):
+def grid_middle(partial_ref, core_ref, own_ref, both_ref, first_ref, second_ref, rows):
     rhs_count = partial_ref.shape[1]
+    half = rhs_count // 2
     for t in range(LINE):
         start = (t ^ 1) * rhs_count
         both = partial_ref[t] + core_ref[start : start + rhs_count].astype(jnp.float32)
         both_ref[t] = both
-        sent_ref[t * rhs_count : (t + 1) * rhs_count] = both.astype(jnp.bfloat16)
+        first_ref[t * half : (t + 1) * half] = both[:half].astype(jnp.bfloat16)
+        second_ref[t * half : (t + 1) * half] = both[half:].astype(jnp.bfloat16)
     rows[...] = jnp.zeros_like(rows)
     for at, ref in enumerate((own_ref, core_ref)):
         rows[3 * at : 3 * at + 3, :] = ref[-EXTRA:, :].astype(jnp.float32)[9:12]
-    sent_ref[LINE * rhs_count :] = rows[...].astype(jnp.bfloat16)
-
-
-def product(scaled_ref, near_ref, rest_ref, s):
+    for ref in (first_ref, second_ref):
+        ref[LINE * half :] = rows[...].astype(jnp.bfloat16)
+
+
+def product(scaled, near_ref, rest_ref, s):
     held = None
     for t in range(LINE):
         near = (t, s) in NEAR
         kernel = near_ref[NEAR.index((t, s))] if near else rest_ref[REST.index((t, s))]
-        term = times(scaled_ref[t], kernel)
+        term = times(scaled(t), kernel)
         held = term if held is None else held + term
     return held
 
 
-def grid_second(rest_ref, both_ref, own_ref, x_ref, scaled_ref, q2_ref, q3_ref):
-    rhs_count = q2_ref.shape[0]
+def grid_second(place, rest_ref, both_ref, own_ref, x_ref, scaled_ref, q2_ref, q3_ref):
+    half = q2_ref.shape[0]
     for t in range(LINE):
-        terms = (own_ref, x_ref)[t // 2][LINE * rhs_count :, :].astype(jnp.float32)
+        terms = (own_ref, x_ref)[t // 2][LINE * half :, :].astype(jnp.float32)
         at = 3 * (t % 2)
         factor = terms[at : at + 1] + terms[at + 1 : at + 2] + terms[at + 2 : at + 3]
-        start = (t ^ 2) * rhs_count
-        total = both_ref[t] + x_ref[start : start + rhs_count].astype(jnp.float32)
+        start = (t ^ 2) * half
+        total = both_ref[t, place * half : (place + 1) * half] + x_ref[
+            start : start + half
+        ].astype(jnp.float32)
         scaled_ref[t] = (factor * total).astype(jnp.bfloat16)
-    q3_ref[...] = product(scaled_ref, None, rest_ref, 3).astype(jnp.bfloat16)
-    q2_ref[...] = product(scaled_ref, None, rest_ref, 2).astype(jnp.bfloat16)
-
-
-def grid_third(near_ref, rest_ref, scaled_ref, q0_ref, q1_ref):
-    q1_ref[...] = product(scaled_ref, None, rest_ref, 1).astype(jnp.bfloat16)
-    q0_ref[...] = product(scaled_ref, near_ref, rest_ref, 0)
-
-
-def grid_last(scale, q3_ref, q2_ref, q1_ref, q0_ref, *rest):
-    total = q0_ref[...]
-    for ref in (q1_ref, q2_ref, q3_ref):
-        total = total + ref[...].astype(jnp.float32)
-    finish(scale, total, *rest)
+    q3_ref[...] = product(lambda t: scaled_ref[t], None, rest_ref, 3).astype(jnp.bfloat16)
+    q2_ref[...] = product(lambda t: scaled_ref[t], None, rest_ref, 2).astype(jnp.bfloat16)
+
+
+def grid_third(near_ref, rest_ref, first_ref, second_ref, q0_ref, first_q1_ref, second_q1_ref):
+    half = first_ref.shape[1]
+    scaled = [jnp.concatenate([first_ref[t], second_ref[t]]) for t in range(LINE)]
+    next_sum = product(lambda t: scaled[t], None, rest_ref, 1).astype(jnp.bfloat16)
+    first_q1_ref[...] = next_sum[:half]
+    second_q1_ref[...] = next_sum[half:]
+    q0_ref[...] = product(lambda t: scaled[t], near_ref, rest_ref, 0)
+
+
+def grid_last(scale, line_refs, q0_ref, *rest):
+    halves = [
+        sum(ref[...].astype(jnp.float32) for ref in refs)
+        for refs in ([line_refs[at] for at in [2, 3, 5]], [line_refs[at] for at in [0, 1, 4]])
+    ]
+    finish(scale, jnp.concatenate(halves) + q0_ref[...], *rest)
 
 
 def on_grid(adjoint_seed, radiosity, emission, reflectance, area, position, visibility):
@@ -346,14 +369,17 @@
     def send(value, step):
         return lax.ppermute(value, "row", [(at, at ^ step) for at in range(devices)])
 
-    arguments = (position, visibility, area, reflectance, adjoint_seed)
-    packed, boost, spot = pl.pallas_call(
+    hbm = pl.BlockSpec(memory_space=pltpu.HBM)
+    arguments = [
+        pltpu.with_memory_space_constraint(value, pltpu.HBM)
+        for value in (position, visibility, area, reflectance, adjoint_seed)
+    ]
+    packed, spot = pl.pallas_call(
         functools.partial(prepare, scale),
-        in_specs=[pl.BlockSpec(memory_space=pltpu.HBM)] * 5,
-        out_specs=[vmem] * 3,
+        in_specs=[hbm] * 5,
+        out_specs=[vmem] * 2,
         out_shape=[
             shaped((rhs_count + EXTRA, own_width), jnp.bfloat16),
-            shaped(field, jnp.float32),
             shaped(position.shape, jnp.float32),
         ],
         scratch_shapes=[pltpu.VMEM((EXTRA, own_width), jnp.float32)]
@@ -361,15 +387,15 @@
         + [pltpu.SemaphoreType.DMA((5,))],
         compiler_params=params,
         name="prepare",
-    )(*[pltpu.with_memory_space_constraint(value, pltpu.HBM) for value in arguments])
+    )(*arguments)
     lines = [send(packed, LINE * step) for step in range(1, LINE)]
     core = send(position, 1)
     pair = send(jnp.stack([spot, core]), 2)
     terms = (TERMS, own_width)
     distance = pltpu.VMEM((2, own_width, own_width), jnp.float32)
     near, partial, row_terms, col_terms = pl.pallas_call(
-        grid_near,
-        in_specs=[smem] + [vmem] * 3,
+        functools.partial(grid_near, scale),
+        in_specs=[smem] + [vmem] * 2 + [hbm] * 2,
         out_specs=[vmem] * 4,
         out_shape=[
             shaped((len(NEAR), own_width, own_width), jnp.bfloat16),
@@ -377,10 +403,16 @@
             shaped((2, own_width, TERMS), jnp.bfloat16),
             shaped(terms, jnp.bfloat16),
         ],
-        scratch_shapes=[pltpu.VMEM((3,) + terms, jnp.float32), distance],
+        scratch_shapes=[
+            pltpu.VMEM((3,) + terms, jnp.float32),
+            distance,
+            pltpu.VMEM(field, jnp.float32),
+            pltpu.VMEM((1, own_width), jnp.float32),
+            pltpu.SemaphoreType.DMA((2,)),
+        ],
         compiler_params=params,
         name="grid_near",
-    )(my_index, packed, core, boost)
+    )(my_index, packed, core, arguments[4], arguments[2])
     sent = shaped((LINE * rhs_count + EXTRA, own_width), jnp.bfloat16)
     rest, partial, terms = pl.pallas_call(
         grid_rest,
@@ -400,46 +432,56 @@
         compiler_params=params,
         name="grid_rest",
     )(my_index, packed, *lines, pair, partial, row_terms, col_terms)
-    both, terms = pl.pallas_call(
+    half = (rhs_count // 2, own_width)
+    both, first, second = pl.pallas_call(
         grid_middle,
         in_specs=[vmem] * 3,
-        out_specs=[vmem] * 2,
-        out_shape=[shaped((LINE,) + field, jnp.float32), sent],
+        out_specs=[vmem] * 3,
+        out_shape=[
+            shaped((LINE,) + field, jnp.float32),
+            shaped((LINE * half[0] + EXTRA, own_width), jnp.bfloat16),
+            shaped((LINE * half[0] + EXTRA, own_width), jnp.bfloat16),
+        ],
         scratch_shapes=[pltpu.VMEM((EXTRA, own_width), jnp.float32)],
         compiler_params=params,
         name="grid_middle",
     )(partial, send(terms, 1), packed)
-    scaled, sum2, sum3 = pl.pallas_call(
-        grid_second,
+    other = [send(first, 2), send(second, 2)]
+    scaled, far = [], []
+    for place in range(2):
+        scaled_half, sum2, sum3 = pl.pallas_call(
+            functools.partial(grid_second, place),
+            in_specs=[vmem] * 4,
+            out_specs=[vmem] * 3,
+            out_shape=[shaped((LINE,) + half, jnp.bfloat16)]
+            + [shaped(half, jnp.bfloat16)] * 2,
+            compiler_params=params,
+            name="grid_second",
+        )(rest, both, first, other[place])
+        scaled.append(scaled_half)
+        far += [send(sum3, 3 * LINE), send(sum2, 2 * LINE)]
+    sum0, *sum1 = pl.pallas_call(
+        grid_third,
         in_specs=[vmem] * 4,
         out_specs=[vmem] * 3,
-        out_shape=[shaped((LINE,) + field, jnp.bfloat16)] + [shaped(field, jnp.bfloat16)] * 2,
+        out_shape=[shaped(field, jnp.float32)] + [shaped(half, jnp.bfloat16)] * 2,
         compiler_params=params,
-        name="grid_second",
-    )(rest, both, terms, send(terms, 2))
-    sum3, sum2 = send(sum3, 3 * LINE), send(sum2, 2 * LINE)
-    sum0, sum1 = pl.pallas_call(
-        grid_third,
-        in_specs=[vmem] * 3,
-        out_specs=[vmem] * 2,
-        out_shape=[shaped(field, jnp.float32), shaped(field, jnp.bfloat16)],
-        compiler_params=params,
-        cost_estimate=pl.CostEstimate(
-            flops=4 * LINE * rhs_count * own_width**2,
-            bytes_accessed=4 * LINE * own_width**2 + 12 * rhs_count * own_width,
-            transcendentals=0,
-        ),
         name="grid_third",
-    )(near, rest, scaled)
-    sum1 = send(sum1, LINE)
+    )(near, rest, *scaled)
+    sum1 = [send(value, LINE) for value in sum1]
+    lines = [far[2], far[3], far[0], far[1], sum1[1], sum1[0]]
+
+    def last(*refs):
+        grid_last(scale, refs[:6], *refs[6:])
+
     adjoint, grad = pl.pallas_call(
-        functools.partial(grid_last, scale),
-        in_specs=[vmem] * 9,
+        last,
+        in_specs=[vmem] * 12,
         out_specs=[vmem, vmem],
         out_shape=[shaped(field, jnp.float32), shaped((1, own_width), jnp.float32)],
         compiler_params=params,
         name="grid_last",
-    )(sum3, sum2, sum1, sum0, adjoint_seed, area, reflectance, radiosity, emission)
+    )(*lines, sum0, adjoint_seed, area, reflectance, radiosity, emission)
     return adjoint, grad.reshape(own_width)
 
 

time: 29.8 us -> 32.9 us (1.10)
  starting transfers between devices: 13.7 us -> 18.1 us
  waiting for transfers between devices: 10.7 us -> 8.94 us
  Pallas kernels: 4.48 us -> 4.92 us
    ppermute x10 -> x14, starting transfers between devices: 13.7 us -> 18.1 us  [send(): lax.ppermute(value, 'row', [(at, at ^ step) for at in range(devices)])]
    ppermute x10 -> x14, waiting for transfers between devices: 10.7 us -> 8.94 us  [send(): lax.ppermute(value, 'row', [(at, at ^ step) for at in range(devices)])]
    pallas_call x6 -> x7, Pallas kernels: 3 us -> 3.44 us  [the longest x1 0.97 us: on_grid(): pl.pallas_call(functools.partial(prepare, scale), in_specs=[hbm] * 5, out...]
  transfers between devices with their start and end apart: 10 -> 14, of which waited for: 6 -> 8; matrix products, arithmetic and copies ran while one was open for 0% -> 0% of each run, Pallas kernels for 7% -> 8%
where the time goes in v4:
time: 32.9 us; the launch traced here: 32.7 us
  starting transfers between devices  18.1 us (55%)
  waiting for transfers between devices  8.94 us (27%)
  Pallas kernels  4.92 us (15%)
  between operations  0.73 us (2%)
    ppermute x14, starting transfers between devices, send(): lax.ppermute(value, 'row', [(at, at ^ step) for at in range(devices)])  18.1 us
    ppermute x14, waiting for transfers between devices, send(): lax.ppermute(value, 'row', [(at, at ^ step) for at in range(devices)])  8.94 us
    pallas_call x1, Pallas kernels, on_grid(): pl.pallas_call(grid_rest, in_specs=[smem] + [vmem] * 8, out_specs=[vmem]...  1.48 us
    pallas_call x1, Pallas kernels, on_grid(): pl.pallas_call(functools.partial(prepare, scale), in_specs=[hbm] * 5, out...  0.97 us
    pallas_call x1, Pallas kernels, on_grid(): pl.pallas_call(functools.partial(grid_near, scale), in_specs=[smem] + [vm...  0.89 us
    pallas_call x1, Pallas kernels, on_grid(): pl.pallas_call(last, in_specs=[vmem] * 12, out_specs=[vmem, vmem], out_sh...  0.67 us
  transfers between devices with their start and end apart: 14, of which 8 were waited for; matrix products, arithmetic and copies ran while one was open for 0% of the time, Pallas kernels for 8%

profile of v4, /device:TPU:0, one launch (start us, length us, event | category | flops | bytes accessed | tf_op | source)
XLA Modules:
  0.0 32.7 jit_solution(6712021421198935901)
XLA Ops:
  0.6 0.5 %collective-permute-start.3 = (f32[3,256]{1,0:T(4,128)}, f32[3,256]{1,0:T(4,128)S(1)}, u32[]{:S(2)}, u32[]{:S(2)}) collective-permute-start(f32[3,256]{1,0:T(4,128)} %refs_0_.1), channel_id=1, source_target_pairs={{0,1},{1,0},{2,3},{3,2},{4,5},{5,4},{6,7},{7,6},{8,9},{9,8},{10,11... | collective-permute-start | bytes 9224 | tf_op jit(solution)/shard_map/ppermute | solution.py:370
  1.1 1.0 %prepare.1 = (bf16[80,256]{1,0:T(8,128)(2,1)S(1)}, f32[3,256]{1,0:T(4,128)S(1)}) custom-call(f32[3,256]{1,0:T(4,128)} %refs_0_.1, s32[2,32]{1,0:T(2,128)} %refs_1_.1, f32[1,256]{1,0:T(1,128)} %bitcast.7, f32[1,256]{1,0:T(1,128)} %bitcast.10, f32[64,256]{1,0:T(8,128)} %refs_7_.1), custom_call_target="tpu_custom_call" | custom-call | tf_op jit(solution)/shard_map/prepare/pallas_call | solution.py:377
  2.1 4.7 %collective-permute-start.2 = (bf16[80,256]{1,0:T(8,128)(2,1)S(1)}, bf16[80,256]{1,0:T(8,128)(2,1)S(1)}, u32[]{:S(2)}, u32[]{:S(2)}) collective-permute-start(bf16[80,256]{1,0:T(8,128)(2,1)S(1)} %get-tuple-element.25.own_ref), channel_id=1, source_target_pairs={{0,12},{1,13},{2,14},{3,15},{4,8},{5,9},{6,10},{7,11},{8,4},{9,5},... | collective-permute-start | bytes 122888 | tf_op jit(solution)/shard_map/ppermute | solution.py:370
  6.8 0.0 collective-permute-start.1
  6.8 0.6 %collective-permute-start = (bf16[80,256]{1,0:T(8,128)(2,1)S(1)}, bf16[80,256]{1,0:T(8,128)(2,1)S(1)}, u32[]{:S(2)}, u32[]{:S(2)}) collective-permute-start(bf16[80,256]{1,0:T(8,128)(2,1)S(1)} %get-tuple-element.25.own_ref), channel_id=1, source_target_pairs={{0,4},{1,5},{2,6},{3,7},{4,0},{5,1},{6,2},{7,3},{8,12},{9,13},{10,... | collective-permute-start | bytes 122888 | tf_op jit(solution)/shard_map/ppermute | solution.py:370
  7.4 0.0 collective-permute-done.3.core_ref
  7.5 1.7 %collective-permute-start.4 = (f32[2,3,256]{2,1,0:T(4,128)S(1)}, f32[2,3,256]{2,1,0:T(4,128)S(1)}, u32[]{:S(2)}, u32[]{:S(2)}) collective-permute-start(f32[2,3,256]{2,1,0:T(4,128)S(1)} %pad_maximum_fusion), channel_id=1, source_target_pairs={{0,2},{1,3},{2,0},{3,1},{4,6},{5,7},{6,4},{7,5},{8,10},{9,11},{10,... | collective-permute-start | bytes 18440 | tf_op jit(solution)/shard_map/ppermute | solution.py:370
  9.2 0.9 %grid_near.1 = (bf16[2,256,256]{2,1,0:T(8,128)(2,1)S(1)}, f32[2,64,256]{2,1,0:T(8,128)S(1)}, bf16[2,256,32]{2,1,0:T(8,128)(2,1)S(1)}, bf16[32,256]{1,0:T(8,128)(2,1)S(1)}) custom-call(s32[1]{0:T(128)} %bitcast.me_ref, bf16[80,256]{1,0:T(8,128)(2,1)S(1)} %get-tuple-element.25.own_ref, f32[3,256]{1,0:T(4,128)S(1)} %collective-permute-done.3.core_ref, ...), custom_call_target="tpu_custom_call" | custom-call | tf_op jit(solution)/shard_map/grid_near/pallas_call | solution.py:396
  10.1 1.1 %collective-permute-done.4.pair_ref = f32[2,3,256]{2,1,0:T(4,128)S(1)} collective-permute-done((f32[2,3,256]{2,1,0:T(4,128)S(1)}, f32[2,3,256]{2,1,0:T(4,128)S(1)}, u32[]{:S(2)}, u32[]{:S(2)}) %collective-permute-start.4) | collective-permute-done | bytes 6176 | tf_op jit(solution)/shard_map/ppermute | solution.py:370
  11.2 0.0 collective-permute-done.2.z3_ref
  11.2 0.5 %collective-permute-done.1.z2_ref = bf16[80,256]{1,0:T(8,128)(2,1)S(1)} collective-permute-done((bf16[80,256]{1,0:T(8,128)(2,1)S(1)}, bf16[80,256]{1,0:T(8,128)(2,1)S(1)}, u32[]{:S(2)}, u32[]{:S(2)}) %collective-permute-start.1) | collective-permute-done | bytes 40992 | tf_op jit(solution)/shard_map/ppermute | solution.py:370
  11.7 0.0 collective-permute-done.z1_ref
  11.7 1.5 %grid_rest.1 = (bf16[14,256,256]{2,1,0:T(8,128)(2,1)S(1)}, f32[4,64,256]{2,1,0:T(8,128)S(1)}, bf16[272,256]{1,0:T(8,128)(2,1)S(1)}) custom-call(s32[1]{0:T(128)} %bitcast.me_ref, bf16[80,256]{1,0:T(8,128)(2,1)S(1)} %get-tuple-element.25.own_ref, bf16[80,256]{1,0:T(8,128)(2,1)S(1)} %collective-permute-done.z1_ref, ...), custom_call_target="tpu_custom_call" | custom-call | tf_op jit(solution)/shard_map/grid_rest/pallas_call | solution.py:417
  13.2 0.1 collective-permute-start.5
  13.3 1.3 %collective-permute-done.5.core_ref = bf16[272,256]{1,0:T(8,128)(2,1)S(1)} collective-permute-done((bf16[272,256]{1,0:T(8,128)(2,1)S(1)}, bf16[272,256]{1,0:T(8,128)(2,1)S(1)}, u32[]{:S(2)}, u32[]{:S(2)}) %collective-permute-start.5) | collective-permute-done | bytes 139296 | tf_op jit(solution)/shard_map/ppermute | solution.py:370
  14.7 1.6 %collective-permute-start.6 = (bf16[144,256]{1,0:T(8,128)(2,1)S(1)}, bf16[144,256]{1,0:T(8,128)(2,1)S(1)}, u32[]{:S(2)}, u32[]{:S(2)}) collective-permute-start(bf16[144,256]{1,0:T(8,128)(2,1)S(1)} %get-tuple-element.35), channel_id=1, source_target_pairs={{0,2},{1,3},{2,0},{3,1},{4,6},{5,7},{6,4},{7,5},{8,10},{9,11},{10,... | collective-permute-start | bytes 221192 | tf_op jit(solution)/shard_map/ppermute | solution.py:370
  16.2 0.5 %collective-permute-start.9 = (bf16[144,256]{1,0:T(8,128)(2,1)S(1)}, bf16[144,256]{1,0:T(8,128)(2,1)S(1)}, u32[]{:S(2)}, u32[]{:S(2)}) collective-permute-start(bf16[144,256]{1,0:T(8,128)(2,1)S(1)} %get-tuple-element.34.own_ref), channel_id=1, source_target_pairs={{0,2},{1,3},{2,0},{3,1},{4,6},{5,7},{6,4},{7,5},{8,10},{9,11},{10,... | collective-permute-start | bytes 221192 | tf_op jit(solution)/shard_map/ppermute | solution.py:370
  16.8 2.8 %collective-permute-done.6.x_ref = bf16[144,256]{1,0:T(8,128)(2,1)S(1)} collective-permute-done((bf16[144,256]{1,0:T(8,128)(2,1)S(1)}, bf16[144,256]{1,0:T(8,128)(2,1)S(1)}, u32[]{:S(2)}, u32[]{:S(2)}) %collective-permute-start.6) | collective-permute-done | bytes 73760 | tf_op jit(solution)/shard_map/ppermute | solution.py:370
  19.6 0.3 grid_second.2
  19.9 3.2 %collective-permute-start.7 = (bf16[32,256]{1,0:T(8,128)(2,1)S(1)}, bf16[32,256]{1,0:T(8,128)(2,1)S(1)}, u32[]{:S(2)}, u32[]{:S(2)}) collective-permute-start(bf16[32,256]{1,0:T(8,128)(2,1)S(1)} %get-tuple-element.36), channel_id=1, source_target_pairs={{0,12},{1,13},{2,14},{3,15},{4,8},{5,9},{6,10},{7,11},{8,4},{9,5},... | collective-permute-start | bytes 49160 | tf_op jit(solution)/shard_map/ppermute | solution.py:370
  23.1 0.0 copy-start
  23.1 0.0 copy-start.1
  23.1 0.0 copy-start.2
  23.1 0.0 copy-start.3
  23.1 0.0 copy-start.4
  23.1 0.1 collective-permute-start.8
  23.2 0.0 collective-permute-done.9.x_ref
  23.2 0.3 grid_second.3
  23.5 1.7 %collective-permute-start.10 = (bf16[32,256]{1,0:T(8,128)(2,1)S(1)}, bf16[32,256]{1,0:T(8,128)(2,1)S(1)}, u32[]{:S(2)}, u32[]{:S(2)}) collective-permute-start(bf16[32,256]{1,0:T(8,128)(2,1)S(1)} %get-tuple-element.38), channel_id=1, source_target_pairs={{0,12},{1,13},{2,14},{3,15},{4,8},{5,9},{6,10},{7,11},{8,4},{9,5},... | collective-permute-start | bytes 49160 | tf_op jit(solution)/shard_map/ppermute | solution.py:370
  25.2 1.3 %collective-permute-start.11 = (bf16[32,256]{1,0:T(8,128)(2,1)S(1)}, bf16[32,256]{1,0:T(8,128)(2,1)S(1)}, u32[]{:S(2)}, u32[]{:S(2)}) collective-permute-start(bf16[32,256]{1,0:T(8,128)(2,1)S(1)} %get-tuple-element.39), channel_id=1, source_target_pairs={{0,8},{1,9},{2,10},{3,11},{4,12},{5,13},{6,14},{7,15},{8,0},{9,1},... | collective-permute-start | bytes 49160 | tf_op jit(solution)/shard_map/ppermute | solution.py:370
  26.5 0.3 grid_third.1
  26.8 1.5 %collective-permute-start.12 = (bf16[32,256]{1,0:T(8,128)(2,1)S(1)}, bf16[32,256]{1,0:T(8,128)(2,1)S(1)}, u32[]{:S(2)}, u32[]{:S(2)}) collective-permute-start(bf16[32,256]{1,0:T(8,128)(2,1)S(1)} %get-tuple-element.43), channel_id=1, source_target_pairs={{0,4},{1,5},{2,6},{3,7},{4,0},{5,1},{6,2},{7,3},{8,12},{9,13},{10,... | collective-permute-start | bytes 49160 | tf_op jit(solution)/shard_map/ppermute | solution.py:370
  28.3 0.0 collective-permute-done.7.refs_0_
  28.3 0.6 %collective-permute-start.13 = (bf16[32,256]{1,0:T(8,128)(2,1)S(1)}, bf16[32,256]{1,0:T(8,128)(2,1)S(1)}, u32[]{:S(2)}, u32[]{:S(2)}) collective-permute-start(bf16[32,256]{1,0:T(8,128)(2,1)S(1)} %get-tuple-element.44), channel_id=1, source_target_pairs={{0,4},{1,5},{2,6},{3,7},{4,0},{5,1},{6,2},{7,3},{8,12},{9,13},{10,... | collective-permute-start | bytes 49160 | tf_op jit(solution)/shard_map/ppermute | solution.py:370
  28.9 0.0 collective-permute-done.8.refs_1_
  28.9 0.1 collective-permute-done.10.refs_2_
  29.0 0.8 %collective-permute-done.11.refs_3_ = bf16[32,256]{1,0:T(8,128)(2,1)S(1)} collective-permute-done((bf16[32,256]{1,0:T(8,128)(2,1)S(1)}, bf16[32,256]{1,0:T(8,128)(2,1)S(1)}, u32[]{:S(2)}, u32[]{:S(2)}) %collective-permute-start.11) | collective-permute-done | bytes 16416 | tf_op jit(solution)/shard_map/ppermute | solution.py:370
  29.8 0.8 %collective-permute-done.12.refs_4_ = bf16[32,256]{1,0:T(8,128)(2,1)S(1)} collective-permute-done((bf16[32,256]{1,0:T(8,128)(2,1)S(1)}, bf16[32,256]{1,0:T(8,128)(2,1)S(1)}, u32[]{:S(2)}, u32[]{:S(2)}) %collective-permute-start.12) | collective-permute-done | bytes 16416 | tf_op jit(solution)/shard_map/ppermute | solution.py:370
  30.6 1.4 %collective-permute-done.13.refs_5_ = bf16[32,256]{1,0:T(8,128)(2,1)S(1)} collective-permute-done((bf16[32,256]{1,0:T(8,128)(2,1)S(1)}, bf16[32,256]{1,0:T(8,128)(2,1)S(1)}, u32[]{:S(2)}, u32[]{:S(2)}) %collective-permute-start.13) | collective-permute-done | bytes 16416 | tf_op jit(solution)/shard_map/ppermute | solution.py:370
  32.0 0.0 copy-done
  32.0 0.0 copy-done.1
  32.0 0.0 copy-done.2
  32.0 0.0 copy-done.3
  32.0 0.0 copy-done.4
  32.0 0.7 %grid_last.1 = (f32[64,256]{1,0:T(8,128)}, f32[1,256]{1,0:T(1,128)}) custom-call(bf16[32,256]{1,0:T(8,128)(2,1)S(1)} %collective-permute-done.7.refs_0_, bf16[32,256]{1,0:T(8,128)(2,1)S(1)} %collective-permute-done.8.refs_1_, bf16[32,256]{1,0:T(8,128)(2,1)S(1)} %collective-permute-done.10.refs_2_, bf16[32,256]{1,0:T(8,128)(2,1)S(1)} %collective-permute-done.11.refs_3_, ...), custom_call_target="tpu_custom_call" | custom-call | tf_op jit(solution)/shard_map/grid_last/pallas_call | solution.py:477
  (2 shorter events, 0.0 us)
Async XLA Ops:
  0.6 6.8 %collective-permute-start.3 = (f32[3,256]{1,0:T(4,128)}, f32[3,256]{1,0:T(4,128)S(1)}, u32[]{:S(2)}, u32[]{:S(2)}) collective-permute-start(f32[3,256]{1,0:T(4,128)} %refs_0_.1), channel_id=1, source_target_pairs={{0,1},{1,0},{2,3},{3,2},{4,5},{5,4},{6,7},{7,6},{8,9},{9,8},{10,11... | collective-permute-start | bytes 9224 | tf_op jit(solution)/shard_map/ppermute | solution.py:370
  2.1 9.0 %collective-permute-start.2 = (bf16[80,256]{1,0:T(8,128)(2,1)S(1)}, bf16[80,256]{1,0:T(8,128)(2,1)S(1)}, u32[]{:S(2)}, u32[]{:S(2)}) collective-permute-start(bf16[80,256]{1,0:T(8,128)(2,1)S(1)} %get-tuple-element.25.own_ref), channel_id=1, source_target_pairs={{0,12},{1,13},{2,14},{3,15},{4,8},{5,9},{6,10},{7,11},{8,4},{9,5},... | collective-permute-start | bytes 122888 | tf_op jit(solution)/shard_map/ppermute | solution.py:370
  6.8 4.9 %collective-permute-start.1 = (bf16[80,256]{1,0:T(8,128)(2,1)S(1)}, bf16[80,256]{1,0:T(8,128)(2,1)S(1)}, u32[]{:S(2)}, u32[]{:S(2)}) collective-permute-start(bf16[80,256]{1,0:T(8,128)(2,1)S(1)} %get-tuple-element.25.own_ref), channel_id=1, source_target_pairs={{0,8},{1,9},{2,10},{3,11},{4,12},{5,13},{6,14},{7,15},{8,0},{9,1},... | collective-permute-start | bytes 122888 | tf_op jit(solution)/shard_map/ppermute | solution.py:370
  6.8 4.9 %collective-permute-start = (bf16[80,256]{1,0:T(8,128)(2,1)S(1)}, bf16[80,256]{1,0:T(8,128)(2,1)S(1)}, u32[]{:S(2)}, u32[]{:S(2)}) collective-permute-start(bf16[80,256]{1,0:T(8,128)(2,1)S(1)} %get-tuple-element.25.own_ref), channel_id=1, source_target_pairs={{0,4},{1,5},{2,6},{3,7},{4,0},{5,1},{6,2},{7,3},{8,12},{9,13},{10,... | collective-permute-start | bytes 122888 | tf_op jit(solution)/shard_map/ppermute | solution.py:370
  7.5 3.7 %collective-permute-start.4 = (f32[2,3,256]{2,1,0:T(4,128)S(1)}, f32[2,3,256]{2,1,0:T(4,128)S(1)}, u32[]{:S(2)}, u32[]{:S(2)}) collective-permute-start(f32[2,3,256]{2,1,0:T(4,128)S(1)} %pad_maximum_fusion), channel_id=1, source_target_pairs={{0,2},{1,3},{2,0},{3,1},{4,6},{5,7},{6,4},{7,5},{8,10},{9,11},{10,... | collective-permute-start | bytes 18440 | tf_op jit(solution)/shard_map/ppermute | solution.py:370
  13.2 1.4 %collective-permute-start.5 = (bf16[272,256]{1,0:T(8,128)(2,1)S(1)}, bf16[272,256]{1,0:T(8,128)(2,1)S(1)}, u32[]{:S(2)}, u32[]{:S(2)}) collective-permute-start(bf16[272,256]{1,0:T(8,128)(2,1)S(1)} %get-tuple-element.32), channel_id=1, source_target_pairs={{0,1},{1,0},{2,3},{3,2},{4,5},{5,4},{6,7},{7,6},{8,9},{9,8},{10,11... | collective-permute-start | bytes 417800 | tf_op jit(solution)/shard_map/ppermute | solution.py:370
  14.7 4.9 %collective-permute-start.6 = (bf16[144,256]{1,0:T(8,128)(2,1)S(1)}, bf16[144,256]{1,0:T(8,128)(2,1)S(1)}, u32[]{:S(2)}, u32[]{:S(2)}) collective-permute-start(bf16[144,256]{1,0:T(8,128)(2,1)S(1)} %get-tuple-element.35), channel_id=1, source_target_pairs={{0,2},{1,3},{2,0},{3,1},{4,6},{5,7},{6,4},{7,5},{8,10},{9,11},{10,... | collective-permute-start | bytes 221192 | tf_op jit(solution)/shard_map/ppermute | solution.py:370
  16.2 7.0 %collective-permute-start.9 = (bf16[144,256]{1,0:T(8,128)(2,1)S(1)}, bf16[144,256]{1,0:T(8,128)(2,1)S(1)}, u32[]{:S(2)}, u32[]{:S(2)}) collective-permute-start(bf16[144,256]{1,0:T(8,128)(2,1)S(1)} %get-tuple-element.34.own_ref), channel_id=1, source_target_pairs={{0,2},{1,3},{2,0},{3,1},{4,6},{5,7},{6,4},{7,5},{8,10},{9,11},{10,... | collective-permute-start | bytes 221192 | tf_op jit(solution)/shard_map/ppermute | solution.py:370
  19.9 8.4 %collective-permute-start.7 = (bf16[32,256]{1,0:T(8,128)(2,1)S(1)}, bf16[32,256]{1,0:T(8,128)(2,1)S(1)}, u32[]{:S(2)}, u32[]{:S(2)}) collective-permute-start(bf16[32,256]{1,0:T(8,128)(2,1)S(1)} %get-tuple-element.36), channel_id=1, source_target_pairs={{0,12},{1,13},{2,14},{3,15},{4,8},{5,9},{6,10},{7,11},{8,4},{9,5},... | collective-permute-start | bytes 49160 | tf_op jit(solution)/shard_map/ppermute | solution.py:370
  23.1 8.9 %copy-start = (f32[64,256]{1,0:T(8,128)S(1)}, f32[64,256]{1,0:T(8,128)}, u32[]{:S(2)}) copy-start(f32[64,256]{1,0:T(8,128)} %refs_7_.1) | copy-start | bytes 196612
  23.1 8.9 %copy-start.1 = (bf16[64,256]{1,0:T(8,128)(2,1)S(1)}, bf16[64,256]{1,0:T(8,128)(2,1)}, u32[]{:S(2)}) copy-start(bf16[64,256]{1,0:T(8,128)(2,1)} %refs_10_.1) | copy-start | bytes 98308
  23.1 8.9 %copy-start.2 = (bf16[64,256]{1,0:T(8,128)(2,1)S(1)}, bf16[64,256]{1,0:T(8,128)(2,1)}, u32[]{:S(2)}) copy-start(bf16[64,256]{1,0:T(8,128)(2,1)} %refs_11_.1) | copy-start | bytes 98308
  23.1 8.9 %copy-start.3 = (f32[256]{0:T(256)S(1)}, f32[256]{0:T(256)}, u32[]{:S(2)}) copy-start(f32[256]{0:T(256)} %param.11) | copy-start | bytes 3076
  23.1 8.9 %copy-start.4 = (f32[256]{0:T(256)S(1)}, f32[256]{0:T(256)}, u32[]{:S(2)}) copy-start(f32[256]{0:T(256)} %param.10) | copy-start | bytes 3076
  23.1 5.8 %collective-permute-start.8 = (bf16[32,256]{1,0:T(8,128)(2,1)S(1)}, bf16[32,256]{1,0:T(8,128)(2,1)S(1)}, u32[]{:S(2)}, u32[]{:S(2)}) collective-permute-start(bf16[32,256]{1,0:T(8,128)(2,1)S(1)} %get-tuple-element.37), channel_id=1, source_target_pairs={{0,8},{1,9},{2,10},{3,11},{4,12},{5,13},{6,14},{7,15},{8,0},{9,1},... | collective-permute-start | bytes 49160 | tf_op jit(solution)/shard_map/ppermute | solution.py:370
  23.5 5.6 %collective-permute-start.10 = (bf16[32,256]{1,0:T(8,128)(2,1)S(1)}, bf16[32,256]{1,0:T(8,128)(2,1)S(1)}, u32[]{:S(2)}, u32[]{:S(2)}) collective-permute-start(bf16[32,256]{1,0:T(8,128)(2,1)S(1)} %get-tuple-element.38), channel_id=1, source_target_pairs={{0,12},{1,13},{2,14},{3,15},{4,8},{5,9},{6,10},{7,11},{8,4},{9,5},... | collective-permute-start | bytes 49160 | tf_op jit(solution)/shard_map/ppermute | solution.py:370
  25.2 4.6 %collective-permute-start.11 = (bf16[32,256]{1,0:T(8,128)(2,1)S(1)}, bf16[32,256]{1,0:T(8,128)(2,1)S(1)}, u32[]{:S(2)}, u32[]{:S(2)}) collective-permute-start(bf16[32,256]{1,0:T(8,128)(2,1)S(1)} %get-tuple-element.39), channel_id=1, source_target_pairs={{0,8},{1,9},{2,10},{3,11},{4,12},{5,13},{6,14},{7,15},{8,0},{9,1},... | collective-permute-start | bytes 49160 | tf_op jit(solution)/shard_map/ppermute | solution.py:370
  26.8 3.8 %collective-permute-start.12 = (bf16[32,256]{1,0:T(8,128)(2,1)S(1)}, bf16[32,256]{1,0:T(8,128)(2,1)S(1)}, u32[]{:S(2)}, u32[]{:S(2)}) collective-permute-start(bf16[32,256]{1,0:T(8,128)(2,1)S(1)} %get-tuple-element.43), channel_id=1, source_target_pairs={{0,4},{1,5},{2,6},{3,7},{4,0},{5,1},{6,2},{7,3},{8,12},{9,13},{10,... | collective-permute-start | bytes 49160 | tf_op jit(solution)/shard_map/ppermute | solution.py:370
  28.3 3.7 %collective-permute-start.13 = (bf16[32,256]{1,0:T(8,128)(2,1)S(1)}, bf16[32,256]{1,0:T(8,128)(2,1)S(1)}, u32[]{:S(2)}, u32[]{:S(2)}) collective-permute-start(bf16[32,256]{1,0:T(8,128)(2,1)S(1)} %get-tuple-element.44), channel_id=1, source_target_pairs={{0,4},{1,5},{2,6},{3,7},{4,0},{5,1},{6,2},{7,3},{8,12},{9,13},{10,... | collective-permute-start | bytes 49160 | tf_op jit(solution)/shard_map/ppermute | solution.py:370

commit v5 on v4

--- a/solution.py
+++ b/solution.py
@@ -12,14 +12,16 @@
 SWEEPS = 2
 GROUP = 16
 LINE = 4
+GRID = 16
+FAR = 8
 EXTRA = 16
 TERMS = 32
 VMEM_BYTES = 48 * 1024 * 1024
 GRID_BYTES = 8 * 1024 * 1024
 
 
-NEAR = [(0, 0), (1, 0)]
-REST = [(t, s) for t in range(LINE) for s in range(LINE) if (t, s) not in NEAR]
+NEAR = [(t, v, 0) for t in range(2) for v in range(LINE)]
+REST = [(t, v, 1) for t in range(2) for v in range(LINE)]
 
 
 def three_terms(value):
@@ -98,24 +100,22 @@
     return 31 - jnp.where(direct, 8 * (group // 2) + lane // 16, 8 * (lane // 32) + group)
 
 
-def block_words(word, t, line, column):
-    start = 2 * (line * LINE + jnp.bitwise_xor(column, t))
+def block_words(word, row_chunk):
     splats = []
     for col_block in range(2):
         lanes = jnp.broadcast_to(word[:, col_block * TILE : (col_block + 1) * TILE], (8, TILE))
-        lanes = pltpu.roll(lanes, TILE - start, 1)
+        lanes = pltpu.roll(lanes, TILE - 2 * row_chunk, 1)
         splats.append(
             [jnp.broadcast_to(lanes[:, at : at + 1], (8, TILE)) for at in range(2)]
         )
     return splats
 
 
-def form_block(t, s, line, column, distance, word, out_ref):
+def form_block(row_chunk, col_chunk, distance, word, out_ref):
     lane = lax.broadcasted_iota(jnp.int32, (8, TILE), 1)
-    row_chunk = line * LINE + jnp.bitwise_xor(column, t)
-    direct = row_chunk < jnp.bitwise_xor(line, s) * LINE + column
+    direct = row_chunk < col_chunk
     shifts = [shift_up(direct, group, lane) for group in range(TILE // GROUP)]
-    splats = block_words(word, t, line, column)
+    splats = block_words(word, row_chunk)
     for row_block in range(2):
         for col_block in range(2):
             lanes = slice(col_block * TILE, (col_block + 1) * TILE)
@@ -131,10 +131,10 @@
                 )
 
 
-def form_own(line, column, distance, word, out_ref):
+def form_own(row_chunk, distance, word, out_ref):
     lane = lax.broadcasted_iota(jnp.int32, (8, TILE), 1)
     row = lax.broadcasted_iota(jnp.int32, (8, TILE), 0)
-    splats = block_words(word, 0, line, column)
+    splats = block_words(word, row_chunk)
     for row_block in range(2):
         for col_block in range(2):
             lanes = slice(col_block * TILE, (col_block + 1) * TILE)
@@ -153,8 +153,8 @@
                 )
 
 
-def read_extra(ref, rhs_count):
-    extra = ref[rhs_count:, :].astype(jnp.float32)
+def read_extra(rows):
+    extra = rows.astype(jnp.float32)
     value = extra[12:16].astype(jnp.int32)
     word = value[0:1]
     for place in range(1, 4):
@@ -162,47 +162,63 @@
     return extra[0:3] + extra[3:6] + extra[6:9], word
 
 
-def form_all(blocks, line, column, row_terms, col_terms, words, fields, start, refs, finish_row):
+def form_all(blocks, me, row_terms, col_terms, words, fields, start, refs, finish_row):
     kernel_ref, distance = refs
     held = {}
 
     def measure(place):
-        t, s = blocks[place]
-        distance[place % 2] = times(row_terms(t), col_terms(s))
+        t, v, w = blocks[place]
+        distance[place % 2] = times(row_terms[t], col_terms[v])
 
     def add(place):
-        t, s = blocks[place]
-        term = times_transpose(fields[s], kernel_ref[place])
+        t, v, w = blocks[place]
+        term = times_transpose(fields(v), kernel_ref[place])
         held[t] = (held[t] if t in held else start(t)) + term
         if place + 1 == len(blocks) or blocks[place + 1][0] != t:
             finish_row(t, held[t])
 
     measure(0)
-    for place, (t, s) in enumerate(blocks):
+    for place, (t, v, w) in enumerate(blocks):
         if place + 1 < len(blocks):
             measure(place + 1)
         slot, out_ref = distance.at[place % 2], kernel_ref.at[place]
-        if t == 0 and s == 0:
-            form_own(line, column, slot, words[s], out_ref)
+        row_chunk = jnp.bitwise_xor(me, FAR * t)
+        if t == 0 and v == 0 and w == 0:
+            form_own(row_chunk, slot, words[v], out_ref)
         else:
-            form_block(t, s, line, column, slot, words[s], out_ref)
+            form_block(row_chunk, jnp.bitwise_xor(me, 2 * v + w), slot, words[v], out_ref)
         if place:
             add(place - 1)
     add(len(blocks) - 1)
 
 
+def column_terms(rows, terms, col_terms):
+    words = []
+    for v in range(LINE):
+        position, word = read_extra(rows(v))
+        words.append(word)
+        distance_terms(position, terms.at[v], False)
+        col_terms[v] = terms[v].astype(jnp.bfloat16)
+    return words
+
+
+def grid_pack(v0_ref, v1_ref, v2_ref, v3_ref, out_ref):
+    for v, ref in enumerate((v0_ref, v1_ref, v2_ref, v3_ref)):
+        out_ref[v] = ref[...]
+
+
 def grid_near(
     scale,
     me_ref,
-    own_ref,
-    core_ref,
+    packed_ref,
+    far_ref,
     seed_hbm,
     area_hbm,
     kernel_ref,
     partial_ref,
     row_terms,
+    terms,
     col_terms,
-    terms,
     distance,
     seed_ref,
     area_ref,
@@ -215,25 +231,24 @@
     for copy in copies:
         copy.start()
     rhs_count = seed_ref.shape[0]
-    line, column = me_ref[0] // LINE, me_ref[0] % LINE
-    position, word = read_extra(own_ref, rhs_count)
-    distance_terms(position, terms.at[0], False)
-    col_terms[...] = terms[0].astype(jnp.bfloat16)
-    for t, value in enumerate((position, core_ref[...])):
-        distance_terms(value, terms.at[1 + t], True)
-        row_terms[t] = jnp.transpose(terms[1 + t]).astype(jnp.bfloat16)
+    me = me_ref[0]
+    words = column_terms(lambda v: packed_ref[v, rhs_count:], terms, col_terms)
+    own, _ = read_extra(packed_ref[0, rhs_count:])
+    for t, value in enumerate((own, far_ref[...])):
+        slot = terms.at[LINE + t]
+        distance_terms(value, slot, True)
+        row_terms[t] = jnp.transpose(slot[...]).astype(jnp.bfloat16)
 
     def finish_row(t, value):
         partial_ref[t] = value
 
     form_all(
         NEAR,
-        line,
-        column,
-        lambda t: row_terms[t],
-        lambda s: col_terms[...],
-        [word],
-        [own_ref[:rhs_count, :]],
+        me,
+        row_terms,
+        col_terms,
+        words,
+        lambda v: packed_ref[v, :rhs_count],
         lambda t: 0.0,
         (kernel_ref, distance),
         finish_row,
@@ -245,36 +260,19 @@
 
 def grid_rest(
     me_ref,
-    own_ref,
-    z1_ref,
-    z2_ref,
-    z3_ref,
-    pair_ref,
+    packed_ref,
+    core_ref,
     before_ref,
-    row_ref,
-    col_ref,
+    row_terms,
     kernel_ref,
     partial_ref,
     sent_ref,
     terms,
-    row_terms,
     col_terms,
     distance,
 ):
     rhs_count = before_ref.shape[1]
-    line, column = me_ref[0] // LINE, me_ref[0] % LINE
-    lines = (own_ref, z1_ref, z2_ref, z3_ref)
-    words = []
-    for s, ref in enumerate(lines):
-        position, word = read_extra(ref, rhs_count)
-        words.append(word)
-        if s:
-            distance_terms(position, terms.at[s], False)
-            col_terms[s] = terms[s].astype(jnp.bfloat16)
-    for t in range(2):
-        slot = terms.at[LINE * t]
-        distance_terms(pair_ref[t], slot, True)
-        row_terms[t] = jnp.transpose(slot[...]).astype(jnp.bfloat16)
+    words = column_terms(lambda v: core_ref[v, rhs_count:], terms, col_terms)
 
     def finish_row(t, value):
         partial_ref[t] = value
@@ -282,80 +280,55 @@
 
     form_all(
         REST,
-        line,
-        column,
-        lambda t: row_ref[t] if t < 2 else row_terms[t - 2],
-        lambda s: col_terms[s] if s else col_ref[...],
+        me_ref[0],
+        row_terms,
+        col_terms,
         words,
-        [ref[:rhs_count, :] for ref in lines],
-        lambda t: before_ref[t] if t < 2 else 0.0,
+        lambda v: core_ref[v, :rhs_count],
+        lambda t: before_ref[t],
         (kernel_ref, distance),
         finish_row,
     )
-    sent_ref[LINE * rhs_count :] = own_ref[rhs_count:]
-
-
-def grid_middle(partial_ref, core_ref, own_ref, both_ref, first_ref, second_ref, rows):
+    sent_ref[2 * rhs_count :] = packed_ref[0, rhs_count:]
+
+
+def product(scaled_ref, kernel_ref, v):
+    return times(scaled_ref[0], kernel_ref[v]) + times(scaled_ref[1], kernel_ref[LINE + v])
+
+
+def grid_second(rest_ref, partial_ref, packed_ref, far_ref, scaled_ref, sent_ref):
     rhs_count = partial_ref.shape[1]
-    half = rhs_count // 2
-    for t in range(LINE):
-        start = (t ^ 1) * rhs_count
-        both = partial_ref[t] + core_ref[start : start + rhs_count].astype(jnp.float32)
-        both_ref[t] = both
-        first_ref[t * half : (t + 1) * half] = both[:half].astype(jnp.bfloat16)
-        second_ref[t * half : (t + 1) * half] = both[half:].astype(jnp.bfloat16)
-    rows[...] = jnp.zeros_like(rows)
-    for at, ref in enumerate((own_ref, core_ref)):
-        rows[3 * at : 3 * at + 3, :] = ref[-EXTRA:, :].astype(jnp.float32)[9:12]
-    for ref in (first_ref, second_ref):
-        ref[LINE * half :] = rows[...].astype(jnp.bfloat16)
-
-
-def product(scaled, near_ref, rest_ref, s):
-    held = None
-    for t in range(LINE):
-        near = (t, s) in NEAR
-        kernel = near_ref[NEAR.index((t, s))] if near else rest_ref[REST.index((t, s))]
-        term = times(scaled(t), kernel)
-        held = term if held is None else held + term
-    return held
-
-
-def grid_second(place, rest_ref, both_ref, own_ref, x_ref, scaled_ref, q2_ref, q3_ref):
-    half = q2_ref.shape[0]
-    for t in range(LINE):
-        terms = (own_ref, x_ref)[t // 2][LINE * half :, :].astype(jnp.float32)
-        at = 3 * (t % 2)
-        factor = terms[at : at + 1] + terms[at + 1 : at + 2] + terms[at + 2 : at + 3]
-        start = (t ^ 2) * half
-        total = both_ref[t, place * half : (place + 1) * half] + x_ref[
-            start : start + half
-        ].astype(jnp.float32)
+    extras = (packed_ref[0, rhs_count:], far_ref[2 * rhs_count :, :])
+    for t in range(2):
+        terms = extras[t].astype(jnp.float32)
+        factor = terms[9:10] + terms[10:11] + terms[11:12]
+        start = (1 - t) * rhs_count
+        total = partial_ref[t] + far_ref[start : start + rhs_count].astype(jnp.float32)
         scaled_ref[t] = (factor * total).astype(jnp.bfloat16)
-    q3_ref[...] = product(lambda t: scaled_ref[t], None, rest_ref, 3).astype(jnp.bfloat16)
-    q2_ref[...] = product(lambda t: scaled_ref[t], None, rest_ref, 2).astype(jnp.bfloat16)
-
-
-def grid_third(near_ref, rest_ref, first_ref, second_ref, q0_ref, first_q1_ref, second_q1_ref):
-    half = first_ref.shape[1]
-    scaled = [jnp.concatenate([first_ref[t], second_ref[t]]) for t in range(LINE)]
-    next_sum = product(lambda t: scaled[t], None, rest_ref, 1).astype(jnp.bfloat16)
-    first_q1_ref[...] = next_sum[:half]
-    second_q1_ref[...] = next_sum[half:]
-    q0_ref[...] = product(lambda t: scaled[t], near_ref, rest_ref, 0)
-
-
-def grid_last(scale, line_refs, q0_ref, *rest):
-    halves = [
-        sum(ref[...].astype(jnp.float32) for ref in refs)
-        for refs in ([line_refs[at] for at in [2, 3, 5]], [line_refs[at] for at in [0, 1, 4]])
-    ]
-    finish(scale, jnp.concatenate(halves) + q0_ref[...], *rest)
+    for v in range(LINE):
+        sent_ref[v] = product(scaled_ref, rest_ref, v).astype(jnp.bfloat16)
+
+
+def grid_third(near_ref, scaled_ref, sum_ref):
+    for v in range(LINE):
+        sum_ref[v] = product(scaled_ref, near_ref, v)
+
+
+def grid_fourth(sum_ref, core_ref, q0_ref, q1_ref, q2_ref, q3_ref):
+    for v, ref in enumerate((q0_ref, q1_ref, q2_ref, q3_ref)):
+        ref[...] = (sum_ref[v] + core_ref[v].astype(jnp.float32)).astype(ref.dtype)
+
+
+def grid_last(scale, q3_ref, q2_ref, q1_ref, q0_ref, *rest):
+    total = q0_ref[...]
+    for ref in (q1_ref, q2_ref, q3_ref):
+        total = total + ref[...].astype(jnp.float32)
+    finish(scale, total, *rest)
 
 
 def on_grid(adjoint_seed, radiosity, emission, reflectance, area, position, visibility):
     rhs_count, own_width = adjoint_seed.shape
-    devices = LINE * LINE
+    devices = GRID
     my_index = lax.axis_index("row").astype(jnp.int32).reshape(1)
     scale = 1.0 / math.sqrt(own_width * devices)
     area = area.reshape(1, own_width)
@@ -374,114 +347,94 @@
         pltpu.with_memory_space_constraint(value, pltpu.HBM)
         for value in (position, visibility, area, reflectance, adjoint_seed)
     ]
-    packed, spot = pl.pallas_call(
+
+    def call(body, name, operands, in_specs, out_shape, scratch_shapes=()):
+        return pl.pallas_call(
+            body,
+            in_specs=in_specs,
+            out_specs=[vmem] * len(out_shape),
+            out_shape=out_shape,
+            scratch_shapes=scratch_shapes,
+            compiler_params=params,
+            name=name,
+        )(*operands)
+
+    packed_rows = rhs_count + EXTRA
+    own, spot = call(
         functools.partial(prepare, scale),
-        in_specs=[hbm] * 5,
-        out_specs=[vmem] * 2,
-        out_shape=[
-            shaped((rhs_count + EXTRA, own_width), jnp.bfloat16),
+        "prepare",
+        arguments,
+        [hbm] * 5,
+        [
+            shaped((packed_rows, own_width), jnp.bfloat16),
             shaped(position.shape, jnp.float32),
         ],
-        scratch_shapes=[pltpu.VMEM((EXTRA, own_width), jnp.float32)]
+        [pltpu.VMEM((EXTRA, own_width), jnp.float32)]
         + [pltpu.VMEM(value.shape, value.dtype) for value in arguments]
         + [pltpu.SemaphoreType.DMA((5,))],
-        compiler_params=params,
-        name="prepare",
-    )(*arguments)
-    lines = [send(packed, LINE * step) for step in range(1, LINE)]
-    core = send(position, 1)
-    pair = send(jnp.stack([spot, core]), 2)
+    )
+    lines = [send(own, 2 * v) for v in range(1, LINE)]
+    far_spot = send(spot, FAR)
+    first, far_spot = lax.optimization_barrier((own, far_spot))
+    packed_shape = shaped((LINE, packed_rows, own_width), jnp.bfloat16)
+    (packed,) = call(grid_pack, "grid_pack", (first, *lines), [vmem] * LINE, [packed_shape])
+    core = send(packed, 1)
     terms = (TERMS, own_width)
-    distance = pltpu.VMEM((2, own_width, own_width), jnp.float32)
-    near, partial, row_terms, col_terms = pl.pallas_call(
+    blocks = shaped((2 * LINE, own_width, own_width), jnp.bfloat16)
+    pair = shaped((2,) + field, jnp.float32)
+    scratch = [
+        pltpu.VMEM((LINE + 2,) + terms, jnp.float32),
+        pltpu.VMEM((LINE,) + terms, jnp.bfloat16),
+        pltpu.VMEM((2, own_width, own_width), jnp.float32),
+    ]
+    near, partial, row_terms = call(
         functools.partial(grid_near, scale),
-        in_specs=[smem] + [vmem] * 2 + [hbm] * 2,
-        out_specs=[vmem] * 4,
-        out_shape=[
-            shaped((len(NEAR), own_width, own_width), jnp.bfloat16),
-            shaped((2,) + field, jnp.float32),
-            shaped((2, own_width, TERMS), jnp.bfloat16),
-            shaped(terms, jnp.bfloat16),
-        ],
-        scratch_shapes=[
-            pltpu.VMEM((3,) + terms, jnp.float32),
-            distance,
+        "grid_near",
+        (my_index, packed, far_spot, arguments[4], arguments[2]),
+        [smem] + [vmem] * 2 + [hbm] * 2,
+        [blocks, pair, shaped((2, own_width, TERMS), jnp.bfloat16)],
+        scratch
+        + [
             pltpu.VMEM(field, jnp.float32),
             pltpu.VMEM((1, own_width), jnp.float32),
             pltpu.SemaphoreType.DMA((2,)),
         ],
-        compiler_params=params,
-        name="grid_near",
-    )(my_index, packed, core, arguments[4], arguments[2])
-    sent = shaped((LINE * rhs_count + EXTRA, own_width), jnp.bfloat16)
-    rest, partial, terms = pl.pallas_call(
+    )
+    rest, partial, sent = call(
         grid_rest,
-        in_specs=[smem] + [vmem] * 8,
-        out_specs=[vmem] * 3,
-        out_shape=[
-            shaped((len(REST), own_width, own_width), jnp.bfloat16),
-            shaped((LINE,) + field, jnp.float32),
-            sent,
-        ],
-        scratch_shapes=[
-            pltpu.VMEM((LINE + 1,) + terms, jnp.float32),
-            pltpu.VMEM((2, own_width, TERMS), jnp.bfloat16),
-            pltpu.VMEM((LINE,) + terms, jnp.bfloat16),
-            distance,
-        ],
-        compiler_params=params,
-        name="grid_rest",
-    )(my_index, packed, *lines, pair, partial, row_terms, col_terms)
-    half = (rhs_count // 2, own_width)
-    both, first, second = pl.pallas_call(
-        grid_middle,
-        in_specs=[vmem] * 3,
-        out_specs=[vmem] * 3,
-        out_shape=[
-            shaped((LINE,) + field, jnp.float32),
-            shaped((LINE * half[0] + EXTRA, own_width), jnp.bfloat16),
-            shaped((LINE * half[0] + EXTRA, own_width), jnp.bfloat16),
-        ],
-        scratch_shapes=[pltpu.VMEM((EXTRA, own_width), jnp.float32)],
-        compiler_params=params,
-        name="grid_middle",
-    )(partial, send(terms, 1), packed)
-    other = [send(first, 2), send(second, 2)]
-    scaled, far = [], []
-    for place in range(2):
-        scaled_half, sum2, sum3 = pl.pallas_call(
-            functools.partial(grid_second, place),
-            in_specs=[vmem] * 4,
-            out_specs=[vmem] * 3,
-            out_shape=[shaped((LINE,) + half, jnp.bfloat16)]
-            + [shaped(half, jnp.bfloat16)] * 2,
-            compiler_params=params,
-            name="grid_second",
-        )(rest, both, first, other[place])
-        scaled.append(scaled_half)
-        far += [send(sum3, 3 * LINE), send(sum2, 2 * LINE)]
-    sum0, *sum1 = pl.pallas_call(
-        grid_third,
-        in_specs=[vmem] * 4,
-        out_specs=[vmem] * 3,
-        out_shape=[shaped(field, jnp.float32)] + [shaped(half, jnp.bfloat16)] * 2,
-        compiler_params=params,
-        name="grid_third",
-    )(near, rest, *scaled)
-    sum1 = [send(value, LINE) for value in sum1]
-    lines = [far[2], far[3], far[0], far[1], sum1[1], sum1[0]]
-
-    def last(*refs):
-        grid_last(scale, refs[:6], *refs[6:])
-
-    adjoint, grad = pl.pallas_call(
-        last,
-        in_specs=[vmem] * 12,
-        out_specs=[vmem, vmem],
-        out_shape=[shaped(field, jnp.float32), shaped((1, own_width), jnp.float32)],
-        compiler_params=params,
-        name="grid_last",
-    )(*lines, sum0, adjoint_seed, area, reflectance, radiosity, emission)
+        "grid_rest",
+        (my_index, packed, core, partial, row_terms),
+        [smem] + [vmem] * 4,
+        [blocks, pair, shaped((2 * rhs_count + EXTRA, own_width), jnp.bfloat16)],
+        scratch,
+    )
+    four = (LINE,) + field
+    scaled, sent = call(
+        grid_second,
+        "grid_second",
+        (rest, partial, packed, send(sent, FAR)),
+        [vmem] * 4,
+        [shaped((2,) + field, jnp.bfloat16), shaped(four, jnp.bfloat16)],
+    )
+    other = send(sent, 1)
+    (sums,) = call(
+        grid_third, "grid_third", (near, scaled), [vmem] * 2, [shaped(four, jnp.float32)]
+    )
+    sums = call(
+        grid_fourth,
+        "grid_fourth",
+        (sums, other),
+        [vmem] * 2,
+        [shaped(field, jnp.float32)] + [shaped(field, jnp.bfloat16)] * 3,
+    )
+    lines = [send(sums[v], 2 * v) for v in range(1, LINE)]
+    adjoint, grad = call(
+        functools.partial(grid_last, scale),
+        "grid_last",
+        (*lines[::-1], sums[0], adjoint_seed, area, reflectance, radiosity, emission),
+        [vmem] * 9,
+        [shaped(field, jnp.float32), shaped((1, own_width), jnp.float32)],
+    )
     return adjoint, grad.reshape(own_width)
 
 
@@ -700,7 +653,7 @@
 
 
 def on_device(adjoint_seed, *rest):
-    on_grid_shape = lax.axis_size("row") == LINE * LINE and adjoint_seed.shape[1] == 2 * TILE
+    on_grid_shape = lax.axis_size("row") == GRID and adjoint_seed.shape[1] == 2 * TILE
     return (on_grid if on_grid_shape else on_rows)(adjoint_seed, *rest)
 
 

time: 32.9 us -> 30.5 us (0.927)
  starting transfers between devices: 18.1 us -> 14.3 us
  waiting for transfers between devices: 8.94 us -> 10.5 us
    ppermute x14 -> x10, starting transfers between devices: 18.1 us -> 14.3 us  [send(): lax.ppermute(value, 'row', [(at, at ^ step) for at in range(devices)])]
    ppermute x14 -> x10, waiting for transfers between devices: 8.94 us -> 10.5 us  [send(): lax.ppermute(value, 'row', [(at, at ^ step) for at in range(devices)])]
  transfers between devices with their start and end apart: 14 -> 10, of which waited for: 8 -> 6; matrix products, arithmetic and copies ran while one was open for 0% -> 0% of each run, Pallas kernels for 8% -> 6%
where the time goes in v5:
time: 30.5 us; the launch traced here: 30.3 us
  starting transfers between devices  14.3 us (47%)
  waiting for transfers between devices  10.5 us (34%)
  Pallas kernels  4.68 us (15%)
  between operations  0.76 us (2%)
    ppermute x10, starting transfers between devices, send(): lax.ppermute(value, 'row', [(at, at ^ step) for at in range(devices)])  14.3 us
    ppermute x10, waiting for transfers between devices, send(): lax.ppermute(value, 'row', [(at, at ^ step) for at in range(devices)])  10.5 us
    pallas_call x8, Pallas kernels, call(): pl.pallas_call(body, in_specs=in_specs, out_specs=[vmem] * len(out_shape)...  4.68 us
  transfers between devices with their start and end apart: 10, of which 6 were waited for; matrix products, arithmetic and copies ran while one was open for 0% of the time, Pallas kernels for 6%

profile of v5, /device:TPU:0, one launch (start us, length us, event | category | flops | bytes accessed | tf_op | source)
XLA Modules:
  0.0 30.3 jit_solution(7036987936103732809)
XLA Ops:
  0.6 1.0 %prepare.1 = (bf16[80,256]{1,0:T(8,128)(2,1)S(1)}, f32[3,256]{1,0:T(4,128)S(1)}) custom-call(f32[3,256]{1,0:T(4,128)} %refs_0_.1, s32[2,32]{1,0:T(2,128)} %refs_1_.1, f32[1,256]{1,0:T(1,128)} %bitcast.4, f32[1,256]{1,0:T(1,128)} %bitcast.7, f32[64,256]{1,0:T(8,128)} %rest_0_.1), custom_call_target="tpu_custom_call" | custom-call | tf_op jit(solution)/shard_map/prepare/pallas_call | solution.py:352
  1.6 4.0 %collective-permute-start.3 = (bf16[80,256]{1,0:T(8,128)(2,1)S(1)}, bf16[80,256]{1,0:T(8,128)(2,1)S(1)}, u32[]{:S(2)}, u32[]{:S(2)}) collective-permute-start(bf16[80,256]{1,0:T(8,128)(2,1)S(1)} %get-tuple-element.22.v0_ref), channel_id=1, source_target_pairs={{0,6},{1,7},{2,4},{3,5},{4,2},{5,3},{6,0},{7,1},{8,14},{9,15},{10,... | collective-permute-start | bytes 122888 | tf_op jit(solution)/shard_map/ppermute | solution.py:343
  5.6 0.4 %collective-permute-start.2 = (bf16[80,256]{1,0:T(8,128)(2,1)S(1)}, bf16[80,256]{1,0:T(8,128)(2,1)S(1)}, u32[]{:S(2)}, u32[]{:S(2)}) collective-permute-start(bf16[80,256]{1,0:T(8,128)(2,1)S(1)} %get-tuple-element.22.v0_ref), channel_id=1, source_target_pairs={{0,4},{1,5},{2,6},{3,7},{4,0},{5,1},{6,2},{7,3},{8,12},{9,13},{10,... | collective-permute-start | bytes 122888 | tf_op jit(solution)/shard_map/ppermute | solution.py:343
  6.1 0.2 collective-permute-start.1
  6.3 2.9 %collective-permute-start = (f32[3,256]{1,0:T(4,128)S(1)}, f32[3,256]{1,0:T(4,128)S(1)}, u32[]{:S(2)}, u32[]{:S(2)}) collective-permute-start(f32[3,256]{1,0:T(4,128)S(1)} %get-tuple-element.21), channel_id=1, source_target_pairs={{0,8},{1,9},{2,10},{3,11},{4,12},{5,13},{6,14},{7,15},{8,0},{9,1},... | collective-permute-start | bytes 9224 | tf_op jit(solution)/shard_map/ppermute | solution.py:343
  9.2 1.6 %collective-permute-done.far_ref = f32[3,256]{1,0:T(4,128)S(1)} collective-permute-done((f32[3,256]{1,0:T(4,128)S(1)}, f32[3,256]{1,0:T(4,128)S(1)}, u32[]{:S(2)}, u32[]{:S(2)}) %collective-permute-start) | collective-permute-done | bytes 3104 | tf_op jit(solution)/shard_map/ppermute | solution.py:343
  10.8 0.0 collective-permute-done.3.v3_ref
  10.8 0.0 collective-permute-done.2.v2_ref
  10.8 0.0 collective-permute-done.1.v1_ref
  10.8 0.1 collective-permute-start.4
  10.9 1.4 %grid_near.1 = (bf16[8,256,256]{2,1,0:T(8,128)(2,1)S(1)}, f32[2,64,256]{2,1,0:T(8,128)S(1)}, bf16[2,256,32]{2,1,0:T(8,128)(2,1)S(1)}) custom-call(s32[1]{0:T(128)} %bitcast.me_ref, bf16[4,80,256]{2,1,0:T(8,128)(2,1)S(1)} %grid_pack.1.packed_ref, f32[3,256]{1,0:T(4,128)S(1)} %collective-permute-done.far_ref, f32[64,256]{1,0:T(8,128)} %rest_0_.1, f32[1,256]{1,0:T(1,128)} %bitcast.5), custom_call_target="tpu_custom_call" | custom-call | tf_op jit(solution)/shard_map/grid_near/pallas_call | solution.py:352
  12.4 0.0 collective-permute-done.4.core_ref
  12.4 1.0 %grid_rest.1 = (bf16[8,256,256]{2,1,0:T(8,128)(2,1)S(1)}, f32[2,64,256]{2,1,0:T(8,128)S(1)}, bf16[144,256]{1,0:T(8,128)(2,1)S(1)}) custom-call(s32[1]{0:T(128)} %bitcast.me_ref, bf16[4,80,256]{2,1,0:T(8,128)(2,1)S(1)} %grid_pack.1.packed_ref, bf16[4,80,256]{2,1,0:T(8,128)(2,1)S(1)} %collective-permute-done.4.core_ref, ...), custom_call_target="tpu_custom_call" | custom-call | tf_op jit(solution)/shard_map/grid_rest/pallas_call | solution.py:352
  13.3 3.0 %collective-permute-start.5 = (bf16[144,256]{1,0:T(8,128)(2,1)S(1)}, bf16[144,256]{1,0:T(8,128)(2,1)S(1)}, u32[]{:S(2)}, u32[]{:S(2)}) collective-permute-start(bf16[144,256]{1,0:T(8,128)(2,1)S(1)} %get-tuple-element.29), channel_id=1, source_target_pairs={{0,8},{1,9},{2,10},{3,11},{4,12},{5,13},{6,14},{7,15},{8,0},{9,1},... | collective-permute-start | bytes 221192 | tf_op jit(solution)/shard_map/ppermute | solution.py:343
  16.3 4.5 %collective-permute-done.5.far_ref = bf16[144,256]{1,0:T(8,128)(2,1)S(1)} collective-permute-done((bf16[144,256]{1,0:T(8,128)(2,1)S(1)}, bf16[144,256]{1,0:T(8,128)(2,1)S(1)}, u32[]{:S(2)}, u32[]{:S(2)}) %collective-permute-start.5) | collective-permute-done | bytes 73760 | tf_op jit(solution)/shard_map/ppermute | solution.py:343
  20.8 0.3 %grid_second.1 = (bf16[2,64,256]{2,1,0:T(8,128)(2,1)S(1)}, bf16[4,64,256]{2,1,0:T(8,128)(2,1)S(1)}) custom-call(bf16[8,256,256]{2,1,0:T(8,128)(2,1)S(1)} %get-tuple-element.27.rest_ref, f32[2,64,256]{2,1,0:T(8,128)S(1)} %get-tuple-element.28.partial_ref, bf16[4,80,256]{2,1,0:T(8,128)(2,1)S(1)} %grid_pack.1.packed_ref, ...), custom_call_target="tpu_custom_call" | custom-call | tf_op jit(solution)/shard_map/grid_second/pallas_call | solution.py:352
  21.1 0.1 collective-permute-start.6
  21.2 0.3 grid_third.1.sum_ref
  21.5 0.0 copy-start
  21.5 0.0 copy-start.1
  21.5 0.0 copy-start.2
  21.6 1.0 %collective-permute-done.6.core_ref = bf16[4,64,256]{2,1,0:T(8,128)(2,1)S(1)} collective-permute-done((bf16[4,64,256]{2,1,0:T(8,128)(2,1)S(1)}, bf16[4,64,256]{2,1,0:T(8,128)(2,1)S(1)}, u32[]{:S(2)}, u32[]{:S(2)}) %collective-permute-start.6) | collective-permute-done | bytes 131104 | tf_op jit(solution)/shard_map/ppermute | solution.py:343
  22.6 1.7 %collective-permute-start.7 = (bf16[64,256]{1,0:T(8,128)(2,1)S(1)}, bf16[64,256]{1,0:T(8,128)(2,1)S(1)}, u32[]{:S(2)}, u32[]{:S(2)}) collective-permute-start(bf16[64,256]{1,0:T(8,128)(2,1)S(1)} %get-tuple-element.32), channel_id=1, source_target_pairs={{0,6},{1,7},{2,4},{3,5},{4,2},{5,3},{6,0},{7,1},{8,14},{9,15},{10,... | collective-permute-start | bytes 98312 | tf_op jit(solution)/shard_map/ppermute | solution.py:343
  24.3 1.3 %collective-permute-start.8 = (bf16[64,256]{1,0:T(8,128)(2,1)S(1)}, bf16[64,256]{1,0:T(8,128)(2,1)S(1)}, u32[]{:S(2)}, u32[]{:S(2)}) collective-permute-start(bf16[64,256]{1,0:T(8,128)(2,1)S(1)} %get-tuple-element.33), channel_id=1, source_target_pairs={{0,4},{1,5},{2,6},{3,7},{4,0},{5,1},{6,2},{7,3},{8,12},{9,13},{10,... | collective-permute-start | bytes 98312 | tf_op jit(solution)/shard_map/ppermute | solution.py:343
  25.6 0.0 copy-start.4
  25.6 0.0 copy-start.3
  25.7 0.5 %collective-permute-start.9 = (bf16[64,256]{1,0:T(8,128)(2,1)S(1)}, bf16[64,256]{1,0:T(8,128)(2,1)S(1)}, u32[]{:S(2)}, u32[]{:S(2)}) collective-permute-start(bf16[64,256]{1,0:T(8,128)(2,1)S(1)} %get-tuple-element.34), channel_id=1, source_target_pairs={{0,2},{1,3},{2,0},{3,1},{4,6},{5,7},{6,4},{7,5},{8,10},{9,11},{10,... | collective-permute-start | bytes 98312 | tf_op jit(solution)/shard_map/ppermute | solution.py:343
  26.1 1.3 %collective-permute-done.7.q3_ref = bf16[64,256]{1,0:T(8,128)(2,1)S(1)} collective-permute-done((bf16[64,256]{1,0:T(8,128)(2,1)S(1)}, bf16[64,256]{1,0:T(8,128)(2,1)S(1)}, u32[]{:S(2)}, u32[]{:S(2)}) %collective-permute-start.7) | collective-permute-done | bytes 32800 | tf_op jit(solution)/shard_map/ppermute | solution.py:343
  27.5 0.8 %collective-permute-done.8.q2_ref = bf16[64,256]{1,0:T(8,128)(2,1)S(1)} collective-permute-done((bf16[64,256]{1,0:T(8,128)(2,1)S(1)}, bf16[64,256]{1,0:T(8,128)(2,1)S(1)}, u32[]{:S(2)}, u32[]{:S(2)}) %collective-permute-start.8) | collective-permute-done | bytes 32800 | tf_op jit(solution)/shard_map/ppermute | solution.py:343
  28.2 1.3 %collective-permute-done.9.q1_ref = bf16[64,256]{1,0:T(8,128)(2,1)S(1)} collective-permute-done((bf16[64,256]{1,0:T(8,128)(2,1)S(1)}, bf16[64,256]{1,0:T(8,128)(2,1)S(1)}, u32[]{:S(2)}, u32[]{:S(2)}) %collective-permute-start.9) | collective-permute-done | bytes 32800 | tf_op jit(solution)/shard_map/ppermute | solution.py:343
  29.6 0.0 copy-done
  29.6 0.0 copy-done.1
  29.6 0.0 copy-done.2
  29.6 0.0 copy-done.4
  29.6 0.0 copy-done.3
  29.6 0.7 %grid_last.1 = (f32[64,256]{1,0:T(8,128)}, f32[1,256]{1,0:T(1,128)}) custom-call(bf16[64,256]{1,0:T(8,128)(2,1)S(1)} %collective-permute-done.7.q3_ref, bf16[64,256]{1,0:T(8,128)(2,1)S(1)} %collective-permute-done.8.q2_ref, bf16[64,256]{1,0:T(8,128)(2,1)S(1)} %collective-permute-done.9.q1_ref, f32[64,256]{1,0:T(8,128)S(1)} %get-tuple-element.35.q0_ref, ...), custom_call_target="tpu_custom_call" | custom-call | tf_op jit(solution)/shard_map/grid_last/pallas_call | solution.py:352
  (2 shorter events, 0.0 us)
Async XLA Ops:
  1.6 9.2 %collective-permute-start.3 = (bf16[80,256]{1,0:T(8,128)(2,1)S(1)}, bf16[80,256]{1,0:T(8,128)(2,1)S(1)}, u32[]{:S(2)}, u32[]{:S(2)}) collective-permute-start(bf16[80,256]{1,0:T(8,128)(2,1)S(1)} %get-tuple-element.22.v0_ref), channel_id=1, source_target_pairs={{0,6},{1,7},{2,4},{3,5},{4,2},{5,3},{6,0},{7,1},{8,14},{9,15},{10,... | collective-permute-start | bytes 122888 | tf_op jit(solution)/shard_map/ppermute | solution.py:343
  5.6 5.2 %collective-permute-start.2 = (bf16[80,256]{1,0:T(8,128)(2,1)S(1)}, bf16[80,256]{1,0:T(8,128)(2,1)S(1)}, u32[]{:S(2)}, u32[]{:S(2)}) collective-permute-start(bf16[80,256]{1,0:T(8,128)(2,1)S(1)} %get-tuple-element.22.v0_ref), channel_id=1, source_target_pairs={{0,4},{1,5},{2,6},{3,7},{4,0},{5,1},{6,2},{7,3},{8,12},{9,13},{10,... | collective-permute-start | bytes 122888 | tf_op jit(solution)/shard_map/ppermute | solution.py:343
  6.1 4.7 %collective-permute-start.1 = (bf16[80,256]{1,0:T(8,128)(2,1)S(1)}, bf16[80,256]{1,0:T(8,128)(2,1)S(1)}, u32[]{:S(2)}, u32[]{:S(2)}) collective-permute-start(bf16[80,256]{1,0:T(8,128)(2,1)S(1)} %get-tuple-element.22.v0_ref), channel_id=1, source_target_pairs={{0,2},{1,3},{2,0},{3,1},{4,6},{5,7},{6,4},{7,5},{8,10},{9,11},{10,... | collective-permute-start | bytes 122888 | tf_op jit(solution)/shard_map/ppermute | solution.py:343
  6.3 4.5 %collective-permute-start = (f32[3,256]{1,0:T(4,128)S(1)}, f32[3,256]{1,0:T(4,128)S(1)}, u32[]{:S(2)}, u32[]{:S(2)}) collective-permute-start(f32[3,256]{1,0:T(4,128)S(1)} %get-tuple-element.21), channel_id=1, source_target_pairs={{0,8},{1,9},{2,10},{3,11},{4,12},{5,13},{6,14},{7,15},{8,0},{9,1},... | collective-permute-start | bytes 9224 | tf_op jit(solution)/shard_map/ppermute | solution.py:343
  10.8 1.5 %collective-permute-start.4 = (bf16[4,80,256]{2,1,0:T(8,128)(2,1)S(1)}, bf16[4,80,256]{2,1,0:T(8,128)(2,1)S(1)}, u32[]{:S(2)}, u32[]{:S(2)}) collective-permute-start(bf16[4,80,256]{2,1,0:T(8,128)(2,1)S(1)} %grid_pack.1.packed_ref), channel_id=1, source_target_pairs={{0,1},{1,0},{2,3},{3,2},{4,5},{5,4},{6,7},{7,6},{8,9},{9,8},{10,11... | collective-permute-start | bytes 491528 | tf_op jit(solution)/shard_map/ppermute | solution.py:343
  13.3 7.5 %collective-permute-start.5 = (bf16[144,256]{1,0:T(8,128)(2,1)S(1)}, bf16[144,256]{1,0:T(8,128)(2,1)S(1)}, u32[]{:S(2)}, u32[]{:S(2)}) collective-permute-start(bf16[144,256]{1,0:T(8,128)(2,1)S(1)} %get-tuple-element.29), channel_id=1, source_target_pairs={{0,8},{1,9},{2,10},{3,11},{4,12},{5,13},{6,14},{7,15},{8,0},{9,1},... | collective-permute-start | bytes 221192 | tf_op jit(solution)/shard_map/ppermute | solution.py:343
  21.1 1.4 %collective-permute-start.6 = (bf16[4,64,256]{2,1,0:T(8,128)(2,1)S(1)}, bf16[4,64,256]{2,1,0:T(8,128)(2,1)S(1)}, u32[]{:S(2)}, u32[]{:S(2)}) collective-permute-start(bf16[4,64,256]{2,1,0:T(8,128)(2,1)S(1)} %get-tuple-element.31), channel_id=1, source_target_pairs={{0,1},{1,0},{2,3},{3,2},{4,5},{5,4},{6,7},{7,6},{8,9},{9,8},{10,11... | collective-permute-start | bytes 393224 | tf_op jit(solution)/shard_map/ppermute | solution.py:343
  21.5 8.1 %copy-start = (f32[64,256]{1,0:T(8,128)S(1)}, f32[64,256]{1,0:T(8,128)}, u32[]{:S(2)}) copy-start(f32[64,256]{1,0:T(8,128)} %rest_0_.1) | copy-start | bytes 196612
  21.5 8.0 %copy-start.1 = (bf16[64,256]{1,0:T(8,128)(2,1)S(1)}, bf16[64,256]{1,0:T(8,128)(2,1)}, u32[]{:S(2)}) copy-start(bf16[64,256]{1,0:T(8,128)(2,1)} %rest_3_.1) | copy-start | bytes 98308
  21.5 8.0 %copy-start.2 = (bf16[64,256]{1,0:T(8,128)(2,1)S(1)}, bf16[64,256]{1,0:T(8,128)(2,1)}, u32[]{:S(2)}) copy-start(bf16[64,256]{1,0:T(8,128)(2,1)} %rest_4_.1) | copy-start | bytes 98308
  22.6 4.9 %collective-permute-start.7 = (bf16[64,256]{1,0:T(8,128)(2,1)S(1)}, bf16[64,256]{1,0:T(8,128)(2,1)S(1)}, u32[]{:S(2)}, u32[]{:S(2)}) collective-permute-start(bf16[64,256]{1,0:T(8,128)(2,1)S(1)} %get-tuple-element.32), channel_id=1, source_target_pairs={{0,6},{1,7},{2,4},{3,5},{4,2},{5,3},{6,0},{7,1},{8,14},{9,15},{10,... | collective-permute-start | bytes 98312 | tf_op jit(solution)/shard_map/ppermute | solution.py:343
  24.3 3.9 %collective-permute-start.8 = (bf16[64,256]{1,0:T(8,128)(2,1)S(1)}, bf16[64,256]{1,0:T(8,128)(2,1)S(1)}, u32[]{:S(2)}, u32[]{:S(2)}) collective-permute-start(bf16[64,256]{1,0:T(8,128)(2,1)S(1)} %get-tuple-element.33), channel_id=1, source_target_pairs={{0,4},{1,5},{2,6},{3,7},{4,0},{5,1},{6,2},{7,3},{8,12},{9,13},{10,... | collective-permute-start | bytes 98312 | tf_op jit(solution)/shard_map/ppermute | solution.py:343
  25.6 3.9 %copy-start.4 = (f32[256]{0:T(256)S(1)}, f32[256]{0:T(256)}, u32[]{:S(2)}) copy-start(f32[256]{0:T(256)} %param.10) | copy-start | bytes 3076
  25.6 3.9 %copy-start.3 = (f32[256]{0:T(256)S(1)}, f32[256]{0:T(256)}, u32[]{:S(2)}) copy-start(f32[256]{0:T(256)} %param.11) | copy-start | bytes 3076
  25.7 3.9 %collective-permute-start.9 = (bf16[64,256]{1,0:T(8,128)(2,1)S(1)}, bf16[64,256]{1,0:T(8,128)(2,1)S(1)}, u32[]{:S(2)}, u32[]{:S(2)}) collective-permute-start(bf16[64,256]{1,0:T(8,128)(2,1)S(1)} %get-tuple-element.34), channel_id=1, source_target_pairs={{0,2},{1,3},{2,0},{3,1},{4,6},{5,7},{6,4},{7,5},{8,10},{9,11},{10,... | collective-permute-start | bytes 98312 | tf_op jit(solution)/shard_map/ppermute | solution.py:343

commit v6 on v5

--- a/solution.py
+++ b/solution.py
@@ -16,6 +16,7 @@
 FAR = 8
 EXTRA = 16
 TERMS = 32
+LONG = pl.CostEstimate(flops=10**11, bytes_accessed=10**8, transcendentals=0)
 VMEM_BYTES = 48 * 1024 * 1024
 GRID_BYTES = 8 * 1024 * 1024
 
@@ -51,7 +52,7 @@
 
 
 def prepare(scale, *refs):
-    arguments, (packed_ref, spot_ref, rows, *held, sems) = refs[:5], refs[5:]
+    arguments, (packed_ref, rows, *held, sems) = refs[:5], refs[5:]
     copies = [
         pltpu.make_async_copy(argument, ref, sems.at[at])
         for at, (argument, ref) in enumerate(zip(arguments, held))
@@ -76,7 +77,6 @@
             rows[12 + place : 13 + place, start : start + count] = part[local : local + 1]
     packed_ref[:rhs_count] = (reflectance_ref[...] * seed_ref[...]).astype(jnp.bfloat16)
     packed_ref[rhs_count:] = rows[...].astype(jnp.bfloat16)
-    spot_ref[...] = pos_ref[...]
 
 
 def distance_terms(position, terms, as_rows):
@@ -202,6 +202,13 @@
     return words
 
 
+def grid_rows(own_ref, far_ref, row_terms, terms):
+    own, _ = read_extra(own_ref[-EXTRA:, :])
+    for t, value in enumerate((own, far_ref[...])):
+        distance_terms(value, terms.at[t], True)
+        row_terms[t] = jnp.transpose(terms[t]).astype(jnp.bfloat16)
+
+
 def grid_pack(v0_ref, v1_ref, v2_ref, v3_ref, out_ref):
     for v, ref in enumerate((v0_ref, v1_ref, v2_ref, v3_ref)):
         out_ref[v] = ref[...]
@@ -211,12 +218,11 @@
     scale,
     me_ref,
     packed_ref,
-    far_ref,
+    row_terms,
     seed_hbm,
     area_hbm,
     kernel_ref,
     partial_ref,
-    row_terms,
     terms,
     col_terms,
     distance,
@@ -233,11 +239,6 @@
     rhs_count = seed_ref.shape[0]
     me = me_ref[0]
     words = column_terms(lambda v: packed_ref[v, rhs_count:], terms, col_terms)
-    own, _ = read_extra(packed_ref[0, rhs_count:])
-    for t, value in enumerate((own, far_ref[...])):
-        slot = terms.at[LINE + t]
-        distance_terms(value, slot, True)
-        row_terms[t] = jnp.transpose(slot[...]).astype(jnp.bfloat16)
 
     def finish_row(t, value):
         partial_ref[t] = value
@@ -348,7 +349,7 @@
         for value in (position, visibility, area, reflectance, adjoint_seed)
     ]
 
-    def call(body, name, operands, in_specs, out_shape, scratch_shapes=()):
+    def call(body, name, operands, in_specs, out_shape, scratch_shapes=(), cost=None):
         return pl.pallas_call(
             body,
             in_specs=in_specs,
@@ -356,43 +357,49 @@
             out_shape=out_shape,
             scratch_shapes=scratch_shapes,
             compiler_params=params,
+            cost_estimate=cost,
             name=name,
         )(*operands)
 
     packed_rows = rhs_count + EXTRA
-    own, spot = call(
+    (own,) = call(
         functools.partial(prepare, scale),
         "prepare",
         arguments,
         [hbm] * 5,
-        [
-            shaped((packed_rows, own_width), jnp.bfloat16),
-            shaped(position.shape, jnp.float32),
-        ],
+        [shaped((packed_rows, own_width), jnp.bfloat16)],
         [pltpu.VMEM((EXTRA, own_width), jnp.float32)]
         + [pltpu.VMEM(value.shape, value.dtype) for value in arguments]
         + [pltpu.SemaphoreType.DMA((5,))],
     )
     lines = [send(own, 2 * v) for v in range(1, LINE)]
-    far_spot = send(spot, FAR)
-    first, far_spot = lax.optimization_barrier((own, far_spot))
+    terms = (TERMS, own_width)
+    (row_terms,) = call(
+        grid_rows,
+        "grid_rows",
+        (own, send(position, FAR)),
+        [vmem] * 2,
+        [shaped((2, own_width, TERMS), jnp.bfloat16)],
+        [pltpu.VMEM((2,) + terms, jnp.float32)],
+        LONG,
+    )
+    first, row_terms = lax.optimization_barrier((own, row_terms))
     packed_shape = shaped((LINE, packed_rows, own_width), jnp.bfloat16)
     (packed,) = call(grid_pack, "grid_pack", (first, *lines), [vmem] * LINE, [packed_shape])
     core = send(packed, 1)
-    terms = (TERMS, own_width)
     blocks = shaped((2 * LINE, own_width, own_width), jnp.bfloat16)
     pair = shaped((2,) + field, jnp.float32)
     scratch = [
-        pltpu.VMEM((LINE + 2,) + terms, jnp.float32),
+        pltpu.VMEM((LINE,) + terms, jnp.float32),
         pltpu.VMEM((LINE,) + terms, jnp.bfloat16),
         pltpu.VMEM((2, own_width, own_width), jnp.float32),
     ]
-    near, partial, row_terms = call(
+    near, partial = call(
         functools.partial(grid_near, scale),
         "grid_near",
-        (my_index, packed, far_spot, arguments[4], arguments[2]),
+        (my_index, packed, row_terms, arguments[4], arguments[2]),
         [smem] + [vmem] * 2 + [hbm] * 2,
-        [blocks, pair, shaped((2, own_width, TERMS), jnp.bfloat16)],
+        [blocks, pair],
         scratch
         + [
             pltpu.VMEM(field, jnp.float32),

time: 30.5 us -> 31.1 us (1.020)
  waiting for transfers between devices: 10.5 us -> 13.6 us
  starting transfers between devices: 14.3 us -> 11.8 us
    ppermute x10, waiting for transfers between devices: 10.5 us -> 13.6 us  [send(): lax.ppermute(value, 'row', [(at, at ^ step) for at in range(devices)])]
    ppermute x10, starting transfers between devices: 14.3 us -> 11.8 us  [send(): lax.ppermute(value, 'row', [(at, at ^ step) for at in range(devices)])]
    pallas_call x8 -> x9, Pallas kernels: 4.68 us -> 4.81 us  [call(): pl.pallas_call(body, in_specs=in_specs, out_specs=[vmem] * len(out_shape)...]
  transfers between devices with their start and end apart: 10 -> 10, of which waited for: 6 -> 7; matrix products, arithmetic and copies ran while one was open for 0% -> 0% of each run, Pallas kernels for 6% -> 9%
where the time goes in v6:
time: 31.1 us; the launch traced here: 30.9 us
  waiting for transfers between devices  13.6 us (44%)
  starting transfers between devices  11.8 us (38%)
  Pallas kernels  4.81 us (15%)
  between operations  0.76 us (2%)
    ppermute x10, waiting for transfers between devices, send(): lax.ppermute(value, 'row', [(at, at ^ step) for at in range(devices)])  13.6 us
    ppermute x10, starting transfers between devices, send(): lax.ppermute(value, 'row', [(at, at ^ step) for at in range(devices)])  11.8 us
    pallas_call x9, Pallas kernels, call(): pl.pallas_call(body, in_specs=in_specs, out_specs=[vmem] * len(out_shape)...  4.81 us
  transfers between devices with their start and end apart: 10, of which 7 were waited for; matrix products, arithmetic and copies ran while one was open for 0% of the time, Pallas kernels for 9%

profile of v6, /device:TPU:0, one launch (start us, length us, event | category | flops | bytes accessed | tf_op | source)
XLA Modules:
  0.0 30.9 jit_solution(13250148213765500394)
XLA Ops:
  0.6 4.1 %collective-permute-start = (f32[3,256]{1,0:T(4,128)}, f32[3,256]{1,0:T(4,128)S(1)}, u32[]{:S(2)}, u32[]{:S(2)}) collective-permute-start(f32[3,256]{1,0:T(4,128)} %refs_0_.1), channel_id=1, source_target_pairs={{0,8},{1,9},{2,10},{3,11},{4,12},{5,13},{6,14},{7,15},{8,0},{9,1},... | collective-permute-start | bytes 9224 | tf_op jit(solution)/shard_map/ppermute | solution.py:344
  4.7 1.0 %prepare.1.own_ref.v0_ref = bf16[80,256]{1,0:T(8,128)(2,1)S(1)} custom-call(f32[3,256]{1,0:T(4,128)} %refs_0_.1, s32[2,32]{1,0:T(2,128)} %refs_1_.1, f32[1,256]{1,0:T(1,128)} %bitcast.4, f32[1,256]{1,0:T(1,128)} %bitcast.7, f32[64,256]{1,0:T(8,128)} %rest_0_.1), custom_call_target="tpu_custom_call" | custom-call | tf_op jit(solution)/shard_map/prepare/pallas_call | solution.py:353
  5.7 2.6 %collective-permute-start.3 = (bf16[80,256]{1,0:T(8,128)(2,1)S(1)}, bf16[80,256]{1,0:T(8,128)(2,1)S(1)}, u32[]{:S(2)}, u32[]{:S(2)}) collective-permute-start(bf16[80,256]{1,0:T(8,128)(2,1)S(1)} %prepare.1.own_ref.v0_ref), channel_id=1, source_target_pairs={{0,6},{1,7},{2,4},{3,5},{4,2},{5,3},{6,0},{7,1},{8,14},{9,15},{10,... | collective-permute-start | bytes 122888 | tf_op jit(solution)/shard_map/ppermute | solution.py:344
  8.3 0.4 %collective-permute-start.2 = (bf16[80,256]{1,0:T(8,128)(2,1)S(1)}, bf16[80,256]{1,0:T(8,128)(2,1)S(1)}, u32[]{:S(2)}, u32[]{:S(2)}) collective-permute-start(bf16[80,256]{1,0:T(8,128)(2,1)S(1)} %prepare.1.own_ref.v0_ref), channel_id=1, source_target_pairs={{0,4},{1,5},{2,6},{3,7},{4,0},{5,1},{6,2},{7,3},{8,12},{9,13},{10,... | collective-permute-start | bytes 122888 | tf_op jit(solution)/shard_map/ppermute | solution.py:344
  8.7 0.5 %collective-permute-start.1 = (bf16[80,256]{1,0:T(8,128)(2,1)S(1)}, bf16[80,256]{1,0:T(8,128)(2,1)S(1)}, u32[]{:S(2)}, u32[]{:S(2)}) collective-permute-start(bf16[80,256]{1,0:T(8,128)(2,1)S(1)} %prepare.1.own_ref.v0_ref), channel_id=1, source_target_pairs={{0,2},{1,3},{2,0},{3,1},{4,6},{5,7},{6,4},{7,5},{8,10},{9,11},{10,... | collective-permute-start | bytes 122888 | tf_op jit(solution)/shard_map/ppermute | solution.py:344
  9.3 0.0 collective-permute-done.far_ref
  9.3 0.1 grid_rows.1.row_terms
  9.4 1.7 %collective-permute-done.3.v3_ref = bf16[80,256]{1,0:T(8,128)(2,1)S(1)} collective-permute-done((bf16[80,256]{1,0:T(8,128)(2,1)S(1)}, bf16[80,256]{1,0:T(8,128)(2,1)S(1)}, u32[]{:S(2)}, u32[]{:S(2)}) %collective-permute-start.3) | collective-permute-done | bytes 40992 | tf_op jit(solution)/shard_map/ppermute | solution.py:344
  11.1 1.2 %collective-permute-done.2.v2_ref = bf16[80,256]{1,0:T(8,128)(2,1)S(1)} collective-permute-done((bf16[80,256]{1,0:T(8,128)(2,1)S(1)}, bf16[80,256]{1,0:T(8,128)(2,1)S(1)}, u32[]{:S(2)}, u32[]{:S(2)}) %collective-permute-start.2) | collective-permute-done | bytes 40992 | tf_op jit(solution)/shard_map/ppermute | solution.py:344
  12.3 0.4 %collective-permute-done.1.v1_ref = bf16[80,256]{1,0:T(8,128)(2,1)S(1)} collective-permute-done((bf16[80,256]{1,0:T(8,128)(2,1)S(1)}, bf16[80,256]{1,0:T(8,128)(2,1)S(1)}, u32[]{:S(2)}, u32[]{:S(2)}) %collective-permute-start.1) | collective-permute-done | bytes 40992 | tf_op jit(solution)/shard_map/ppermute | solution.py:344
  12.8 0.1 collective-permute-start.4
  12.8 1.4 %grid_near.1 = (bf16[8,256,256]{2,1,0:T(8,128)(2,1)S(1)}, f32[2,64,256]{2,1,0:T(8,128)S(1)}) custom-call(s32[1]{0:T(128)} %bitcast.me_ref, bf16[4,80,256]{2,1,0:T(8,128)(2,1)S(1)} %grid_pack.1.packed_ref, bf16[2,256,32]{2,1,0:T(8,128)(2,1)S(1)} %grid_rows.1.row_terms, f32[64,256]{1,0:T(8,128)} %rest_0_.1, f32[1,256]{1,0:T(1,128)} %bitcast.5), custom_call_target="tpu_custom_call" | custom-call | tf_op jit(solution)/shard_map/grid_near/pallas_call | solution.py:353
  14.3 0.0 collective-permute-done.4.core_ref
  14.3 1.0 %grid_rest.1 = (bf16[8,256,256]{2,1,0:T(8,128)(2,1)S(1)}, f32[2,64,256]{2,1,0:T(8,128)S(1)}, bf16[144,256]{1,0:T(8,128)(2,1)S(1)}) custom-call(s32[1]{0:T(128)} %bitcast.me_ref, bf16[4,80,256]{2,1,0:T(8,128)(2,1)S(1)} %grid_pack.1.packed_ref, bf16[4,80,256]{2,1,0:T(8,128)(2,1)S(1)} %collective-permute-done.4.core_ref, ...), custom_call_target="tpu_custom_call" | custom-call | tf_op jit(solution)/shard_map/grid_rest/pallas_call | solution.py:353
  15.2 0.4 %collective-permute-start.5 = (bf16[144,256]{1,0:T(8,128)(2,1)S(1)}, bf16[144,256]{1,0:T(8,128)(2,1)S(1)}, u32[]{:S(2)}, u32[]{:S(2)}) collective-permute-start(bf16[144,256]{1,0:T(8,128)(2,1)S(1)} %get-tuple-element.23), channel_id=1, source_target_pairs={{0,8},{1,9},{2,10},{3,11},{4,12},{5,13},{6,14},{7,15},{8,0},{9,1},... | collective-permute-start | bytes 221192 | tf_op jit(solution)/shard_map/ppermute | solution.py:344
  15.6 6.8 %collective-permute-done.5.far_ref = bf16[144,256]{1,0:T(8,128)(2,1)S(1)} collective-permute-done((bf16[144,256]{1,0:T(8,128)(2,1)S(1)}, bf16[144,256]{1,0:T(8,128)(2,1)S(1)}, u32[]{:S(2)}, u32[]{:S(2)}) %collective-permute-start.5) | collective-permute-done | bytes 73760 | tf_op jit(solution)/shard_map/ppermute | solution.py:344
  22.5 0.3 grid_second.1
  22.8 0.1 collective-permute-start.6
  22.9 0.3 grid_third.1.sum_ref
  23.2 0.0 copy-start
  23.2 0.0 copy-start.1
  23.2 0.0 copy-start.2
  23.2 1.0 %collective-permute-done.6.core_ref = bf16[4,64,256]{2,1,0:T(8,128)(2,1)S(1)} collective-permute-done((bf16[4,64,256]{2,1,0:T(8,128)(2,1)S(1)}, bf16[4,64,256]{2,1,0:T(8,128)(2,1)S(1)}, u32[]{:S(2)}, u32[]{:S(2)}) %collective-permute-start.6) | collective-permute-done | bytes 131104 | tf_op jit(solution)/shard_map/ppermute | solution.py:344
  24.2 0.1 collective-permute-start.7
  24.4 1.9 %collective-permute-start.8 = (bf16[64,256]{1,0:T(8,128)(2,1)S(1)}, bf16[64,256]{1,0:T(8,128)(2,1)S(1)}, u32[]{:S(2)}, u32[]{:S(2)}) collective-permute-start(bf16[64,256]{1,0:T(8,128)(2,1)S(1)} %get-tuple-element.27), channel_id=1, source_target_pairs={{0,4},{1,5},{2,6},{3,7},{4,0},{5,1},{6,2},{7,3},{8,12},{9,13},{10,... | collective-permute-start | bytes 98312 | tf_op jit(solution)/shard_map/ppermute | solution.py:344
  26.3 0.0 copy-start.4
  26.3 0.0 copy-start.3
  26.3 1.5 %collective-permute-start.9 = (bf16[64,256]{1,0:T(8,128)(2,1)S(1)}, bf16[64,256]{1,0:T(8,128)(2,1)S(1)}, u32[]{:S(2)}, u32[]{:S(2)}) collective-permute-start(bf16[64,256]{1,0:T(8,128)(2,1)S(1)} %get-tuple-element.28), channel_id=1, source_target_pairs={{0,2},{1,3},{2,0},{3,1},{4,6},{5,7},{6,4},{7,5},{8,10},{9,11},{10,... | collective-permute-start | bytes 98312 | tf_op jit(solution)/shard_map/ppermute | solution.py:344
  27.8 1.4 %collective-permute-done.7.q3_ref = bf16[64,256]{1,0:T(8,128)(2,1)S(1)} collective-permute-done((bf16[64,256]{1,0:T(8,128)(2,1)S(1)}, bf16[64,256]{1,0:T(8,128)(2,1)S(1)}, u32[]{:S(2)}, u32[]{:S(2)}) %collective-permute-start.7) | collective-permute-done | bytes 32800 | tf_op jit(solution)/shard_map/ppermute | solution.py:344
  29.2 0.0 collective-permute-done.8.q2_ref
  29.2 1.0 %collective-permute-done.9.q1_ref = bf16[64,256]{1,0:T(8,128)(2,1)S(1)} collective-permute-done((bf16[64,256]{1,0:T(8,128)(2,1)S(1)}, bf16[64,256]{1,0:T(8,128)(2,1)S(1)}, u32[]{:S(2)}, u32[]{:S(2)}) %collective-permute-start.9) | collective-permute-done | bytes 32800 | tf_op jit(solution)/shard_map/ppermute | solution.py:344
  30.2 0.0 copy-done
  30.2 0.0 copy-done.1
  30.2 0.0 copy-done.2
  30.2 0.0 copy-done.4
  30.2 0.0 copy-done.3
  30.2 0.7 %grid_last.1 = (f32[64,256]{1,0:T(8,128)}, f32[1,256]{1,0:T(1,128)}) custom-call(bf16[64,256]{1,0:T(8,128)(2,1)S(1)} %collective-permute-done.7.q3_ref, bf16[64,256]{1,0:T(8,128)(2,1)S(1)} %collective-permute-done.8.q2_ref, bf16[64,256]{1,0:T(8,128)(2,1)S(1)} %collective-permute-done.9.q1_ref, f32[64,256]{1,0:T(8,128)S(1)} %get-tuple-element.29.q0_ref, ...), custom_call_target="tpu_custom_call" | custom-call | tf_op jit(solution)/shard_map/grid_last/pallas_call | solution.py:353
  (2 shorter events, 0.0 us)
Async XLA Ops:
  0.6 8.6 %collective-permute-start = (f32[3,256]{1,0:T(4,128)}, f32[3,256]{1,0:T(4,128)S(1)}, u32[]{:S(2)}, u32[]{:S(2)}) collective-permute-start(f32[3,256]{1,0:T(4,128)} %refs_0_.1), channel_id=1, source_target_pairs={{0,8},{1,9},{2,10},{3,11},{4,12},{5,13},{6,14},{7,15},{8,0},{9,1},... | collective-permute-start | bytes 9224 | tf_op jit(solution)/shard_map/ppermute | solution.py:344
  5.7 5.4 %collective-permute-start.3 = (bf16[80,256]{1,0:T(8,128)(2,1)S(1)}, bf16[80,256]{1,0:T(8,128)(2,1)S(1)}, u32[]{:S(2)}, u32[]{:S(2)}) collective-permute-start(bf16[80,256]{1,0:T(8,128)(2,1)S(1)} %prepare.1.own_ref.v0_ref), channel_id=1, source_target_pairs={{0,6},{1,7},{2,4},{3,5},{4,2},{5,3},{6,0},{7,1},{8,14},{9,15},{10,... | collective-permute-start | bytes 122888 | tf_op jit(solution)/shard_map/ppermute | solution.py:344
  8.3 4.0 %collective-permute-start.2 = (bf16[80,256]{1,0:T(8,128)(2,1)S(1)}, bf16[80,256]{1,0:T(8,128)(2,1)S(1)}, u32[]{:S(2)}, u32[]{:S(2)}) collective-permute-start(bf16[80,256]{1,0:T(8,128)(2,1)S(1)} %prepare.1.own_ref.v0_ref), channel_id=1, source_target_pairs={{0,4},{1,5},{2,6},{3,7},{4,0},{5,1},{6,2},{7,3},{8,12},{9,13},{10,... | collective-permute-start | bytes 122888 | tf_op jit(solution)/shard_map/ppermute | solution.py:344
  8.7 4.0 %collective-permute-start.1 = (bf16[80,256]{1,0:T(8,128)(2,1)S(1)}, bf16[80,256]{1,0:T(8,128)(2,1)S(1)}, u32[]{:S(2)}, u32[]{:S(2)}) collective-permute-start(bf16[80,256]{1,0:T(8,128)(2,1)S(1)} %prepare.1.own_ref.v0_ref), channel_id=1, source_target_pairs={{0,2},{1,3},{2,0},{3,1},{4,6},{5,7},{6,4},{7,5},{8,10},{9,11},{10,... | collective-permute-start | bytes 122888 | tf_op jit(solution)/shard_map/ppermute | solution.py:344
  12.8 1.5 %collective-permute-start.4 = (bf16[4,80,256]{2,1,0:T(8,128)(2,1)S(1)}, bf16[4,80,256]{2,1,0:T(8,128)(2,1)S(1)}, u32[]{:S(2)}, u32[]{:S(2)}) collective-permute-start(bf16[4,80,256]{2,1,0:T(8,128)(2,1)S(1)} %grid_pack.1.packed_ref), channel_id=1, source_target_pairs={{0,1},{1,0},{2,3},{3,2},{4,5},{5,4},{6,7},{7,6},{8,9},{9,8},{10,11... | collective-permute-start | bytes 491528 | tf_op jit(solution)/shard_map/ppermute | solution.py:344
  15.2 7.2 %collective-permute-start.5 = (bf16[144,256]{1,0:T(8,128)(2,1)S(1)}, bf16[144,256]{1,0:T(8,128)(2,1)S(1)}, u32[]{:S(2)}, u32[]{:S(2)}) collective-permute-start(bf16[144,256]{1,0:T(8,128)(2,1)S(1)} %get-tuple-element.23), channel_id=1, source_target_pairs={{0,8},{1,9},{2,10},{3,11},{4,12},{5,13},{6,14},{7,15},{8,0},{9,1},... | collective-permute-start | bytes 221192 | tf_op jit(solution)/shard_map/ppermute | solution.py:344
  22.8 1.4 %collective-permute-start.6 = (bf16[4,64,256]{2,1,0:T(8,128)(2,1)S(1)}, bf16[4,64,256]{2,1,0:T(8,128)(2,1)S(1)}, u32[]{:S(2)}, u32[]{:S(2)}) collective-permute-start(bf16[4,64,256]{2,1,0:T(8,128)(2,1)S(1)} %get-tuple-element.25), channel_id=1, source_target_pairs={{0,1},{1,0},{2,3},{3,2},{4,5},{5,4},{6,7},{7,6},{8,9},{9,8},{10,11... | collective-permute-start | bytes 393224 | tf_op jit(solution)/shard_map/ppermute | solution.py:344
  23.2 7.0 %copy-start = (f32[64,256]{1,0:T(8,128)S(1)}, f32[64,256]{1,0:T(8,128)}, u32[]{:S(2)}) copy-start(f32[64,256]{1,0:T(8,128)} %rest_0_.1) | copy-start | bytes 196612
  23.2 7.0 %copy-start.1 = (bf16[64,256]{1,0:T(8,128)(2,1)S(1)}, bf16[64,256]{1,0:T(8,128)(2,1)}, u32[]{:S(2)}) copy-start(bf16[64,256]{1,0:T(8,128)(2,1)} %rest_3_.1) | copy-start | bytes 98308
  23.2 7.0 %copy-start.2 = (bf16[64,256]{1,0:T(8,128)(2,1)S(1)}, bf16[64,256]{1,0:T(8,128)(2,1)}, u32[]{:S(2)}) copy-start(bf16[64,256]{1,0:T(8,128)(2,1)} %rest_4_.1) | copy-start | bytes 98308
  24.2 5.0 %collective-permute-start.7 = (bf16[64,256]{1,0:T(8,128)(2,1)S(1)}, bf16[64,256]{1,0:T(8,128)(2,1)S(1)}, u32[]{:S(2)}, u32[]{:S(2)}) collective-permute-start(bf16[64,256]{1,0:T(8,128)(2,1)S(1)} %get-tuple-element.26), channel_id=1, source_target_pairs={{0,6},{1,7},{2,4},{3,5},{4,2},{5,3},{6,0},{7,1},{8,14},{9,15},{10,... | collective-permute-start | bytes 98312 | tf_op jit(solution)/shard_map/ppermute | solution.py:344
  24.4 4.8 %collective-permute-start.8 = (bf16[64,256]{1,0:T(8,128)(2,1)S(1)}, bf16[64,256]{1,0:T(8,128)(2,1)S(1)}, u32[]{:S(2)}, u32[]{:S(2)}) collective-permute-start(bf16[64,256]{1,0:T(8,128)(2,1)S(1)} %get-tuple-element.27), channel_id=1, source_target_pairs={{0,4},{1,5},{2,6},{3,7},{4,0},{5,1},{6,2},{7,3},{8,12},{9,13},{10,... | collective-permute-start | bytes 98312 | tf_op jit(solution)/shard_map/ppermute | solution.py:344
  26.3 3.9 %copy-start.4 = (f32[256]{0:T(256)S(1)}, f32[256]{0:T(256)}, u32[]{:S(2)}) copy-start(f32[256]{0:T(256)} %param.10) | copy-start | bytes 3076
  26.3 3.9 %copy-start.3 = (f32[256]{0:T(256)S(1)}, f32[256]{0:T(256)}, u32[]{:S(2)}) copy-start(f32[256]{0:T(256)} %param.11) | copy-start | bytes 3076
  26.3 3.9 %collective-permute-start.9 = (bf16[64,256]{1,0:T(8,128)(2,1)S(1)}, bf16[64,256]{1,0:T(8,128)(2,1)S(1)}, u32[]{:S(2)}, u32[]{:S(2)}) collective-permute-start(bf16[64,256]{1,0:T(8,128)(2,1)S(1)} %get-tuple-element.28), channel_id=1, source_target_pairs={{0,2},{1,3},{2,0},{3,1},{4,6},{5,7},{6,4},{7,5},{8,10},{9,11},{10,... | collective-permute-start | bytes 98312 | tf_op jit(solution)/shard_map/ppermute | solution.py:344

commit v7 on v5

--- a/solution.py
+++ b/solution.py
@@ -13,7 +13,8 @@
 GROUP = 16
 LINE = 4
 GRID = 16
-FAR = 8
+STEP = 4
+FAR = 2
 EXTRA = 16
 TERMS = 32
 VMEM_BYTES = 48 * 1024 * 1024
@@ -186,7 +187,7 @@
         if t == 0 and v == 0 and w == 0:
             form_own(row_chunk, slot, words[v], out_ref)
         else:
-            form_block(row_chunk, jnp.bitwise_xor(me, 2 * v + w), slot, words[v], out_ref)
+            form_block(row_chunk, jnp.bitwise_xor(me, STEP * v + w), slot, words[v], out_ref)
         if place:
             add(place - 1)
     add(len(blocks) - 1)
@@ -373,7 +374,7 @@
         + [pltpu.VMEM(value.shape, value.dtype) for value in arguments]
         + [pltpu.SemaphoreType.DMA((5,))],
     )
-    lines = [send(own, 2 * v) for v in range(1, LINE)]
+    lines = [send(own, STEP * v) for v in range(1, LINE)]
     far_spot = send(spot, FAR)
     first, far_spot = lax.optimization_barrier((own, far_spot))
     packed_shape = shaped((LINE, packed_rows, own_width), jnp.bfloat16)
@@ -427,7 +428,7 @@
         [vmem] * 2,
         [shaped(field, jnp.float32)] + [shaped(field, jnp.bfloat16)] * 3,
     )
-    lines = [send(sums[v], 2 * v) for v in range(1, LINE)]
+    lines = [send(sums[v], STEP * v) for v in range(1, LINE)]
     adjoint, grad = call(
         functools.partial(grid_last, scale),
         "grid_last",

time: 30.5 us -> 29.5 us (0.967)
  starting transfers between devices: 14.3 us -> 13.5 us
    ppermute x10, starting transfers between devices: 14.3 us -> 13.5 us  [send(): lax.ppermute(value, 'row', [(at, at ^ step) for at in range(devices)])]
where the time goes in v7:
time: 29.5 us; the launch traced here: 29.3 us
  starting transfers between devices  13.5 us (46%)
  waiting for transfers between devices  10.3 us (35%)
  Pallas kernels  4.68 us (16%)
  between operations  0.76 us (3%)
    ppermute x10, starting transfers between devices, send(): lax.ppermute(value, 'row', [(at, at ^ step) for at in range(devices)])  13.5 us
    ppermute x10, waiting for transfers between devices, send(): lax.ppermute(value, 'row', [(at, at ^ step) for at in range(devices)])  10.3 us
    pallas_call x8, Pallas kernels, call(): pl.pallas_call(body, in_specs=in_specs, out_specs=[vmem] * len(out_shape)...  4.68 us
  transfers between devices with their start and end apart: 10, of which 6 were waited for; matrix products, arithmetic and copies ran while one was open for 0% of the time, Pallas kernels for 6%

profile of v7, /device:TPU:0, one launch (start us, length us, event | category | flops | bytes accessed | tf_op | source)
XLA Modules:
  0.0 29.3 jit_solution(18412451089203592465)
XLA Ops:
  0.6 1.0 %prepare.1 = (bf16[80,256]{1,0:T(8,128)(2,1)S(1)}, f32[3,256]{1,0:T(4,128)S(1)}) custom-call(f32[3,256]{1,0:T(4,128)} %refs_0_.1, s32[2,32]{1,0:T(2,128)} %refs_1_.1, f32[1,256]{1,0:T(1,128)} %bitcast.4, f32[1,256]{1,0:T(1,128)} %bitcast.7, f32[64,256]{1,0:T(8,128)} %rest_0_.1), custom_call_target="tpu_custom_call" | custom-call | tf_op jit(solution)/shard_map/prepare/pallas_call | solution.py:353
  1.6 5.1 %collective-permute-start.3 = (bf16[80,256]{1,0:T(8,128)(2,1)S(1)}, bf16[80,256]{1,0:T(8,128)(2,1)S(1)}, u32[]{:S(2)}, u32[]{:S(2)}) collective-permute-start(bf16[80,256]{1,0:T(8,128)(2,1)S(1)} %get-tuple-element.22.v0_ref), channel_id=1, source_target_pairs={{0,12},{1,13},{2,14},{3,15},{4,8},{5,9},{6,10},{7,11},{8,4},{9,5},... | collective-permute-start | bytes 122888 | tf_op jit(solution)/shard_map/ppermute | solution.py:344
  6.7 0.0 collective-permute-start.2
  6.7 0.6 %collective-permute-start.1 = (bf16[80,256]{1,0:T(8,128)(2,1)S(1)}, bf16[80,256]{1,0:T(8,128)(2,1)S(1)}, u32[]{:S(2)}, u32[]{:S(2)}) collective-permute-start(bf16[80,256]{1,0:T(8,128)(2,1)S(1)} %get-tuple-element.22.v0_ref), channel_id=1, source_target_pairs={{0,4},{1,5},{2,6},{3,7},{4,0},{5,1},{6,2},{7,3},{8,12},{9,13},{10,... | collective-permute-start | bytes 122888 | tf_op jit(solution)/shard_map/ppermute | solution.py:344
  7.4 1.6 %collective-permute-start = (f32[3,256]{1,0:T(4,128)S(1)}, f32[3,256]{1,0:T(4,128)S(1)}, u32[]{:S(2)}, u32[]{:S(2)}) collective-permute-start(f32[3,256]{1,0:T(4,128)S(1)} %get-tuple-element.21), channel_id=1, source_target_pairs={{0,2},{1,3},{2,0},{3,1},{4,6},{5,7},{6,4},{7,5},{8,10},{9,11},{10,... | collective-permute-start | bytes 9224 | tf_op jit(solution)/shard_map/ppermute | solution.py:344
  9.0 2.0 %collective-permute-done.far_ref = f32[3,256]{1,0:T(4,128)S(1)} collective-permute-done((f32[3,256]{1,0:T(4,128)S(1)}, f32[3,256]{1,0:T(4,128)S(1)}, u32[]{:S(2)}, u32[]{:S(2)}) %collective-permute-start) | collective-permute-done | bytes 3104 | tf_op jit(solution)/shard_map/ppermute | solution.py:344
  11.0 0.0 collective-permute-done.3.v3_ref
  11.0 0.6 %collective-permute-done.2.v2_ref = bf16[80,256]{1,0:T(8,128)(2,1)S(1)} collective-permute-done((bf16[80,256]{1,0:T(8,128)(2,1)S(1)}, bf16[80,256]{1,0:T(8,128)(2,1)S(1)}, u32[]{:S(2)}, u32[]{:S(2)}) %collective-permute-start.2) | collective-permute-done | bytes 40992 | tf_op jit(solution)/shard_map/ppermute | solution.py:344
  11.6 0.0 collective-permute-done.1.v1_ref
  11.6 0.1 collective-permute-start.4
  11.7 1.4 %grid_near.1 = (bf16[8,256,256]{2,1,0:T(8,128)(2,1)S(1)}, f32[2,64,256]{2,1,0:T(8,128)S(1)}, bf16[2,256,32]{2,1,0:T(8,128)(2,1)S(1)}) custom-call(s32[1]{0:T(128)} %bitcast.me_ref, bf16[4,80,256]{2,1,0:T(8,128)(2,1)S(1)} %grid_pack.1.packed_ref, f32[3,256]{1,0:T(4,128)S(1)} %collective-permute-done.far_ref, f32[64,256]{1,0:T(8,128)} %rest_0_.1, f32[1,256]{1,0:T(1,128)} %bitcast.5), custom_call_target="tpu_custom_call" | custom-call | tf_op jit(solution)/shard_map/grid_near/pallas_call | solution.py:353
  13.2 0.0 collective-permute-done.4.core_ref
  13.2 1.0 %grid_rest.1 = (bf16[8,256,256]{2,1,0:T(8,128)(2,1)S(1)}, f32[2,64,256]{2,1,0:T(8,128)S(1)}, bf16[144,256]{1,0:T(8,128)(2,1)S(1)}) custom-call(s32[1]{0:T(128)} %bitcast.me_ref, bf16[4,80,256]{2,1,0:T(8,128)(2,1)S(1)} %grid_pack.1.packed_ref, bf16[4,80,256]{2,1,0:T(8,128)(2,1)S(1)} %collective-permute-done.4.core_ref, ...), custom_call_target="tpu_custom_call" | custom-call | tf_op jit(solution)/shard_map/grid_rest/pallas_call | solution.py:353
  14.2 1.6 %collective-permute-start.5 = (bf16[144,256]{1,0:T(8,128)(2,1)S(1)}, bf16[144,256]{1,0:T(8,128)(2,1)S(1)}, u32[]{:S(2)}, u32[]{:S(2)}) collective-permute-start(bf16[144,256]{1,0:T(8,128)(2,1)S(1)} %get-tuple-element.29), channel_id=1, source_target_pairs={{0,2},{1,3},{2,0},{3,1},{4,6},{5,7},{6,4},{7,5},{8,10},{9,11},{10,... | collective-permute-start | bytes 221192 | tf_op jit(solution)/shard_map/ppermute | solution.py:344
  15.7 3.2 %collective-permute-done.5.far_ref = bf16[144,256]{1,0:T(8,128)(2,1)S(1)} collective-permute-done((bf16[144,256]{1,0:T(8,128)(2,1)S(1)}, bf16[144,256]{1,0:T(8,128)(2,1)S(1)}, u32[]{:S(2)}, u32[]{:S(2)}) %collective-permute-start.5) | collective-permute-done | bytes 73760 | tf_op jit(solution)/shard_map/ppermute | solution.py:344
  18.9 0.3 %grid_second.1 = (bf16[2,64,256]{2,1,0:T(8,128)(2,1)S(1)}, bf16[4,64,256]{2,1,0:T(8,128)(2,1)S(1)}) custom-call(bf16[8,256,256]{2,1,0:T(8,128)(2,1)S(1)} %get-tuple-element.27.rest_ref, f32[2,64,256]{2,1,0:T(8,128)S(1)} %get-tuple-element.28.partial_ref, bf16[4,80,256]{2,1,0:T(8,128)(2,1)S(1)} %grid_pack.1.packed_ref, ...), custom_call_target="tpu_custom_call" | custom-call | tf_op jit(solution)/shard_map/grid_second/pallas_call | solution.py:353
  19.2 0.1 collective-permute-start.6
  19.3 0.3 %grid_third.1.sum_ref = f32[4,64,256]{2,1,0:T(8,128)S(1)} custom-call(bf16[8,256,256]{2,1,0:T(8,128)(2,1)S(1)} %get-tuple-element.24.near_ref, bf16[2,64,256]{2,1,0:T(8,128)(2,1)S(1)} %get-tuple-element.30.scaled_ref), custom_call_target="tpu_custom_call" | custom-call | tf_op jit(solution)/shard_map/grid_third/pallas_call | solution.py:353
  19.6 0.0 copy-start
  19.6 0.0 copy-start.1
  19.6 0.0 copy-start.2
  19.6 1.0 %collective-permute-done.6.core_ref = bf16[4,64,256]{2,1,0:T(8,128)(2,1)S(1)} collective-permute-done((bf16[4,64,256]{2,1,0:T(8,128)(2,1)S(1)}, bf16[4,64,256]{2,1,0:T(8,128)(2,1)S(1)}, u32[]{:S(2)}, u32[]{:S(2)}) %collective-permute-start.6) | collective-permute-done | bytes 131104 | tf_op jit(solution)/shard_map/ppermute | solution.py:344
  20.6 3.2 %collective-permute-start.7 = (bf16[64,256]{1,0:T(8,128)(2,1)S(1)}, bf16[64,256]{1,0:T(8,128)(2,1)S(1)}, u32[]{:S(2)}, u32[]{:S(2)}) collective-permute-start(bf16[64,256]{1,0:T(8,128)(2,1)S(1)} %get-tuple-element.32), channel_id=1, source_target_pairs={{0,12},{1,13},{2,14},{3,15},{4,8},{5,9},{6,10},{7,11},{8,4},{9,5},... | collective-permute-start | bytes 98312 | tf_op jit(solution)/shard_map/ppermute | solution.py:344
  23.8 0.0 collective-permute-start.8
  23.8 0.0 copy-start.4
  23.8 0.0 copy-start.3
  23.8 1.3 %collective-permute-start.9 = (bf16[64,256]{1,0:T(8,128)(2,1)S(1)}, bf16[64,256]{1,0:T(8,128)(2,1)S(1)}, u32[]{:S(2)}, u32[]{:S(2)}) collective-permute-start(bf16[64,256]{1,0:T(8,128)(2,1)S(1)} %get-tuple-element.34), channel_id=1, source_target_pairs={{0,4},{1,5},{2,6},{3,7},{4,0},{5,1},{6,2},{7,3},{8,12},{9,13},{10,... | collective-permute-start | bytes 98312 | tf_op jit(solution)/shard_map/ppermute | solution.py:344
  25.1 1.6 %collective-permute-done.7.q3_ref = bf16[64,256]{1,0:T(8,128)(2,1)S(1)} collective-permute-done((bf16[64,256]{1,0:T(8,128)(2,1)S(1)}, bf16[64,256]{1,0:T(8,128)(2,1)S(1)}, u32[]{:S(2)}, u32[]{:S(2)}) %collective-permute-start.7) | collective-permute-done | bytes 32800 | tf_op jit(solution)/shard_map/ppermute | solution.py:344
  26.7 1.9 %collective-permute-done.8.q2_ref = bf16[64,256]{1,0:T(8,128)(2,1)S(1)} collective-permute-done((bf16[64,256]{1,0:T(8,128)(2,1)S(1)}, bf16[64,256]{1,0:T(8,128)(2,1)S(1)}, u32[]{:S(2)}, u32[]{:S(2)}) %collective-permute-start.8) | collective-permute-done | bytes 32800 | tf_op jit(solution)/shard_map/ppermute | solution.py:344
  28.6 0.0 collective-permute-done.9.q1_ref
  28.6 0.0 copy-done
  28.6 0.0 copy-done.1
  28.6 0.0 copy-done.2
  28.6 0.0 copy-done.4
  28.7 0.0 copy-done.3
  28.7 0.7 %grid_last.1 = (f32[64,256]{1,0:T(8,128)}, f32[1,256]{1,0:T(1,128)}) custom-call(bf16[64,256]{1,0:T(8,128)(2,1)S(1)} %collective-permute-done.7.q3_ref, bf16[64,256]{1,0:T(8,128)(2,1)S(1)} %collective-permute-done.8.q2_ref, bf16[64,256]{1,0:T(8,128)(2,1)S(1)} %collective-permute-done.9.q1_ref, f32[64,256]{1,0:T(8,128)S(1)} %get-tuple-element.35.q0_ref, ...), custom_call_target="tpu_custom_call" | custom-call | tf_op jit(solution)/shard_map/grid_last/pallas_call | solution.py:353
  (2 shorter events, 0.0 us)
Async XLA Ops:
  1.6 9.4 %collective-permute-start.3 = (bf16[80,256]{1,0:T(8,128)(2,1)S(1)}, bf16[80,256]{1,0:T(8,128)(2,1)S(1)}, u32[]{:S(2)}, u32[]{:S(2)}) collective-permute-start(bf16[80,256]{1,0:T(8,128)(2,1)S(1)} %get-tuple-element.22.v0_ref), channel_id=1, source_target_pairs={{0,12},{1,13},{2,14},{3,15},{4,8},{5,9},{6,10},{7,11},{8,4},{9,5},... | collective-permute-start | bytes 122888 | tf_op jit(solution)/shard_map/ppermute | solution.py:344
  6.7 4.9 %collective-permute-start.2 = (bf16[80,256]{1,0:T(8,128)(2,1)S(1)}, bf16[80,256]{1,0:T(8,128)(2,1)S(1)}, u32[]{:S(2)}, u32[]{:S(2)}) collective-permute-start(bf16[80,256]{1,0:T(8,128)(2,1)S(1)} %get-tuple-element.22.v0_ref), channel_id=1, source_target_pairs={{0,8},{1,9},{2,10},{3,11},{4,12},{5,13},{6,14},{7,15},{8,0},{9,1},... | collective-permute-start | bytes 122888 | tf_op jit(solution)/shard_map/ppermute | solution.py:344
  6.7 4.9 %collective-permute-start.1 = (bf16[80,256]{1,0:T(8,128)(2,1)S(1)}, bf16[80,256]{1,0:T(8,128)(2,1)S(1)}, u32[]{:S(2)}, u32[]{:S(2)}) collective-permute-start(bf16[80,256]{1,0:T(8,128)(2,1)S(1)} %get-tuple-element.22.v0_ref), channel_id=1, source_target_pairs={{0,4},{1,5},{2,6},{3,7},{4,0},{5,1},{6,2},{7,3},{8,12},{9,13},{10,... | collective-permute-start | bytes 122888 | tf_op jit(solution)/shard_map/ppermute | solution.py:344
  7.4 3.6 %collective-permute-start = (f32[3,256]{1,0:T(4,128)S(1)}, f32[3,256]{1,0:T(4,128)S(1)}, u32[]{:S(2)}, u32[]{:S(2)}) collective-permute-start(f32[3,256]{1,0:T(4,128)S(1)} %get-tuple-element.21), channel_id=1, source_target_pairs={{0,2},{1,3},{2,0},{3,1},{4,6},{5,7},{6,4},{7,5},{8,10},{9,11},{10,... | collective-permute-start | bytes 9224 | tf_op jit(solution)/shard_map/ppermute | solution.py:344
  11.6 1.5 %collective-permute-start.4 = (bf16[4,80,256]{2,1,0:T(8,128)(2,1)S(1)}, bf16[4,80,256]{2,1,0:T(8,128)(2,1)S(1)}, u32[]{:S(2)}, u32[]{:S(2)}) collective-permute-start(bf16[4,80,256]{2,1,0:T(8,128)(2,1)S(1)} %grid_pack.1.packed_ref), channel_id=1, source_target_pairs={{0,1},{1,0},{2,3},{3,2},{4,5},{5,4},{6,7},{7,6},{8,9},{9,8},{10,11... | collective-permute-start | bytes 491528 | tf_op jit(solution)/shard_map/ppermute | solution.py:344
  14.2 4.7 %collective-permute-start.5 = (bf16[144,256]{1,0:T(8,128)(2,1)S(1)}, bf16[144,256]{1,0:T(8,128)(2,1)S(1)}, u32[]{:S(2)}, u32[]{:S(2)}) collective-permute-start(bf16[144,256]{1,0:T(8,128)(2,1)S(1)} %get-tuple-element.29), channel_id=1, source_target_pairs={{0,2},{1,3},{2,0},{3,1},{4,6},{5,7},{6,4},{7,5},{8,10},{9,11},{10,... | collective-permute-start | bytes 221192 | tf_op jit(solution)/shard_map/ppermute | solution.py:344
  19.2 1.4 %collective-permute-start.6 = (bf16[4,64,256]{2,1,0:T(8,128)(2,1)S(1)}, bf16[4,64,256]{2,1,0:T(8,128)(2,1)S(1)}, u32[]{:S(2)}, u32[]{:S(2)}) collective-permute-start(bf16[4,64,256]{2,1,0:T(8,128)(2,1)S(1)} %get-tuple-element.31), channel_id=1, source_target_pairs={{0,1},{1,0},{2,3},{3,2},{4,5},{5,4},{6,7},{7,6},{8,9},{9,8},{10,11... | collective-permute-start | bytes 393224 | tf_op jit(solution)/shard_map/ppermute | solution.py:344
  19.6 9.1 %copy-start = (f32[64,256]{1,0:T(8,128)S(1)}, f32[64,256]{1,0:T(8,128)}, u32[]{:S(2)}) copy-start(f32[64,256]{1,0:T(8,128)} %rest_0_.1) | copy-start | bytes 196612
  19.6 9.0 %copy-start.1 = (bf16[64,256]{1,0:T(8,128)(2,1)S(1)}, bf16[64,256]{1,0:T(8,128)(2,1)}, u32[]{:S(2)}) copy-start(bf16[64,256]{1,0:T(8,128)(2,1)} %rest_3_.1) | copy-start | bytes 98308
  19.6 9.0 %copy-start.2 = (bf16[64,256]{1,0:T(8,128)(2,1)S(1)}, bf16[64,256]{1,0:T(8,128)(2,1)}, u32[]{:S(2)}) copy-start(bf16[64,256]{1,0:T(8,128)(2,1)} %rest_4_.1) | copy-start | bytes 98308
  20.6 6.1 %collective-permute-start.7 = (bf16[64,256]{1,0:T(8,128)(2,1)S(1)}, bf16[64,256]{1,0:T(8,128)(2,1)S(1)}, u32[]{:S(2)}, u32[]{:S(2)}) collective-permute-start(bf16[64,256]{1,0:T(8,128)(2,1)S(1)} %get-tuple-element.32), channel_id=1, source_target_pairs={{0,12},{1,13},{2,14},{3,15},{4,8},{5,9},{6,10},{7,11},{8,4},{9,5},... | collective-permute-start | bytes 98312 | tf_op jit(solution)/shard_map/ppermute | solution.py:344
  23.8 4.8 %collective-permute-start.8 = (bf16[64,256]{1,0:T(8,128)(2,1)S(1)}, bf16[64,256]{1,0:T(8,128)(2,1)S(1)}, u32[]{:S(2)}, u32[]{:S(2)}) collective-permute-start(bf16[64,256]{1,0:T(8,128)(2,1)S(1)} %get-tuple-element.33), channel_id=1, source_target_pairs={{0,8},{1,9},{2,10},{3,11},{4,12},{5,13},{6,14},{7,15},{8,0},{9,1},... | collective-permute-start | bytes 98312 | tf_op jit(solution)/shard_map/ppermute | solution.py:344
  23.8 4.8 %copy-start.4 = (f32[256]{0:T(256)S(1)}, f32[256]{0:T(256)}, u32[]{:S(2)}) copy-start(f32[256]{0:T(256)} %param.10) | copy-start | bytes 3076
  23.8 4.8 %copy-start.3 = (f32[256]{0:T(256)S(1)}, f32[256]{0:T(256)}, u32[]{:S(2)}) copy-start(f32[256]{0:T(256)} %param.11) | copy-start | bytes 3076
  23.8 4.8 %collective-permute-start.9 = (bf16[64,256]{1,0:T(8,128)(2,1)S(1)}, bf16[64,256]{1,0:T(8,128)(2,1)S(1)}, u32[]{:S(2)}, u32[]{:S(2)}) collective-permute-start(bf16[64,256]{1,0:T(8,128)(2,1)S(1)} %get-tuple-element.34), channel_id=1, source_target_pairs={{0,4},{1,5},{2,6},{3,7},{4,0},{5,1},{6,2},{7,3},{8,12},{9,13},{10,... | collective-permute-start | bytes 98312 | tf_op jit(solution)/shard_map/ppermute | solution.py:344

commit v8 on v5

--- a/solution.py
+++ b/solution.py
@@ -11,17 +11,20 @@
 TILE = 128
 SWEEPS = 2
 GROUP = 16
-LINE = 4
+LINE = 8
 GRID = 16
-FAR = 8
+STEP = 2
+FAR = 1
 EXTRA = 16
 TERMS = 32
 VMEM_BYTES = 48 * 1024 * 1024
 GRID_BYTES = 8 * 1024 * 1024
 
 
-NEAR = [(t, v, 0) for t in range(2) for v in range(LINE)]
-REST = [(t, v, 1) for t in range(2) for v in range(LINE)]
+FIRST = (0, 7, 6, 5, 4)
+THEN = (3, 2, 1)
+NEAR = [(t, v) for t in range(2) for v in FIRST]
+REST = [(t, v) for t in range(2) for v in THEN]
 
 
 def three_terms(value):
@@ -167,63 +170,46 @@
     held = {}
 
     def measure(place):
-        t, v, w = blocks[place]
+        t, v = blocks[place]
         distance[place % 2] = times(row_terms[t], col_terms[v])
 
     def add(place):
-        t, v, w = blocks[place]
+        t, v = blocks[place]
         term = times_transpose(fields(v), kernel_ref[place])
         held[t] = (held[t] if t in held else start(t)) + term
         if place + 1 == len(blocks) or blocks[place + 1][0] != t:
             finish_row(t, held[t])
 
     measure(0)
-    for place, (t, v, w) in enumerate(blocks):
+    for place, (t, v) in enumerate(blocks):
         if place + 1 < len(blocks):
             measure(place + 1)
         slot, out_ref = distance.at[place % 2], kernel_ref.at[place]
         row_chunk = jnp.bitwise_xor(me, FAR * t)
-        if t == 0 and v == 0 and w == 0:
+        if t == 0 and v == 0:
             form_own(row_chunk, slot, words[v], out_ref)
         else:
-            form_block(row_chunk, jnp.bitwise_xor(me, 2 * v + w), slot, words[v], out_ref)
+            form_block(row_chunk, jnp.bitwise_xor(me, STEP * v), slot, words[v], out_ref)
         if place:
             add(place - 1)
     add(len(blocks) - 1)
 
 
-def column_terms(rows, terms, col_terms):
-    words = []
-    for v in range(LINE):
-        position, word = read_extra(rows(v))
-        words.append(word)
-        distance_terms(position, terms.at[v], False)
-        col_terms[v] = terms[v].astype(jnp.bfloat16)
+def column_terms(refs, rhs_count, terms, col_terms):
+    words = {}
+    for at, (v, ref) in enumerate(refs.items()):
+        position, words[v] = read_extra(ref[rhs_count:])
+        distance_terms(position, terms.at[at], False)
+        col_terms[v] = terms[at].astype(jnp.bfloat16)
     return words
 
 
-def grid_pack(v0_ref, v1_ref, v2_ref, v3_ref, out_ref):
-    for v, ref in enumerate((v0_ref, v1_ref, v2_ref, v3_ref)):
-        out_ref[v] = ref[...]
-
-
-def grid_near(
-    scale,
-    me_ref,
-    packed_ref,
-    far_ref,
-    seed_hbm,
-    area_hbm,
-    kernel_ref,
-    partial_ref,
-    row_terms,
-    terms,
-    col_terms,
-    distance,
-    seed_ref,
-    area_ref,
-    sems,
-):
+def grid_near(scale, me_ref, far_ref, seed_hbm, area_hbm, *refs):
+    count = len(FIRST)
+    lines = dict(zip(FIRST, refs[:count]))
+    kernel_ref, partial_ref, row_terms, terms, col_terms, distance, seed_ref, area_ref, sems = refs[
+        count:
+    ]
     copies = [
         pltpu.make_async_copy(seed_hbm, seed_ref, sems.at[0]),
         pltpu.make_async_copy(area_hbm, area_ref, sems.at[1]),
@@ -231,24 +217,23 @@
     for copy in copies:
         copy.start()
     rhs_count = seed_ref.shape[0]
-    me = me_ref[0]
-    words = column_terms(lambda v: packed_ref[v, rhs_count:], terms, col_terms)
-    own, _ = read_extra(packed_ref[0, rhs_count:])
+    own, _ = read_extra(lines[0][rhs_count:])
     for t, value in enumerate((own, far_ref[...])):
-        slot = terms.at[LINE + t]
+        slot = terms.at[count + t]
         distance_terms(value, slot, True)
         row_terms[t] = jnp.transpose(slot[...]).astype(jnp.bfloat16)
+    words = column_terms(lines, rhs_count, terms, col_terms)
 
     def finish_row(t, value):
         partial_ref[t] = value
 
     form_all(
         NEAR,
-        me,
+        me_ref[0],
         row_terms,
         col_terms,
         words,
-        lambda v: packed_ref[v, :rhs_count],
+        lambda v: lines[v][:rhs_count],
         lambda t: 0.0,
         (kernel_ref, distance),
         finish_row,
@@ -258,21 +243,12 @@
     partial_ref[0] = partial_ref[0] + seed_ref[...] * (1.0 / (area_ref[...] * scale))
 
 
-def grid_rest(
-    me_ref,
-    packed_ref,
-    core_ref,
-    before_ref,
-    row_terms,
-    kernel_ref,
-    partial_ref,
-    sent_ref,
-    terms,
-    col_terms,
-    distance,
-):
+def grid_rest(me_ref, own_ref, before_ref, row_terms, *refs):
+    count = len(THEN)
+    lines = dict(zip(THEN, refs[:count]))
+    kernel_ref, partial_ref, sent_ref, terms, col_terms, distance = refs[count:]
     rhs_count = before_ref.shape[1]
-    words = column_terms(lambda v: core_ref[v, rhs_count:], terms, col_terms)
+    words = column_terms(lines, rhs_count, terms, col_terms)
 
     def finish_row(t, value):
         partial_ref[t] = value
@@ -284,46 +260,46 @@
         row_terms,
         col_terms,
         words,
-        lambda v: core_ref[v, :rhs_count],
+        lambda v: lines[v][:rhs_count],
         lambda t: before_ref[t],
         (kernel_ref, distance),
         finish_row,
     )
-    sent_ref[2 * rhs_count :] = packed_ref[0, rhs_count:]
-
-
-def product(scaled_ref, kernel_ref, v):
-    return times(scaled_ref[0], kernel_ref[v]) + times(scaled_ref[1], kernel_ref[LINE + v])
-
-
-def grid_second(rest_ref, partial_ref, packed_ref, far_ref, scaled_ref, sent_ref):
+    sent_ref[2 * rhs_count :] = own_ref[rhs_count:]
+
+
+def product(scaled_ref, kernel_ref, places):
+    return times(scaled_ref[0], kernel_ref[places[0]]) + times(
+        scaled_ref[1], kernel_ref[places[1]]
+    )
+
+
+def grid_second(near_ref, partial_ref, own_ref, far_ref, scaled_ref, *out_refs):
     rhs_count = partial_ref.shape[1]
-    extras = (packed_ref[0, rhs_count:], far_ref[2 * rhs_count :, :])
+    extras = (own_ref[rhs_count:], far_ref[2 * rhs_count :, :])
     for t in range(2):
         terms = extras[t].astype(jnp.float32)
         factor = terms[9:10] + terms[10:11] + terms[11:12]
         start = (1 - t) * rhs_count
         total = partial_ref[t] + far_ref[start : start + rhs_count].astype(jnp.float32)
         scaled_ref[t] = (factor * total).astype(jnp.bfloat16)
-    for v in range(LINE):
-        sent_ref[v] = product(scaled_ref, rest_ref, v).astype(jnp.bfloat16)
-
-
-def grid_third(near_ref, scaled_ref, sum_ref):
-    for v in range(LINE):
-        sum_ref[v] = product(scaled_ref, near_ref, v)
-
-
-def grid_fourth(sum_ref, core_ref, q0_ref, q1_ref, q2_ref, q3_ref):
-    for v, ref in enumerate((q0_ref, q1_ref, q2_ref, q3_ref)):
-        ref[...] = (sum_ref[v] + core_ref[v].astype(jnp.float32)).astype(ref.dtype)
-
-
-def grid_last(scale, q3_ref, q2_ref, q1_ref, q0_ref, *rest):
-    total = q0_ref[...]
-    for ref in (q1_ref, q2_ref, q3_ref):
+    for v, ref in zip(FIRST[1:], out_refs):
+        places = [NEAR.index((t, v)) for t in range(2)]
+        ref[...] = product(scaled_ref, near_ref, places).astype(jnp.bfloat16)
+
+
+def grid_third(near_ref, rest_ref, scaled_ref, own_ref, *out_refs):
+    for v, ref in zip(THEN, out_refs):
+        places = [REST.index((t, v)) for t in range(2)]
+        ref[...] = product(scaled_ref, rest_ref, places).astype(jnp.bfloat16)
+    own_ref[...] = product(scaled_ref, near_ref, [NEAR.index((t, 0)) for t in range(2)])
+
+
+def grid_last(scale, *refs):
+    total = refs[LINE - 1][...]
+    for ref in refs[: LINE - 1]:
         total = total + ref[...].astype(jnp.float32)
-    finish(scale, total, *rest)
+    finish(scale, total, *refs[LINE:])
 
 
 def on_grid(adjoint_seed, radiosity, emission, reflectance, area, position, visibility):
@@ -373,27 +349,30 @@
         + [pltpu.VMEM(value.shape, value.dtype) for value in arguments]
         + [pltpu.SemaphoreType.DMA((5,))],
     )
-    lines = [send(own, 2 * v) for v in range(1, LINE)]
-    far_spot = send(spot, FAR)
-    first, far_spot = lax.optimization_barrier((own, far_spot))
-    packed_shape = shaped((LINE, packed_rows, own_width), jnp.bfloat16)
-    (packed,) = call(grid_pack, "grid_pack", (first, *lines), [vmem] * LINE, [packed_shape])
-    core = send(packed, 1)
+    lines = {v: send(own, STEP * v) for v in FIRST[1:] + THEN}
+    lines[0] = own
+    far_spot = send(position, FAR)
     terms = (TERMS, own_width)
-    blocks = shaped((2 * LINE, own_width, own_width), jnp.bfloat16)
     pair = shaped((2,) + field, jnp.float32)
-    scratch = [
-        pltpu.VMEM((LINE + 2,) + terms, jnp.float32),
-        pltpu.VMEM((LINE,) + terms, jnp.bfloat16),
-        pltpu.VMEM((2, own_width, own_width), jnp.float32),
-    ]
+    bfloat16 = shaped(field, jnp.bfloat16)
+
+    def blocks(places):
+        return shaped((len(places), own_width, own_width), jnp.bfloat16)
+
+    def scratch(count):
+        return [
+            pltpu.VMEM((count,) + terms, jnp.float32),
+            pltpu.VMEM((LINE,) + terms, jnp.bfloat16),
+            pltpu.VMEM((2, own_width, own_width), jnp.float32),
+        ]
+
     near, partial, row_terms = call(
         functools.partial(grid_near, scale),
         "grid_near",
-        (my_index, packed, far_spot, arguments[4], arguments[2]),
-        [smem] + [vmem] * 2 + [hbm] * 2,
-        [blocks, pair, shaped((2, own_width, TERMS), jnp.bfloat16)],
-        scratch
+        (my_index, far_spot, arguments[4], arguments[2], *[lines[v] for v in FIRST]),
+        [smem, vmem, hbm, hbm] + [vmem] * len(FIRST),
+        [blocks(NEAR), pair, shaped((2, own_width, TERMS), jnp.bfloat16)],
+        scratch(len(FIRST) + 2)
         + [
             pltpu.VMEM(field, jnp.float32),
             pltpu.VMEM((1, own_width), jnp.float32),
@@ -403,36 +382,32 @@
     rest, partial, sent = call(
         grid_rest,
         "grid_rest",
-        (my_index, packed, core, partial, row_terms),
-        [smem] + [vmem] * 4,
-        [blocks, pair, shaped((2 * rhs_count + EXTRA, own_width), jnp.bfloat16)],
-        scratch,
-    )
-    four = (LINE,) + field
-    scaled, sent = call(
+        (my_index, own, partial, row_terms, *[lines[v] for v in THEN]),
+        [smem] + [vmem] * (3 + len(THEN)),
+        [blocks(REST), pair, shaped((2 * rhs_count + EXTRA, own_width), jnp.bfloat16)],
+        scratch(len(THEN)),
+    )
+    scaled, *sums = call(
         grid_second,
         "grid_second",
-        (rest, partial, packed, send(sent, FAR)),
+        (near, partial, own, send(sent, FAR)),
         [vmem] * 4,
-        [shaped((2,) + field, jnp.bfloat16), shaped(four, jnp.bfloat16)],
-    )
-    other = send(sent, 1)
-    (sums,) = call(
-        grid_third, "grid_third", (near, scaled), [vmem] * 2, [shaped(four, jnp.float32)]
-    )
-    sums = call(
-        grid_fourth,
-        "grid_fourth",
-        (sums, other),
-        [vmem] * 2,
-        [shaped(field, jnp.float32)] + [shaped(field, jnp.bfloat16)] * 3,
-    )
-    lines = [send(sums[v], 2 * v) for v in range(1, LINE)]
+        [shaped((2,) + field, jnp.bfloat16)] + [bfloat16] * (len(FIRST) - 1),
+    )
+    lines = [send(value, STEP * v) for v, value in zip(FIRST[1:], sums)]
+    own_sum, *sums = call(
+        grid_third,
+        "grid_third",
+        (near, rest, scaled),
+        [vmem] * 3,
+        [shaped(field, jnp.float32)] + [bfloat16] * len(THEN),
+    )
+    lines += [send(value, STEP * v) for v, value in zip(THEN, sums)]
     adjoint, grad = call(
         functools.partial(grid_last, scale),
         "grid_last",
-        (*lines[::-1], sums[0], adjoint_seed, area, reflectance, radiosity, emission),
-        [vmem] * 9,
+        (*lines, own_sum, adjoint_seed, area, reflectance, radiosity, emission),
+        [vmem] * (LINE + 5),
         [shaped(field, jnp.float32), shaped((1, own_width), jnp.float32)],
     )
     return adjoint, grad.reshape(own_width)

time: 30.5 us -> 37.3 us (1.22)
  starting transfers between devices: 14.3 us -> 24.2 us
  waiting for transfers between devices: 10.5 us -> 6.49 us
  Pallas kernels: 4.68 us -> 5.62 us
    ppermute x10 -> x16, starting transfers between devices: 14.3 us -> 24.2 us  [send(): lax.ppermute(value, 'row', [(at, at ^ step) for at in range(devices)])]
    ppermute x10 -> x16, waiting for transfers between devices: 10.5 us -> 6.49 us  [send(): lax.ppermute(value, 'row', [(at, at ^ step) for at in range(devices)])]
    pallas_call x8 -> x6, Pallas kernels: 4.68 us -> 5.62 us  [call(): pl.pallas_call(body, in_specs=in_specs, out_specs=[vmem] * len(out_shape)...]
  transfers between devices with their start and end apart: 10 -> 16, of which waited for: 6 -> 4; matrix products, arithmetic and copies ran while one was open for 0% -> 0% of each run, Pallas kernels for 6% -> 6%
where the time goes in v8:
time: 37.3 us; the launch traced here: 37.1 us
  starting transfers between devices  24.2 us (65%)
  waiting for transfers between devices  6.49 us (17%)
  Pallas kernels  5.62 us (15%)
  between operations  0.79 us (2%)
    ppermute x16, starting transfers between devices, send(): lax.ppermute(value, 'row', [(at, at ^ step) for at in range(devices)])  24.2 us
    ppermute x16, waiting for transfers between devices, send(): lax.ppermute(value, 'row', [(at, at ^ step) for at in range(devices)])  6.49 us
    pallas_call x6, Pallas kernels, call(): pl.pallas_call(body, in_specs=in_specs, out_specs=[vmem] * len(out_shape)...  5.62 us
  transfers between devices with their start and end apart: 16, of which 4 were waited for; matrix products, arithmetic and copies ran while one was open for 0% of the time, Pallas kernels for 6%

profile of v8, /device:TPU:0, one launch (start us, length us, event | category | flops | bytes accessed | tf_op | source)
XLA Modules:
  0.0 37.1 jit_solution(10860404120963293727)
XLA Ops:
  0.6 1.5 %prepare.1 = (bf16[80,256]{1,0:T(8,128)(2,1)S(1)}, f32[3,256]{1,0:T(4,128)}) custom-call(f32[3,256]{1,0:T(4,128)} %refs_0_.1, s32[2,32]{1,0:T(2,128)} %refs_1_.1, f32[1,256]{1,0:T(1,128)} %bitcast.4, f32[1,256]{1,0:T(1,128)} %bitcast.7, f32[64,256]{1,0:T(8,128)} %refs_8_.1), custom_call_target="tpu_custom_call" | custom-call | tf_op jit(solution)/shard_map/prepare/pallas_call | solution.py:328
  2.2 4.1 %collective-permute-start.4 = (bf16[80,256]{1,0:T(8,128)(2,1)S(1)}, bf16[80,256]{1,0:T(8,128)(2,1)S(1)}, u32[]{:S(2)}, u32[]{:S(2)}) collective-permute-start(bf16[80,256]{1,0:T(8,128)(2,1)S(1)} %get-tuple-element.20.refs_0_.own_ref), channel_id=1, source_target_pairs={{0,8},{1,9},{2,10},{3,11},{4,12},{5,13},{6,14},{7,15},{8,0},{9,1},... | collective-permute-start | bytes 122888 | tf_op jit(solution)/shard_map/ppermute | solution.py:319
  6.3 1.3 %collective-permute-start.3 = (bf16[80,256]{1,0:T(8,128)(2,1)S(1)}, bf16[80,256]{1,0:T(8,128)(2,1)S(1)}, u32[]{:S(2)}, u32[]{:S(2)}) collective-permute-start(bf16[80,256]{1,0:T(8,128)(2,1)S(1)} %get-tuple-element.20.refs_0_.own_ref), channel_id=1, source_target_pairs={{0,10},{1,11},{2,8},{3,9},{4,14},{5,15},{6,12},{7,13},{8,2},{9,3},... | collective-permute-start | bytes 122888 | tf_op jit(solution)/shard_map/ppermute | solution.py:319
  7.5 0.0 collective-permute-start
  7.5 3.6 %collective-permute-start.2 = (bf16[80,256]{1,0:T(8,128)(2,1)S(1)}, bf16[80,256]{1,0:T(8,128)(2,1)S(1)}, u32[]{:S(2)}, u32[]{:S(2)}) collective-permute-start(bf16[80,256]{1,0:T(8,128)(2,1)S(1)} %get-tuple-element.20.refs_0_.own_ref), channel_id=1, source_target_pairs={{0,12},{1,13},{2,14},{3,15},{4,8},{5,9},{6,10},{7,11},{8,4},{9,5},... | collective-permute-start | bytes 122888 | tf_op jit(solution)/shard_map/ppermute | solution.py:319
  11.2 0.0 collective-permute-start.1
  11.2 0.0 collective-permute-done.far_ref
  11.2 1.7 %collective-permute-start.7 = (bf16[80,256]{1,0:T(8,128)(2,1)S(1)}, bf16[80,256]{1,0:T(8,128)(2,1)S(1)}, u32[]{:S(2)}, u32[]{:S(2)}) collective-permute-start(bf16[80,256]{1,0:T(8,128)(2,1)S(1)} %get-tuple-element.20.refs_0_.own_ref), channel_id=1, source_target_pairs={{0,2},{1,3},{2,0},{3,1},{4,6},{5,7},{6,4},{7,5},{8,10},{9,11},{10,... | collective-permute-start | bytes 122888 | tf_op jit(solution)/shard_map/ppermute | solution.py:319
  12.8 0.0 collective-permute-done.4.refs_4_
  12.8 0.0 collective-permute-start.6
  12.8 0.0 collective-permute-done.3.refs_3_
  12.9 2.2 %collective-permute-start.5 = (bf16[80,256]{1,0:T(8,128)(2,1)S(1)}, bf16[80,256]{1,0:T(8,128)(2,1)S(1)}, u32[]{:S(2)}, u32[]{:S(2)}) collective-permute-start(bf16[80,256]{1,0:T(8,128)(2,1)S(1)} %get-tuple-element.20.refs_0_.own_ref), channel_id=1, source_target_pairs={{0,6},{1,7},{2,4},{3,5},{4,2},{5,3},{6,0},{7,1},{8,14},{9,15},{10,... | collective-permute-start | bytes 122888 | tf_op jit(solution)/shard_map/ppermute | solution.py:319
  15.1 0.0 collective-permute-done.2.refs_2_
  15.1 2.9 %collective-permute-done.1.refs_1_ = bf16[80,256]{1,0:T(8,128)(2,1)S(1)} collective-permute-done((bf16[80,256]{1,0:T(8,128)(2,1)S(1)}, bf16[80,256]{1,0:T(8,128)(2,1)S(1)}, u32[]{:S(2)}, u32[]{:S(2)}) %collective-permute-start.1) | collective-permute-done | bytes 40992 | tf_op jit(solution)/shard_map/ppermute | solution.py:319
  18.0 1.9 %grid_near.1 = (bf16[10,256,256]{2,1,0:T(8,128)(2,1)S(1)}, f32[2,64,256]{2,1,0:T(8,128)S(1)}, bf16[2,256,32]{2,1,0:T(8,128)(2,1)S(1)}) custom-call(s32[1]{0:T(128)} %bitcast.me_ref, f32[3,256]{1,0:T(4,128)S(1)} %collective-permute-done.far_ref, f32[64,256]{1,0:T(8,128)} %refs_8_.1, f32[1,256]{1,0:T(1,128)} %bitcast.5, ...), custom_call_target="tpu_custom_call" | custom-call | tf_op jit(solution)/shard_map/grid_near/pallas_call | solution.py:328
  19.9 0.0 collective-permute-done.7.refs_2_
  20.0 0.0 collective-permute-done.6.refs_1_
  20.0 0.0 collective-permute-done.5.refs_0_
  20.0 0.8 %grid_rest.1 = (bf16[6,256,256]{2,1,0:T(8,128)(2,1)S(1)}, f32[2,64,256]{2,1,0:T(8,128)S(1)}, bf16[144,256]{1,0:T(8,128)(2,1)S(1)}) custom-call(s32[1]{0:T(128)} %bitcast.me_ref, bf16[80,256]{1,0:T(8,128)(2,1)S(1)} %get-tuple-element.20.refs_0_.own_ref, f32[2,64,256]{2,1,0:T(8,128)S(1)} %get-tuple-element.22.before_ref, ...), custom_call_target="tpu_custom_call" | custom-call | tf_op jit(solution)/shard_map/grid_rest/pallas_call | solution.py:328
  20.8 0.1 collective-permute-start.8
  20.9 1.3 %collective-permute-done.8.far_ref = bf16[144,256]{1,0:T(8,128)(2,1)S(1)} collective-permute-done((bf16[144,256]{1,0:T(8,128)(2,1)S(1)}, bf16[144,256]{1,0:T(8,128)(2,1)S(1)}, u32[]{:S(2)}, u32[]{:S(2)}) %collective-permute-start.8) | collective-permute-done | bytes 73760 | tf_op jit(solution)/shard_map/ppermute | solution.py:319
  22.2 0.3 grid_second.1
  22.5 0.0 copy-start
  22.5 0.0 copy-start.1
  22.5 0.0 copy-start.2
  22.5 0.0 copy-start.3
  22.5 0.0 copy-start.4
  22.5 1.9 %collective-permute-start.9 = (bf16[64,256]{1,0:T(8,128)(2,1)S(1)}, bf16[64,256]{1,0:T(8,128)(2,1)S(1)}, u32[]{:S(2)}, u32[]{:S(2)}) collective-permute-start(bf16[64,256]{1,0:T(8,128)(2,1)S(1)} %get-tuple-element.26), channel_id=1, source_target_pairs={{0,14},{1,15},{2,12},{3,13},{4,10},{5,11},{6,8},{7,9},{8,6},{9,7},... | collective-permute-start | bytes 98312 | tf_op jit(solution)/shard_map/ppermute | solution.py:319
  24.4 1.9 %collective-permute-start.10 = (bf16[64,256]{1,0:T(8,128)(2,1)S(1)}, bf16[64,256]{1,0:T(8,128)(2,1)S(1)}, u32[]{:S(2)}, u32[]{:S(2)}) collective-permute-start(bf16[64,256]{1,0:T(8,128)(2,1)S(1)} %get-tuple-element.27), channel_id=1, source_target_pairs={{0,12},{1,13},{2,14},{3,15},{4,8},{5,9},{6,10},{7,11},{8,4},{9,5},... | collective-permute-start | bytes 98312 | tf_op jit(solution)/shard_map/ppermute | solution.py:319
  26.3 1.2 %collective-permute-start.11 = (bf16[64,256]{1,0:T(8,128)(2,1)S(1)}, bf16[64,256]{1,0:T(8,128)(2,1)S(1)}, u32[]{:S(2)}, u32[]{:S(2)}) collective-permute-start(bf16[64,256]{1,0:T(8,128)(2,1)S(1)} %get-tuple-element.28), channel_id=1, source_target_pairs={{0,10},{1,11},{2,8},{3,9},{4,14},{5,15},{6,12},{7,13},{8,2},{9,3},... | collective-permute-start | bytes 98312 | tf_op jit(solution)/shard_map/ppermute | solution.py:319
  27.5 2.8 %collective-permute-start.12 = (bf16[64,256]{1,0:T(8,128)(2,1)S(1)}, bf16[64,256]{1,0:T(8,128)(2,1)S(1)}, u32[]{:S(2)}, u32[]{:S(2)}) collective-permute-start(bf16[64,256]{1,0:T(8,128)(2,1)S(1)} %get-tuple-element.29), channel_id=1, source_target_pairs={{0,8},{1,9},{2,10},{3,11},{4,12},{5,13},{6,14},{7,15},{8,0},{9,1},... | collective-permute-start | bytes 98312 | tf_op jit(solution)/shard_map/ppermute | solution.py:319
  30.2 0.3 grid_third.1
  30.5 0.1 collective-permute-start.13
  30.6 0.0 collective-permute-done.9.refs_0_
  30.6 1.8 %collective-permute-start.14 = (bf16[64,256]{1,0:T(8,128)(2,1)S(1)}, bf16[64,256]{1,0:T(8,128)(2,1)S(1)}, u32[]{:S(2)}, u32[]{:S(2)}) collective-permute-start(bf16[64,256]{1,0:T(8,128)(2,1)S(1)} %get-tuple-element.33), channel_id=1, source_target_pairs={{0,4},{1,5},{2,6},{3,7},{4,0},{5,1},{6,2},{7,3},{8,12},{9,13},{10,... | collective-permute-start | bytes 98312 | tf_op jit(solution)/shard_map/ppermute | solution.py:319
  32.5 0.0 collective-permute-done.10.refs_1_
  32.5 1.6 %collective-permute-start.15 = (bf16[64,256]{1,0:T(8,128)(2,1)S(1)}, bf16[64,256]{1,0:T(8,128)(2,1)S(1)}, u32[]{:S(2)}, u32[]{:S(2)}) collective-permute-start(bf16[64,256]{1,0:T(8,128)(2,1)S(1)} %get-tuple-element.34), channel_id=1, source_target_pairs={{0,2},{1,3},{2,0},{3,1},{4,6},{5,7},{6,4},{7,5},{8,10},{9,11},{10,... | collective-permute-start | bytes 98312 | tf_op jit(solution)/shard_map/ppermute | solution.py:319
  34.1 0.0 collective-permute-done.11.refs_2_
  34.1 0.0 collective-permute-done.12.refs_3_
  34.1 1.3 %collective-permute-done.13.refs_4_ = bf16[64,256]{1,0:T(8,128)(2,1)S(1)} collective-permute-done((bf16[64,256]{1,0:T(8,128)(2,1)S(1)}, bf16[64,256]{1,0:T(8,128)(2,1)S(1)}, u32[]{:S(2)}, u32[]{:S(2)}) %collective-permute-start.13) | collective-permute-done | bytes 32800 | tf_op jit(solution)/shard_map/ppermute | solution.py:319
  35.4 0.0 collective-permute-done.14.refs_5_
  35.4 1.0 %collective-permute-done.15.refs_6_ = bf16[64,256]{1,0:T(8,128)(2,1)S(1)} collective-permute-done((bf16[64,256]{1,0:T(8,128)(2,1)S(1)}, bf16[64,256]{1,0:T(8,128)(2,1)S(1)}, u32[]{:S(2)}, u32[]{:S(2)}) %collective-permute-start.15) | collective-permute-done | bytes 32800 | tf_op jit(solution)/shard_map/ppermute | solution.py:319
  36.4 0.0 copy-done
  36.4 0.0 copy-done.1
  36.4 0.0 copy-done.2
  36.4 0.0 copy-done.3
  36.4 0.0 copy-done.4
  36.4 0.7 %grid_last.1 = (f32[64,256]{1,0:T(8,128)}, f32[1,256]{1,0:T(1,128)}) custom-call(bf16[64,256]{1,0:T(8,128)(2,1)S(1)} %collective-permute-done.9.refs_0_, bf16[64,256]{1,0:T(8,128)(2,1)S(1)} %collective-permute-done.10.refs_1_, bf16[64,256]{1,0:T(8,128)(2,1)S(1)} %collective-permute-done.11.refs_2_, bf16[64,256]{1,0:T(8,128)(2,1)S(1)} %collective-permute-done.12.refs_3_, ...), custom_call_target="tpu_custom_call" | custom-call | tf_op jit(solution)/shard_map/grid_last/pallas_call | solution.py:328
Async XLA Ops:
  2.2 10.7 %collective-permute-start.4 = (bf16[80,256]{1,0:T(8,128)(2,1)S(1)}, bf16[80,256]{1,0:T(8,128)(2,1)S(1)}, u32[]{:S(2)}, u32[]{:S(2)}) collective-permute-start(bf16[80,256]{1,0:T(8,128)(2,1)S(1)} %get-tuple-element.20.refs_0_.own_ref), channel_id=1, source_target_pairs={{0,8},{1,9},{2,10},{3,11},{4,12},{5,13},{6,14},{7,15},{8,0},{9,1},... | collective-permute-start | bytes 122888 | tf_op jit(solution)/shard_map/ppermute | solution.py:319
  6.3 6.6 %collective-permute-start.3 = (bf16[80,256]{1,0:T(8,128)(2,1)S(1)}, bf16[80,256]{1,0:T(8,128)(2,1)S(1)}, u32[]{:S(2)}, u32[]{:S(2)}) collective-permute-start(bf16[80,256]{1,0:T(8,128)(2,1)S(1)} %get-tuple-element.20.refs_0_.own_ref), channel_id=1, source_target_pairs={{0,10},{1,11},{2,8},{3,9},{4,14},{5,15},{6,12},{7,13},{8,2},{9,3},... | collective-permute-start | bytes 122888 | tf_op jit(solution)/shard_map/ppermute | solution.py:319
  7.5 3.6 %collective-permute-start = (f32[3,256]{1,0:T(4,128)}, f32[3,256]{1,0:T(4,128)S(1)}, u32[]{:S(2)}, u32[]{:S(2)}) collective-permute-start(f32[3,256]{1,0:T(4,128)} %refs_0_.1), channel_id=1, source_target_pairs={{0,1},{1,0},{2,3},{3,2},{4,5},{5,4},{6,7},{7,6},{8,9},{9,8},{10,11... | collective-permute-start | bytes 9224 | tf_op jit(solution)/shard_map/ppermute | solution.py:319
  7.5 7.5 %collective-permute-start.2 = (bf16[80,256]{1,0:T(8,128)(2,1)S(1)}, bf16[80,256]{1,0:T(8,128)(2,1)S(1)}, u32[]{:S(2)}, u32[]{:S(2)}) collective-permute-start(bf16[80,256]{1,0:T(8,128)(2,1)S(1)} %get-tuple-element.20.refs_0_.own_ref), channel_id=1, source_target_pairs={{0,12},{1,13},{2,14},{3,15},{4,8},{5,9},{6,10},{7,11},{8,4},{9,5},... | collective-permute-start | bytes 122888 | tf_op jit(solution)/shard_map/ppermute | solution.py:319
  11.2 6.8 %collective-permute-start.1 = (bf16[80,256]{1,0:T(8,128)(2,1)S(1)}, bf16[80,256]{1,0:T(8,128)(2,1)S(1)}, u32[]{:S(2)}, u32[]{:S(2)}) collective-permute-start(bf16[80,256]{1,0:T(8,128)(2,1)S(1)} %get-tuple-element.20.refs_0_.own_ref), channel_id=1, source_target_pairs={{0,14},{1,15},{2,12},{3,13},{4,10},{5,11},{6,8},{7,9},{8,6},{9,7},... | collective-permute-start | bytes 122888 | tf_op jit(solution)/shard_map/ppermute | solution.py:319
  11.2 8.8 %collective-permute-start.7 = (bf16[80,256]{1,0:T(8,128)(2,1)S(1)}, bf16[80,256]{1,0:T(8,128)(2,1)S(1)}, u32[]{:S(2)}, u32[]{:S(2)}) collective-permute-start(bf16[80,256]{1,0:T(8,128)(2,1)S(1)} %get-tuple-element.20.refs_0_.own_ref), channel_id=1, source_target_pairs={{0,2},{1,3},{2,0},{3,1},{4,6},{5,7},{6,4},{7,5},{8,10},{9,11},{10,... | collective-permute-start | bytes 122888 | tf_op jit(solution)/shard_map/ppermute | solution.py:319
  12.8 7.1 %collective-permute-start.6 = (bf16[80,256]{1,0:T(8,128)(2,1)S(1)}, bf16[80,256]{1,0:T(8,128)(2,1)S(1)}, u32[]{:S(2)}, u32[]{:S(2)}) collective-permute-start(bf16[80,256]{1,0:T(8,128)(2,1)S(1)} %get-tuple-element.20.refs_0_.own_ref), channel_id=1, source_target_pairs={{0,4},{1,5},{2,6},{3,7},{4,0},{5,1},{6,2},{7,3},{8,12},{9,13},{10,... | collective-permute-start | bytes 122888 | tf_op jit(solution)/shard_map/ppermute | solution.py:319
  12.9 7.1 %collective-permute-start.5 = (bf16[80,256]{1,0:T(8,128)(2,1)S(1)}, bf16[80,256]{1,0:T(8,128)(2,1)S(1)}, u32[]{:S(2)}, u32[]{:S(2)}) collective-permute-start(bf16[80,256]{1,0:T(8,128)(2,1)S(1)} %get-tuple-element.20.refs_0_.own_ref), channel_id=1, source_target_pairs={{0,6},{1,7},{2,4},{3,5},{4,2},{5,3},{6,0},{7,1},{8,14},{9,15},{10,... | collective-permute-start | bytes 122888 | tf_op jit(solution)/shard_map/ppermute | solution.py:319
  20.8 1.3 %collective-permute-start.8 = (bf16[144,256]{1,0:T(8,128)(2,1)S(1)}, bf16[144,256]{1,0:T(8,128)(2,1)S(1)}, u32[]{:S(2)}, u32[]{:S(2)}) collective-permute-start(bf16[144,256]{1,0:T(8,128)(2,1)S(1)} %get-tuple-element.25), channel_id=1, source_target_pairs={{0,1},{1,0},{2,3},{3,2},{4,5},{5,4},{6,7},{7,6},{8,9},{9,8},{10,11... | collective-permute-start | bytes 221192 | tf_op jit(solution)/shard_map/ppermute | solution.py:319
  22.5 13.9 %copy-start = (f32[64,256]{1,0:T(8,128)S(1)}, f32[64,256]{1,0:T(8,128)}, u32[]{:S(2)}) copy-start(f32[64,256]{1,0:T(8,128)} %refs_8_.1) | copy-start | bytes 196612
  22.5 13.9 %copy-start.1 = (bf16[64,256]{1,0:T(8,128)(2,1)S(1)}, bf16[64,256]{1,0:T(8,128)(2,1)}, u32[]{:S(2)}) copy-start(bf16[64,256]{1,0:T(8,128)(2,1)} %refs_11_.1) | copy-start | bytes 98308
  22.5 13.9 %copy-start.2 = (bf16[64,256]{1,0:T(8,128)(2,1)S(1)}, bf16[64,256]{1,0:T(8,128)(2,1)}, u32[]{:S(2)}) copy-start(bf16[64,256]{1,0:T(8,128)(2,1)} %refs_12_.1) | copy-start | bytes 98308
  22.5 13.9 %copy-start.3 = (f32[256]{0:T(256)S(1)}, f32[256]{0:T(256)}, u32[]{:S(2)}) copy-start(f32[256]{0:T(256)} %param.11) | copy-start | bytes 3076
  22.5 13.9 %copy-start.4 = (f32[256]{0:T(256)S(1)}, f32[256]{0:T(256)}, u32[]{:S(2)}) copy-start(f32[256]{0:T(256)} %param.10) | copy-start | bytes 3076
  22.5 8.1 %collective-permute-start.9 = (bf16[64,256]{1,0:T(8,128)(2,1)S(1)}, bf16[64,256]{1,0:T(8,128)(2,1)S(1)}, u32[]{:S(2)}, u32[]{:S(2)}) collective-permute-start(bf16[64,256]{1,0:T(8,128)(2,1)S(1)} %get-tuple-element.26), channel_id=1, source_target_pairs={{0,14},{1,15},{2,12},{3,13},{4,10},{5,11},{6,8},{7,9},{8,6},{9,7},... | collective-permute-start | bytes 98312 | tf_op jit(solution)/shard_map/ppermute | solution.py:319
  24.4 8.1 %collective-permute-start.10 = (bf16[64,256]{1,0:T(8,128)(2,1)S(1)}, bf16[64,256]{1,0:T(8,128)(2,1)S(1)}, u32[]{:S(2)}, u32[]{:S(2)}) collective-permute-start(bf16[64,256]{1,0:T(8,128)(2,1)S(1)} %get-tuple-element.27), channel_id=1, source_target_pairs={{0,12},{1,13},{2,14},{3,15},{4,8},{5,9},{6,10},{7,11},{8,4},{9,5},... | collective-permute-start | bytes 98312 | tf_op jit(solution)/shard_map/ppermute | solution.py:319
  26.3 7.9 %collective-permute-start.11 = (bf16[64,256]{1,0:T(8,128)(2,1)S(1)}, bf16[64,256]{1,0:T(8,128)(2,1)S(1)}, u32[]{:S(2)}, u32[]{:S(2)}) collective-permute-start(bf16[64,256]{1,0:T(8,128)(2,1)S(1)} %get-tuple-element.28), channel_id=1, source_target_pairs={{0,10},{1,11},{2,8},{3,9},{4,14},{5,15},{6,12},{7,13},{8,2},{9,3},... | collective-permute-start | bytes 98312 | tf_op jit(solution)/shard_map/ppermute | solution.py:319
  27.5 6.7 %collective-permute-start.12 = (bf16[64,256]{1,0:T(8,128)(2,1)S(1)}, bf16[64,256]{1,0:T(8,128)(2,1)S(1)}, u32[]{:S(2)}, u32[]{:S(2)}) collective-permute-start(bf16[64,256]{1,0:T(8,128)(2,1)S(1)} %get-tuple-element.29), channel_id=1, source_target_pairs={{0,8},{1,9},{2,10},{3,11},{4,12},{5,13},{6,14},{7,15},{8,0},{9,1},... | collective-permute-start | bytes 98312 | tf_op jit(solution)/shard_map/ppermute | solution.py:319
  30.5 4.9 %collective-permute-start.13 = (bf16[64,256]{1,0:T(8,128)(2,1)S(1)}, bf16[64,256]{1,0:T(8,128)(2,1)S(1)}, u32[]{:S(2)}, u32[]{:S(2)}) collective-permute-start(bf16[64,256]{1,0:T(8,128)(2,1)S(1)} %get-tuple-element.32), channel_id=1, source_target_pairs={{0,6},{1,7},{2,4},{3,5},{4,2},{5,3},{6,0},{7,1},{8,14},{9,15},{10,... | collective-permute-start | bytes 98312 | tf_op jit(solution)/shard_map/ppermute | solution.py:319
  30.6 4.8 %collective-permute-start.14 = (bf16[64,256]{1,0:T(8,128)(2,1)S(1)}, bf16[64,256]{1,0:T(8,128)(2,1)S(1)}, u32[]{:S(2)}, u32[]{:S(2)}) collective-permute-start(bf16[64,256]{1,0:T(8,128)(2,1)S(1)} %get-tuple-element.33), channel_id=1, source_target_pairs={{0,4},{1,5},{2,6},{3,7},{4,0},{5,1},{6,2},{7,3},{8,12},{9,13},{10,... | collective-permute-start | bytes 98312 | tf_op jit(solution)/shard_map/ppermute | solution.py:319
  32.5 3.9 %collective-permute-start.15 = (bf16[64,256]{1,0:T(8,128)(2,1)S(1)}, bf16[64,256]{1,0:T(8,128)(2,1)S(1)}, u32[]{:S(2)}, u32[]{:S(2)}) collective-permute-start(bf16[64,256]{1,0:T(8,128)(2,1)S(1)} %get-tuple-element.34), channel_id=1, source_target_pairs={{0,2},{1,3},{2,0},{3,1},{4,6},{5,7},{6,4},{7,5},{8,10},{9,11},{10,... | collective-permute-start | bytes 98312 | tf_op jit(solution)/shard_map/ppermute | solution.py:319

commit v9 on v7

--- a/solution.py
+++ b/solution.py
@@ -57,10 +57,10 @@
         pltpu.make_async_copy(argument, ref, sems.at[at])
         for at, (argument, ref) in enumerate(zip(arguments, held))
     ]
-    for copy in copies:
+    for copy in copies[::-1]:
         copy.start()
     rows[...] = jnp.zeros_like(rows)
-    for copy in copies:
+    for copy in copies[:-1]:
         copy.wait()
     pos_ref, words_ref, area_ref, reflectance_ref, seed_ref = held
     rhs_count = seed_ref.shape[0]
@@ -75,8 +75,9 @@
         for local in range(words_ref.shape[0]):
             start = local * TILE
             rows[12 + place : 13 + place, start : start + count] = part[local : local + 1]
+    packed_ref[rhs_count:] = rows[...].astype(jnp.bfloat16)
+    copies[-1].wait()
     packed_ref[:rhs_count] = (reflectance_ref[...] * seed_ref[...]).astype(jnp.bfloat16)
-    packed_ref[rhs_count:] = rows[...].astype(jnp.bfloat16)
     spot_ref[...] = pos_ref[...]
 
 
@@ -297,8 +298,9 @@
     return times(scaled_ref[0], kernel_ref[v]) + times(scaled_ref[1], kernel_ref[LINE + v])
 
 
-def grid_second(rest_ref, partial_ref, packed_ref, far_ref, scaled_ref, sent_ref):
+def grid_second(me_ref, rest_ref, partial_ref, packed_ref, both_ref, scaled_ref, sent_ref):
     rhs_count = partial_ref.shape[1]
+    far_ref = both_ref.at[1 - me_ref[0] // FAR % 2]
     extras = (packed_ref[0, rhs_count:], far_ref[2 * rhs_count :, :])
     for t in range(2):
         terms = extras[t].astype(jnp.float32)
@@ -410,11 +412,13 @@
         scratch,
     )
     four = (LINE,) + field
+    pairs = [[at, at + FAR] for at in range(devices) if at // FAR % 2 == 0]
+    both = lax.all_gather(sent, "row", axis_index_groups=pairs)
     scaled, sent = call(
         grid_second,
         "grid_second",
-        (rest, partial, packed, send(sent, FAR)),
-        [vmem] * 4,
+        (my_index, rest, partial, packed, both),
+        [smem] + [vmem] * 4,
         [shaped((2,) + field, jnp.bfloat16), shaped(four, jnp.bfloat16)],
     )
     other = send(sent, 1)

time: 29.5 us -> 30.1 us (1.020)
  blocking collectives: 0 us -> 5.34 us
  waiting for transfers between devices: 10.3 us -> 7.15 us
  starting transfers between devices: 13.5 us -> 12 us
    all_gather x0 -> x1, blocking collectives: none -> 5.34 us  [on_grid(): both = lax.all_gather(sent, 'row', axis_index_groups=pairs)]
    ppermute x10 -> x9, waiting for transfers between devices: 10.3 us -> 7.15 us  [send(): lax.ppermute(value, 'row', [(at, at ^ step) for at in range(devices)])]
    ppermute x10 -> x9, starting transfers between devices: 13.5 us -> 12 us  [send(): lax.ppermute(value, 'row', [(at, at ^ step) for at in range(devices)])]
  transfers between devices with their start and end apart: 10 -> 9, of which waited for: 6 -> 5; matrix products, arithmetic and copies ran while one was open for 0% -> 0% of each run, Pallas kernels for 6% -> 6%
where the time goes in v9:
time: 30.1 us; the launch traced here: 29.9 us
  starting transfers between devices  12 us (40%)
  waiting for transfers between devices  7.15 us (24%)
  blocking collectives  5.34 us (18%)
  Pallas kernels  4.6 us (15%)
  between operations  0.76 us (3%)
    ppermute x9, starting transfers between devices, send(): lax.ppermute(value, 'row', [(at, at ^ step) for at in range(devices)])  12 us
    ppermute x9, waiting for transfers between devices, send(): lax.ppermute(value, 'row', [(at, at ^ step) for at in range(devices)])  7.15 us
    all_gather x1, blocking collectives, on_grid(): both = lax.all_gather(sent, 'row', axis_index_groups=pairs)  5.34 us
    pallas_call x8, Pallas kernels, call(): pl.pallas_call(body, in_specs=in_specs, out_specs=[vmem] * len(out_shape)...  4.6 us
  transfers between devices with their start and end apart: 9, of which 5 were waited for; matrix products, arithmetic and copies ran while one was open for 0% of the time, Pallas kernels for 6%

profile of v9, /device:TPU:0, one launch (start us, length us, event | category | flops | bytes accessed | tf_op | source)
XLA Modules:
  0.0 29.9 jit_solution(1494910392611658591)
XLA Ops:
  0.6 0.9 %prepare.1 = (bf16[80,256]{1,0:T(8,128)(2,1)S(1)}, f32[3,256]{1,0:T(4,128)S(1)}) custom-call(f32[3,256]{1,0:T(4,128)} %refs_0_.1, s32[2,32]{1,0:T(2,128)} %refs_1_.1, f32[1,256]{1,0:T(1,128)} %bitcast.6, f32[1,256]{1,0:T(1,128)} %bitcast.9, f32[64,256]{1,0:T(8,128)} %rest_0_.1), custom_call_target="tpu_custom_call" | custom-call | tf_op jit(solution)/shard_map/prepare/pallas_call | solution.py:355
  1.5 5.1 %collective-permute-start.3 = (bf16[80,256]{1,0:T(8,128)(2,1)S(1)}, bf16[80,256]{1,0:T(8,128)(2,1)S(1)}, u32[]{:S(2)}, u32[]{:S(2)}) collective-permute-start(bf16[80,256]{1,0:T(8,128)(2,1)S(1)} %get-tuple-element.22.v0_ref), channel_id=1, source_target_pairs={{0,12},{1,13},{2,14},{3,15},{4,8},{5,9},{6,10},{7,11},{8,4},{9,5},... | collective-permute-start | bytes 122888 | tf_op jit(solution)/shard_map/ppermute | solution.py:346
  6.6 0.0 collective-permute-start.2
  6.6 0.6 %collective-permute-start.1 = (bf16[80,256]{1,0:T(8,128)(2,1)S(1)}, bf16[80,256]{1,0:T(8,128)(2,1)S(1)}, u32[]{:S(2)}, u32[]{:S(2)}) collective-permute-start(bf16[80,256]{1,0:T(8,128)(2,1)S(1)} %get-tuple-element.22.v0_ref), channel_id=1, source_target_pairs={{0,4},{1,5},{2,6},{3,7},{4,0},{5,1},{6,2},{7,3},{8,12},{9,13},{10,... | collective-permute-start | bytes 122888 | tf_op jit(solution)/shard_map/ppermute | solution.py:346
  7.3 1.6 %collective-permute-start = (f32[3,256]{1,0:T(4,128)S(1)}, f32[3,256]{1,0:T(4,128)S(1)}, u32[]{:S(2)}, u32[]{:S(2)}) collective-permute-start(f32[3,256]{1,0:T(4,128)S(1)} %get-tuple-element.21), channel_id=1, source_target_pairs={{0,2},{1,3},{2,0},{3,1},{4,6},{5,7},{6,4},{7,5},{8,10},{9,11},{10,... | collective-permute-start | bytes 9224 | tf_op jit(solution)/shard_map/ppermute | solution.py:346
  8.9 2.0 %collective-permute-done.far_ref = f32[3,256]{1,0:T(4,128)S(1)} collective-permute-done((f32[3,256]{1,0:T(4,128)S(1)}, f32[3,256]{1,0:T(4,128)S(1)}, u32[]{:S(2)}, u32[]{:S(2)}) %collective-permute-start) | collective-permute-done | bytes 3104 | tf_op jit(solution)/shard_map/ppermute | solution.py:346
  10.9 0.0 collective-permute-done.3.v3_ref
  10.9 0.6 %collective-permute-done.2.v2_ref = bf16[80,256]{1,0:T(8,128)(2,1)S(1)} collective-permute-done((bf16[80,256]{1,0:T(8,128)(2,1)S(1)}, bf16[80,256]{1,0:T(8,128)(2,1)S(1)}, u32[]{:S(2)}, u32[]{:S(2)}) %collective-permute-start.2) | collective-permute-done | bytes 40992 | tf_op jit(solution)/shard_map/ppermute | solution.py:346
  11.5 0.0 collective-permute-done.1.v1_ref
  11.6 0.1 collective-permute-start.4
  11.6 1.4 %grid_near.1 = (bf16[8,256,256]{2,1,0:T(8,128)(2,1)S(1)}, f32[2,64,256]{2,1,0:T(8,128)S(1)}, bf16[2,256,32]{2,1,0:T(8,128)(2,1)S(1)}) custom-call(s32[1]{0:T(128)} %bitcast.me_ref, bf16[4,80,256]{2,1,0:T(8,128)(2,1)S(1)} %grid_pack.1.packed_ref, f32[3,256]{1,0:T(4,128)S(1)} %collective-permute-done.far_ref, f32[64,256]{1,0:T(8,128)} %rest_0_.1, f32[1,256]{1,0:T(1,128)} %bitcast.7), custom_call_target="tpu_custom_call" | custom-call | tf_op jit(solution)/shard_map/grid_near/pallas_call | solution.py:355
  13.1 0.0 collective-permute-done.4.core_ref
  13.1 1.0 %grid_rest.1 = (bf16[8,256,256]{2,1,0:T(8,128)(2,1)S(1)}, f32[2,64,256]{2,1,0:T(8,128)S(1)}, bf16[144,256]{1,0:T(8,128)(2,1)S(1)}) custom-call(s32[1]{0:T(128)} %bitcast.me_ref, bf16[4,80,256]{2,1,0:T(8,128)(2,1)S(1)} %grid_pack.1.packed_ref, bf16[4,80,256]{2,1,0:T(8,128)(2,1)S(1)} %collective-permute-done.4.core_ref, ...), custom_call_target="tpu_custom_call" | custom-call | tf_op jit(solution)/shard_map/grid_rest/pallas_call | solution.py:355
  14.1 5.3 %all-gather = bf16[288,256]{1,0:T(8,128)(2,1)S(1)} all-gather(bf16[144,256]{1,0:T(8,128)(2,1)S(1)} %get-tuple-element.29), channel_id=2, replica_groups={{0,2},{1,3},{4,6},{5,7},{8,10},{9,11},{12,14},{13,15},{16,18},{17,19},{..., dimensions={0}, use_global_device_ids=true | all-gather | bytes 221184 | tf_op jit(solution)/shard_map/all_gather | solution.py:416
  19.4 0.3 %grid_second.1 = (bf16[2,64,256]{2,1,0:T(8,128)(2,1)S(1)}, bf16[4,64,256]{2,1,0:T(8,128)(2,1)S(1)}) custom-call(s32[1]{0:T(128)} %bitcast.me_ref, bf16[8,256,256]{2,1,0:T(8,128)(2,1)S(1)} %get-tuple-element.27.rest_ref, f32[2,64,256]{2,1,0:T(8,128)S(1)} %get-tuple-element.28.partial_ref, bf16[4,80,256]{2,1,0:T(8,128)(2,1)S(1)} %grid_pack.1.packed_ref, ...), custom_call_target="tpu_custom_call" | custom-call | tf_op jit(solution)/shard_map/grid_second/pallas_call | solution.py:355
  19.7 0.1 collective-permute-start.5
  19.8 0.3 grid_third.1.sum_ref
  20.1 0.0 copy-start
  20.1 0.0 copy-start.1
  20.1 0.0 copy-start.2
  20.1 1.0 %collective-permute-done.5.core_ref = bf16[4,64,256]{2,1,0:T(8,128)(2,1)S(1)} collective-permute-done((bf16[4,64,256]{2,1,0:T(8,128)(2,1)S(1)}, bf16[4,64,256]{2,1,0:T(8,128)(2,1)S(1)}, u32[]{:S(2)}, u32[]{:S(2)}) %collective-permute-start.5) | collective-permute-done | bytes 131104 | tf_op jit(solution)/shard_map/ppermute | solution.py:346
  21.2 3.2 %collective-permute-start.6 = (bf16[64,256]{1,0:T(8,128)(2,1)S(1)}, bf16[64,256]{1,0:T(8,128)(2,1)S(1)}, u32[]{:S(2)}, u32[]{:S(2)}) collective-permute-start(bf16[64,256]{1,0:T(8,128)(2,1)S(1)} %get-tuple-element.32), channel_id=1, source_target_pairs={{0,12},{1,13},{2,14},{3,15},{4,8},{5,9},{6,10},{7,11},{8,4},{9,5},... | collective-permute-start | bytes 98312 | tf_op jit(solution)/shard_map/ppermute | solution.py:346
  24.3 0.0 collective-permute-start.7
  24.3 0.0 copy-start.4
  24.3 0.0 copy-start.3
  24.4 1.3 %collective-permute-start.8 = (bf16[64,256]{1,0:T(8,128)(2,1)S(1)}, bf16[64,256]{1,0:T(8,128)(2,1)S(1)}, u32[]{:S(2)}, u32[]{:S(2)}) collective-permute-start(bf16[64,256]{1,0:T(8,128)(2,1)S(1)} %get-tuple-element.34), channel_id=1, source_target_pairs={{0,4},{1,5},{2,6},{3,7},{4,0},{5,1},{6,2},{7,3},{8,12},{9,13},{10,... | collective-permute-start | bytes 98312 | tf_op jit(solution)/shard_map/ppermute | solution.py:346
  25.6 1.6 %collective-permute-done.6.q3_ref = bf16[64,256]{1,0:T(8,128)(2,1)S(1)} collective-permute-done((bf16[64,256]{1,0:T(8,128)(2,1)S(1)}, bf16[64,256]{1,0:T(8,128)(2,1)S(1)}, u32[]{:S(2)}, u32[]{:S(2)}) %collective-permute-start.6) | collective-permute-done | bytes 32800 | tf_op jit(solution)/shard_map/ppermute | solution.py:346
  27.3 1.9 %collective-permute-done.7.q2_ref = bf16[64,256]{1,0:T(8,128)(2,1)S(1)} collective-permute-done((bf16[64,256]{1,0:T(8,128)(2,1)S(1)}, bf16[64,256]{1,0:T(8,128)(2,1)S(1)}, u32[]{:S(2)}, u32[]{:S(2)}) %collective-permute-start.7) | collective-permute-done | bytes 32800 | tf_op jit(solution)/shard_map/ppermute | solution.py:346
  29.2 0.0 collective-permute-done.8.q1_ref
  29.2 0.0 copy-done
  29.2 0.0 copy-done.1
  29.2 0.0 copy-done.2
  29.2 0.0 copy-done.4
  29.2 0.0 copy-done.3
  29.2 0.7 %grid_last.1 = (f32[64,256]{1,0:T(8,128)}, f32[1,256]{1,0:T(1,128)}) custom-call(bf16[64,256]{1,0:T(8,128)(2,1)S(1)} %collective-permute-done.6.q3_ref, bf16[64,256]{1,0:T(8,128)(2,1)S(1)} %collective-permute-done.7.q2_ref, bf16[64,256]{1,0:T(8,128)(2,1)S(1)} %collective-permute-done.8.q1_ref, f32[64,256]{1,0:T(8,128)S(1)} %get-tuple-element.35.q0_ref, ...), custom_call_target="tpu_custom_call" | custom-call | tf_op jit(solution)/shard_map/grid_last/pallas_call | solution.py:355
  (2 shorter events, 0.0 us)
Async XLA Ops:
  1.5 9.4 %collective-permute-start.3 = (bf16[80,256]{1,0:T(8,128)(2,1)S(1)}, bf16[80,256]{1,0:T(8,128)(2,1)S(1)}, u32[]{:S(2)}, u32[]{:S(2)}) collective-permute-start(bf16[80,256]{1,0:T(8,128)(2,1)S(1)} %get-tuple-element.22.v0_ref), channel_id=1, source_target_pairs={{0,12},{1,13},{2,14},{3,15},{4,8},{5,9},{6,10},{7,11},{8,4},{9,5},... | collective-permute-start | bytes 122888 | tf_op jit(solution)/shard_map/ppermute | solution.py:346
  6.6 4.9 %collective-permute-start.2 = (bf16[80,256]{1,0:T(8,128)(2,1)S(1)}, bf16[80,256]{1,0:T(8,128)(2,1)S(1)}, u32[]{:S(2)}, u32[]{:S(2)}) collective-permute-start(bf16[80,256]{1,0:T(8,128)(2,1)S(1)} %get-tuple-element.22.v0_ref), channel_id=1, source_target_pairs={{0,8},{1,9},{2,10},{3,11},{4,12},{5,13},{6,14},{7,15},{8,0},{9,1},... | collective-permute-start | bytes 122888 | tf_op jit(solution)/shard_map/ppermute | solution.py:346
  6.6 4.9 %collective-permute-start.1 = (bf16[80,256]{1,0:T(8,128)(2,1)S(1)}, bf16[80,256]{1,0:T(8,128)(2,1)S(1)}, u32[]{:S(2)}, u32[]{:S(2)}) collective-permute-start(bf16[80,256]{1,0:T(8,128)(2,1)S(1)} %get-tuple-element.22.v0_ref), channel_id=1, source_target_pairs={{0,4},{1,5},{2,6},{3,7},{4,0},{5,1},{6,2},{7,3},{8,12},{9,13},{10,... | collective-permute-start | bytes 122888 | tf_op jit(solution)/shard_map/ppermute | solution.py:346
  7.3 3.6 %collective-permute-start = (f32[3,256]{1,0:T(4,128)S(1)}, f32[3,256]{1,0:T(4,128)S(1)}, u32[]{:S(2)}, u32[]{:S(2)}) collective-permute-start(f32[3,256]{1,0:T(4,128)S(1)} %get-tuple-element.21), channel_id=1, source_target_pairs={{0,2},{1,3},{2,0},{3,1},{4,6},{5,7},{6,4},{7,5},{8,10},{9,11},{10,... | collective-permute-start | bytes 9224 | tf_op jit(solution)/shard_map/ppermute | solution.py:346
  11.6 1.5 %collective-permute-start.4 = (bf16[4,80,256]{2,1,0:T(8,128)(2,1)S(1)}, bf16[4,80,256]{2,1,0:T(8,128)(2,1)S(1)}, u32[]{:S(2)}, u32[]{:S(2)}) collective-permute-start(bf16[4,80,256]{2,1,0:T(8,128)(2,1)S(1)} %grid_pack.1.packed_ref), channel_id=1, source_target_pairs={{0,1},{1,0},{2,3},{3,2},{4,5},{5,4},{6,7},{7,6},{8,9},{9,8},{10,11... | collective-permute-start | bytes 491528 | tf_op jit(solution)/shard_map/ppermute | solution.py:346
  19.7 1.4 %collective-permute-start.5 = (bf16[4,64,256]{2,1,0:T(8,128)(2,1)S(1)}, bf16[4,64,256]{2,1,0:T(8,128)(2,1)S(1)}, u32[]{:S(2)}, u32[]{:S(2)}) collective-permute-start(bf16[4,64,256]{2,1,0:T(8,128)(2,1)S(1)} %get-tuple-element.31), channel_id=1, source_target_pairs={{0,1},{1,0},{2,3},{3,2},{4,5},{5,4},{6,7},{7,6},{8,9},{9,8},{10,11... | collective-permute-start | bytes 393224 | tf_op jit(solution)/shard_map/ppermute | solution.py:346
  20.1 9.1 %copy-start = (f32[64,256]{1,0:T(8,128)S(1)}, f32[64,256]{1,0:T(8,128)}, u32[]{:S(2)}) copy-start(f32[64,256]{1,0:T(8,128)} %rest_0_.1) | copy-start | bytes 196612
  20.1 9.0 %copy-start.1 = (bf16[64,256]{1,0:T(8,128)(2,1)S(1)}, bf16[64,256]{1,0:T(8,128)(2,1)}, u32[]{:S(2)}) copy-start(bf16[64,256]{1,0:T(8,128)(2,1)} %rest_3_.1) | copy-start | bytes 98308
  20.1 9.0 %copy-start.2 = (bf16[64,256]{1,0:T(8,128)(2,1)S(1)}, bf16[64,256]{1,0:T(8,128)(2,1)}, u32[]{:S(2)}) copy-start(bf16[64,256]{1,0:T(8,128)(2,1)} %rest_4_.1) | copy-start | bytes 98308
  21.2 6.1 %collective-permute-start.6 = (bf16[64,256]{1,0:T(8,128)(2,1)S(1)}, bf16[64,256]{1,0:T(8,128)(2,1)S(1)}, u32[]{:S(2)}, u32[]{:S(2)}) collective-permute-start(bf16[64,256]{1,0:T(8,128)(2,1)S(1)} %get-tuple-element.32), channel_id=1, source_target_pairs={{0,12},{1,13},{2,14},{3,15},{4,8},{5,9},{6,10},{7,11},{8,4},{9,5},... | collective-permute-start | bytes 98312 | tf_op jit(solution)/shard_map/ppermute | solution.py:346
  24.3 4.8 %collective-permute-start.7 = (bf16[64,256]{1,0:T(8,128)(2,1)S(1)}, bf16[64,256]{1,0:T(8,128)(2,1)S(1)}, u32[]{:S(2)}, u32[]{:S(2)}) collective-permute-start(bf16[64,256]{1,0:T(8,128)(2,1)S(1)} %get-tuple-element.33), channel_id=1, source_target_pairs={{0,8},{1,9},{2,10},{3,11},{4,12},{5,13},{6,14},{7,15},{8,0},{9,1},... | collective-permute-start | bytes 98312 | tf_op jit(solution)/shard_map/ppermute | solution.py:346
  24.3 4.8 %copy-start.4 = (f32[256]{0:T(256)S(1)}, f32[256]{0:T(256)}, u32[]{:S(2)}) copy-start(f32[256]{0:T(256)} %param.10) | copy-start | bytes 3076
  24.3 4.8 %copy-start.3 = (f32[256]{0:T(256)S(1)}, f32[256]{0:T(256)}, u32[]{:S(2)}) copy-start(f32[256]{0:T(256)} %param.11) | copy-start | bytes 3076
  24.4 4.8 %collective-permute-start.8 = (bf16[64,256]{1,0:T(8,128)(2,1)S(1)}, bf16[64,256]{1,0:T(8,128)(2,1)S(1)}, u32[]{:S(2)}, u32[]{:S(2)}) collective-permute-start(bf16[64,256]{1,0:T(8,128)(2,1)S(1)} %get-tuple-element.34), channel_id=1, source_target_pairs={{0,4},{1,5},{2,6},{3,7},{4,0},{5,1},{6,2},{7,3},{8,12},{9,13},{10,... | collective-permute-start | bytes 98312 | tf_op jit(solution)/shard_map/ppermute | solution.py:346

commit v10 on v7

--- a/solution.py
+++ b/solution.py
@@ -57,10 +57,10 @@
         pltpu.make_async_copy(argument, ref, sems.at[at])
         for at, (argument, ref) in enumerate(zip(arguments, held))
     ]
-    for copy in copies:
+    for copy in copies[::-1]:
         copy.start()
     rows[...] = jnp.zeros_like(rows)
-    for copy in copies:
+    for copy in copies[:-1]:
         copy.wait()
     pos_ref, words_ref, area_ref, reflectance_ref, seed_ref = held
     rhs_count = seed_ref.shape[0]
@@ -75,8 +75,9 @@
         for local in range(words_ref.shape[0]):
             start = local * TILE
             rows[12 + place : 13 + place, start : start + count] = part[local : local + 1]
+    packed_ref[rhs_count:] = rows[...].astype(jnp.bfloat16)
+    copies[-1].wait()
     packed_ref[:rhs_count] = (reflectance_ref[...] * seed_ref[...]).astype(jnp.bfloat16)
-    packed_ref[rhs_count:] = rows[...].astype(jnp.bfloat16)
     spot_ref[...] = pos_ref[...]
 
 
@@ -118,18 +119,18 @@
     shifts = [shift_up(direct, group, lane) for group in range(TILE // GROUP)]
     splats = block_words(word, row_chunk)
     for row_block in range(2):
+        values = distance(row_block)
         for col_block in range(2):
             lanes = slice(col_block * TILE, (col_block + 1) * TILE)
             for group, shift in enumerate(shifts):
-                first = row_block * TILE + group * GROUP
+                first = group * GROUP
                 seen = jnp.left_shift(splats[col_block][row_block], shift) < 0
                 halves = []
                 for half in range(first, first + GROUP, 8):
-                    value = pl.reciprocal(distance[half : half + 8, lanes], approx=True)
+                    value = pl.reciprocal(values[half : half + 8, lanes], approx=True)
                     halves.append(jnp.where(seen, value, 0.0))
-                out_ref[first : first + GROUP, lanes] = jnp.concatenate(halves).astype(
-                    jnp.bfloat16
-                )
+                rows = slice(row_block * TILE + first, row_block * TILE + first + GROUP)
+                out_ref[rows, lanes] = jnp.concatenate(halves).astype(jnp.bfloat16)
 
 
 def form_own(row_chunk, distance, word, out_ref):
@@ -137,21 +138,21 @@
     row = lax.broadcasted_iota(jnp.int32, (8, TILE), 0)
     splats = block_words(word, row_chunk)
     for row_block in range(2):
+        values = distance(row_block)
         for col_block in range(2):
             lanes = slice(col_block * TILE, (col_block + 1) * TILE)
             for group in range(TILE // GROUP):
-                first = row_block * TILE + group * GROUP
+                first = group * GROUP
                 halves = []
                 for half in range(first, first + GROUP, 8):
-                    i, j = row + half, lane + col_block * TILE
+                    i, j = row + half + row_block * TILE, lane + col_block * TILE
                     low, high = jnp.minimum(i, j) % TILE, jnp.maximum(i, j) % TILE
                     shift = 31 - (8 * (low // 32) + high // 16)
                     seen = jnp.left_shift(splats[col_block][row_block], shift) < 0
-                    value = pl.reciprocal(distance[half : half + 8, lanes], approx=True)
+                    value = pl.reciprocal(values[half : half + 8, lanes], approx=True)
                     halves.append(jnp.where(seen, value, 0.0))
-                out_ref[first : first + GROUP, lanes] = jnp.concatenate(halves).astype(
-                    jnp.bfloat16
-                )
+                rows = slice(row_block * TILE + first, row_block * TILE + first + GROUP)
+                out_ref[rows, lanes] = jnp.concatenate(halves).astype(jnp.bfloat16)
 
 
 def read_extra(rows):
@@ -163,13 +164,8 @@
     return extra[0:3] + extra[3:6] + extra[6:9], word
 
 
-def form_all(blocks, me, row_terms, col_terms, words, fields, start, refs, finish_row):
-    kernel_ref, distance = refs
+def form_all(blocks, me, row_terms, col_terms, words, fields, start, kernel_ref, finish_row):
     held = {}
-
-    def measure(place):
-        t, v, w = blocks[place]
-        distance[place % 2] = times(row_terms[t], col_terms[v])
 
     def add(place):
         t, v, w = blocks[place]
@@ -178,16 +174,20 @@
         if place + 1 == len(blocks) or blocks[place + 1][0] != t:
             finish_row(t, held[t])
 
-    measure(0)
     for place, (t, v, w) in enumerate(blocks):
-        if place + 1 < len(blocks):
-            measure(place + 1)
-        slot, out_ref = distance.at[place % 2], kernel_ref.at[place]
+
+        def distance(row_block):
+            rows = slice(row_block * TILE, (row_block + 1) * TILE)
+            return times(row_terms[t, rows, :], col_terms[v])
+
+        out_ref = kernel_ref.at[place]
         row_chunk = jnp.bitwise_xor(me, FAR * t)
         if t == 0 and v == 0 and w == 0:
-            form_own(row_chunk, slot, words[v], out_ref)
+            form_own(row_chunk, distance, words[v], out_ref)
         else:
-            form_block(row_chunk, jnp.bitwise_xor(me, STEP * v + w), slot, words[v], out_ref)
+            form_block(
+                row_chunk, jnp.bitwise_xor(me, STEP * v + w), distance, words[v], out_ref
+            )
         if place:
             add(place - 1)
     add(len(blocks) - 1)
@@ -220,7 +220,6 @@
     row_terms,
     terms,
     col_terms,
-    distance,
     seed_ref,
     area_ref,
     sems,
@@ -251,7 +250,7 @@
         words,
         lambda v: packed_ref[v, :rhs_count],
         lambda t: 0.0,
-        (kernel_ref, distance),
+        kernel_ref,
         finish_row,
     )
     for copy in copies:
@@ -270,7 +269,6 @@
     sent_ref,
     terms,
     col_terms,
-    distance,
 ):
     rhs_count = before_ref.shape[1]
     words = column_terms(lambda v: core_ref[v, rhs_count:], terms, col_terms)
@@ -287,7 +285,7 @@
         words,
         lambda v: core_ref[v, :rhs_count],
         lambda t: before_ref[t],
-        (kernel_ref, distance),
+        kernel_ref,
         finish_row,
     )
     sent_ref[2 * rhs_count :] = packed_ref[0, rhs_count:]
@@ -386,7 +384,6 @@
     scratch = [
         pltpu.VMEM((LINE + 2,) + terms, jnp.float32),
         pltpu.VMEM((LINE,) + terms, jnp.bfloat16),
-        pltpu.VMEM((2, own_width, own_width), jnp.float32),
     ]
     near, partial, row_terms = call(
         functools.partial(grid_near, scale),

time: 29.5 us -> 29.8 us (1.010)
  no operation moved by 1% of the time
where the time goes in v10:
time: 29.8 us; the launch traced here: 29.6 us
  starting transfers between devices  13.5 us (45%)
  waiting for transfers between devices  10.3 us (35%)
  Pallas kernels  4.92 us (17%)
  between operations  0.76 us (3%)
    ppermute x10, starting transfers between devices, send(): lax.ppermute(value, 'row', [(at, at ^ step) for at in range(devices)])  13.5 us
    ppermute x10, waiting for transfers between devices, send(): lax.ppermute(value, 'row', [(at, at ^ step) for at in range(devices)])  10.3 us
    pallas_call x8, Pallas kernels, call(): pl.pallas_call(body, in_specs=in_specs, out_specs=[vmem] * len(out_shape)...  4.92 us
  transfers between devices with their start and end apart: 10, of which 6 were waited for; matrix products, arithmetic and copies ran while one was open for 0% of the time, Pallas kernels for 6%

profile of v10, /device:TPU:0, one launch (start us, length us, event | category | flops | bytes accessed | tf_op | source)
XLA Modules:
  0.0 29.6 jit_solution(590681907798037124)
XLA Ops:
  0.6 0.9 %prepare.1 = (bf16[80,256]{1,0:T(8,128)(2,1)S(1)}, f32[3,256]{1,0:T(4,128)S(1)}) custom-call(f32[3,256]{1,0:T(4,128)} %refs_0_.1, s32[2,32]{1,0:T(2,128)} %refs_1_.1, f32[1,256]{1,0:T(1,128)} %bitcast.4, f32[1,256]{1,0:T(1,128)} %bitcast.7, f32[64,256]{1,0:T(8,128)} %rest_0_.1), custom_call_target="tpu_custom_call" | custom-call | tf_op jit(solution)/shard_map/prepare/pallas_call | solution.py:351
  1.5 5.1 %collective-permute-start.3 = (bf16[80,256]{1,0:T(8,128)(2,1)S(1)}, bf16[80,256]{1,0:T(8,128)(2,1)S(1)}, u32[]{:S(2)}, u32[]{:S(2)}) collective-permute-start(bf16[80,256]{1,0:T(8,128)(2,1)S(1)} %get-tuple-element.22.v0_ref), channel_id=1, source_target_pairs={{0,12},{1,13},{2,14},{3,15},{4,8},{5,9},{6,10},{7,11},{8,4},{9,5},... | collective-permute-start | bytes 122888 | tf_op jit(solution)/shard_map/ppermute | solution.py:342
  6.6 0.0 collective-permute-start.2
  6.6 0.6 %collective-permute-start.1 = (bf16[80,256]{1,0:T(8,128)(2,1)S(1)}, bf16[80,256]{1,0:T(8,128)(2,1)S(1)}, u32[]{:S(2)}, u32[]{:S(2)}) collective-permute-start(bf16[80,256]{1,0:T(8,128)(2,1)S(1)} %get-tuple-element.22.v0_ref), channel_id=1, source_target_pairs={{0,4},{1,5},{2,6},{3,7},{4,0},{5,1},{6,2},{7,3},{8,12},{9,13},{10,... | collective-permute-start | bytes 122888 | tf_op jit(solution)/shard_map/ppermute | solution.py:342
  7.3 1.6 %collective-permute-start = (f32[3,256]{1,0:T(4,128)S(1)}, f32[3,256]{1,0:T(4,128)S(1)}, u32[]{:S(2)}, u32[]{:S(2)}) collective-permute-start(f32[3,256]{1,0:T(4,128)S(1)} %get-tuple-element.21), channel_id=1, source_target_pairs={{0,2},{1,3},{2,0},{3,1},{4,6},{5,7},{6,4},{7,5},{8,10},{9,11},{10,... | collective-permute-start | bytes 9224 | tf_op jit(solution)/shard_map/ppermute | solution.py:342
  8.9 2.0 %collective-permute-done.far_ref = f32[3,256]{1,0:T(4,128)S(1)} collective-permute-done((f32[3,256]{1,0:T(4,128)S(1)}, f32[3,256]{1,0:T(4,128)S(1)}, u32[]{:S(2)}, u32[]{:S(2)}) %collective-permute-start) | collective-permute-done | bytes 3104 | tf_op jit(solution)/shard_map/ppermute | solution.py:342
  10.9 0.0 collective-permute-done.3.v3_ref
  10.9 0.6 %collective-permute-done.2.v2_ref = bf16[80,256]{1,0:T(8,128)(2,1)S(1)} collective-permute-done((bf16[80,256]{1,0:T(8,128)(2,1)S(1)}, bf16[80,256]{1,0:T(8,128)(2,1)S(1)}, u32[]{:S(2)}, u32[]{:S(2)}) %collective-permute-start.2) | collective-permute-done | bytes 40992 | tf_op jit(solution)/shard_map/ppermute | solution.py:342
  11.5 0.0 collective-permute-done.1.v1_ref
  11.6 0.1 collective-permute-start.4
  11.6 1.6 %grid_near.1 = (bf16[8,256,256]{2,1,0:T(8,128)(2,1)S(1)}, f32[2,64,256]{2,1,0:T(8,128)S(1)}, bf16[2,256,32]{2,1,0:T(8,128)(2,1)S(1)}) custom-call(s32[1]{0:T(128)} %bitcast.me_ref, bf16[4,80,256]{2,1,0:T(8,128)(2,1)S(1)} %grid_pack.1.packed_ref, f32[3,256]{1,0:T(4,128)S(1)} %collective-permute-done.far_ref, f32[64,256]{1,0:T(8,128)} %rest_0_.1, f32[1,256]{1,0:T(1,128)} %bitcast.5), custom_call_target="tpu_custom_call" | custom-call | tf_op jit(solution)/shard_map/grid_near/pallas_call | solution.py:351
  13.3 0.0 collective-permute-done.4.core_ref
  13.3 1.1 %grid_rest.1 = (bf16[8,256,256]{2,1,0:T(8,128)(2,1)S(1)}, f32[2,64,256]{2,1,0:T(8,128)S(1)}, bf16[144,256]{1,0:T(8,128)(2,1)S(1)}) custom-call(s32[1]{0:T(128)} %bitcast.me_ref, bf16[4,80,256]{2,1,0:T(8,128)(2,1)S(1)} %grid_pack.1.packed_ref, bf16[4,80,256]{2,1,0:T(8,128)(2,1)S(1)} %collective-permute-done.4.core_ref, ...), custom_call_target="tpu_custom_call" | custom-call | tf_op jit(solution)/shard_map/grid_rest/pallas_call | solution.py:351
  14.4 1.6 %collective-permute-start.5 = (bf16[144,256]{1,0:T(8,128)(2,1)S(1)}, bf16[144,256]{1,0:T(8,128)(2,1)S(1)}, u32[]{:S(2)}, u32[]{:S(2)}) collective-permute-start(bf16[144,256]{1,0:T(8,128)(2,1)S(1)} %get-tuple-element.29), channel_id=1, source_target_pairs={{0,2},{1,3},{2,0},{3,1},{4,6},{5,7},{6,4},{7,5},{8,10},{9,11},{10,... | collective-permute-start | bytes 221192 | tf_op jit(solution)/shard_map/ppermute | solution.py:342
  16.0 3.2 %collective-permute-done.5.far_ref = bf16[144,256]{1,0:T(8,128)(2,1)S(1)} collective-permute-done((bf16[144,256]{1,0:T(8,128)(2,1)S(1)}, bf16[144,256]{1,0:T(8,128)(2,1)S(1)}, u32[]{:S(2)}, u32[]{:S(2)}) %collective-permute-start.5) | collective-permute-done | bytes 73760 | tf_op jit(solution)/shard_map/ppermute | solution.py:342
  19.1 0.3 %grid_second.1 = (bf16[2,64,256]{2,1,0:T(8,128)(2,1)S(1)}, bf16[4,64,256]{2,1,0:T(8,128)(2,1)S(1)}) custom-call(bf16[8,256,256]{2,1,0:T(8,128)(2,1)S(1)} %get-tuple-element.27.rest_ref, f32[2,64,256]{2,1,0:T(8,128)S(1)} %get-tuple-element.28.partial_ref, bf16[4,80,256]{2,1,0:T(8,128)(2,1)S(1)} %grid_pack.1.packed_ref, ...), custom_call_target="tpu_custom_call" | custom-call | tf_op jit(solution)/shard_map/grid_second/pallas_call | solution.py:351
  19.4 0.1 collective-permute-start.6
  19.5 0.3 %grid_third.1.sum_ref = f32[4,64,256]{2,1,0:T(8,128)S(1)} custom-call(bf16[8,256,256]{2,1,0:T(8,128)(2,1)S(1)} %get-tuple-element.24.near_ref, bf16[2,64,256]{2,1,0:T(8,128)(2,1)S(1)} %get-tuple-element.30.scaled_ref), custom_call_target="tpu_custom_call" | custom-call | tf_op jit(solution)/shard_map/grid_third/pallas_call | solution.py:351
  19.8 0.0 copy-start
  19.8 0.0 copy-start.1
  19.8 0.0 copy-start.2
  19.9 1.0 %collective-permute-done.6.core_ref = bf16[4,64,256]{2,1,0:T(8,128)(2,1)S(1)} collective-permute-done((bf16[4,64,256]{2,1,0:T(8,128)(2,1)S(1)}, bf16[4,64,256]{2,1,0:T(8,128)(2,1)S(1)}, u32[]{:S(2)}, u32[]{:S(2)}) %collective-permute-start.6) | collective-permute-done | bytes 131104 | tf_op jit(solution)/shard_map/ppermute | solution.py:342
  20.9 3.2 %collective-permute-start.7 = (bf16[64,256]{1,0:T(8,128)(2,1)S(1)}, bf16[64,256]{1,0:T(8,128)(2,1)S(1)}, u32[]{:S(2)}, u32[]{:S(2)}) collective-permute-start(bf16[64,256]{1,0:T(8,128)(2,1)S(1)} %get-tuple-element.32), channel_id=1, source_target_pairs={{0,12},{1,13},{2,14},{3,15},{4,8},{5,9},{6,10},{7,11},{8,4},{9,5},... | collective-permute-start | bytes 98312 | tf_op jit(solution)/shard_map/ppermute | solution.py:342
  24.1 0.0 collective-permute-start.8
  24.1 0.0 copy-start.4
  24.1 0.0 copy-start.3
  24.1 1.3 %collective-permute-start.9 = (bf16[64,256]{1,0:T(8,128)(2,1)S(1)}, bf16[64,256]{1,0:T(8,128)(2,1)S(1)}, u32[]{:S(2)}, u32[]{:S(2)}) collective-permute-start(bf16[64,256]{1,0:T(8,128)(2,1)S(1)} %get-tuple-element.34), channel_id=1, source_target_pairs={{0,4},{1,5},{2,6},{3,7},{4,0},{5,1},{6,2},{7,3},{8,12},{9,13},{10,... | collective-permute-start | bytes 98312 | tf_op jit(solution)/shard_map/ppermute | solution.py:342
  25.3 1.6 %collective-permute-done.7.q3_ref = bf16[64,256]{1,0:T(8,128)(2,1)S(1)} collective-permute-done((bf16[64,256]{1,0:T(8,128)(2,1)S(1)}, bf16[64,256]{1,0:T(8,128)(2,1)S(1)}, u32[]{:S(2)}, u32[]{:S(2)}) %collective-permute-start.7) | collective-permute-done | bytes 32800 | tf_op jit(solution)/shard_map/ppermute | solution.py:342
  27.0 1.9 %collective-permute-done.8.q2_ref = bf16[64,256]{1,0:T(8,128)(2,1)S(1)} collective-permute-done((bf16[64,256]{1,0:T(8,128)(2,1)S(1)}, bf16[64,256]{1,0:T(8,128)(2,1)S(1)}, u32[]{:S(2)}, u32[]{:S(2)}) %collective-permute-start.8) | collective-permute-done | bytes 32800 | tf_op jit(solution)/shard_map/ppermute | solution.py:342
  28.9 0.0 collective-permute-done.9.q1_ref
  28.9 0.0 copy-done
  28.9 0.0 copy-done.1
  28.9 0.0 copy-done.2
  28.9 0.0 copy-done.4
  28.9 0.0 copy-done.3
  28.9 0.7 %grid_last.1 = (f32[64,256]{1,0:T(8,128)}, f32[1,256]{1,0:T(1,128)}) custom-call(bf16[64,256]{1,0:T(8,128)(2,1)S(1)} %collective-permute-done.7.q3_ref, bf16[64,256]{1,0:T(8,128)(2,1)S(1)} %collective-permute-done.8.q2_ref, bf16[64,256]{1,0:T(8,128)(2,1)S(1)} %collective-permute-done.9.q1_ref, f32[64,256]{1,0:T(8,128)S(1)} %get-tuple-element.35.q0_ref, ...), custom_call_target="tpu_custom_call" | custom-call | tf_op jit(solution)/shard_map/grid_last/pallas_call | solution.py:351
  (2 shorter events, 0.0 us)
Async XLA Ops:
  1.5 9.4 %collective-permute-start.3 = (bf16[80,256]{1,0:T(8,128)(2,1)S(1)}, bf16[80,256]{1,0:T(8,128)(2,1)S(1)}, u32[]{:S(2)}, u32[]{:S(2)}) collective-permute-start(bf16[80,256]{1,0:T(8,128)(2,1)S(1)} %get-tuple-element.22.v0_ref), channel_id=1, source_target_pairs={{0,12},{1,13},{2,14},{3,15},{4,8},{5,9},{6,10},{7,11},{8,4},{9,5},... | collective-permute-start | bytes 122888 | tf_op jit(solution)/shard_map/ppermute | solution.py:342
  6.6 4.9 %collective-permute-start.2 = (bf16[80,256]{1,0:T(8,128)(2,1)S(1)}, bf16[80,256]{1,0:T(8,128)(2,1)S(1)}, u32[]{:S(2)}, u32[]{:S(2)}) collective-permute-start(bf16[80,256]{1,0:T(8,128)(2,1)S(1)} %get-tuple-element.22.v0_ref), channel_id=1, source_target_pairs={{0,8},{1,9},{2,10},{3,11},{4,12},{5,13},{6,14},{7,15},{8,0},{9,1},... | collective-permute-start | bytes 122888 | tf_op jit(solution)/shard_map/ppermute | solution.py:342
  6.6 4.9 %collective-permute-start.1 = (bf16[80,256]{1,0:T(8,128)(2,1)S(1)}, bf16[80,256]{1,0:T(8,128)(2,1)S(1)}, u32[]{:S(2)}, u32[]{:S(2)}) collective-permute-start(bf16[80,256]{1,0:T(8,128)(2,1)S(1)} %get-tuple-element.22.v0_ref), channel_id=1, source_target_pairs={{0,4},{1,5},{2,6},{3,7},{4,0},{5,1},{6,2},{7,3},{8,12},{9,13},{10,... | collective-permute-start | bytes 122888 | tf_op jit(solution)/shard_map/ppermute | solution.py:342
  7.3 3.6 %collective-permute-start = (f32[3,256]{1,0:T(4,128)S(1)}, f32[3,256]{1,0:T(4,128)S(1)}, u32[]{:S(2)}, u32[]{:S(2)}) collective-permute-start(f32[3,256]{1,0:T(4,128)S(1)} %get-tuple-element.21), channel_id=1, source_target_pairs={{0,2},{1,3},{2,0},{3,1},{4,6},{5,7},{6,4},{7,5},{8,10},{9,11},{10,... | collective-permute-start | bytes 9224 | tf_op jit(solution)/shard_map/ppermute | solution.py:342
  11.6 1.7 %collective-permute-start.4 = (bf16[4,80,256]{2,1,0:T(8,128)(2,1)S(1)}, bf16[4,80,256]{2,1,0:T(8,128)(2,1)S(1)}, u32[]{:S(2)}, u32[]{:S(2)}) collective-permute-start(bf16[4,80,256]{2,1,0:T(8,128)(2,1)S(1)} %grid_pack.1.packed_ref), channel_id=1, source_target_pairs={{0,1},{1,0},{2,3},{3,2},{4,5},{5,4},{6,7},{7,6},{8,9},{9,8},{10,11... | collective-permute-start | bytes 491528 | tf_op jit(solution)/shard_map/ppermute | solution.py:342
  14.4 4.7 %collective-permute-start.5 = (bf16[144,256]{1,0:T(8,128)(2,1)S(1)}, bf16[144,256]{1,0:T(8,128)(2,1)S(1)}, u32[]{:S(2)}, u32[]{:S(2)}) collective-permute-start(bf16[144,256]{1,0:T(8,128)(2,1)S(1)} %get-tuple-element.29), channel_id=1, source_target_pairs={{0,2},{1,3},{2,0},{3,1},{4,6},{5,7},{6,4},{7,5},{8,10},{9,11},{10,... | collective-permute-start | bytes 221192 | tf_op jit(solution)/shard_map/ppermute | solution.py:342
  19.4 1.4 %collective-permute-start.6 = (bf16[4,64,256]{2,1,0:T(8,128)(2,1)S(1)}, bf16[4,64,256]{2,1,0:T(8,128)(2,1)S(1)}, u32[]{:S(2)}, u32[]{:S(2)}) collective-permute-start(bf16[4,64,256]{2,1,0:T(8,128)(2,1)S(1)} %get-tuple-element.31), channel_id=1, source_target_pairs={{0,1},{1,0},{2,3},{3,2},{4,5},{5,4},{6,7},{7,6},{8,9},{9,8},{10,11... | collective-permute-start | bytes 393224 | tf_op jit(solution)/shard_map/ppermute | solution.py:342
  19.8 9.1 %copy-start = (f32[64,256]{1,0:T(8,128)S(1)}, f32[64,256]{1,0:T(8,128)}, u32[]{:S(2)}) copy-start(f32[64,256]{1,0:T(8,128)} %rest_0_.1) | copy-start | bytes 196612
  19.8 9.0 %copy-start.1 = (bf16[64,256]{1,0:T(8,128)(2,1)S(1)}, bf16[64,256]{1,0:T(8,128)(2,1)}, u32[]{:S(2)}) copy-start(bf16[64,256]{1,0:T(8,128)(2,1)} %rest_3_.1) | copy-start | bytes 98308
  19.8 9.0 %copy-start.2 = (bf16[64,256]{1,0:T(8,128)(2,1)S(1)}, bf16[64,256]{1,0:T(8,128)(2,1)}, u32[]{:S(2)}) copy-start(bf16[64,256]{1,0:T(8,128)(2,1)} %rest_4_.1) | copy-start | bytes 98308
  20.9 6.1 %collective-permute-start.7 = (bf16[64,256]{1,0:T(8,128)(2,1)S(1)}, bf16[64,256]{1,0:T(8,128)(2,1)S(1)}, u32[]{:S(2)}, u32[]{:S(2)}) collective-permute-start(bf16[64,256]{1,0:T(8,128)(2,1)S(1)} %get-tuple-element.32), channel_id=1, source_target_pairs={{0,12},{1,13},{2,14},{3,15},{4,8},{5,9},{6,10},{7,11},{8,4},{9,5},... | collective-permute-start | bytes 98312 | tf_op jit(solution)/shard_map/ppermute | solution.py:342
  24.1 4.8 %collective-permute-start.8 = (bf16[64,256]{1,0:T(8,128)(2,1)S(1)}, bf16[64,256]{1,0:T(8,128)(2,1)S(1)}, u32[]{:S(2)}, u32[]{:S(2)}) collective-permute-start(bf16[64,256]{1,0:T(8,128)(2,1)S(1)} %get-tuple-element.33), channel_id=1, source_target_pairs={{0,8},{1,9},{2,10},{3,11},{4,12},{5,13},{6,14},{7,15},{8,0},{9,1},... | collective-permute-start | bytes 98312 | tf_op jit(solution)/shard_map/ppermute | solution.py:342
  24.1 4.8 %copy-start.4 = (f32[256]{0:T(256)S(1)}, f32[256]{0:T(256)}, u32[]{:S(2)}) copy-start(f32[256]{0:T(256)} %param.10) | copy-start | bytes 3076
  24.1 4.8 %copy-start.3 = (f32[256]{0:T(256)S(1)}, f32[256]{0:T(256)}, u32[]{:S(2)}) copy-start(f32[256]{0:T(256)} %param.11) | copy-start | bytes 3076
  24.1 4.8 %collective-permute-start.9 = (bf16[64,256]{1,0:T(8,128)(2,1)S(1)}, bf16[64,256]{1,0:T(8,128)(2,1)S(1)}, u32[]{:S(2)}, u32[]{:S(2)}) collective-permute-start(bf16[64,256]{1,0:T(8,128)(2,1)S(1)} %get-tuple-element.34), channel_id=1, source_target_pairs={{0,4},{1,5},{2,6},{3,7},{4,0},{5,1},{6,2},{7,3},{8,12},{9,13},{10,... | collective-permute-start | bytes 98312 | tf_op jit(solution)/shard_map/ppermute | solution.py:342

commit v11 on v6

--- a/solution.py
+++ b/solution.py
@@ -13,10 +13,10 @@
 GROUP = 16
 LINE = 4
 GRID = 16
-FAR = 8
+STEP = 4
+FAR = 2
 EXTRA = 16
 TERMS = 32
-LONG = pl.CostEstimate(flops=10**11, bytes_accessed=10**8, transcendentals=0)
 VMEM_BYTES = 48 * 1024 * 1024
 GRID_BYTES = 8 * 1024 * 1024
 
@@ -52,15 +52,15 @@
 
 
 def prepare(scale, *refs):
-    arguments, (packed_ref, rows, *held, sems) = refs[:5], refs[5:]
+    arguments, (packed_ref, spot_ref, rows, *held, sems) = refs[:5], refs[5:]
     copies = [
         pltpu.make_async_copy(argument, ref, sems.at[at])
         for at, (argument, ref) in enumerate(zip(arguments, held))
     ]
-    for copy in copies:
+    for copy in copies[::-1]:
         copy.start()
     rows[...] = jnp.zeros_like(rows)
-    for copy in copies:
+    for copy in copies[:-1]:
         copy.wait()
     pos_ref, words_ref, area_ref, reflectance_ref, seed_ref = held
     rhs_count = seed_ref.shape[0]
@@ -75,8 +75,10 @@
         for local in range(words_ref.shape[0]):
             start = local * TILE
             rows[12 + place : 13 + place, start : start + count] = part[local : local + 1]
+    packed_ref[rhs_count:] = rows[...].astype(jnp.bfloat16)
+    copies[-1].wait()
     packed_ref[:rhs_count] = (reflectance_ref[...] * seed_ref[...]).astype(jnp.bfloat16)
-    packed_ref[rhs_count:] = rows[...].astype(jnp.bfloat16)
+    spot_ref[...] = pos_ref[...]
 
 
 def distance_terms(position, terms, as_rows):
@@ -186,7 +188,7 @@
         if t == 0 and v == 0 and w == 0:
             form_own(row_chunk, slot, words[v], out_ref)
         else:
-            form_block(row_chunk, jnp.bitwise_xor(me, 2 * v + w), slot, words[v], out_ref)
+            form_block(row_chunk, jnp.bitwise_xor(me, STEP * v + w), slot, words[v], out_ref)
         if place:
             add(place - 1)
     add(len(blocks) - 1)
@@ -202,16 +204,16 @@
     return words
 
 
+def grid_pack(v0_ref, v1_ref, v2_ref, v3_ref, out_ref):
+    for v, ref in enumerate((v0_ref, v1_ref, v2_ref, v3_ref)):
+        out_ref[v] = ref[...]
+
+
 def grid_rows(own_ref, far_ref, row_terms, terms):
     own, _ = read_extra(own_ref[-EXTRA:, :])
     for t, value in enumerate((own, far_ref[...])):
         distance_terms(value, terms.at[t], True)
         row_terms[t] = jnp.transpose(terms[t]).astype(jnp.bfloat16)
-
-
-def grid_pack(v0_ref, v1_ref, v2_ref, v3_ref, out_ref):
-    for v, ref in enumerate((v0_ref, v1_ref, v2_ref, v3_ref)):
-        out_ref[v] = ref[...]
 
 
 def grid_near(
@@ -349,7 +351,7 @@
         for value in (position, visibility, area, reflectance, adjoint_seed)
     ]
 
-    def call(body, name, operands, in_specs, out_shape, scratch_shapes=(), cost=None):
+    def call(body, name, operands, in_specs, out_shape, scratch_shapes=()):
         return pl.pallas_call(
             body,
             in_specs=in_specs,
@@ -357,31 +359,32 @@
             out_shape=out_shape,
             scratch_shapes=scratch_shapes,
             compiler_params=params,
-            cost_estimate=cost,
             name=name,
         )(*operands)
 
     packed_rows = rhs_count + EXTRA
-    (own,) = call(
+    own, spot = call(
         functools.partial(prepare, scale),
         "prepare",
         arguments,
         [hbm] * 5,
-        [shaped((packed_rows, own_width), jnp.bfloat16)],
+        [
+            shaped((packed_rows, own_width), jnp.bfloat16),
+            shaped(position.shape, jnp.float32),
+        ],
         [pltpu.VMEM((EXTRA, own_width), jnp.float32)]
         + [pltpu.VMEM(value.shape, value.dtype) for value in arguments]
         + [pltpu.SemaphoreType.DMA((5,))],
     )
-    lines = [send(own, 2 * v) for v in range(1, LINE)]
+    lines = [send(own, STEP * v) for v in range(1, LINE)]
     terms = (TERMS, own_width)
     (row_terms,) = call(
         grid_rows,
         "grid_rows",
-        (own, send(position, FAR)),
+        (own, send(spot, FAR)),
         [vmem] * 2,
         [shaped((2, own_width, TERMS), jnp.bfloat16)],
         [pltpu.VMEM((2,) + terms, jnp.float32)],
-        LONG,
     )
     first, row_terms = lax.optimization_barrier((own, row_terms))
     packed_shape = shaped((LINE, packed_rows, own_width), jnp.bfloat16)
@@ -434,7 +437,7 @@
         [vmem] * 2,
         [shaped(field, jnp.float32)] + [shaped(field, jnp.bfloat16)] * 3,
     )
-    lines = [send(sums[v], 2 * v) for v in range(1, LINE)]
+    lines = [send(sums[v], STEP * v) for v in range(1, LINE)]
     adjoint, grad = call(
         functools.partial(grid_last, scale),
         "grid_last",

time: 31.1 us -> 29.6 us (0.952)
  waiting for transfers between devices: 13.6 us -> 10.3 us
  starting transfers between devices: 11.8 us -> 13.5 us
    ppermute x10, waiting for transfers between devices: 13.6 us -> 10.3 us  [send(): lax.ppermute(value, 'row', [(at, at ^ step) for at in range(devices)])]
    ppermute x10, starting transfers between devices: 11.8 us -> 13.5 us  [send(): lax.ppermute(value, 'row', [(at, at ^ step) for at in range(devices)])]
  transfers between devices with their start and end apart: 10 -> 10, of which waited for: 7 -> 6; matrix products, arithmetic and copies ran while one was open for 0% -> 0% of each run, Pallas kernels for 9% -> 6%
where the time goes in v11:
time: 29.6 us; the launch traced here: 29.4 us
  starting transfers between devices  13.5 us (46%)
  waiting for transfers between devices  10.3 us (35%)
  Pallas kernels  4.73 us (16%)
  between operations  0.78 us (3%)
    ppermute x10, starting transfers between devices, send(): lax.ppermute(value, 'row', [(at, at ^ step) for at in range(devices)])  13.5 us
    ppermute x10, waiting for transfers between devices, send(): lax.ppermute(value, 'row', [(at, at ^ step) for at in range(devices)])  10.3 us
    pallas_call x9, Pallas kernels, call(): pl.pallas_call(body, in_specs=in_specs, out_specs=[vmem] * len(out_shape)...  4.73 us
  transfers between devices with their start and end apart: 10, of which 6 were waited for; matrix products, arithmetic and copies ran while one was open for 0% of the time, Pallas kernels for 6%

profile of v11, /device:TPU:0, one launch (start us, length us, event | category | flops | bytes accessed | tf_op | source)
XLA Modules:
  0.0 29.4 jit_solution(2005523083793487308)
XLA Ops:
  0.6 0.9 %prepare.1 = (bf16[80,256]{1,0:T(8,128)(2,1)S(1)}, f32[3,256]{1,0:T(4,128)S(1)}) custom-call(f32[3,256]{1,0:T(4,128)} %refs_0_.1, s32[2,32]{1,0:T(2,128)} %refs_1_.1, f32[1,256]{1,0:T(1,128)} %bitcast.4, f32[1,256]{1,0:T(1,128)} %bitcast.7, f32[64,256]{1,0:T(8,128)} %rest_0_.1), custom_call_target="tpu_custom_call" | custom-call | tf_op jit(solution)/shard_map/prepare/pallas_call | solution.py:355
  1.5 5.1 %collective-permute-start.3 = (bf16[80,256]{1,0:T(8,128)(2,1)S(1)}, bf16[80,256]{1,0:T(8,128)(2,1)S(1)}, u32[]{:S(2)}, u32[]{:S(2)}) collective-permute-start(bf16[80,256]{1,0:T(8,128)(2,1)S(1)} %get-tuple-element.21.own_ref.v0_ref), channel_id=1, source_target_pairs={{0,12},{1,13},{2,14},{3,15},{4,8},{5,9},{6,10},{7,11},{8,4},{9,5},... | collective-permute-start | bytes 122888 | tf_op jit(solution)/shard_map/ppermute | solution.py:346
  6.6 0.0 collective-permute-start.2
  6.6 0.6 %collective-permute-start.1 = (bf16[80,256]{1,0:T(8,128)(2,1)S(1)}, bf16[80,256]{1,0:T(8,128)(2,1)S(1)}, u32[]{:S(2)}, u32[]{:S(2)}) collective-permute-start(bf16[80,256]{1,0:T(8,128)(2,1)S(1)} %get-tuple-element.21.own_ref.v0_ref), channel_id=1, source_target_pairs={{0,4},{1,5},{2,6},{3,7},{4,0},{5,1},{6,2},{7,3},{8,12},{9,13},{10,... | collective-permute-start | bytes 122888 | tf_op jit(solution)/shard_map/ppermute | solution.py:346
  7.3 1.6 %collective-permute-start = (f32[3,256]{1,0:T(4,128)S(1)}, f32[3,256]{1,0:T(4,128)S(1)}, u32[]{:S(2)}, u32[]{:S(2)}) collective-permute-start(f32[3,256]{1,0:T(4,128)S(1)} %get-tuple-element.20), channel_id=1, source_target_pairs={{0,2},{1,3},{2,0},{3,1},{4,6},{5,7},{6,4},{7,5},{8,10},{9,11},{10,... | collective-permute-start | bytes 9224 | tf_op jit(solution)/shard_map/ppermute | solution.py:346
  8.9 2.0 %collective-permute-done.far_ref = f32[3,256]{1,0:T(4,128)S(1)} collective-permute-done((f32[3,256]{1,0:T(4,128)S(1)}, f32[3,256]{1,0:T(4,128)S(1)}, u32[]{:S(2)}, u32[]{:S(2)}) %collective-permute-start) | collective-permute-done | bytes 3104 | tf_op jit(solution)/shard_map/ppermute | solution.py:346
  10.9 0.1 grid_rows.1.row_terms
  11.0 0.0 collective-permute-done.3.v3_ref
  11.0 0.5 %collective-permute-done.2.v2_ref = bf16[80,256]{1,0:T(8,128)(2,1)S(1)} collective-permute-done((bf16[80,256]{1,0:T(8,128)(2,1)S(1)}, bf16[80,256]{1,0:T(8,128)(2,1)S(1)}, u32[]{:S(2)}, u32[]{:S(2)}) %collective-permute-start.2) | collective-permute-done | bytes 40992 | tf_op jit(solution)/shard_map/ppermute | solution.py:346
  11.5 0.0 collective-permute-done.1.v1_ref
  11.6 0.1 collective-permute-start.4
  11.6 1.4 %grid_near.1 = (bf16[8,256,256]{2,1,0:T(8,128)(2,1)S(1)}, f32[2,64,256]{2,1,0:T(8,128)S(1)}) custom-call(s32[1]{0:T(128)} %bitcast.me_ref, bf16[4,80,256]{2,1,0:T(8,128)(2,1)S(1)} %grid_pack.1.packed_ref, bf16[2,256,32]{2,1,0:T(8,128)(2,1)S(1)} %grid_rows.1.row_terms, f32[64,256]{1,0:T(8,128)} %rest_0_.1, f32[1,256]{1,0:T(1,128)} %bitcast.5), custom_call_target="tpu_custom_call" | custom-call | tf_op jit(solution)/shard_map/grid_near/pallas_call | solution.py:355
  13.1 0.0 collective-permute-done.4.core_ref
  13.1 1.0 %grid_rest.1 = (bf16[8,256,256]{2,1,0:T(8,128)(2,1)S(1)}, f32[2,64,256]{2,1,0:T(8,128)S(1)}, bf16[144,256]{1,0:T(8,128)(2,1)S(1)}) custom-call(s32[1]{0:T(128)} %bitcast.me_ref, bf16[4,80,256]{2,1,0:T(8,128)(2,1)S(1)} %grid_pack.1.packed_ref, bf16[4,80,256]{2,1,0:T(8,128)(2,1)S(1)} %collective-permute-done.4.core_ref, ...), custom_call_target="tpu_custom_call" | custom-call | tf_op jit(solution)/shard_map/grid_rest/pallas_call | solution.py:355
  14.1 1.6 %collective-permute-start.5 = (bf16[144,256]{1,0:T(8,128)(2,1)S(1)}, bf16[144,256]{1,0:T(8,128)(2,1)S(1)}, u32[]{:S(2)}, u32[]{:S(2)}) collective-permute-start(bf16[144,256]{1,0:T(8,128)(2,1)S(1)} %get-tuple-element.27), channel_id=1, source_target_pairs={{0,2},{1,3},{2,0},{3,1},{4,6},{5,7},{6,4},{7,5},{8,10},{9,11},{10,... | collective-permute-start | bytes 221192 | tf_op jit(solution)/shard_map/ppermute | solution.py:346
  15.6 3.2 %collective-permute-done.5.far_ref = bf16[144,256]{1,0:T(8,128)(2,1)S(1)} collective-permute-done((bf16[144,256]{1,0:T(8,128)(2,1)S(1)}, bf16[144,256]{1,0:T(8,128)(2,1)S(1)}, u32[]{:S(2)}, u32[]{:S(2)}) %collective-permute-start.5) | collective-permute-done | bytes 73760 | tf_op jit(solution)/shard_map/ppermute | solution.py:346
  18.8 0.3 %grid_second.1 = (bf16[2,64,256]{2,1,0:T(8,128)(2,1)S(1)}, bf16[4,64,256]{2,1,0:T(8,128)(2,1)S(1)}) custom-call(bf16[8,256,256]{2,1,0:T(8,128)(2,1)S(1)} %get-tuple-element.25.rest_ref, f32[2,64,256]{2,1,0:T(8,128)S(1)} %get-tuple-element.26.partial_ref, bf16[4,80,256]{2,1,0:T(8,128)(2,1)S(1)} %grid_pack.1.packed_ref, ...), custom_call_target="tpu_custom_call" | custom-call | tf_op jit(solution)/shard_map/grid_second/pallas_call | solution.py:355
  19.1 0.1 collective-permute-start.6
  19.2 0.3 %grid_third.1.sum_ref = f32[4,64,256]{2,1,0:T(8,128)S(1)} custom-call(bf16[8,256,256]{2,1,0:T(8,128)(2,1)S(1)} %get-tuple-element.23.near_ref, bf16[2,64,256]{2,1,0:T(8,128)(2,1)S(1)} %get-tuple-element.28.scaled_ref), custom_call_target="tpu_custom_call" | custom-call | tf_op jit(solution)/shard_map/grid_third/pallas_call | solution.py:355
  19.5 0.0 copy-start
  19.5 0.0 copy-start.1
  19.5 0.0 copy-start.2
  19.5 1.0 %collective-permute-done.6.core_ref = bf16[4,64,256]{2,1,0:T(8,128)(2,1)S(1)} collective-permute-done((bf16[4,64,256]{2,1,0:T(8,128)(2,1)S(1)}, bf16[4,64,256]{2,1,0:T(8,128)(2,1)S(1)}, u32[]{:S(2)}, u32[]{:S(2)}) %collective-permute-start.6) | collective-permute-done | bytes 131104 | tf_op jit(solution)/shard_map/ppermute | solution.py:346
  20.5 3.3 %collective-permute-start.7 = (bf16[64,256]{1,0:T(8,128)(2,1)S(1)}, bf16[64,256]{1,0:T(8,128)(2,1)S(1)}, u32[]{:S(2)}, u32[]{:S(2)}) collective-permute-start(bf16[64,256]{1,0:T(8,128)(2,1)S(1)} %get-tuple-element.30), channel_id=1, source_target_pairs={{0,12},{1,13},{2,14},{3,15},{4,8},{5,9},{6,10},{7,11},{8,4},{9,5},... | collective-permute-start | bytes 98312 | tf_op jit(solution)/shard_map/ppermute | solution.py:346
  23.9 0.0 collective-permute-start.8
  23.9 0.0 copy-start.4
  23.9 0.0 copy-start.3
  23.9 1.1 %collective-permute-start.9 = (bf16[64,256]{1,0:T(8,128)(2,1)S(1)}, bf16[64,256]{1,0:T(8,128)(2,1)S(1)}, u32[]{:S(2)}, u32[]{:S(2)}) collective-permute-start(bf16[64,256]{1,0:T(8,128)(2,1)S(1)} %get-tuple-element.32), channel_id=1, source_target_pairs={{0,4},{1,5},{2,6},{3,7},{4,0},{5,1},{6,2},{7,3},{8,12},{9,13},{10,... | collective-permute-start | bytes 98312 | tf_op jit(solution)/shard_map/ppermute | solution.py:346
  25.0 1.6 %collective-permute-done.7.q3_ref = bf16[64,256]{1,0:T(8,128)(2,1)S(1)} collective-permute-done((bf16[64,256]{1,0:T(8,128)(2,1)S(1)}, bf16[64,256]{1,0:T(8,128)(2,1)S(1)}, u32[]{:S(2)}, u32[]{:S(2)}) %collective-permute-start.7) | collective-permute-done | bytes 32800 | tf_op jit(solution)/shard_map/ppermute | solution.py:346
  26.6 2.1 %collective-permute-done.8.q2_ref = bf16[64,256]{1,0:T(8,128)(2,1)S(1)} collective-permute-done((bf16[64,256]{1,0:T(8,128)(2,1)S(1)}, bf16[64,256]{1,0:T(8,128)(2,1)S(1)}, u32[]{:S(2)}, u32[]{:S(2)}) %collective-permute-start.8) | collective-permute-done | bytes 32800 | tf_op jit(solution)/shard_map/ppermute | solution.py:346
  28.7 0.0 collective-permute-done.9.q1_ref
  28.7 0.0 copy-done
  28.7 0.0 copy-done.1
  28.7 0.0 copy-done.2
  28.7 0.0 copy-done.4
  28.7 0.0 copy-done.3
  28.7 0.7 %grid_last.1 = (f32[64,256]{1,0:T(8,128)}, f32[1,256]{1,0:T(1,128)}) custom-call(bf16[64,256]{1,0:T(8,128)(2,1)S(1)} %collective-permute-done.7.q3_ref, bf16[64,256]{1,0:T(8,128)(2,1)S(1)} %collective-permute-done.8.q2_ref, bf16[64,256]{1,0:T(8,128)(2,1)S(1)} %collective-permute-done.9.q1_ref, f32[64,256]{1,0:T(8,128)S(1)} %get-tuple-element.33.q0_ref, ...), custom_call_target="tpu_custom_call" | custom-call | tf_op jit(solution)/shard_map/grid_last/pallas_call | solution.py:355
  (2 shorter events, 0.0 us)
Async XLA Ops:
  1.5 9.5 %collective-permute-start.3 = (bf16[80,256]{1,0:T(8,128)(2,1)S(1)}, bf16[80,256]{1,0:T(8,128)(2,1)S(1)}, u32[]{:S(2)}, u32[]{:S(2)}) collective-permute-start(bf16[80,256]{1,0:T(8,128)(2,1)S(1)} %get-tuple-element.21.own_ref.v0_ref), channel_id=1, source_target_pairs={{0,12},{1,13},{2,14},{3,15},{4,8},{5,9},{6,10},{7,11},{8,4},{9,5},... | collective-permute-start | bytes 122888 | tf_op jit(solution)/shard_map/ppermute | solution.py:346
  6.6 4.9 %collective-permute-start.2 = (bf16[80,256]{1,0:T(8,128)(2,1)S(1)}, bf16[80,256]{1,0:T(8,128)(2,1)S(1)}, u32[]{:S(2)}, u32[]{:S(2)}) collective-permute-start(bf16[80,256]{1,0:T(8,128)(2,1)S(1)} %get-tuple-element.21.own_ref.v0_ref), channel_id=1, source_target_pairs={{0,8},{1,9},{2,10},{3,11},{4,12},{5,13},{6,14},{7,15},{8,0},{9,1},... | collective-permute-start | bytes 122888 | tf_op jit(solution)/shard_map/ppermute | solution.py:346
  6.6 4.9 %collective-permute-start.1 = (bf16[80,256]{1,0:T(8,128)(2,1)S(1)}, bf16[80,256]{1,0:T(8,128)(2,1)S(1)}, u32[]{:S(2)}, u32[]{:S(2)}) collective-permute-start(bf16[80,256]{1,0:T(8,128)(2,1)S(1)} %get-tuple-element.21.own_ref.v0_ref), channel_id=1, source_target_pairs={{0,4},{1,5},{2,6},{3,7},{4,0},{5,1},{6,2},{7,3},{8,12},{9,13},{10,... | collective-permute-start | bytes 122888 | tf_op jit(solution)/shard_map/ppermute | solution.py:346
  7.3 3.6 %collective-permute-start = (f32[3,256]{1,0:T(4,128)S(1)}, f32[3,256]{1,0:T(4,128)S(1)}, u32[]{:S(2)}, u32[]{:S(2)}) collective-permute-start(f32[3,256]{1,0:T(4,128)S(1)} %get-tuple-element.20), channel_id=1, source_target_pairs={{0,2},{1,3},{2,0},{3,1},{4,6},{5,7},{6,4},{7,5},{8,10},{9,11},{10,... | collective-permute-start | bytes 9224 | tf_op jit(solution)/shard_map/ppermute | solution.py:346
  11.6 1.5 %collective-permute-start.4 = (bf16[4,80,256]{2,1,0:T(8,128)(2,1)S(1)}, bf16[4,80,256]{2,1,0:T(8,128)(2,1)S(1)}, u32[]{:S(2)}, u32[]{:S(2)}) collective-permute-start(bf16[4,80,256]{2,1,0:T(8,128)(2,1)S(1)} %grid_pack.1.packed_ref), channel_id=1, source_target_pairs={{0,1},{1,0},{2,3},{3,2},{4,5},{5,4},{6,7},{7,6},{8,9},{9,8},{10,11... | collective-permute-start | bytes 491528 | tf_op jit(solution)/shard_map/ppermute | solution.py:346
  14.1 4.7 %collective-permute-start.5 = (bf16[144,256]{1,0:T(8,128)(2,1)S(1)}, bf16[144,256]{1,0:T(8,128)(2,1)S(1)}, u32[]{:S(2)}, u32[]{:S(2)}) collective-permute-start(bf16[144,256]{1,0:T(8,128)(2,1)S(1)} %get-tuple-element.27), channel_id=1, source_target_pairs={{0,2},{1,3},{2,0},{3,1},{4,6},{5,7},{6,4},{7,5},{8,10},{9,11},{10,... | collective-permute-start | bytes 221192 | tf_op jit(solution)/shard_map/ppermute | solution.py:346
  19.1 1.4 %collective-permute-start.6 = (bf16[4,64,256]{2,1,0:T(8,128)(2,1)S(1)}, bf16[4,64,256]{2,1,0:T(8,128)(2,1)S(1)}, u32[]{:S(2)}, u32[]{:S(2)}) collective-permute-start(bf16[4,64,256]{2,1,0:T(8,128)(2,1)S(1)} %get-tuple-element.29), channel_id=1, source_target_pairs={{0,1},{1,0},{2,3},{3,2},{4,5},{5,4},{6,7},{7,6},{8,9},{9,8},{10,11... | collective-permute-start | bytes 393224 | tf_op jit(solution)/shard_map/ppermute | solution.py:346
  19.5 9.2 %copy-start = (f32[64,256]{1,0:T(8,128)S(1)}, f32[64,256]{1,0:T(8,128)}, u32[]{:S(2)}) copy-start(f32[64,256]{1,0:T(8,128)} %rest_0_.1) | copy-start | bytes 196612
  19.5 9.2 %copy-start.1 = (bf16[64,256]{1,0:T(8,128)(2,1)S(1)}, bf16[64,256]{1,0:T(8,128)(2,1)}, u32[]{:S(2)}) copy-start(bf16[64,256]{1,0:T(8,128)(2,1)} %rest_3_.1) | copy-start | bytes 98308
  19.5 9.2 %copy-start.2 = (bf16[64,256]{1,0:T(8,128)(2,1)S(1)}, bf16[64,256]{1,0:T(8,128)(2,1)}, u32[]{:S(2)}) copy-start(bf16[64,256]{1,0:T(8,128)(2,1)} %rest_4_.1) | copy-start | bytes 98308
  20.5 6.1 %collective-permute-start.7 = (bf16[64,256]{1,0:T(8,128)(2,1)S(1)}, bf16[64,256]{1,0:T(8,128)(2,1)S(1)}, u32[]{:S(2)}, u32[]{:S(2)}) collective-permute-start(bf16[64,256]{1,0:T(8,128)(2,1)S(1)} %get-tuple-element.30), channel_id=1, source_target_pairs={{0,12},{1,13},{2,14},{3,15},{4,8},{5,9},{6,10},{7,11},{8,4},{9,5},... | collective-permute-start | bytes 98312 | tf_op jit(solution)/shard_map/ppermute | solution.py:346
  23.9 4.8 %collective-permute-start.8 = (bf16[64,256]{1,0:T(8,128)(2,1)S(1)}, bf16[64,256]{1,0:T(8,128)(2,1)S(1)}, u32[]{:S(2)}, u32[]{:S(2)}) collective-permute-start(bf16[64,256]{1,0:T(8,128)(2,1)S(1)} %get-tuple-element.31), channel_id=1, source_target_pairs={{0,8},{1,9},{2,10},{3,11},{4,12},{5,13},{6,14},{7,15},{8,0},{9,1},... | collective-permute-start | bytes 98312 | tf_op jit(solution)/shard_map/ppermute | solution.py:346
  23.9 4.8 %copy-start.4 = (f32[256]{0:T(256)S(1)}, f32[256]{0:T(256)}, u32[]{:S(2)}) copy-start(f32[256]{0:T(256)} %param.10) | copy-start | bytes 3076
  23.9 4.8 %copy-start.3 = (f32[256]{0:T(256)S(1)}, f32[256]{0:T(256)}, u32[]{:S(2)}) copy-start(f32[256]{0:T(256)} %param.11) | copy-start | bytes 3076
  23.9 4.8 %collective-permute-start.9 = (bf16[64,256]{1,0:T(8,128)(2,1)S(1)}, bf16[64,256]{1,0:T(8,128)(2,1)S(1)}, u32[]{:S(2)}, u32[]{:S(2)}) collective-permute-start(bf16[64,256]{1,0:T(8,128)(2,1)S(1)} %get-tuple-element.32), channel_id=1, source_target_pairs={{0,4},{1,5},{2,6},{3,7},{4,0},{5,1},{6,2},{7,3},{8,12},{9,13},{10,... | collective-permute-start | bytes 98312 | tf_op jit(solution)/shard_map/ppermute | solution.py:346

commit v12 on v11

--- a/solution.py
+++ b/solution.py
@@ -217,28 +217,9 @@
 
 
 def grid_near(
-    scale,
-    me_ref,
-    packed_ref,
-    row_terms,
-    seed_hbm,
-    area_hbm,
-    kernel_ref,
-    partial_ref,
-    terms,
-    col_terms,
-    distance,
-    seed_ref,
-    area_ref,
-    sems,
+    me_ref, packed_ref, row_terms, boost_ref, kernel_ref, partial_ref, terms, col_terms, distance
 ):
-    copies = [
-        pltpu.make_async_copy(seed_hbm, seed_ref, sems.at[0]),
-        pltpu.make_async_copy(area_hbm, area_ref, sems.at[1]),
-    ]
-    for copy in copies:
-        copy.start()
-    rhs_count = seed_ref.shape[0]
+    rhs_count = boost_ref.shape[0]
     me = me_ref[0]
     words = column_terms(lambda v: packed_ref[v, rhs_count:], terms, col_terms)
 
@@ -252,13 +233,10 @@
         col_terms,
         words,
         lambda v: packed_ref[v, :rhs_count],
-        lambda t: 0.0,
+        lambda t: 0.0 if t else boost_ref[...],
         (kernel_ref, distance),
         finish_row,
     )
-    for copy in copies:
-        copy.wait()
-    partial_ref[0] = partial_ref[0] + seed_ref[...] * (1.0 / (area_ref[...] * scale))
 
 
 def grid_rest(
@@ -386,7 +364,8 @@
         [shaped((2, own_width, TERMS), jnp.bfloat16)],
         [pltpu.VMEM((2,) + terms, jnp.float32)],
     )
-    first, row_terms = lax.optimization_barrier((own, row_terms))
+    boost = adjoint_seed * (1.0 / (area * scale))
+    first, row_terms, boost = lax.optimization_barrier((own, row_terms, boost))
     packed_shape = shaped((LINE, packed_rows, own_width), jnp.bfloat16)
     (packed,) = call(grid_pack, "grid_pack", (first, *lines), [vmem] * LINE, [packed_shape])
     core = send(packed, 1)
@@ -398,17 +377,12 @@
         pltpu.VMEM((2, own_width, own_width), jnp.float32),
     ]
     near, partial = call(
-        functools.partial(grid_near, scale),
+        grid_near,
         "grid_near",
-        (my_index, packed, row_terms, arguments[4], arguments[2]),
-        [smem] + [vmem] * 2 + [hbm] * 2,
+        (my_index, packed, row_terms, boost),
+        [smem] + [vmem] * 3,
         [blocks, pair],
-        scratch
-        + [
-            pltpu.VMEM(field, jnp.float32),
-            pltpu.VMEM((1, own_width), jnp.float32),
-            pltpu.SemaphoreType.DMA((2,)),
-        ],
+        scratch,
     )
     rest, partial, sent = call(
         grid_rest,

time: 29.6 us -> 29.3 us (0.990)
  transfers between devices with their start and end apart: 10 -> 10, of which waited for: 6 -> 7; matrix products, arithmetic and copies ran while one was open for 0% -> 0% of each run, Pallas kernels for 6% -> 5%
where the time goes in v12:
time: 29.3 us; the launch traced here: 29.2 us
  starting transfers between devices  13.5 us (46%)
  waiting for transfers between devices  10.3 us (35%)
  Pallas kernels  4.48 us (15%)
  between operations  0.77 us (3%)
    ppermute x10, starting transfers between devices, send(): lax.ppermute(value, 'row', [(at, at ^ step) for at in range(devices)])  13.5 us
    ppermute x10, waiting for transfers between devices, send(): lax.ppermute(value, 'row', [(at, at ^ step) for at in range(devices)])  10.3 us
    pallas_call x9, Pallas kernels, call(): pl.pallas_call(body, in_specs=in_specs, out_specs=[vmem] * len(out_shape)...  4.48 us
  transfers between devices with their start and end apart: 10, of which 7 were waited for; matrix products, arithmetic and copies ran while one was open for 0% of the time, Pallas kernels for 5%

profile of v12, /device:TPU:0, one launch (start us, length us, event | category | flops | bytes accessed | tf_op | source)
XLA Modules:
  0.0 29.2 jit_solution(4906791607725970896)
XLA Ops:
  0.6 0.0 copy-start
  0.6 1.0 %prepare.1 = (bf16[80,256]{1,0:T(8,128)(2,1)S(1)}, f32[3,256]{1,0:T(4,128)S(1)}) custom-call(f32[3,256]{1,0:T(4,128)} %refs_0_.1, s32[2,32]{1,0:T(2,128)} %refs_1_.1, f32[1,256]{1,0:T(1,128)} %bitcast.4, f32[1,256]{1,0:T(1,128)} %bitcast.6, f32[64,256]{1,0:T(8,128)} %rest_0_.1), custom_call_target="tpu_custom_call" | custom-call | tf_op jit(solution)/shard_map/prepare/pallas_call | solution.py:333
  1.6 0.0 copy-start.3
  1.6 5.1 %collective-permute-start.3 = (bf16[80,256]{1,0:T(8,128)(2,1)S(1)}, bf16[80,256]{1,0:T(8,128)(2,1)S(1)}, u32[]{:S(2)}, u32[]{:S(2)}) collective-permute-start(bf16[80,256]{1,0:T(8,128)(2,1)S(1)} %get-tuple-element.22.own_ref.v0_ref), channel_id=1, source_target_pairs={{0,12},{1,13},{2,14},{3,15},{4,8},{5,9},{6,10},{7,11},{8,4},{9,5},... | collective-permute-start | bytes 122888 | tf_op jit(solution)/shard_map/ppermute | solution.py:324
  6.7 0.0 collective-permute-start.2
  6.7 0.6 %collective-permute-start.1 = (bf16[80,256]{1,0:T(8,128)(2,1)S(1)}, bf16[80,256]{1,0:T(8,128)(2,1)S(1)}, u32[]{:S(2)}, u32[]{:S(2)}) collective-permute-start(bf16[80,256]{1,0:T(8,128)(2,1)S(1)} %get-tuple-element.22.own_ref.v0_ref), channel_id=1, source_target_pairs={{0,4},{1,5},{2,6},{3,7},{4,0},{5,1},{6,2},{7,3},{8,12},{9,13},{10,... | collective-permute-start | bytes 122888 | tf_op jit(solution)/shard_map/ppermute | solution.py:324
  7.4 1.6 %collective-permute-start = (f32[3,256]{1,0:T(4,128)S(1)}, f32[3,256]{1,0:T(4,128)S(1)}, u32[]{:S(2)}, u32[]{:S(2)}) collective-permute-start(f32[3,256]{1,0:T(4,128)S(1)} %get-tuple-element.21), channel_id=1, source_target_pairs={{0,2},{1,3},{2,0},{3,1},{4,6},{5,7},{6,4},{7,5},{8,10},{9,11},{10,... | collective-permute-start | bytes 9224 | tf_op jit(solution)/shard_map/ppermute | solution.py:324
  9.0 0.0 copy-done.3
  9.0 0.0 copy-done
  9.0 1.9 %collective-permute-done.far_ref = f32[3,256]{1,0:T(4,128)S(1)} collective-permute-done((f32[3,256]{1,0:T(4,128)S(1)}, f32[3,256]{1,0:T(4,128)S(1)}, u32[]{:S(2)}, u32[]{:S(2)}) %collective-permute-start) | collective-permute-done | bytes 3104 | tf_op jit(solution)/shard_map/ppermute | solution.py:324
  11.0 0.1 grid_rows.1.row_terms
  11.1 0.0 collective-permute-done.3.v3_ref
  11.1 0.5 %collective-permute-done.2.v2_ref = bf16[80,256]{1,0:T(8,128)(2,1)S(1)} collective-permute-done((bf16[80,256]{1,0:T(8,128)(2,1)S(1)}, bf16[80,256]{1,0:T(8,128)(2,1)S(1)}, u32[]{:S(2)}, u32[]{:S(2)}) %collective-permute-start.2) | collective-permute-done | bytes 40992 | tf_op jit(solution)/shard_map/ppermute | solution.py:324
  11.6 0.0 collective-permute-done.1.v1_ref
  11.6 0.1 collective-permute-start.4
  11.7 1.1 %grid_near.1 = (bf16[8,256,256]{2,1,0:T(8,128)(2,1)S(1)}, f32[2,64,256]{2,1,0:T(8,128)S(1)}) custom-call(s32[1]{0:T(128)} %bitcast.me_ref, bf16[4,80,256]{2,1,0:T(8,128)(2,1)S(1)} %grid_pack.1.packed_ref, bf16[2,256,32]{2,1,0:T(8,128)(2,1)S(1)} %grid_rows.1.row_terms, f32[64,256]{1,0:T(8,128)S(1)} %broadcast_multiply_fusion.boost_ref), custom_call_target="tpu_custom_call" | custom-call | tf_op jit(solution)/shard_map/grid_near/pallas_call | solution.py:333
  12.9 0.2 collective-permute-done.4.core_ref
  13.1 1.0 %grid_rest.1 = (bf16[8,256,256]{2,1,0:T(8,128)(2,1)S(1)}, f32[2,64,256]{2,1,0:T(8,128)S(1)}, bf16[144,256]{1,0:T(8,128)(2,1)S(1)}) custom-call(s32[1]{0:T(128)} %bitcast.me_ref, bf16[4,80,256]{2,1,0:T(8,128)(2,1)S(1)} %grid_pack.1.packed_ref, bf16[4,80,256]{2,1,0:T(8,128)(2,1)S(1)} %collective-permute-done.4.core_ref, ...), custom_call_target="tpu_custom_call" | custom-call | tf_op jit(solution)/shard_map/grid_rest/pallas_call | solution.py:333
  14.1 1.6 %collective-permute-start.5 = (bf16[144,256]{1,0:T(8,128)(2,1)S(1)}, bf16[144,256]{1,0:T(8,128)(2,1)S(1)}, u32[]{:S(2)}, u32[]{:S(2)}) collective-permute-start(bf16[144,256]{1,0:T(8,128)(2,1)S(1)} %get-tuple-element.29), channel_id=1, source_target_pairs={{0,2},{1,3},{2,0},{3,1},{4,6},{5,7},{6,4},{7,5},{8,10},{9,11},{10,... | collective-permute-start | bytes 221192 | tf_op jit(solution)/shard_map/ppermute | solution.py:324
  15.6 2.9 %collective-permute-done.5.far_ref = bf16[144,256]{1,0:T(8,128)(2,1)S(1)} collective-permute-done((bf16[144,256]{1,0:T(8,128)(2,1)S(1)}, bf16[144,256]{1,0:T(8,128)(2,1)S(1)}, u32[]{:S(2)}, u32[]{:S(2)}) %collective-permute-start.5) | collective-permute-done | bytes 73760 | tf_op jit(solution)/shard_map/ppermute | solution.py:324
  18.6 0.3 %grid_second.1 = (bf16[2,64,256]{2,1,0:T(8,128)(2,1)S(1)}, bf16[4,64,256]{2,1,0:T(8,128)(2,1)S(1)}) custom-call(bf16[8,256,256]{2,1,0:T(8,128)(2,1)S(1)} %get-tuple-element.27.rest_ref, f32[2,64,256]{2,1,0:T(8,128)S(1)} %get-tuple-element.28.partial_ref, bf16[4,80,256]{2,1,0:T(8,128)(2,1)S(1)} %grid_pack.1.packed_ref, ...), custom_call_target="tpu_custom_call" | custom-call | tf_op jit(solution)/shard_map/grid_second/pallas_call | solution.py:333
  18.9 0.1 collective-permute-start.6
  19.0 0.3 %grid_third.1.sum_ref = f32[4,64,256]{2,1,0:T(8,128)S(1)} custom-call(bf16[8,256,256]{2,1,0:T(8,128)(2,1)S(1)} %get-tuple-element.25.near_ref, bf16[2,64,256]{2,1,0:T(8,128)(2,1)S(1)} %get-tuple-element.30.scaled_ref), custom_call_target="tpu_custom_call" | custom-call | tf_op jit(solution)/shard_map/grid_third/pallas_call | solution.py:333
  19.3 0.0 copy-start.1
  19.3 0.0 copy-start.2
  19.3 1.0 %collective-permute-done.6.core_ref = bf16[4,64,256]{2,1,0:T(8,128)(2,1)S(1)} collective-permute-done((bf16[4,64,256]{2,1,0:T(8,128)(2,1)S(1)}, bf16[4,64,256]{2,1,0:T(8,128)(2,1)S(1)}, u32[]{:S(2)}, u32[]{:S(2)}) %collective-permute-start.6) | collective-permute-done | bytes 131104 | tf_op jit(solution)/shard_map/ppermute | solution.py:324
  20.3 3.3 %collective-permute-start.7 = (bf16[64,256]{1,0:T(8,128)(2,1)S(1)}, bf16[64,256]{1,0:T(8,128)(2,1)S(1)}, u32[]{:S(2)}, u32[]{:S(2)}) collective-permute-start(bf16[64,256]{1,0:T(8,128)(2,1)S(1)} %get-tuple-element.32), channel_id=1, source_target_pairs={{0,12},{1,13},{2,14},{3,15},{4,8},{5,9},{6,10},{7,11},{8,4},{9,5},... | collective-permute-start | bytes 98312 | tf_op jit(solution)/shard_map/ppermute | solution.py:324
  23.7 0.0 collective-permute-start.8
  23.7 0.0 copy-start.4
  23.7 1.1 %collective-permute-start.9 = (bf16[64,256]{1,0:T(8,128)(2,1)S(1)}, bf16[64,256]{1,0:T(8,128)(2,1)S(1)}, u32[]{:S(2)}, u32[]{:S(2)}) collective-permute-start(bf16[64,256]{1,0:T(8,128)(2,1)S(1)} %get-tuple-element.34), channel_id=1, source_target_pairs={{0,4},{1,5},{2,6},{3,7},{4,0},{5,1},{6,2},{7,3},{8,12},{9,13},{10,... | collective-permute-start | bytes 98312 | tf_op jit(solution)/shard_map/ppermute | solution.py:324
  24.8 1.6 %collective-permute-done.7.q3_ref = bf16[64,256]{1,0:T(8,128)(2,1)S(1)} collective-permute-done((bf16[64,256]{1,0:T(8,128)(2,1)S(1)}, bf16[64,256]{1,0:T(8,128)(2,1)S(1)}, u32[]{:S(2)}, u32[]{:S(2)}) %collective-permute-start.7) | collective-permute-done | bytes 32800 | tf_op jit(solution)/shard_map/ppermute | solution.py:324
  26.4 2.1 %collective-permute-done.8.q2_ref = bf16[64,256]{1,0:T(8,128)(2,1)S(1)} collective-permute-done((bf16[64,256]{1,0:T(8,128)(2,1)S(1)}, bf16[64,256]{1,0:T(8,128)(2,1)S(1)}, u32[]{:S(2)}, u32[]{:S(2)}) %collective-permute-start.8) | collective-permute-done | bytes 32800 | tf_op jit(solution)/shard_map/ppermute | solution.py:324
  28.5 0.0 collective-permute-done.9.q1_ref
  28.5 0.0 copy-done.1
  28.5 0.0 copy-done.2
  28.5 0.0 copy-done.4
  28.5 0.7 %grid_last.1 = (f32[64,256]{1,0:T(8,128)}, f32[1,256]{1,0:T(1,128)}) custom-call(bf16[64,256]{1,0:T(8,128)(2,1)S(1)} %collective-permute-done.7.q3_ref, bf16[64,256]{1,0:T(8,128)(2,1)S(1)} %collective-permute-done.8.q2_ref, bf16[64,256]{1,0:T(8,128)(2,1)S(1)} %collective-permute-done.9.q1_ref, f32[64,256]{1,0:T(8,128)S(1)} %get-tuple-element.35.q0_ref, ...), custom_call_target="tpu_custom_call" | custom-call | tf_op jit(solution)/shard_map/grid_last/pallas_call | solution.py:333
  (4 shorter events, 0.0 us)
Async XLA Ops:
  0.6 8.4 %copy-start = (f32[64,256]{1,0:T(8,128)S(1)}, f32[64,256]{1,0:T(8,128)}, u32[]{:S(2)}) copy-start(f32[64,256]{1,0:T(8,128)} %rest_0_.1) | copy-start | bytes 196612
  1.6 7.4 %copy-start.3 = (f32[256]{0:T(256)S(1)}, f32[256]{0:T(256)}, u32[]{:S(2)}) copy-start(f32[256]{0:T(256)} %param.11) | copy-start | bytes 3076
  1.6 9.5 %collective-permute-start.3 = (bf16[80,256]{1,0:T(8,128)(2,1)S(1)}, bf16[80,256]{1,0:T(8,128)(2,1)S(1)}, u32[]{:S(2)}, u32[]{:S(2)}) collective-permute-start(bf16[80,256]{1,0:T(8,128)(2,1)S(1)} %get-tuple-element.22.own_ref.v0_ref), channel_id=1, source_target_pairs={{0,12},{1,13},{2,14},{3,15},{4,8},{5,9},{6,10},{7,11},{8,4},{9,5},... | collective-permute-start | bytes 122888 | tf_op jit(solution)/shard_map/ppermute | solution.py:324
  6.7 4.9 %collective-permute-start.2 = (bf16[80,256]{1,0:T(8,128)(2,1)S(1)}, bf16[80,256]{1,0:T(8,128)(2,1)S(1)}, u32[]{:S(2)}, u32[]{:S(2)}) collective-permute-start(bf16[80,256]{1,0:T(8,128)(2,1)S(1)} %get-tuple-element.22.own_ref.v0_ref), channel_id=1, source_target_pairs={{0,8},{1,9},{2,10},{3,11},{4,12},{5,13},{6,14},{7,15},{8,0},{9,1},... | collective-permute-start | bytes 122888 | tf_op jit(solution)/shard_map/ppermute | solution.py:324
  6.7 4.9 %collective-permute-start.1 = (bf16[80,256]{1,0:T(8,128)(2,1)S(1)}, bf16[80,256]{1,0:T(8,128)(2,1)S(1)}, u32[]{:S(2)}, u32[]{:S(2)}) collective-permute-start(bf16[80,256]{1,0:T(8,128)(2,1)S(1)} %get-tuple-element.22.own_ref.v0_ref), channel_id=1, source_target_pairs={{0,4},{1,5},{2,6},{3,7},{4,0},{5,1},{6,2},{7,3},{8,12},{9,13},{10,... | collective-permute-start | bytes 122888 | tf_op jit(solution)/shard_map/ppermute | solution.py:324
  7.4 3.6 %collective-permute-start = (f32[3,256]{1,0:T(4,128)S(1)}, f32[3,256]{1,0:T(4,128)S(1)}, u32[]{:S(2)}, u32[]{:S(2)}) collective-permute-start(f32[3,256]{1,0:T(4,128)S(1)} %get-tuple-element.21), channel_id=1, source_target_pairs={{0,2},{1,3},{2,0},{3,1},{4,6},{5,7},{6,4},{7,5},{8,10},{9,11},{10,... | collective-permute-start | bytes 9224 | tf_op jit(solution)/shard_map/ppermute | solution.py:324
  11.6 1.5 %collective-permute-start.4 = (bf16[4,80,256]{2,1,0:T(8,128)(2,1)S(1)}, bf16[4,80,256]{2,1,0:T(8,128)(2,1)S(1)}, u32[]{:S(2)}, u32[]{:S(2)}) collective-permute-start(bf16[4,80,256]{2,1,0:T(8,128)(2,1)S(1)} %grid_pack.1.packed_ref), channel_id=1, source_target_pairs={{0,1},{1,0},{2,3},{3,2},{4,5},{5,4},{6,7},{7,6},{8,9},{9,8},{10,11... | collective-permute-start | bytes 491528 | tf_op jit(solution)/shard_map/ppermute | solution.py:324
  14.1 4.5 %collective-permute-start.5 = (bf16[144,256]{1,0:T(8,128)(2,1)S(1)}, bf16[144,256]{1,0:T(8,128)(2,1)S(1)}, u32[]{:S(2)}, u32[]{:S(2)}) collective-permute-start(bf16[144,256]{1,0:T(8,128)(2,1)S(1)} %get-tuple-element.29), channel_id=1, source_target_pairs={{0,2},{1,3},{2,0},{3,1},{4,6},{5,7},{6,4},{7,5},{8,10},{9,11},{10,... | collective-permute-start | bytes 221192 | tf_op jit(solution)/shard_map/ppermute | solution.py:324
  18.9 1.4 %collective-permute-start.6 = (bf16[4,64,256]{2,1,0:T(8,128)(2,1)S(1)}, bf16[4,64,256]{2,1,0:T(8,128)(2,1)S(1)}, u32[]{:S(2)}, u32[]{:S(2)}) collective-permute-start(bf16[4,64,256]{2,1,0:T(8,128)(2,1)S(1)} %get-tuple-element.31), channel_id=1, source_target_pairs={{0,1},{1,0},{2,3},{3,2},{4,5},{5,4},{6,7},{7,6},{8,9},{9,8},{10,11... | collective-permute-start | bytes 393224 | tf_op jit(solution)/shard_map/ppermute | solution.py:324
  19.3 9.2 %copy-start.1 = (bf16[64,256]{1,0:T(8,128)(2,1)S(1)}, bf16[64,256]{1,0:T(8,128)(2,1)}, u32[]{:S(2)}) copy-start(bf16[64,256]{1,0:T(8,128)(2,1)} %rest_3_.1) | copy-start | bytes 98308
  19.3 9.2 %copy-start.2 = (bf16[64,256]{1,0:T(8,128)(2,1)S(1)}, bf16[64,256]{1,0:T(8,128)(2,1)}, u32[]{:S(2)}) copy-start(bf16[64,256]{1,0:T(8,128)(2,1)} %rest_4_.1) | copy-start | bytes 98308
  20.3 6.1 %collective-permute-start.7 = (bf16[64,256]{1,0:T(8,128)(2,1)S(1)}, bf16[64,256]{1,0:T(8,128)(2,1)S(1)}, u32[]{:S(2)}, u32[]{:S(2)}) collective-permute-start(bf16[64,256]{1,0:T(8,128)(2,1)S(1)} %get-tuple-element.32), channel_id=1, source_target_pairs={{0,12},{1,13},{2,14},{3,15},{4,8},{5,9},{6,10},{7,11},{8,4},{9,5},... | collective-permute-start | bytes 98312 | tf_op jit(solution)/shard_map/ppermute | solution.py:324
  23.7 4.8 %collective-permute-start.8 = (bf16[64,256]{1,0:T(8,128)(2,1)S(1)}, bf16[64,256]{1,0:T(8,128)(2,1)S(1)}, u32[]{:S(2)}, u32[]{:S(2)}) collective-permute-start(bf16[64,256]{1,0:T(8,128)(2,1)S(1)} %get-tuple-element.33), channel_id=1, source_target_pairs={{0,8},{1,9},{2,10},{3,11},{4,12},{5,13},{6,14},{7,15},{8,0},{9,1},... | collective-permute-start | bytes 98312 | tf_op jit(solution)/shard_map/ppermute | solution.py:324
  23.7 4.8 %copy-start.4 = (f32[256]{0:T(256)S(1)}, f32[256]{0:T(256)}, u32[]{:S(2)}) copy-start(f32[256]{0:T(256)} %param.10) | copy-start | bytes 3076
  23.7 4.8 %collective-permute-start.9 = (bf16[64,256]{1,0:T(8,128)(2,1)S(1)}, bf16[64,256]{1,0:T(8,128)(2,1)S(1)}, u32[]{:S(2)}, u32[]{:S(2)}) collective-permute-start(bf16[64,256]{1,0:T(8,128)(2,1)S(1)} %get-tuple-element.34), channel_id=1, source_target_pairs={{0,4},{1,5},{2,6},{3,7},{4,0},{5,1},{6,2},{7,3},{8,12},{9,13},{10,... | collective-permute-start | bytes 98312 | tf_op jit(solution)/shard_map/ppermute | solution.py:324
